TPU v7x, 32 devices: a whole 2x2x4 slice. The times are simulated.
32 devices in a mesh: seq: 4 (over y, core), dp: 8 (over z, x).
Axes of the slice: x: 2, y: 2, z: 4, core: 2. Of those that a mesh axis runs over, the one named last changes fastest.
Arguments:
- tokens: bfloat16 [16, 1024, 1024], P('dp', 'seq'), may hold values from -6 to 6
- first_values: bfloat16 [16, 1024, 1024], P('dp', 'seq'), may hold values from -6 to 6
- seq_counts: int32 [8], P('dp'), may hold values from 1 to 2, as said below
- norm1_gain: bfloat16 [1024], P('dp'), may hold values from 0.5 to 1.5
- query_weight: bfloat16 [1024, 1024], P('dp', 'seq'), may hold values from -0.1875 to 0.1875
- key_weight: bfloat16 [1024, 1024], P('dp', 'seq'), may hold values from -0.1875 to 0.1875
- value_weight: bfloat16 [1024, 1024], P('dp', 'seq'), may hold values from -0.1875 to 0.1875
- out_weight: bfloat16 [1024, 1024], P('dp', 'seq'), may hold values from -1.5 to 1.5
- norm2_gain: bfloat16 [1024], P('dp'), may hold values from 0.5 to 1.5
- gate_weight: bfloat16 [1024, 2816], P('dp', 'seq'), may hold values from -0.1875 to 0.1875
- up_weight: bfloat16 [1024, 2816], P('dp', 'seq'), may hold values from -0.1875 to 0.1875
- down_weight: bfloat16 [2816, 1024], P('dp', 'seq'), may hold values from -0.109375 to 0.109375
- output_cotangent: bfloat16 [16, 1024, 1024], P('dp', 'seq'), may hold values from -6 to 6
Outputs:
- output: bfloat16 [16, 1024, 1024], P('dp', 'seq')
- input_grad: float32 [16, 1024, 1024], P('dp', 'seq')
- first_values_grad: float32 [16, 1024, 1024], P('dp', 'seq')
- norm1_gain_grad: float32 [1024], P('dp')
- query_weight_grad: float32 [1024, 1024], P('dp', 'seq')
- key_weight_grad: float32 [1024, 1024], P('dp', 'seq')
- value_weight_grad: float32 [1024, 1024], P('dp', 'seq')
- out_weight_grad: float32 [1024, 1024], P('dp', 'seq')
- norm2_gain_grad: float32 [1024], P('dp')
- gate_weight_grad: float32 [1024, 2816], P('dp', 'seq')
- up_weight_grad: float32 [1024, 2816], P('dp', 'seq')
- down_weight_grad: float32 [2816, 1024], P('dp', 'seq')
Inputs may be any that keep to these rules, and one draw needn't show every extreme that they name: `seq_counts`: sequence s is slot s mod 2 of group s // 2; a group's live sequences fill its first slots. Some group uses all 2 slots and some group uses one.
All inputs are finite; a program needn't handle non-finite values.
Results may differ from a plain program's by a relative error of at most 0.019.
Values may be sent and summed in bfloat16 or wider, within the bound.
No kernel may reach another device: no remote copies, remote signals or barrier semaphores. Data moves between devices by JAX's collectives and lax.ppermute only.
A program may use at most 256 MiB of HBM per device.

v0:
```python
import jax
import jax.numpy as jnp
from jax import lax
from jax.sharding import PartitionSpec as P

HEADS = 16


EPSILON = 1e-06


def from_behind(shard, axis, by):
    devices = lax.axis_size(axis)
    pairs = [(i, i + by) for i in range(devices) if 0 <= i + by < devices]
    return lax.ppermute(shard, axis, pairs)


def passed_along(block, axis, distance):
    devices = range(lax.axis_size(axis))
    route = [((i - distance) % len(devices), i) for i in devices]
    return lax.ppermute(block, axis, route)


def scaled_norm(values, gain_vec):
    inverse = lax.rsqrt(jnp.mean(values * values, axis=-1, keepdims=True) + EPSILON)
    return values * inverse * gain_vec


def rotate(values, positions, head_count, direction):
    row_count, model_width = values.shape
    head_size = model_width // head_count
    half_size = head_size // 2
    frequency = 10000.0 ** (-(jnp.arange(half_size).astype(jnp.float32) * 2.0) / head_size)
    angles = positions.astype(jnp.float32)[:, None] * frequency[None, :]
    cosine = jnp.cos(angles)[:, None, :]
    sine_part = direction * jnp.sin(angles)[:, None, :]
    shaped = values.reshape(row_count, head_count, head_size)
    first_half = shaped[..., :half_size]
    second = shaped[..., half_size:]
    turned = jnp.concatenate(
        [first_half * cosine - second * sine_part, second * cosine + first_half * sine_part],
        axis=-1,
    )
    return turned.reshape(row_count, model_width)


def swiglu(gate_in, up_in):
    return jax.nn.silu(gate_in) * up_in


def dot_plain(left, right):
    return jnp.dot(left, right, preferred_element_type=jnp.float32)


def dot_rows(left, right):
    return lax.dot_general(
        left, right, (((0,), (0,)), ((), ())), preferred_element_type=jnp.float32
    )


def dot_cols(left, right):
    return lax.dot_general(
        left, right, (((1,), (1,)), ((), ())), preferred_element_type=jnp.float32
    )


def on_device(
    tokens,
    first_values,
    seq_counts,
    norm1_gain,
    query_weight,
    key_weight,
    value_weight,
    out_weight,
    norm2_gain,
    gate_weight,
    up_weight,
    down_weight,
    output_cotangent,
):
    slot_count, seg_tokens, model_width = tokens.shape
    row_count = slot_count * seg_tokens
    head_count = HEADS
    head_size = model_width // head_count
    piece_count = lax.axis_size("seq")
    place = lax.axis_index("seq")
    attn_rows = (
        lax.all_gather(norm1_gain, "dp", axis=0, tiled=True),
        lax.all_gather(query_weight, "dp", axis=0, tiled=True),
        lax.all_gather(key_weight, "dp", axis=0, tiled=True),
        lax.all_gather(value_weight, "dp", axis=0, tiled=True),
        lax.all_gather(out_weight, "dp", axis=0, tiled=True),
    )
    gain_one = attn_rows[0]
    w_query, w_key, w_value, w_out = (
        lax.all_gather(attn_rows[1], "seq", axis=1, tiled=True),
        lax.all_gather(attn_rows[2], "seq", axis=1, tiled=True),
        lax.all_gather(attn_rows[3], "seq", axis=1, tiled=True),
        lax.all_gather(attn_rows[4], "seq", axis=1, tiled=True),
    )
    ffn_rows = (
        lax.all_gather(norm2_gain, "dp", axis=0, tiled=True),
        lax.all_gather(gate_weight, "dp", axis=0, tiled=True),
        lax.all_gather(up_weight, "dp", axis=0, tiled=True),
        lax.all_gather(down_weight, "dp", axis=0, tiled=True),
    )
    gain_two = ffn_rows[0]
    w_gate, w_up, w_down = (
        lax.all_gather(ffn_rows[1], "seq", axis=1, tiled=True),
        lax.all_gather(ffn_rows[2], "seq", axis=1, tiled=True),
        lax.all_gather(ffn_rows[3], "seq", axis=1, tiled=True),
    )
    live_rows = (jnp.arange(row_count) // seg_tokens < seq_counts[0]).astype(jnp.float32)[:, None]
    local_pos = jnp.arange(seg_tokens)
    positions = place * seg_tokens + jnp.tile(local_pos, slot_count)
    inputs = tokens.astype(jnp.float32).reshape(row_count, model_width)
    gain_first = gain_one.astype(jnp.float32)
    h_first = scaled_norm(inputs, gain_first).astype(jnp.bfloat16)
    query = rotate(dot_plain(h_first, w_query), positions, head_count, 1.0).astype(jnp.bfloat16)
    key_rot = rotate(dot_plain(h_first, w_key), positions, head_count, 1.0).astype(jnp.bfloat16)
    own_first = first_values.astype(jnp.float32).reshape(row_count, model_width)
    blended = (0.5 * dot_plain(h_first, w_value) + 0.5 * own_first).astype(jnp.bfloat16)
    held_pair = jnp.stack(
        [
            key_rot.reshape(slot_count, seg_tokens, model_width),
            blended.reshape(slot_count, seg_tokens, model_width),
        ]
    )
    stored = [held_pair]
    for hop_index in range(1, piece_count):
        held_pair = from_behind(held_pair, "seq", 1)
        stored.append(held_pair)
    query_heads = query.reshape(slot_count, seg_tokens, head_count, head_size)

    def piece_scores(hop_index):
        source = (place - hop_index) % piece_count
        key_rows = stored[hop_index][0].reshape(slot_count, seg_tokens, head_count, head_size)
        value_rows = stored[hop_index][1].reshape(slot_count, seg_tokens, head_count, head_size)
        raw_scores = (
            jnp.einsum("sqhd,skhd->shqk", query_heads, key_rows, preferred_element_type=jnp.float32)
            * 0.125
        )
        visible = (
            source * seg_tokens + local_pos[None, :] <= place * seg_tokens + local_pos[:, None]
        )
        masked = jnp.where(visible, raw_scores, -1e30)
        return (source, key_rows, value_rows, masked, visible)

    running_max = jnp.full((slot_count, head_count, seg_tokens), -1e30, jnp.float32)
    running_sum = jnp.zeros((slot_count, head_count, seg_tokens), jnp.float32)
    for hop_index in range(piece_count):
        source, key_rows, value_rows, masked, visible = piece_scores(hop_index)
        new_max = jnp.maximum(running_max, jnp.max(masked, axis=-1))
        running_sum = running_sum * jnp.exp(running_max - new_max) + jnp.sum(
            jnp.exp(masked - new_max[..., None]), axis=-1
        )
        running_max = new_max
    log_total = running_max + jnp.log(running_sum)
    mixed = jnp.zeros((slot_count, seg_tokens, head_count, head_size), jnp.float32)
    for hop_index in range(piece_count):
        source, key_rows, value_rows, masked, visible = piece_scores(hop_index)
        prob_low = jnp.where(visible, jnp.exp(masked - log_total[..., None]), 0.0).astype(
            jnp.bfloat16
        )
        mixed = mixed + jnp.einsum(
            "shqk,skhd->sqhd", prob_low, value_rows, preferred_element_type=jnp.float32
        )
    attended = mixed.reshape(row_count, model_width).astype(jnp.bfloat16)
    middle = inputs + dot_plain(attended, w_out)
    gain_second = gain_two.astype(jnp.float32)
    h_second = scaled_norm(middle, gain_second).astype(jnp.bfloat16)
    gate = dot_plain(h_second, w_gate)
    up_part = dot_plain(h_second, w_up)
    hidden = swiglu(gate, up_part).astype(jnp.bfloat16)
    result = dot_plain(hidden, w_down)
    output = (
        (live_rows * (middle + result))
        .reshape(slot_count, seg_tokens, model_width)
        .astype(jnp.bfloat16)
    )
    grad_out = output_cotangent.astype(jnp.float32).reshape(row_count, model_width) * live_rows
    grad_low = grad_out.astype(jnp.bfloat16)
    grad_wdown = dot_rows(hidden, grad_low)
    grad_hidden = dot_cols(grad_low, w_down)
    _, swiglu_back = jax.vjp(swiglu, gate, up_part)
    grad_gate, grad_up = swiglu_back(grad_hidden)
    grad_gate = grad_gate.astype(jnp.bfloat16)
    grad_up = grad_up.astype(jnp.bfloat16)
    grad_wgate = dot_rows(h_second, grad_gate)
    grad_wup = dot_rows(h_second, grad_up)
    grad_hsecond = dot_cols(grad_gate, w_gate) + dot_cols(grad_up, w_up)
    _, second_back = jax.vjp(scaled_norm, middle, gain_second)
    grad_mid_norm, grad_gain_two = second_back(grad_hsecond)
    grad_middle = grad_out + grad_mid_norm
    grad_branch = grad_middle.astype(jnp.bfloat16)
    grad_wout = dot_rows(attended, grad_branch)
    grad_att = (
        dot_cols(grad_branch, w_out)
        .astype(jnp.bfloat16)
        .reshape(slot_count, seg_tokens, head_count, head_size)
    )
    delta = jnp.einsum("sqhd,sqhd->shq", grad_att.astype(jnp.float32), mixed)
    grad_query_acc = jnp.zeros((slot_count, seg_tokens, head_count, head_size), jnp.float32)
    carried = jnp.zeros((2, slot_count, seg_tokens, model_width), jnp.float32)
    for hop_index in range(piece_count):
        source, key_rows, value_rows, masked, visible = piece_scores(hop_index)
        prob_full = jnp.where(visible, jnp.exp(masked - log_total[..., None]), 0.0)
        grad_probs = jnp.einsum(
            "sqhd,skhd->shqk", grad_att, value_rows, preferred_element_type=jnp.float32
        )
        grad_vals = jnp.einsum(
            "shqk,sqhd->skhd",
            prob_full.astype(jnp.bfloat16),
            grad_att,
            preferred_element_type=jnp.float32,
        )
        grad_scores = (prob_full * (grad_probs - delta[..., None])).astype(jnp.bfloat16)
        grad_query_acc = grad_query_acc + 0.125 * jnp.einsum(
            "shqk,skhd->sqhd", grad_scores, key_rows, preferred_element_type=jnp.float32
        )
        grad_keys = 0.125 * jnp.einsum(
            "shqk,sqhd->skhd", grad_scores, query_heads, preferred_element_type=jnp.float32
        )
        grad_term = jnp.stack(
            [
                grad_keys.reshape(slot_count, seg_tokens, model_width),
                grad_vals.reshape(slot_count, seg_tokens, model_width),
            ]
        )
        carried = passed_along((carried + grad_term).astype(jnp.bfloat16), "seq", 1).astype(
            jnp.float32
        )
    grad_krot = carried[0].reshape(row_count, model_width)
    grad_blend = carried[1].reshape(row_count, model_width)
    grad_query = rotate(
        grad_query_acc.reshape(row_count, model_width), positions, head_count, -1.0
    ).astype(jnp.bfloat16)
    grad_key = rotate(grad_krot, positions, head_count, -1.0).astype(jnp.bfloat16)
    grad_value = (0.5 * grad_blend).astype(jnp.bfloat16)
    grad_first_vals = (0.5 * grad_blend).reshape(slot_count, seg_tokens, model_width)
    grad_wquery = dot_rows(h_first, grad_query)
    grad_wkey = dot_rows(h_first, grad_key)
    grad_wvalue = dot_rows(h_first, grad_value)
    grad_hfirst = (
        dot_cols(grad_query, w_query) + dot_cols(grad_key, w_key) + dot_cols(grad_value, w_value)
    )
    _, first_back = jax.vjp(scaled_norm, inputs, gain_first)
    grad_in_norm, grad_gain_one = first_back(grad_hfirst)
    grad_inputs = (grad_middle + grad_in_norm).reshape(slot_count, seg_tokens, model_width)
    tiled_one = jnp.tile(grad_gain_one, piece_count).reshape(1, -1)
    tiled_two = jnp.tile(grad_gain_two, piece_count).reshape(1, -1)
    summed_seq = (
        lax.psum_scatter(
            tiled_one.astype(jnp.bfloat16), "seq", scatter_dimension=1, tiled=True
        ).astype(jnp.float32),
        lax.psum_scatter(
            grad_wquery.astype(jnp.bfloat16), "seq", scatter_dimension=1, tiled=True
        ).astype(jnp.float32),
        lax.psum_scatter(
            grad_wkey.astype(jnp.bfloat16), "seq", scatter_dimension=1, tiled=True
        ).astype(jnp.float32),
        lax.psum_scatter(
            grad_wvalue.astype(jnp.bfloat16), "seq", scatter_dimension=1, tiled=True
        ).astype(jnp.float32),
        lax.psum_scatter(
            grad_wout.astype(jnp.bfloat16), "seq", scatter_dimension=1, tiled=True
        ).astype(jnp.float32),
        lax.psum_scatter(
            tiled_two.astype(jnp.bfloat16), "seq", scatter_dimension=1, tiled=True
        ).astype(jnp.float32),
        lax.psum_scatter(
            grad_wgate.astype(jnp.bfloat16), "seq", scatter_dimension=1, tiled=True
        ).astype(jnp.float32),
        lax.psum_scatter(
            grad_wup.astype(jnp.bfloat16), "seq", scatter_dimension=1, tiled=True
        ).astype(jnp.float32),
        lax.psum_scatter(
            grad_wdown.astype(jnp.bfloat16), "seq", scatter_dimension=1, tiled=True
        ).astype(jnp.float32),
    )
    finished = (
        lax.psum_scatter(summed_seq[0].reshape(-1), "dp", scatter_dimension=0, tiled=True),
        lax.psum_scatter(summed_seq[1], "dp", scatter_dimension=0, tiled=True),
        lax.psum_scatter(summed_seq[2], "dp", scatter_dimension=0, tiled=True),
        lax.psum_scatter(summed_seq[3], "dp", scatter_dimension=0, tiled=True),
        lax.psum_scatter(summed_seq[4], "dp", scatter_dimension=0, tiled=True),
        lax.psum_scatter(summed_seq[5].reshape(-1), "dp", scatter_dimension=0, tiled=True),
        lax.psum_scatter(summed_seq[6], "dp", scatter_dimension=0, tiled=True),
        lax.psum_scatter(summed_seq[7], "dp", scatter_dimension=0, tiled=True),
        lax.psum_scatter(summed_seq[8], "dp", scatter_dimension=0, tiled=True),
    )
    gain_sum_one = finished[0]
    gain_sum_two = finished[5]
    return (
        output,
        grad_inputs,
        grad_first_vals,
        gain_sum_one,
        finished[1],
        finished[2],
        finished[3],
        finished[4],
        gain_sum_two,
        finished[6],
        finished[7],
        finished[8],
    )


def solution(mesh):
    return jax.shard_map(
        on_device,
        mesh=mesh,
        in_specs=(
            P("dp", "seq", None),
            P("dp", "seq", None),
            P("dp"),
            P("dp"),
            P("dp", "seq"),
            P("dp", "seq"),
            P("dp", "seq"),
            P("dp", "seq"),
            P("dp"),
            P("dp", "seq"),
            P("dp", "seq"),
            P("dp", "seq"),
            P("dp", "seq", None),
        ),
        out_specs=(
            P("dp", "seq", None),
            P("dp", "seq", None),
            P("dp", "seq", None),
            P("dp"),
            P("dp", "seq"),
            P("dp", "seq"),
            P("dp", "seq"),
            P("dp", "seq"),
            P("dp"),
            P("dp", "seq"),
            P("dp", "seq"),
            P("dp", "seq"),
        ),
        check_vma=False,
    )
```

profile of v0, /device:TPU:0, one launch (start us, length us, event | category | flops | bytes accessed | tf_op | source)
XLA Modules:
  0.0 1428.2 jit_solution(66438624774911545)
XLA Ops:
  8.7 36.2 %all_gather.53 = bf16[1024,256]{1,0:T(8,128)(2,1)} all-gather(bf16[128,256]{1,0:T(8,128)(2,1)} %param.18), channel_id=1, replica_groups=mesh['seq'=4,'dp'=8] {'dp'}, dimensions={0}, use_global_device_ids=true | all-gather | bytes 589824 | tf_op jit(solution)/shard_map/all_gather | solution.py:91
  45.0 34.3 %all_gather.49 = bf16[1024,256]{1,0:T(8,128)(2,1)} all-gather(bf16[128,256]{1,0:T(8,128)(2,1)} %param.19), channel_id=1, replica_groups=mesh['seq'=4,'dp'=8] {'dp'}, dimensions={0}, use_global_device_ids=true | all-gather | bytes 589824 | tf_op jit(solution)/shard_map/all_gather | solution.py:92
  80.0 33.9 %all_gather.51 = bf16[1024,256]{1,0:T(8,128)(2,1)} all-gather(bf16[128,256]{1,0:T(8,128)(2,1)} %param.17), channel_id=1, replica_groups=mesh['seq'=4,'dp'=8] {'dp'}, dimensions={0}, use_global_device_ids=true | all-gather | bytes 589824 | tf_op jit(solution)/shard_map/all_gather | solution.py:90
  113.9 33.8 %all_gather.55 = bf16[1024,256]{1,0:T(8,128)(2,1)} all-gather(bf16[128,256]{1,0:T(8,128)(2,1)} %param.20), channel_id=1, replica_groups=mesh['seq'=4,'dp'=8] {'dp'}, dimensions={0}, use_global_device_ids=true | all-gather | bytes 589824 | tf_op jit(solution)/shard_map/all_gather | solution.py:93
  149.4 20.6 %all-gather = bf16[8,1,128]{2,1,0:T(2,128)(2,1)S(1)} all-gather(bf16[1,1,128]{2,1,0:T(2,128)(2,1)S(1)} %bitcast.298), channel_id=1, replica_groups=mesh['seq'=4,'dp'=8] {'dp'}, dimensions={0}, use_global_device_ids=true | all-gather | bytes 2304 | tf_op jit(solution)/shard_map/all_gather | solution.py:89
  183.1 3.5 fusion.19
  192.9 29.3 %collective-permute-start.1 = (bf16[2,2,256,1024]{3,2,1,0:T(8,128)(2,1)}, bf16[2,2,256,1024]{3,2,1,0:T(8,128)(2,1)}, u32[]{:S(2)}, u32[]{:S(2)}) collective-permute-start(bf16[2,2,256,1024]{3,2,1,0:T(8,128)(2,1)} %collective-permute-done), channel_id=1, source_target_pairs={{0,8},{8,16},{16,24},{1,9},{9,17},{17,25},{2,10},{10,18},{18,26},{... | collective-permute-start | bytes 6291464 | tf_op jit(solution)/shard_map/ppermute | solution.py:15
  222.2 16.1 %all-gather.1 = bf16[8,1,128]{2,1,0:T(2,128)(2,1)S(1)} all-gather(bf16[1,1,128]{2,1,0:T(2,128)(2,1)S(1)} %bitcast.299), channel_id=1, replica_groups=mesh['seq'=4,'dp'=8] {'dp'}, dimensions={0}, use_global_device_ids=true | all-gather | bytes 2304 | tf_op jit(solution)/shard_map/all_gather | solution.py:103
  240.7 4.0 copy.147
  248.0 14.7 %collective-permute-start.2 = (bf16[2,2,256,1024]{3,2,1,0:T(8,128)(2,1)}, bf16[2,2,256,1024]{3,2,1,0:T(8,128)(2,1)}, u32[]{:S(2)}, u32[]{:S(2)}) collective-permute-start(bf16[2,2,256,1024]{3,2,1,0:T(8,128)(2,1)} %collective-permute-done.1), channel_id=1, source_target_pairs={{0,8},{8,16},{16,24},{1,9},{9,17},{17,25},{2,10},{10,18},{18,26},{... | collective-permute-start | bytes 6291464 | tf_op jit(solution)/shard_map/ppermute | solution.py:15
  262.8 4.0 reshape.457
  266.8 3.5 copy.158
  270.4 4.7 fusion.8
  282.3 4.8 fusion.9
  294.3 4.8 fusion.10
  303.6 5.4 fusion.11
  311.4 7.9 exponential_reduce_fusion.2
  319.6 7.0 exponential_reduce_fusion
  328.9 6.0 fusion.87
  337.0 3.7 bitcast_convert_fusion
  343.1 3.3 multiply_reduce_fusion.2
  348.9 7.8 fusion.96
  356.7 5.9 all-gather.27.cloned.1.call-done
  362.6 8.8 fusion.97
  371.4 36.8 %all-gather.31.cloned.1.call-done = bf16[2816,1024]{1,0:T(8,128)(2,1)} async-done(((bf16[2816,256]{1,0:T(8,128)(2,1)}), bf16[2816,1024]{1,0:T(8,128)(2,1)}) %all-gather.31.cloned.1.call-update) | async-done | bytes 5767184 | tf_op jit(solution)/shard_map/all_gather | solution.py:112
  408.2 11.0 multiply_convert_fusion.4
  419.2 7.3 fusion.98
  426.6 3.6 multiply_reduce_fusion
  437.4 6.6 convolution_convert_fusion.7
  445.3 5.3 multiply_convert_fusion.3
  463.0 5.3 multiply_convert_fusion.2
  475.9 6.7 fusion.62
  488.5 5.0 fusion.12
  493.5 5.3 multiply_convert_fusion.1
  506.5 6.7 fusion.60
  519.2 5.0 fusion.13
  527.0 5.3 multiply_convert_fusion
  537.2 6.8 fusion.58
  547.1 8.2 collective-permute-done.5
  568.5 15.6 %collective-permute-done.6 = bf16[2,2,256,1024]{3,2,1,0:T(8,128)(2,1)S(1)} collective-permute-done((bf16[2,2,256,1024]{3,2,1,0:T(8,128)(2,1)S(1)}, bf16[2,2,256,1024]{3,2,1,0:T(8,128)(2,1)S(1)}, u32[]{:S(2)}, u32[]{:S(2)}) %collective-permute-start.6) | collective-permute-done | bytes 2097184 | tf_op jit(solution)/shard_map/ppermute | solution.py:21
  585.6 4.1 copy.207
  589.7 3.9 reshape_reshape_squeeze.3
  601.5 3.9 convolution_convert_fusion.6
  610.3 6.9 convolution_convert_fusion.2
  617.6 6.9 convolution_convert_fusion.1
  625.7 6.9 convolution_convert_fusion
  648.6 17.3 %reduce-scatter.21.cloned.1.call-done = bf16[1024,256]{1,0:T(8,128)(2,1)} async-done(((bf16[1024,1024]{1,0:T(8,128)(2,1)}), bf16[1024,256]{1,0:T(8,128)(2,1)}) %reduce-scatter.21.cloned.1.call-update) | async-done | bytes 524304 | tf_op jit(solution)/shard_map/reduce_scatter | solution.py:257
  668.1 31.8 %reduce-scatter.29.cloned.1.call-done = bf16[1024,256]{1,0:T(8,128)(2,1)} async-done(((bf16[1024,1024]{1,0:T(8,128)(2,1)}), bf16[1024,256]{1,0:T(8,128)(2,1)}) %reduce-scatter.29.cloned.1.call-update) | async-done | bytes 524304 | tf_op jit(solution)/shard_map/reduce_scatter | solution.py:263
  702.1 55.1 %reduce-scatter.37.cloned.1.call-done = bf16[1024,704]{0,1:T(8,128)(2,1)} async-done(((bf16[1024,2816]{0,1:T(8,128)(2,1)}), bf16[1024,704]{0,1:T(8,128)(2,1)}) %reduce-scatter.37.cloned.1.call-update) | async-done | bytes 1441808 | tf_op jit(solution)/shard_map/reduce_scatter | solution.py:272
  760.6 54.1 %reduce-scatter.41.cloned.1.call-done = bf16[1024,704]{0,1:T(8,128)(2,1)} async-done(((bf16[1024,2816]{0,1:T(8,128)(2,1)}), bf16[1024,704]{0,1:T(8,128)(2,1)}) %reduce-scatter.41.cloned.1.call-update) | async-done | bytes 1441808 | tf_op jit(solution)/shard_map/reduce_scatter | solution.py:275
  814.7 3.3 convert_element_type.331
  818.4 53.6 %reduce-scatter.45.cloned.1.call-done = bf16[2816,256]{1,0:T(8,128)(2,1)} async-done(((bf16[2816,1024]{1,0:T(8,128)(2,1)}), bf16[2816,256]{1,0:T(8,128)(2,1)}) %reduce-scatter.45.cloned.1.call-update) | async-done | bytes 1441808 | tf_op jit(solution)/shard_map/reduce_scatter | solution.py:278
  876.4 7.6 multiply_convert_fusion.7
  884.1 15.4 %reduce-scatter.51.cloned.1.call-done = bf16[1024,1]{1,0:T(8,128)(2,1)} async-done(((bf16[4096,1]{1,0:T(8,128)(2,1)}), bf16[1024,1]{1,0:T(8,128)(2,1)}) %reduce-scatter.51.cloned.1.call-update) | async-done | bytes 2064
  900.6 4.1 fusion.16
  904.7 22.2 %reduce-scatter.49.cloned.1.call-done = bf16[1024,1]{1,0:T(8,128)(2,1)} async-done(((bf16[4096,1]{1,0:T(8,128)(2,1)}), bf16[1024,1]{1,0:T(8,128)(2,1)}) %reduce-scatter.49.cloned.1.call-update) | async-done | bytes 2064
  928.1 21.7 %all-reduce.2 = (f32[1024]{0:T(1024)S(1)}, f32[1024]{0:T(1024)S(1)}) all-reduce(f32[1024]{0:T(1024)S(1)} %bitcast.296, f32[1024]{0:T(1024)S(1)} %bitcast.295), channel_id=3, replica_groups=mesh['seq'=4,'dp'=8] {'dp'}, use_global_device_ids=true, to_apply=%region_14.15.clone | all-reduce | flops 2048 | bytes 16384
  950.9 43.7 %reduce-scatter.35.cloned.1.call-done = f32[128,256]{1,0:T(8,128)} async-done(((f32[1024,256]{1,0:T(8,128)}), f32[128,256]{1,0:T(8,128)}) %reduce-scatter.35.cloned.1.call-update) | async-done | bytes 131088 | tf_op jit(solution)/shard_map/reduce_scatter | solution.py:287
  994.6 66.4 %reduce-scatter.27.cloned.1.call-done = f32[128,256]{1,0:T(8,128)} async-done(((f32[1024,256]{1,0:T(8,128)}), f32[128,256]{1,0:T(8,128)}) %reduce-scatter.27.cloned.1.call-update) | async-done | bytes 131088 | tf_op jit(solution)/shard_map/reduce_scatter | solution.py:285
  1061.0 66.7 %reduce-scatter.23.cloned.1.call-done = f32[128,256]{1,0:T(8,128)} async-done(((f32[1024,256]{1,0:T(8,128)}), f32[128,256]{1,0:T(8,128)}) %reduce-scatter.23.cloned.1.call-update) | async-done | bytes 131088 | tf_op jit(solution)/shard_map/reduce_scatter | solution.py:284
  1127.7 66.4 %reduce-scatter.31.cloned.1.call-done = f32[128,256]{1,0:T(8,128)} async-done(((f32[1024,256]{1,0:T(8,128)}), f32[128,256]{1,0:T(8,128)}) %reduce-scatter.31.cloned.1.call-update) | async-done | bytes 131088 | tf_op jit(solution)/shard_map/reduce_scatter | solution.py:286
  1194.1 75.7 %reduce-scatter.39.cloned.1.call-done = f32[128,704]{0,1:T(8,128)} async-done(((f32[1024,704]{0,1:T(8,128)}), f32[128,704]{0,1:T(8,128)}) %reduce-scatter.39.cloned.1.call-update) | async-done | bytes 360464 | tf_op jit(solution)/shard_map/reduce_scatter | solution.py:289
  1269.7 76.0 %reduce-scatter.43.cloned.1.call-done = f32[128,704]{0,1:T(8,128)} async-done(((f32[1024,704]{0,1:T(8,128)}), f32[128,704]{0,1:T(8,128)}) %reduce-scatter.43.cloned.1.call-update) | async-done | bytes 360464 | tf_op jit(solution)/shard_map/reduce_scatter | solution.py:290
  1345.7 75.5 %reduce-scatter.47.cloned.1.call-done = f32[352,256]{1,0:T(8,128)} async-done(((f32[2816,256]{1,0:T(8,128)}), f32[352,256]{1,0:T(8,128)}) %reduce-scatter.47.cloned.1.call-update) | async-done | bytes 360464 | tf_op jit(solution)/shard_map/reduce_scatter | solution.py:291
  (322 shorter events, 177.2 us)
Async XLA Ops:
  7.2 142.2 %copy-start.58 = (bf16[128]{0:T(256)(128)(2,1)S(1)}, bf16[128]{0:T(256)(128)(2,1)}, u32[]{:S(2)}) copy-start(bf16[128]{0:T(256)(128)(2,1)} %param.16) | copy-start | bytes 772
  7.2 162.8 %copy-start = (bf16[2,256,1024]{2,1,0:T(8,128)(2,1)S(1)}, bf16[2,256,1024]{2,1,0:T(8,128)(2,1)}, u32[]{:S(2)}) copy-start(bf16[2,256,1024]{2,1,0:T(8,128)(2,1)} %param.13) | copy-start | bytes 3145732
  7.2 140.7 %all-gather.21.cloned.1.call-start = ((), (), s32[]{:S(2)}) async-start(), calls=%async_computation.20 | async-start | bytes 1622016 | tf_op jit(solution)/shard_map/all_gather | solution.py:104
  7.9 140.7 %all-gather.25.cloned.1.call-start = ((), (), s32[]{:S(2)}) async-start(), calls=%async_computation.22 | async-start | bytes 1622016 | tf_op jit(solution)/shard_map/all_gather | solution.py:105
  8.7 165.7 %all-gather.17.cloned.1.call-start = ((), (), s32[]{:S(2)}) async-start(), calls=%async_computation.18 | async-start | bytes 2621440 | tf_op jit(solution)/shard_map/all_gather | solution.py:98
  45.0 138.1 %all-gather.13.cloned.1.call-start = ((), (), s32[]{:S(2)}) async-start(), calls=%async_computation.16 | async-start | bytes 2621440 | tf_op jit(solution)/shard_map/all_gather | solution.py:99
  79.4 161.2 %all-gather.29.cloned.1.call-start = ((), (), s32[]{:S(2)}) async-start(), calls=%async_computation.24 | async-start | bytes 1622016 | tf_op jit(solution)/shard_map/all_gather | solution.py:106
  79.9 160.7 %all-gather.15.cloned.1.call-start = ((), (), s32[]{:S(2)}) async-start(), calls=%async_computation.17 | async-start | bytes 2621440 | tf_op jit(solution)/shard_map/all_gather | solution.py:97
  113.9 229.2 %all-gather.19.cloned.1.call-start = ((), (), s32[]{:S(2)}) async-start(), calls=%async_computation.19 | async-start | bytes 2621440 | tf_op jit(solution)/shard_map/all_gather | solution.py:100
  147.8 200.1 %all-gather.23.cloned.1.call-start = ((), (), s32[]{:S(2)}) async-start(), calls=%async_computation.21 | async-start | bytes 7208960 | tf_op jit(solution)/shard_map/all_gather | solution.py:110
  148.5 214.1 %all-gather.27.cloned.1.call-start = ((), (), s32[]{:S(2)}) async-start(), calls=%async_computation.23 | async-start | bytes 7208960 | tf_op jit(solution)/shard_map/all_gather | solution.py:111
  149.3 258.9 %all-gather.31.cloned.1.call-start = ((), (), s32[]{:S(2)}) async-start(), calls=%async_computation.25 | async-start | bytes 7208960 | tf_op jit(solution)/shard_map/all_gather | solution.py:112
  170.0 7.3 copy-start.52
  170.3 7.0 copy-start.54
  171.8 75.8 %copy-start.32 = (f32[512,32]{0,1:T(8,128)}, f32[512,32]{0,1:T(8,128)S(1)}, u32[]{:S(2)}) copy-start(f32[512,32]{0,1:T(8,128)S(1)} %get-tuple-element.45) | copy-start | bytes 196612
  180.3 90.1 %copy-start.13 = (bf16[512,16,64]{0,2,1:T(8,128)(2,1)}, bf16[512,16,64]{0,2,1:T(8,128)(2,1)S(1)}, u32[]{:S(2)}) copy-start(bf16[512,16,64]{0,2,1:T(8,128)(2,1)S(1)} %maximum_convert_fusion) | copy-start | bytes 3145732
  186.6 35.6 %copy-start.59 = (bf16[128]{0:T(256)(128)(2,1)S(1)}, bf16[128]{0:T(256)(128)(2,1)}, u32[]{:S(2)}) copy-start(bf16[128]{0:T(256)(128)(2,1)} %param.21) | copy-start | bytes 772
  186.6 52.7 %copy-start.24 = (bf16[2,256,1024]{2,1,0:T(8,128)(2,1)S(1)}, bf16[2,256,1024]{2,1,0:T(8,128)(2,1)}, u32[]{:S(2)}) copy-start(bf16[2,256,1024]{2,1,0:T(8,128)(2,1)} %param.25) | copy-start | bytes 3145732
  187.7 5.2 collective-permute-start
  192.9 55.0 %collective-permute-start.1 = (bf16[2,2,256,1024]{3,2,1,0:T(8,128)(2,1)}, bf16[2,2,256,1024]{3,2,1,0:T(8,128)(2,1)}, u32[]{:S(2)}, u32[]{:S(2)}) collective-permute-start(bf16[2,2,256,1024]{3,2,1,0:T(8,128)(2,1)} %collective-permute-done), channel_id=1, source_target_pairs={{0,8},{8,16},{16,24},{1,9},{9,17},{17,25},{2,10},{10,18},{18,26},{... | collective-permute-start | bytes 6291464 | tf_op jit(solution)/shard_map/ppermute | solution.py:15
  240.6 403.6 %reduce-scatter.33.cloned.1.call-start = ((), (), s32[]{:S(2)}) async-start(), calls=%async_computation.32 | async-start | bytes 2621440 | tf_op jit(solution)/shard_map/reduce_scatter | solution.py:266
  248.0 51.1 %collective-permute-start.2 = (bf16[2,2,256,1024]{3,2,1,0:T(8,128)(2,1)}, bf16[2,2,256,1024]{3,2,1,0:T(8,128)(2,1)}, u32[]{:S(2)}, u32[]{:S(2)}) collective-permute-start(bf16[2,2,256,1024]{3,2,1,0:T(8,128)(2,1)} %collective-permute-done.1), channel_id=1, source_target_pairs={{0,8},{8,16},{16,24},{1,9},{9,17},{17,25},{2,10},{10,18},{18,26},{... | collective-permute-start | bytes 6291464 | tf_op jit(solution)/shard_map/ppermute | solution.py:15
  279.6 7.5 copy-start.15
  291.6 7.5 copy-start.17
  311.3 7.9 slice-start
  311.3 8.3 slice-start.1
  311.3 15.4 %slice-start.4 = ((s8[8388608]{0:T(1024)(128)(4,1)}), s8[4194304]{0:T(1024)(128)(4,1)S(1)}, s32[]{:S(2)}) async-start(s8[8388608]{0:T(1024)(128)(4,1)} %bitcast.239), calls=%async_computation.46 | async-start | bytes 8388608
  319.6 7.1 slice-start.5
  319.6 7.1 copy-start.45
  326.8 8.1 slice-start.2
  356.7 51.5 %copy-start.39 = (bf16[512,1024]{1,0:T(8,128)(2,1)S(1)}, bf16[512,1024]{1,0:T(8,128)(2,1)}, u32[]{:S(2)}) copy-start(bf16[512,1024]{1,0:T(8,128)(2,1)} %fusion.17) | copy-start | bytes 3145732
  419.2 7.3 copy-start.63
  419.2 7.3 copy-start.62
  419.2 7.3 copy-start.3
  419.2 7.3 copy-start.60
  462.7 25.8 %collective-permute-start.3 = (bf16[2,2,256,1024]{3,2,1,0:T(8,128)(2,1)}, bf16[2,2,256,1024]{3,2,1,0:T(8,128)(2,1)}, u32[]{:S(2)}, u32[]{:S(2)}) collective-permute-start(bf16[2,2,256,1024]{3,2,1,0:T(8,128)(2,1)} %pad_maximum_fusion.1), channel_id=1, source_target_pairs={{24,0},{0,8},{8,16},{16,24},{25,1},{1,9},{9,17},{17,25},{26,2},{2,... | collective-permute-start | bytes 6291464 | tf_op jit(solution)/shard_map/ppermute | solution.py:21
  485.5 7.9 copy-start.44
  493.5 25.8 %collective-permute-start.4 = (bf16[2,2,256,1024]{3,2,1,0:T(8,128)(2,1)}, bf16[2,2,256,1024]{3,2,1,0:T(8,128)(2,1)}, u32[]{:S(2)}, u32[]{:S(2)}) collective-permute-start(bf16[2,2,256,1024]{3,2,1,0:T(8,128)(2,1)} %fusion.12), channel_id=1, source_target_pairs={{24,0},{0,8},{8,16},{16,24},{25,1},{1,9},{9,17},{17,25},{26,2},{2,... | collective-permute-start | bytes 6291464 | tf_op jit(solution)/shard_map/ppermute | solution.py:21
  516.1 8.2 copy-start.23
  516.1 8.3 copy-start.27
  524.2 31.1 %collective-permute-start.5 = (bf16[2,2,256,1024]{3,2,1,0:T(8,128)(2,1)}, bf16[2,2,256,1024]{3,2,1,0:T(8,128)(2,1)}, u32[]{:S(2)}, u32[]{:S(2)}) collective-permute-start(bf16[2,2,256,1024]{3,2,1,0:T(8,128)(2,1)} %fusion.13), channel_id=1, source_target_pairs={{24,0},{0,8},{8,16},{16,24},{25,1},{1,9},{9,17},{17,25},{26,2},{2,... | collective-permute-start | bytes 6291464 | tf_op jit(solution)/shard_map/ppermute | solution.py:21
  527.0 119.5 %reduce-scatter.25.cloned.1.call-start = ((), (), s32[]{:S(2)}) async-start(), calls=%async_computation.28 | async-start | bytes 2621440 | tf_op jit(solution)/shard_map/reduce_scatter | solution.py:260
  547.1 11.5 copy-start.6
  547.1 11.5 copy-start.14
  558.3 25.7 %collective-permute-start.6 = (bf16[2,2,256,1024]{3,2,1,0:T(8,128)(2,1)S(1)}, bf16[2,2,256,1024]{3,2,1,0:T(8,128)(2,1)S(1)}, u32[]{:S(2)}, u32[]{:S(2)}) collective-permute-start(bf16[2,2,256,1024]{3,2,1,0:T(8,128)(2,1)S(1)} %fusion.14), channel_id=1, source_target_pairs={{24,0},{0,8},{8,16},{16,24},{25,1},{1,9},{9,17},{17,25},{26,2},{2,... | collective-permute-start | bytes 6291464 | tf_op jit(solution)/shard_map/ppermute | solution.py:21
  585.6 8.0 copy-start.33
  585.6 8.0 copy-start.51
  600.4 65.6 %reduce-scatter.21.cloned.1.call-start = ((), (), s32[]{:S(2)}) async-start(), calls=%async_computation.26 | async-start | bytes 2621440 | tf_op jit(solution)/shard_map/reduce_scatter | solution.py:257
  605.4 94.5 %reduce-scatter.29.cloned.1.call-start = ((), (), s32[]{:S(2)}) async-start(), calls=%async_computation.30 | async-start | bytes 2621440 | tf_op jit(solution)/shard_map/reduce_scatter | solution.py:263
  610.3 146.9 %reduce-scatter.37.cloned.1.call-start = ((), (), s32[]{:S(2)}) async-start(), calls=%async_computation.34 | async-start | bytes 7208960 | tf_op jit(solution)/shard_map/reduce_scatter | solution.py:272
  617.3 197.4 %reduce-scatter.41.cloned.1.call-start = ((), (), s32[]{:S(2)}) async-start(), calls=%async_computation.36 | async-start | bytes 7208960 | tf_op jit(solution)/shard_map/reduce_scatter | solution.py:275
  624.5 247.4 %reduce-scatter.45.cloned.1.call-start = ((), (), s32[]{:S(2)}) async-start(), calls=%async_computation.38 | async-start | bytes 7208960 | tf_op jit(solution)/shard_map/reduce_scatter | solution.py:278
  632.7 266.8 %reduce-scatter.51.cloned.1.call-start = ((), (), s32[]{:S(2)}) async-start(), calls=%async_computation.41 | async-start | bytes 1310720
  634.4 292.5 %reduce-scatter.49.cloned.1.call-start = ((), (), s32[]{:S(2)}) async-start(), calls=%async_computation.40 | async-start | bytes 1310720
  644.1 350.4 %reduce-scatter.35.cloned.1.call-start = ((), (), s32[]{:S(2)}) async-start(), calls=%async_computation.33 | async-start | bytes 1179648 | tf_op jit(solution)/shard_map/reduce_scatter | solution.py:287
  646.4 414.6 %reduce-scatter.27.cloned.1.call-start = ((), (), s32[]{:S(2)}) async-start(), calls=%async_computation.29 | async-start | bytes 1179648 | tf_op jit(solution)/shard_map/reduce_scatter | solution.py:285
  648.6 479.1 %reduce-scatter.23.cloned.1.call-start = ((), (), s32[]{:S(2)}) async-start(), calls=%async_computation.27 | async-start | bytes 1179648 | tf_op jit(solution)/shard_map/reduce_scatter | solution.py:284
  668.1 526.0 %reduce-scatter.31.cloned.1.call-start = ((), (), s32[]{:S(2)}) async-start(), calls=%async_computation.31 | async-start | bytes 1179648 | tf_op jit(solution)/shard_map/reduce_scatter | solution.py:286
  702.1 567.6 %reduce-scatter.39.cloned.1.call-start = ((), (), s32[]{:S(2)}) async-start(), calls=%async_computation.35 | async-start | bytes 3244032 | tf_op jit(solution)/shard_map/reduce_scatter | solution.py:289
  760.5 585.2 %reduce-scatter.43.cloned.1.call-start = ((), (), s32[]{:S(2)}) async-start(), calls=%async_computation.37 | async-start | bytes 3244032 | tf_op jit(solution)/shard_map/reduce_scatter | solution.py:290
  818.0 57.1 %copy-start.61 = (u32[32]{0:T(128)S(1)}, u32[32]{0:T(128)}, u32[]{:S(2)}) copy-start(u32[32]{0:T(128)} %constant.116) | copy-start | bytes 388
  818.0 58.4 %copy-start.4 = (f32[512,1024]{1,0:T(8,128)S(1)}, f32[512,1024]{1,0:T(8,128)}, u32[]{:S(2)}) copy-start(f32[512,1024]{1,0:T(8,128)} %copy-done.2) | copy-start | bytes 6291460
  818.0 603.1 %reduce-scatter.47.cloned.1.call-start = ((), (), s32[]{:S(2)}) async-start(), calls=%async_computation.39 | async-start | bytes 3244032 | tf_op jit(solution)/shard_map/reduce_scatter | solution.py:291
  876.4 24.2 %copy-start.57 = (f32[1,2,2,128]{3,1,2,0:T(2,128)S(1)}, f32[1,2,2,128]{3,1,2,0:T(2,128)}, u32[]{:S(2)}) copy-start(f32[1,2,2,128]{3,1,2,0:T(2,128)} %copy-done.56) | copy-start | bytes 6148
  (39 other events, 100.0 us)
Sparse Core Ops, SparseCore 0:
  10.1 50.9 all-gather.20
  63.1 47.1 all-gather.24
  111.9 22.9 all-gather.16
  136.3 22.8 all-gather.12
  161.2 43.0 all-gather.28
  205.7 21.1 all-gather.14
  228.5 28.9 all-gather.18
  259.1 58.5 all-gather.22
  319.2 43.3 all-gather.26
  364.0 44.1 all-gather.30
  527.1 35.2 reduce-scatter.32
  600.5 31.4 reduce-scatter.24
  634.5 31.4 reduce-scatter.20
  668.5 31.4 reduce-scatter.28
  702.3 54.8 reduce-scatter.36
  759.8 54.8 reduce-scatter.40
  817.1 54.8 reduce-scatter.44
  874.5 24.8 reduce-scatter.50
  902.0 24.8 reduce-scatter.48
  931.1 63.4 reduce-scatter.34
  998.6 62.3 reduce-scatter.26
  1065.3 62.2 reduce-scatter.22
  1131.6 62.3 reduce-scatter.30
  1198.5 71.2 reduce-scatter.38
  1274.3 71.3 reduce-scatter.42
  1350.1 71.0 reduce-scatter.46
where the time goes:
time: 1440 us; the launch traced here: 1430 us
  waiting for transfers between devices  799 us (55%)
  blocking collectives  197 us (14%)
  matrix products  195 us (14%)
  local copies, waits for them, and re-layouts  102 us (7%)
  other arithmetic  69.8 us (5%)
  starting transfers between devices  48.9 us (3%)
  between operations  17.1 us (1%)
    reduce_scatter x1, waiting for transfers between devices, on_device(): lax.psum_scatter(summed_seq[7], 'dp', scatter_dimension=0, tiled=True)  76 us
    reduce_scatter x1, waiting for transfers between devices, on_device(): lax.psum_scatter(summed_seq[6], 'dp', scatter_dimension=0, tiled=True)  75.7 us
    reduce_scatter x1, waiting for transfers between devices, on_device(): lax.psum_scatter(summed_seq[8], 'dp', scatter_dimension=0, tiled=True)  75.5 us
    reduce_scatter x1, waiting for transfers between devices, on_device(): lax.psum_scatter(summed_seq[1], 'dp', scatter_dimension=0, tiled=True)  66.7 us
    reduce_scatter x1, waiting for transfers between devices, on_device(): lax.psum_scatter(summed_seq[3], 'dp', scatter_dimension=0, tiled=True)  66.4 us
    reduce_scatter x1, waiting for transfers between devices, on_device(): lax.psum_scatter(summed_seq[2], 'dp', scatter_dimension=0, tiled=True)  66.4 us
    reduce_scatter x1, waiting for transfers between devices, on_device(): lax.psum_scatter(grad_wgate.astype(jnp.bfloat16), 'seq', scatter_dimensio...  55.1 us
    reduce_scatter x1, waiting for transfers between devices, on_device(): lax.psum_scatter(grad_wup.astype(jnp.bfloat16), 'seq', scatter_dimension=...  54.1 us
  transfers between devices with their start and end apart: 33, of which 21 were waited for; matrix products, arithmetic and copies ran while one was open for 20% of the time, Pallas kernels for 0%

commit v1 on v0

v1 whole, which is shorter than its diff:
```python
import functools

import jax
import jax.numpy as jnp
from jax import lax
from jax.experimental import pallas as pl
from jax.experimental.pallas import tpu as pltpu
from jax.sharding import PartitionSpec as P

HEAD = 64
EPSILON = 1e-06
TILE = 256
BLOCKS = 8
F32 = jnp.float32
BF16 = jnp.bfloat16
VMEM_LIMIT = 56 * 1024 * 1024
MESH_Y, MESH_C = 2, 1
ZM, Z1, X1 = 6, 2, 1


def dot_nn(a, b):
    return lax.dot_general(a, b, (((1,), (0,)), ((), ())), preferred_element_type=F32)


def dot_nt(a, b):
    return lax.dot_general(a, b, (((1,), (1,)), ((), ())), preferred_element_type=F32)


def dot_tn(a, b):
    return lax.dot_general(a, b, (((0,), (0,)), ((), ())), preferred_element_type=F32)


def flip(value, axis, mask):
    pairs = [(i, i ^ mask) for i in range(lax.axis_size(axis))]
    return lax.ppermute(value, axis, pairs)


def pick(flag, when_one, when_zero):
    return jnp.where(flag == 1, when_one, when_zero)


def call(body, outs, ins, scratch, flops, moved, exps=0, grid=None, in_specs=None, out_specs=None):
    spaces = {"v": pltpu.VMEM, "s": pltpu.SMEM, "a": pl.ANY}
    if in_specs is None:
        in_specs = [pl.BlockSpec(memory_space=spaces[kind]) for kind, _ in ins]
        out_specs = [pl.BlockSpec(memory_space=pltpu.VMEM) for _ in outs]
    kwargs = {} if grid is None else {"grid": grid}
    return pl.pallas_call(
        body,
        out_shape=[jax.ShapeDtypeStruct(shape, kind) for shape, kind in outs],
        in_specs=in_specs,
        out_specs=out_specs,
        scratch_shapes=scratch,
        cost_estimate=pl.CostEstimate(flops=flops, bytes_accessed=moved, transcendentals=exps),
        compiler_params=pltpu.CompilerParams(vmem_limit_bytes=VMEM_LIMIT),
        **kwargs,
    )(*[value for _, value in ins])


def run_copies(copies):
    for copy in copies:
        copy.start()
    for copy in copies:
        copy.wait()


def turned(values, cosine, signed_sine):
    lane = lax.broadcasted_iota(jnp.int32, values.shape, 1)
    ahead = pltpu.roll(values, 128 - HEAD // 2, 1)
    behind = pltpu.roll(values, HEAD // 2, 1)
    partner = jnp.where(lane % HEAD < HEAD // 2, ahead, behind)
    return values * cosine + partner * signed_sine


def place_of(info, bx, b1, bm):
    z = info[3] ^ b1 ^ (3 * bm)
    return z * 2 + (info[4] ^ bx)


def qkv_body(info, x, fv, cosine, sine, a10, a11, a20, a21, h1, q, k, b, w, sem):
    cut = a10.shape[1]
    copies = []
    for by in range(2):
        for bx in range(2):
            for b1 in range(2):
                for bm in range(2):
                    d = place_of(info, bx, b1, bm)
                    i = len(copies)
                    first, second = (a10, a11)[by], (a20, a21)[bx]
                    copies.append(pltpu.make_async_copy(
                        first.at[bx * 4 + b1 * 2 + bm], w.at[by, d, pl.ds(0, cut)], sem.at[i]))
                    copies.append(pltpu.make_async_copy(
                        second.at[by * 4 + b1 * 2 + bm],
                        w.at[by, d, pl.ds(cut, w.shape[2] - cut)], sem.at[i + 1]))
    run_copies(copies)
    rows = 128
    width = w.shape[3]
    model = x.shape[1]
    gains = w[0, :, 3 * rows : 3 * rows + 16, 0:rows]
    gain = jnp.concatenate([gains[d, 0:1, :] for d in range(BLOCKS)], axis=1).astype(F32)

    def step(t, carry):
        at = pl.ds(pl.multiple_of(t * TILE, TILE), TILE)
        xt = x[at, :].astype(F32)
        inverse = lax.rsqrt(jnp.mean(xt * xt, axis=-1, keepdims=True) + EPSILON)
        h = (xt * inverse * gain).astype(BF16)
        h1[at, :] = h
        cos_t, sin_t = cosine[at, :], sine[at, :]
        for by in range(2):
            for n in range(3):
                weight = w[by, :, n * rows : (n + 1) * rows, :].reshape(model, width)
                acc = dot_nn(h, weight)
                cols = pl.ds(by * width, width)
                if n == 2:
                    column = pl.multiple_of(((info[0] ^ by) * 2 + info[1]) * width, width)
                    first = fv[at, pl.ds(column, width)].astype(F32)
                    b[at, cols] = (0.5 * acc + 0.5 * first).astype(BF16)
                else:
                    parts = [
                        turned(acc[:, j : j + 128], cos_t, sin_t) for j in range(0, width, 128)
                    ]
                    (q, k)[n][at, cols] = jnp.concatenate(parts, axis=1).astype(BF16)
        return carry

    lax.fori_loop(0, x.shape[0] // TILE, step, 0)


def split_heads(pair):
    lane = lax.broadcasted_iota(jnp.int32, pair.shape, 1)
    zero = jnp.zeros_like(pair)
    return jnp.concatenate(
        [jnp.where(lane < HEAD, pair, zero), jnp.where(lane < HEAD, zero, pair)], axis=0
    )


def join_heads(both):
    half = both.shape[0] // 2
    lane = lax.broadcasted_iota(jnp.int32, (half, both.shape[1]), 1)
    return jnp.where(lane < HEAD, both[:half], both[half:])


def hide_later(scores, fill):
    length, width = scores.shape
    key_at = lax.broadcasted_iota(jnp.int32, (TILE, width), 0)
    query_at = lax.broadcasted_iota(jnp.int32, (TILE, width), 1) % TILE
    last = jnp.where(key_at <= query_at, scores[length - TILE :], fill)
    if length == TILE:
        return last
    return jnp.concatenate([scores[: length - TILE], last], axis=0)


def attend_body(q, k, b, att, lse):
    for i in range(q.shape[0] // TILE):
        length = (i + 1) * TILE
        queries = split_heads(q[i * TILE : length, :])
        scores = hide_later(dot_nt(k[:length, :], queries) * 0.125, -1e30)
        top = jnp.max(scores, axis=0, keepdims=True)
        grown = jnp.exp(scores - top)
        total = jnp.sum(grown, axis=0, keepdims=True)
        logs = top + jnp.log(total)
        probs = (grown * (1.0 / total)).astype(BF16)
        att[i * TILE : length, :] = join_heads(dot_tn(probs, b[:length, :])).astype(BF16)
        lse[0, 0:1, i * TILE : length] = logs[:, :TILE]
        lse[0, 1:2, i * TILE : length] = logs[:, TILE:]


def attend_back_body(q, k, b, datt, lse, cosine, sine, dq, dk, dv, k_acc, v_acc):
    k_acc[...] = jnp.zeros_like(k_acc)
    v_acc[...] = jnp.zeros_like(v_acc)
    for i in range(q.shape[0] // TILE):
        length = (i + 1) * TILE
        at = slice(i * TILE, length)
        queries = split_heads(q[at, :])
        grads = split_heads(datt[at, :])
        keys = k[:length, :]
        logs = jnp.concatenate([lse[0, 0:1, at], lse[0, 1:2, at]], axis=1)
        scores = dot_nt(keys, queries) * 0.125
        probs = jnp.exp(hide_later(scores - logs, -1e30))
        grad_probs = dot_nt(b[:length, :], grads)
        delta = jnp.sum(probs * grad_probs, axis=0, keepdims=True)
        grad_scores = (probs * (grad_probs - delta)).astype(BF16)
        v_acc[:length, :] += dot_nn(probs.astype(BF16), grads)
        k_acc[:length, :] += dot_nn(grad_scores, queries)
        turned_back = turned(
            0.125 * join_heads(dot_tn(grad_scores, keys)), cosine[at, :], -sine[at, :]
        )
        dq[at, :] = turned_back.astype(BF16)
    for i in range(q.shape[0] // TILE):
        at = slice(i * TILE, (i + 1) * TILE)
        dk[at, :] = turned(0.125 * k_acc[at, :], cosine[at, :], -sine[at, :]).astype(BF16)
        dv[at, :] = (0.5 * v_acc[at, :]).astype(BF16)


def row_spot(info, hidden_block):
    even = (info[3] & 1) ^ info[1]
    t = hidden_block ^ info[0] ^ (info[3] >> 1) ^ even
    return t, t ^ even


def row_copies(info, hidden_block, od0, od1, odx, target, rows, first, sem, start):
    t, bm = row_spot(info, hidden_block)
    copies = []
    count = rows.stop - rows.start
    for by in range(2):
        for bx in range(2):
            row = first + (info[4] ^ bx) * count
            for own in range(2):
                core = info[1] ^ (1 - own)
                column = pl.multiple_of(((info[0] ^ by) * 2 + core) * 256, 256)
                if own:
                    source = (od0, od1)[by].at[bx * 4 + t * 2 + bm, pl.ds(rows.start, count)]
                else:
                    source = odx.at[by, bx, t, pl.ds(rows.start, count)]
                copies.append(pltpu.make_async_copy(
                    source, target.at[pl.ds(pl.multiple_of(row, 16), count), pl.ds(column, 256)],
                    sem.at[start + len(copies)]))
    return copies


def out_copies(info, od0, od1, odx, wo, sem):
    copies = []
    for block in range(2):
        copies += row_copies(
            info, block, od0, od1, odx, wo, slice(0, 128), block * 256, sem, len(copies))
    return copies


def out_body(info, att, od0, od1, odx, part, wo, sem):
    run_copies(out_copies(info, od0, od1, odx, wo, sem))

    def step(t, carry):
        at = pl.ds(pl.multiple_of(t * TILE, TILE), TILE)
        part[at, :] = dot_nn(att[at, :], wo[...]).astype(BF16)
        return carry

    lax.fori_loop(0, att.shape[0] // TILE, step, 0)


def out_back_body(info, gb, att, od0, od1, odx, datt, keep, send, wo, sem):
    run_copies(out_copies(info, od0, od1, odx, wo, sem))

    def step(t, carry):
        at = pl.ds(pl.multiple_of(t * TILE, TILE), TILE)
        datt[at, :] = dot_nt(gb[at, :], wo[...]).astype(BF16)
        return carry

    lax.fori_loop(0, att.shape[0] // TILE, step, 0)
    for by in range(2):
        for own in range(2):
            core = info[1] ^ (1 - own)
            column = pl.multiple_of(((info[0] ^ by) * 2 + core) * 256, 256)
            grad = dot_tn(att[...], gb[:, pl.ds(column, 256)]).astype(BF16)
            for block in range(2):
                t, _ = row_spot(info, block)
                for bx in range(2):
                    row = [grad[block * 256 + j * 128 : block * 256 + (j + 1) * 128] for j in (0, 1)]
                    (send, keep)[own][by, bx, t] = jnp.where((info[4] ^ bx) == 1, row[1], row[0])


def ffn_body(
    info, h2, gy, g0, g1, od0, od1, odx,
    gh2, gux0, gux1, dkeep, dsend, rkeep, rsend,
    wgu, wd, ggu, hid, gh2_acc, res_acc, sem,
):
    units = wd.shape[0]
    half = units // 2
    tiles = h2.shape[0] // TILE
    for block in (1, 0):
        copies = row_copies(info, block, od0, od1, odx, wd, slice(128, 128 + half), 0, sem, 0)
        for bx in range(2):
            for b1 in range(2):
                for bm in range(2):
                    d = place_of(info, bx, b1, bm)
                    for part in range(2):
                        copies.append(pltpu.make_async_copy(
                            (g0, g1)[bx].at[block * 4 + b1 * 2 + bm, :, pl.ds(part * 128, 128)],
                            wgu.at[pl.ds(part * units, units),
                                   pl.ds(pl.multiple_of(d * 128, 128), 128)],
                            sem.at[len(copies)]))
        run_copies(copies)

        def step(t, carry, block=block):
            at = pl.ds(pl.multiple_of(t * TILE, TILE), TILE)
            both = dot_nt(wgu[...], h2[at, :])
            gate, up = both[:units], both[units:]
            sig = 1.0 / (1.0 + jnp.exp(-gate))
            act = gate * sig
            hidden = (act * up).astype(BF16)
            hid[:, at] = hidden
            grad_hidden = dot_nt(wd[...], gy[at, :])
            grad_gate = (grad_hidden * up * (sig + act * (1.0 - sig))).astype(BF16)
            grad_up = (grad_hidden * act).astype(BF16)
            ggu[:units, at] = grad_gate
            ggu[units:, at] = grad_up
            grad_h = dot_tn(ggu[:, at], wgu[...])
            result = dot_tn(hidden, wd[...])
            if block == 1:
                gh2_acc[at, :] = grad_h
                res_acc[at, :] = result
            else:
                gh2[at, :] = (gh2_acc[at, :] + grad_h).astype(BF16)
                result = res_acc[at, :] + result

                @pl.when((t & 1) == info[1])
                def _():
                    rkeep[t >> 1] = result

                @pl.when((t & 1) != info[1])
                def _():
                    rsend[t >> 1] = result.astype(BF16)

            return carry

        lax.fori_loop(0, tiles, step, 0)

        for b1 in range(2):
            for bm in range(2):
                z = info[3] ^ b1 ^ (3 * bm)
                column = pl.multiple_of(z * 256, 256)
                grad = dot_nn(ggu[...], h2[:, pl.ds(column, 256)]).astype(BF16)
                lo, hi = grad[:, :128], grad[:, 128:]
                swap = info[4] == 1
                for bx, part in ((0, jnp.where(swap, hi, lo)), (1, jnp.where(swap, lo, hi))):
                    target = (gux0, gux1)[bx]
                    target[block, b1 * 2 + bm, :, 0:128] = part[:units]
                    target[block, b1 * 2 + bm, :, 128:256] = part[units:]
        t_spot, _ = row_spot(info, block)
        for by in range(2):
            for own in range(2):
                core = info[1] ^ (1 - own)
                column = pl.multiple_of(((info[0] ^ by) * 2 + core) * 256, 256)
                grad = dot_nn(hid[...], gy[:, pl.ds(column, 256)]).astype(BF16)
                for bx in range(2):
                    (dsend, dkeep)[own][by, bx, t_spot] = jnp.where(
                        (info[4] ^ bx) == 1, grad[half:], grad[:half])


def qkv_back_body(
    info, dq, dk, dv, h1, x, gain2, of0, of1, a10, a11, a20, a21,
    out0, out1, gkeep, gsend, w, acc, sem,
):
    cut = a10.shape[1]
    copies = []
    for by in range(2):
        for bx in range(2):
            for b1 in range(2):
                for bm in range(2):
                    d = place_of(info, bx, b1, bm)
                    i = len(copies)
                    first, second = (a10, a11)[by], (a20, a21)[bx]
                    copies.append(pltpu.make_async_copy(
                        first.at[bx * 4 + b1 * 2 + bm], w.at[by, d, pl.ds(0, cut)], sem.at[i]))
                    copies.append(pltpu.make_async_copy(
                        second.at[by * 4 + b1 * 2 + bm],
                        w.at[by, d, pl.ds(cut, w.shape[2] - cut)], sem.at[i + 1]))
    for copy in copies:
        copy.start()
    width = w.shape[3]
    model = x.shape[1]
    for by in (1, 0):
        cols = slice(by * width, (by + 1) * width)
        three = jnp.concatenate([dq[:, cols], dk[:, cols], dv[:, cols]], axis=1)
        for b1 in range(2):
            for bm in range(2):
                z = info[3] ^ b1 ^ (3 * bm)
                grad = dot_tn(h1[:, pl.ds(pl.multiple_of(z * 256, 256), 256)], three).astype(BF16)
                for bx in range(2):
                    part = jnp.where((info[4] ^ bx) == 1, grad[128:], grad[:128])
                    for n in range(3):
                        (out0, out1)[by][bx * 4 + b1 * 2 + bm, n * 128 : (n + 1) * 128, :] = (
                            part[:, n * width : (n + 1) * width])
    for copy in copies:
        copy.wait()
    acc[...] = jnp.zeros_like(acc)

    def step(t, carry):
        at = pl.ds(pl.multiple_of(t * TILE, TILE), TILE)
        grad_h = jnp.zeros((TILE, model), F32)
        for by in range(2):
            cols = slice(by * width, (by + 1) * width)
            for n, grad in enumerate((dq, dk, dv)):
                weight = w[by, :, n * 128 : (n + 1) * 128, :].reshape(model, width)
                grad_h = grad_h + dot_nt(grad[at, cols], weight)
        xt = x[at, :].astype(F32)
        inverse = lax.rsqrt(jnp.mean(xt * xt, axis=-1, keepdims=True) + EPSILON)
        acc[0:1, :] += jnp.sum(grad_h * xt * inverse, axis=0, keepdims=True)

        @pl.when((t & 1) == info[1])
        def _():
            gkeep[t >> 1] = grad_h

        @pl.when((t & 1) != info[1])
        def _():
            gsend[t >> 1] = grad_h.astype(BF16)

        return carry

    lax.fori_loop(0, x.shape[0] // TILE, step, 0)
    for b1 in range(2):
        for bm in range(2):
            for bx in range(2):
                d = place_of(info, bx, b1, bm)
                spot = pl.ds(pl.multiple_of(d * 128, 128), 128)
                row = jnp.concatenate([acc[0:1, spot], gain2[0:1, spot]], axis=1)
                full = jnp.broadcast_to(row, (16, 256)).astype(BF16)
                p = bx * 4 + b1 * 2 + bm
                out0[p, 384:400, :] = full
                out1[p, 384:400, :] = full
                out0[p, 400:528, :] = of0[p]
                out1[p, 400:528, :] = of1[p]


def gathered(shard, flips):
    held = shard[None]
    for axis, mask in flips[:-1]:
        held = jnp.concatenate([held, flip(held, axis, mask)], axis=0)
    return held, flip(held, *flips[-1])


def scattered(send, keep, flips):
    total = keep.astype(F32) + flip(send, *flips[0]).astype(F32)
    for axis, mask in flips[1:]:
        half = total.shape[0] // 2
        outgoing = total[half:].astype(BF16)
        total = total[:half] + flip(outgoing, axis, mask).astype(F32)
    return total[0]


def on_device(
    tokens, first_values, seq_counts, norm1_gain, query_weight, key_weight, value_weight,
    out_weight, norm2_gain, gate_weight, up_weight, down_weight, output_cotangent,
):
    slots, piece, model = tokens.shape
    length = piece * lax.axis_size("seq")
    wide = lax.axis_size("dp") // BLOCKS
    s = lax.axis_index("seq")
    place = lax.axis_index("dp")
    y, c = s // 2, s % 2
    d = place // wide
    z, x_at = d // 2, d % 2
    info = jnp.stack([y, c, d, z, x_at]).astype(jnp.int32)
    even = (z & 1) ^ c

    def pregather(shard):
        step = 1
        while step < wide:
            other = flip(shard, "dp", step)
            bit = (place // step) % 2
            shard = pick(
                bit, jnp.concatenate([other, shard]), jnp.concatenate([shard, other]))
            step *= 2
        return shard

    def postscatter(total):
        step = wide // 2
        while step >= 1:
            half = total.shape[0] // 2
            bit = (place // step) % 2
            lo, hi = total[:half], total[half:]
            total = pick(bit, hi, lo) + flip(pick(bit, lo, hi), "dp", step)
            step //= 2
        return total

    zm, z1, xf = (("dp", mask * wide) for mask in (ZM, Z1, X1))
    yf, cf = ("seq", MESH_Y), ("seq", MESH_C)
    y_last, x_last = (zm, z1, xf, yf), (zm, z1, yf, xf)

    def swap_slots(block):
        keep, send = pick(y, block[1], block[0]), pick(y, block[0], block[1])
        recv = flip(send, *yf)
        return pick(y, jnp.stack([recv, keep]), jnp.stack([keep, recv]))

    def join_cores(half):
        other = flip(half, *cf)
        return pick(c, jnp.stack([other, half], 1), jnp.stack([half, other], 1))

    x_full = join_cores(swap_slots(tokens)).reshape(length, model)

    gains = jnp.pad(
        jnp.concatenate([pregather(norm1_gain), pregather(norm2_gain)])[None], ((0, 15), (0, 0)))
    attn = jnp.concatenate(
        [pregather(query_weight), pregather(key_weight), pregather(value_weight), gains])
    cut = 208
    a10, a11 = gathered(attn[:cut], y_last)
    a20, a21 = gathered(attn[cut:], x_last)
    rows = jnp.concatenate([pregather(out_weight), pregather(down_weight)])
    od0, od1 = gathered(rows, y_last)
    ffn = jnp.concatenate([pregather(gate_weight).T, pregather(up_weight).T], axis=1)
    g0, g1 = gathered(ffn, x_last)

    def for_core(od):
        od = od.reshape(2, 2, 2, *od.shape[1:])
        spread = [[pick(even, od[:, t, t], od[:, t, 1 - t])] for t in range(2)]
        return jnp.concatenate([jnp.stack(part, 1) for part in spread], axis=1)

    odx = flip(jnp.stack([for_core(od0), for_core(od1)]), *cf)

    pair = jnp.stack([first_values, output_cotangent], axis=1)
    pair = join_cores(swap_slots(pair))
    fv_full = pair[:, :, 0].reshape(length, model)
    live = (y < seq_counts[0]).astype(BF16)
    gy_full = pair[:, :, 1].reshape(length, model) * live

    half = HEAD // 2
    frequency = 10000.0 ** (-(jnp.arange(half).astype(F32) * 2.0) / HEAD)
    angles = jnp.arange(length).astype(F32)[:, None] * frequency[None, :]
    cosine = jnp.tile(jnp.cos(angles), (1, 4))
    sine = jnp.tile(jnp.concatenate([-jnp.sin(angles), jnp.sin(angles)], axis=1), (1, 2))

    local = model // 2
    width = local // 2
    units = gate_weight.shape[1]
    rows_all = attn.shape[0]
    h1, q, k, b = call(
        qkv_body,
        [((length, model), BF16)] + [((length, local), BF16)] * 3,
        [("s", info), ("v", x_full), ("v", fv_full), ("v", cosine), ("v", sine)]
        + [("a", part) for part in (a10, a11, a20, a21)],
        [pltpu.VMEM((2, BLOCKS, rows_all, width), BF16), pltpu.SemaphoreType.DMA((32,))],
        6 * length * model * local, 14 << 20,
    )
    head_specs = [pl.BlockSpec((length, 128), lambda i: (0, i))] * 3
    lse_spec = pl.BlockSpec((1, 2, length), lambda i: (i, 0, 0))
    pairs = local // 128
    att, lse = call(
        attend_body,
        [((length, local), BF16), ((pairs, 2, length), F32)],
        [("v", q), ("v", k), ("v", b)], [],
        4 * length * length * local, 4 << 20, length * length * pairs * 2,
        grid=(pairs,), in_specs=head_specs, out_specs=[head_specs[0], lse_spec],
    )
    weights_od = [("a", od0), ("a", od1), ("a", odx)]
    (part,) = call(
        out_body, [((length, model), BF16)],
        [("s", info), ("v", att)] + weights_od,
        [pltpu.VMEM((local, model), BF16), pltpu.SemaphoreType.DMA((16,))],
        2 * length * model * local, 5 << 20,
    )
    x32 = x_full.astype(F32)
    middle = x32 + (part.astype(F32) + flip(part, *cf).astype(F32))
    gain_rows = jnp.zeros((BLOCKS, 128), BF16)
    spots = [(bx, b1, bm) for bx in range(2) for b1 in range(2) for bm in range(2)]
    ranks = jnp.stack([place_of(info, *spot) for spot in spots])
    order = jnp.zeros((BLOCKS,), jnp.int32).at[ranks].set(jnp.arange(BLOCKS))
    gain_by_p = jnp.concatenate(
        [a20[:4, 400 - cut - 16, 128:256], a21[:4, 400 - cut - 16, 128:256]])
    gain2 = jnp.take(gain_by_p, order, axis=0).reshape(1, model).astype(F32)
    del gain_rows
    inverse2 = lax.rsqrt(jnp.mean(middle * middle, axis=-1, keepdims=True) + EPSILON)
    h2 = (middle * inverse2 * gain2).astype(BF16)

    tile = (2, piece, model)
    gh2, gux0, gux1, dkeep, dsend, rkeep, rsend = call(
        ffn_body,
        [((length, model), BF16), ((2, 4, units, 256), BF16), ((2, 4, units, 256), BF16),
         ((2, 2, 2, units // 2, 256), BF16), ((2, 2, 2, units // 2, 256), BF16),
         (tile, F32), (tile, BF16)],
        [("s", info), ("v", h2), ("v", gy_full), ("a", g0), ("a", g1)] + weights_od,
        [pltpu.VMEM((2 * units, model), BF16), pltpu.VMEM((units, model), BF16),
         pltpu.VMEM((2 * units, length), BF16), pltpu.VMEM((units, length), BF16),
         pltpu.VMEM((length, model), F32), pltpu.VMEM((length, model), F32),
         pltpu.SemaphoreType.DMA((24,))],
        36 * length * model * units, 40 << 20, 2 * length * units,
    )

    def own_tokens(full):
        cut_up = full.reshape(2, 2, piece, full.shape[-1])
        return pick(c, cut_up[:, 1], cut_up[:, 0])

    def to_owner(halves):
        keep, send = pick(y, halves[1], halves[0]), pick(y, halves[0], halves[1])
        recv = flip(send.astype(BF16), *yf).astype(halves.dtype)
        return pick(y, jnp.stack([recv, keep]), jnp.stack([keep, recv]))

    middle_own = own_tokens(middle)
    output = to_owner(
        (live.astype(F32) * (middle_own + (rkeep + flip(rsend, *cf).astype(F32)))).astype(BF16))

    def whole_rows(keep, send):
        recv = flip(send, *cf)
        cells = []
        for b1 in range(2):
            for bm in range(2):
                mine = even if b1 != bm else 1 - even
                cells.append(pick(mine, keep[:, :, b1], recv[:, :, b1]))
        full = jnp.stack(cells, axis=2)
        return full.reshape(2, BLOCKS, *full.shape[3:])

    down_full = whole_rows(dkeep, dsend)

    gy32 = gy_full.astype(F32)
    grad_h2 = gh2.astype(F32) + flip(gh2, *cf).astype(F32)
    scaled = grad_h2 * gain2
    grad_gain2 = jnp.sum(grad_h2 * middle * inverse2, axis=0, keepdims=True)
    grad_middle = (
        gy32 + inverse2 * scaled
        - middle * (inverse2 * inverse2 * inverse2)
        * jnp.mean(scaled * middle, axis=-1, keepdims=True))
    grad_branch = grad_middle.astype(BF16)
    datt, okeep, osend = call(
        out_back_body,
        [((length, local), BF16), ((2, 2, 2, 128, 256), BF16), ((2, 2, 2, 128, 256), BF16)],
        [("s", info), ("v", grad_branch), ("v", att)] + weights_od,
        [pltpu.VMEM((local, model), BF16), pltpu.SemaphoreType.DMA((16,))],
        4 * length * model * local, 6 << 20,
    )
    out_full = whole_rows(okeep, osend)
    table_spec = pl.BlockSpec((length, 128), lambda i: (0, 0))
    dq, dk, dv = call(
        attend_back_body,
        [((length, local), BF16)] * 3,
        [("v", q), ("v", k), ("v", b), ("v", datt), ("v", lse), ("v", cosine), ("v", sine)],
        [pltpu.VMEM((length, 128), F32), pltpu.VMEM((length, 128), F32)],
        10 * length * length * local, 8 << 20, length * length * pairs * 2,
        grid=(pairs,),
        in_specs=head_specs + [head_specs[0], lse_spec, table_spec, table_spec],
        out_specs=head_specs,
    )
    dv_cut = dv.reshape(2, 2, piece, local)
    dv_keep, dv_send = pick(c, dv_cut[:, 1], dv_cut[:, 0]), pick(c, dv_cut[:, 0], dv_cut[:, 1])
    dv_recv = flip(dv_send, *cf)
    blocks = []
    for column_y in range(2):
        for column_c in range(2):
            by = y ^ column_y
            mine = pick(by, dv_keep[..., width:], dv_keep[..., :width])
            theirs = pick(by, dv_recv[..., width:], dv_recv[..., :width])
            blocks.append(pick(c ^ column_c, theirs, mine))
    grad_first = to_owner(jnp.concatenate(blocks, axis=-1)).astype(F32)

    out0, out1, gkeep, gsend = call(
        qkv_back_body,
        [((BLOCKS, 528, width), BF16), ((BLOCKS, 528, width), BF16), (tile, F32), (tile, BF16)],
        [("s", info), ("v", dq), ("v", dk), ("v", dv), ("v", h1), ("v", x_full),
         ("v", grad_gain2), ("v", out_full[0]), ("v", out_full[1])]
        + [("a", part) for part in (a10, a11, a20, a21)],
        [pltpu.VMEM((2, BLOCKS, rows_all, width), BF16), pltpu.VMEM((8, model), F32),
         pltpu.SemaphoreType.DMA((32,))],
        12 * length * model * local, 20 << 20,
    )

    grad_h1 = gkeep + flip(gsend, *cf).astype(F32)
    x_own = own_tokens(x_full).astype(F32)
    gain_by_p1 = jnp.concatenate([a20[:4, 400 - cut - 16, :128], a21[:4, 400 - cut - 16, :128]])
    gain1 = jnp.take(gain_by_p1, order, axis=0).reshape(1, 1, model).astype(F32)
    inverse1 = lax.rsqrt(jnp.mean(x_own * x_own, axis=-1, keepdims=True) + EPSILON)
    scaled1 = grad_h1 * gain1
    grad_input = to_owner(
        own_tokens(grad_middle) + inverse1 * scaled1
        - x_own * (inverse1 * inverse1 * inverse1)
        * jnp.mean(scaled1 * x_own, axis=-1, keepdims=True))

    gu_send = gux1.reshape(8, units, 256)
    gu_keep = gux0.reshape(8, units, 256)
    gu_total = scattered(gu_send, gu_keep, (xf, yf, z1, zm))
    down_total = scattered(down_full[1], down_full[0], (yf, xf, z1, zm))
    attn_total = scattered(out1, out0, (yf, xf, z1, zm))
    gain_total = attn_total[384]
    gain_other = flip(jnp.broadcast_to(gain_total[None, :128], (8, 128)), *cf)[0]
    return (
        output,
        grad_input,
        grad_first,
        postscatter(gain_total[:128] + gain_other),
        postscatter(attn_total[:128]),
        postscatter(attn_total[128:256]),
        postscatter(attn_total[256:384]),
        postscatter(attn_total[400:]),
        postscatter(gain_total[128:]),
        postscatter(gu_total[:, :128].T),
        postscatter(gu_total[:, 128:].T),
        postscatter(down_total),
    )


def solution(mesh):
    cut = P("dp", "seq")
    flat = P("dp")
    whole = P("dp", "seq", None)
    return jax.shard_map(
        on_device,
        mesh=mesh,
        in_specs=(whole, whole, flat, flat, cut, cut, cut, cut, flat, cut, cut, cut, whole),
        out_specs=(whole, whole, whole, flat, cut, cut, cut, cut, flat, cut, cut, cut),
        check_vma=False,
    )
```

time: 1440 us -> 539 us (0.37)
  waiting for transfers between devices: 799 us -> 254 us
  blocking collectives: 197 us -> 0 us
  matrix products: 195 us -> 0 us
  Pallas kernels: 0 us -> 126 us
  local copies, waits for them, and re-layouts: 102 us -> 16.9 us
  between operations: 17.1 us -> 2.37 us
    reduce_scatter x14 -> x0, waiting for transfers between devices: 682 us -> none  [the longest x1 76 us: on_device(): lax.psum_scatter(summed_seq[7], 'dp', scatter_dimension=0, tiled=True)]
    ppermute x7 -> x44, waiting for transfers between devices: 32.4 us -> 254 us  [flip(): return lax.ppermute(value, axis, pairs)]
    dot_general x45 -> x0, matrix products: 195 us -> none  [the longest x7 36.4 us: dot_plain(): return jnp.dot(left, right, preferred_element_type=jnp.float32)]
    all_gather x6 -> x0, blocking collectives: 175 us -> none  [the longest x1 36.2 us: on_device(): lax.all_gather(key_weight, 'dp', axis=0, tiled=True)]
    pallas_call x0 -> x7, Pallas kernels: none -> 126 us  [call(): pl.pallas_call(body, out_shape=[jax.ShapeDtypeStruct(shape, kind) for sha...]
    all_gather x10 -> x0, waiting for transfers between devices: 42.8 us -> none  [the longest x1 36.8 us: on_device(): lax.all_gather(ffn_rows[3], 'seq', axis=1, tiled=True)]
    unnamed x28 -> x0, waiting for transfers between devices: 41.1 us -> none
    another operation x12 -> x6, local copies, waits for them, and re-layouts: 34.5 us -> 2.85 us  [the longest x2 1.04 us: on_device(): cosine = jnp.tile(jnp.cos(angles), (1, 4))]
  transfers between devices with their start and end apart: 33 -> 44, of which waited for: 21 -> 22; matrix products, arithmetic and copies ran while one was open for 20% -> 17% of each run, Pallas kernels for 0% -> 15%
where the time goes in v1:
time: 539 us; the launch traced here: 530 us
  waiting for transfers between devices  254 us (47%)
  Pallas kernels  126 us (23%)
  other arithmetic  78.5 us (15%)
  starting transfers between devices  51.9 us (10%)
  local copies, waits for them, and re-layouts  16.9 us (3%)
    ppermute x44, waiting for transfers between devices, flip(): return lax.ppermute(value, axis, pairs)  254 us
    pallas_call x7, Pallas kernels, call(): pl.pallas_call(body, out_shape=[jax.ShapeDtypeStruct(shape, kind) for sha...  126 us
    ppermute x44, starting transfers between devices, flip(): return lax.ppermute(value, axis, pairs)  51.9 us
    select_n x21, other arithmetic, pick(): return jnp.where(flag == 1, when_one, when_zero)  23.5 us
    concatenate x12, other arithmetic, gathered(): held = jnp.concatenate([held, flip(held, axis, mask)], axis=0)  15.7 us
  transfers between devices with their start and end apart: 44, of which 22 were waited for; matrix products, arithmetic and copies ran while one was open for 17% of the time, Pallas kernels for 15%

profile of v1, /device:TPU:0, one launch (start us, length us, event | category | flops | bytes accessed | tf_op | source)
XLA Modules:
  0.0 529.9 jit_solution(9953617542229089040)
XLA Ops:
  1.7 5.1 collective-permute-start.12
  6.8 6.1 %collective-permute-done.12 = bf16[1,480,256]{2,1,0:T(8,128)(2,1)S(1)} collective-permute-done((bf16[1,480,256]{2,1,0:T(8,128)(2,1)S(1)}, bf16[1,480,256]{2,1,0:T(8,128)(2,1)S(1)}, u32[]{:S(2)}, u32[]{:S(2)}) %collective-permute-start.12) | collective-permute-done | bytes 245792 | tf_op jit(solution)/shard_map/ppermute | solution.py:35
  12.9 4.9 collective-permute-start.13
  20.1 2.5 collective-permute-start.8
  22.5 6.2 %collective-permute-done.13 = bf16[2,480,256]{2,1,0:T(8,128)(2,1)S(1)} collective-permute-done((bf16[2,480,256]{2,1,0:T(8,128)(2,1)S(1)}, bf16[2,480,256]{2,1,0:T(8,128)(2,1)S(1)}, u32[]{:S(2)}, u32[]{:S(2)}) %collective-permute-start.13) | collective-permute-done | bytes 491552 | tf_op jit(solution)/shard_map/ppermute | solution.py:35
  29.8 1.5 collective-permute-start.14
  32.0 2.6 collective-permute-start.4
  37.1 1.5 collective-permute-start.2
  40.0 2.1 select_bitcast_fusion.4
  42.1 10.0 %collective-permute-done.14 = bf16[4,480,256]{2,1,0:T(8,128)(2,1)} collective-permute-done((bf16[4,480,256]{2,1,0:T(8,128)(2,1)}, bf16[4,480,256]{2,1,0:T(8,128)(2,1)}, u32[]{:S(2)}, u32[]{:S(2)}) %collective-permute-start.14) | collective-permute-done | bytes 983072 | tf_op jit(solution)/shard_map/ppermute | solution.py:35
  52.0 1.5 pad_maximum_fusion.2.od0
  53.5 1.6 collective-permute-start.15
  55.2 1.5 fusion.28
  57.4 1.6 pad_maximum_fusion.17
  66.1 1.7 collective-permute-start.5
  69.0 2.6 maximum_select_fusion.2
  73.0 1.6 collective-permute-start.6
  75.6 41.2 %collective-permute-done = bf16[256,1024]{1,0:T(8,128)(2,1)S(1)} collective-permute-done((bf16[256,1024]{1,0:T(8,128)(2,1)}, bf16[256,1024]{1,0:T(8,128)(2,1)S(1)}, u32[]{:S(2)}, u32[]{:S(2)}) %collective-permute-start) | collective-permute-done | bytes 524320 | tf_op jit(solution)/shard_map/ppermute | solution.py:35
  117.3 4.2 collective-permute-done.10
  123.4 1.6 fusion.22
  127.8 2.2 maximum_select_fusion.3
  130.0 1.6 collective-permute-start.7
  131.5 2.2 pad_maximum_fusion.4
  137.0 2.3 slice_multiply_fusion
  139.3 3.5 collective-permute-done.11.a21
  142.8 9.0 %collective-permute-done.7.a11 = bf16[8,208,256]{2,1,0:T(8,128)(2,1)S(1)} collective-permute-done((bf16[8,208,256]{2,1,0:T(8,128)(2,1)S(1)}, bf16[8,208,256]{2,1,0:T(8,128)(2,1)S(1)}, u32[]{:S(2)}, u32[]{:S(2)}) %collective-permute-start.7) | collective-permute-done | bytes 852000 | tf_op jit(solution)/shard_map/ppermute | solution.py:35
  152.7 11.8 %shard_map.220 = (bf16[1024,1024]{1,0:T(8,128)(2,1)}, bf16[1024,512]{1,0:T(8,128)(2,1)}, bf16[1024,512]{1,0:T(8,128)(2,1)}, bf16[1024,512]{1,0:T(8,128)(2,1)}) custom-call(s32[5]{0:T(128)} %stack.199.info, bf16[1024,1024]{1,0:T(8,128)(2,1)} %bitcast.256, bf16[1024,1024]{1,0:T(8,128)(2,1)} %bitcast.269, f32[1024,128]{1,0:T(8,128)} %copy.110.cosine, ...), custom_call_target="tpu_custom_call" | custom-call | flops 3221225472 | bytes 14680064 | tf_op jit(solution)/shard_map/pallas_call | solution.py:48
  164.5 15.5 %shard_map.221 = (bf16[1024,512]{1,0:T(8,128)(2,1)}, f32[4,2,1024]{2,1,0:T(2,128)}) custom-call(bf16[1024,512]{1,0:T(8,128)(2,1)} %get-tuple-element.36.q, bf16[1024,512]{1,0:T(8,128)(2,1)} %get-tuple-element.37.k, bf16[1024,512]{1,0:T(8,128)(2,1)} %get-tuple-element.38.b), custom_call_target="tpu_custom_call" | custom-call | flops 2147483648 | bytes 4194304 | tf_op jit(solution)/shard_map/pallas_call | solution.py:48
  181.3 5.8 %shard_map.222 = bf16[1024,1024]{1,0:T(8,128)(2,1)} custom-call(s32[5]{0:T(128)} %stack.199.info, bf16[1024,512]{1,0:T(8,128)(2,1)} %get-tuple-element.39.att, bf16[8,480,256]{2,1,0:T(8,128)(2,1)} %copy-done.2, bf16[8,480,256]{2,1,0:T(8,128)(2,1)} %collective-permute-done.15.od1, bf16[2,2,2,480,256]{4,3,2,1,0:T(8,128)(2,1)} %copy-done.6), custom_call_target="tpu_custom_call" | custom-call | flops 1073741824 | bytes 5242880 | tf_op jit(solution)/shard_map/pallas_call | solution.py:48
  187.1 2.9 pad_maximum_fusion.g0
  194.2 3.9 multiply_reduce_fusion.2
  198.1 2.0 multiply_convert_fusion.h2
  200.7 54.5 %collective-permute-done.21.g1 = bf16[8,704,256]{2,1,0:T(8,128)(2,1)} collective-permute-done((bf16[8,704,256]{2,1,0:T(8,128)(2,1)}, bf16[8,704,256]{2,1,0:T(8,128)(2,1)}, u32[]{:S(2)}, u32[]{:S(2)}) %collective-permute-start.21) | collective-permute-done | bytes 2883616 | tf_op jit(solution)/shard_map/ppermute | solution.py:35
  255.2 49.0 %shard_map.223 = (bf16[1024,1024]{1,0:T(8,128)(2,1)}, bf16[2,4,704,256]{3,2,1,0:T(8,128)(2,1)}, bf16[2,4,704,256]{3,2,1,0:T(8,128)(2,1)}, bf16[2,2,2,352,256]{4,...) custom-call(s32[5]{0:T(128)} %stack.199.info, ...), custom_call_target="tpu_custom_call" | custom-call | flops 26575110144 | bytes 41943040 | tf_op jit(solution)/shard_map/pallas_call | solution.py:48
  306.3 5.4 %collective-permute-done.22 = bf16[2,256,1024]{2,1,0:T(8,128)(2,1)} collective-permute-done((bf16[2,256,1024]{2,1,0:T(8,128)(2,1)}, bf16[2,256,1024]{2,1,0:T(8,128)(2,1)}, u32[]{:S(2)}, u32[]{:S(2)}) %collective-permute-start.22) | collective-permute-done | bytes 1048608 | tf_op jit(solution)/shard_map/ppermute | solution.py:35
  311.7 4.1 fusion.12
  316.9 1.5 collective-permute-start.23
  319.6 2.9 broadcast_select_fusion.3
  322.5 3.9 multiply_reduce_fusion
  326.4 4.0 fusion.39
  330.4 7.5 %shard_map.224 = (bf16[1024,512]{1,0:T(8,128)(2,1)}, bf16[2,2,2,128,256]{4,3,2,1,0:T(8,128)(2,1)}, bf16[2,2,2,128,256]{4,3,2,1,0:T(8,128)(2,1)}) custom-call(s32[5]{0:T(128)} %stack.199.info, bf16[1024,1024]{1,0:T(8,128)(2,1)} %get-tuple-element.64.gb, bf16[1024,512]{1,0:T(8,128)(2,1)} %get-tuple-element.39.att, bf16[8,480,256]{2,1,0:T(8,128)(2,1)} %copy-done.2, ...), custom_call_target="tpu_custom_call" | custom-call | flops 2147483648 | bytes 6291456 | tf_op jit(solution)/shard_map/pallas_call | solution.py:48
  337.8 20.1 %shard_map.225 = (bf16[1024,512]{1,0:T(8,128)(2,1)}, bf16[1024,512]{1,0:T(8,128)(2,1)}, bf16[1024,512]{1,0:T(8,128)(2,1)}) custom-call(bf16[1024,512]{1,0:T(8,128)(2,1)} %get-tuple-element.36.q, bf16[1024,512]{1,0:T(8,128)(2,1)} %get-tuple-element.37.k, bf16[1024,512]{1,0:T(8,128)(2,1)} %get-tuple-element.38.b, bf16[1024,512]{1,0:T(8,128)(2,1)} %get-tuple-element.43.datt, ...), custom_call_target="tpu_custom_call" | custom-call | flops 5368709120 | bytes 8388608 | tf_op jit(solution)/shard_map/pallas_call | solution.py:48
  363.2 1.5 collective-permute-start.29
  366.0 16.6 %shard_map.226 = (bf16[8,528,256]{2,1,0:T(8,128)(2,1)}, bf16[8,528,256]{2,1,0:T(8,128)(2,1)}, f32[2,256,1024]{2,1,0:T(8,128)}, bf16[2,256,1024]{2,1,0:T(8,128)(2,1)}) custom-call(s32[5]{0:T(128)} %stack.199.info, bf16[1024,512]{1,0:T(8,128)(2,1)} %get-tuple-element.45.dq, bf16[1024,512]{1,0:T(8,128)(2,1)} %get-tuple-element.46.dk, ...), custom_call_target="tpu_custom_call" | custom-call | flops 6442450944 | bytes 20971520 | tf_op jit(solution)/shard_map/pallas_call | solution.py:48
  382.8 13.1 %collective-permute-done.40 = bf16[8,352,256]{2,1,0:T(8,128)(2,1)} collective-permute-done((bf16[8,352,256]{2,1,0:T(8,128)(2,1)}, bf16[8,352,256]{2,1,0:T(8,128)(2,1)}, u32[]{:S(2)}, u32[]{:S(2)}) %collective-permute-start.40) | collective-permute-done | bytes 1441824 | tf_op jit(solution)/shard_map/ppermute | solution.py:35
  396.0 1.8 convert_add_fusion.3
  397.9 1.6 collective-permute-start.41
  399.5 2.4 maximum_select_fusion.7
  402.4 2.5 convert_add_fusion
  405.0 1.6 collective-permute-start.36
  407.2 2.7 fusion.15
  409.9 5.0 collective-permute-done.41
  417.7 35.8 %collective-permute-done.30 = bf16[8,528,256]{2,1,0:T(8,128)(2,1)S(1)} collective-permute-done((bf16[8,528,256]{2,1,0:T(8,128)(2,1)S(1)}, bf16[8,528,256]{2,1,0:T(8,128)(2,1)S(1)}, u32[]{:S(2)}, u32[]{:S(2)}) %collective-permute-start.30) | collective-permute-done | bytes 2162720 | tf_op jit(solution)/shard_map/ppermute | solution.py:35
  454.0 1.6 collective-permute-start.31
  455.9 2.2 collective-permute-start.43
  458.1 26.3 %collective-permute-done.36 = bf16[4,704,256]{2,1,0:T(8,128)(2,1)S(1)} collective-permute-done((bf16[4,704,256]{2,1,0:T(8,128)(2,1)S(1)}, bf16[4,704,256]{2,1,0:T(8,128)(2,1)S(1)}, u32[]{:S(2)}, u32[]{:S(2)}) %collective-permute-start.36) | collective-permute-done | bytes 1441824 | tf_op jit(solution)/shard_map/ppermute | solution.py:35
  485.9 2.1 collective-permute-start.32
  488.0 7.0 %collective-permute-done.27 = bf16[256,1024]{1,0:T(8,128)(2,1)S(1)} collective-permute-done((bf16[256,1024]{1,0:T(8,128)(2,1)S(1)}, bf16[256,1024]{1,0:T(8,128)(2,1)S(1)}, u32[]{:S(2)}, u32[]{:S(2)}) %collective-permute-start.27) | collective-permute-done | bytes 524320 | tf_op jit(solution)/shard_map/ppermute | solution.py:35
  495.1 8.8 %collective-permute-done.37 = bf16[2,704,256]{2,1,0:T(8,128)(2,1)S(1)} collective-permute-done((bf16[2,704,256]{2,1,0:T(8,128)(2,1)S(1)}, bf16[2,704,256]{2,1,0:T(8,128)(2,1)S(1)}, u32[]{:S(2)}, u32[]{:S(2)}) %collective-permute-start.37) | collective-permute-done | bytes 720928 | tf_op jit(solution)/shard_map/ppermute | solution.py:35
  504.1 2.2 collective-permute-start.38
  507.7 7.1 %collective-permute-done.32 = bf16[2,528,256]{2,1,0:T(8,128)(2,1)S(1)} collective-permute-done((bf16[2,528,256]{2,1,0:T(8,128)(2,1)S(1)}, bf16[2,528,256]{2,1,0:T(8,128)(2,1)S(1)}, u32[]{:S(2)}, u32[]{:S(2)}) %collective-permute-start.32) | collective-permute-done | bytes 540704 | tf_op jit(solution)/shard_map/ppermute | solution.py:35
  515.0 2.6 collective-permute-start.33
  517.5 5.9 %collective-permute-done.38 = bf16[1,704,256]{2,1,0:T(8,128)(2,1)S(1)} collective-permute-done((bf16[1,704,256]{2,1,0:T(8,128)(2,1)S(1)}, bf16[1,704,256]{2,1,0:T(8,128)(2,1)S(1)}, u32[]{:S(2)}, u32[]{:S(2)}) %collective-permute-start.38) | collective-permute-done | bytes 360480 | tf_op jit(solution)/shard_map/ppermute | solution.py:35
  524.4 3.0 collective-permute-done.33
  (218 shorter events, 57.6 us)
Async XLA Ops:
  0.6 30.7 %copy-start.29 = (bf16[128,256]{1,0:T(8,128)(2,1)S(1)}, bf16[128,256]{1,0:T(8,128)(2,1)}, u32[]{:S(2)}) copy-start(bf16[128,256]{1,0:T(8,128)(2,1)} %param.20) | copy-start | bytes 196612
  0.7 30.7 %copy-start.32 = (bf16[128,256]{1,0:T(8,128)(2,1)S(1)}, bf16[128,256]{1,0:T(8,128)(2,1)}, u32[]{:S(2)}) copy-start(bf16[128,256]{1,0:T(8,128)(2,1)} %param.19) | copy-start | bytes 196612
  0.7 33.9 %copy-start.30 = (bf16[128,704]{0,1:T(8,128)(2,1)S(1)}, bf16[128,704]{0,1:T(8,128)(2,1)}, u32[]{:S(2)}) copy-start(bf16[128,704]{0,1:T(8,128)(2,1)} %param.25) | copy-start | bytes 540676
  0.7 33.9 %copy-start.31 = (bf16[128,704]{0,1:T(8,128)(2,1)S(1)}, bf16[128,704]{0,1:T(8,128)(2,1)}, u32[]{:S(2)}) copy-start(bf16[128,704]{0,1:T(8,128)(2,1)} %param.24) | copy-start | bytes 540676
  1.7 34.2 %copy-start.8 = (bf16[2,256,1024]{2,1,0:T(8,128)(2,1)S(1)}, bf16[2,256,1024]{2,1,0:T(8,128)(2,1)}, u32[]{:S(2)}) copy-start(bf16[2,256,1024]{2,1,0:T(8,128)(2,1)} %param.27) | copy-start | bytes 3145732
  1.7 34.2 %copy-start.10 = (bf16[2,256,1024]{2,1,0:T(8,128)(2,1)S(1)}, bf16[2,256,1024]{2,1,0:T(8,128)(2,1)}, u32[]{:S(2)}) copy-start(bf16[2,256,1024]{2,1,0:T(8,128)(2,1)} %param.16) | copy-start | bytes 3145732
  1.7 11.2 %collective-permute-start.12 = (bf16[1,480,256]{2,1,0:T(8,128)(2,1)S(1)}, bf16[1,480,256]{2,1,0:T(8,128)(2,1)S(1)}, u32[]{:S(2)}, u32[]{:S(2)}) collective-permute-start(bf16[1,480,256]{2,1,0:T(8,128)(2,1)S(1)} %maximum_bitcast_fusion.3), channel_id=1, source_target_pairs={{0,6},{1,7},{2,4},{3,5},{4,2},{5,3},{6,0},{7,1},{8,14},{9,15},{10,... | collective-permute-start | bytes 737288 | tf_op jit(solution)/shard_map/ppermute | solution.py:35
  12.9 15.8 %collective-permute-start.13 = (bf16[2,480,256]{2,1,0:T(8,128)(2,1)S(1)}, bf16[2,480,256]{2,1,0:T(8,128)(2,1)S(1)}, u32[]{:S(2)}, u32[]{:S(2)}) collective-permute-start(bf16[2,480,256]{2,1,0:T(8,128)(2,1)S(1)} %pad_maximum_fusion.12), channel_id=1, source_target_pairs={{0,2},{1,3},{2,0},{3,1},{4,6},{5,7},{6,4},{7,5},{8,10},{9,11},{10,... | collective-permute-start | bytes 1474568 | tf_op jit(solution)/shard_map/ppermute | solution.py:35
  20.1 37.3 %collective-permute-start.8 = (bf16[1,192,256]{2,1,0:T(8,128)(2,1)}, bf16[1,192,256]{2,1,0:T(8,128)(2,1)}, u32[]{:S(2)}, u32[]{:S(2)}) collective-permute-start(bf16[1,192,256]{2,1,0:T(8,128)(2,1)} %fusion.33), channel_id=1, source_target_pairs={{0,6},{1,7},{2,4},{3,5},{4,2},{5,3},{6,0},{7,1},{8,14},{9,15},{10,... | collective-permute-start | bytes 294920 | tf_op jit(solution)/shard_map/ppermute | solution.py:35
  28.7 5.9 %copy-start.20 = (bf16[2,480,256]{2,1,0:T(8,128)(2,1)}, bf16[2,480,256]{2,1,0:T(8,128)(2,1)S(1)}, u32[]{:S(2)}) copy-start(bf16[2,480,256]{2,1,0:T(8,128)(2,1)S(1)} %collective-permute-done.13) | copy-start | bytes 1474564
  29.8 22.2 %collective-permute-start.14 = (bf16[4,480,256]{2,1,0:T(8,128)(2,1)}, bf16[4,480,256]{2,1,0:T(8,128)(2,1)}, u32[]{:S(2)}, u32[]{:S(2)}) collective-permute-start(bf16[4,480,256]{2,1,0:T(8,128)(2,1)} %pad_maximum_fusion.8), channel_id=1, source_target_pairs={{0,1},{1,0},{2,3},{3,2},{4,5},{5,4},{6,7},{7,6},{8,9},{9,8},{10,11... | collective-permute-start | bytes 2949128 | tf_op jit(solution)/shard_map/ppermute | solution.py:35
  32.0 31.9 %collective-permute-start.4 = (bf16[1,208,256]{2,1,0:T(8,128)(2,1)}, bf16[1,208,256]{2,1,0:T(8,128)(2,1)}, u32[]{:S(2)}, u32[]{:S(2)}) collective-permute-start(bf16[1,208,256]{2,1,0:T(8,128)(2,1)} %fusion.31), channel_id=1, source_target_pairs={{0,6},{1,7},{2,4},{3,5},{4,2},{5,3},{6,0},{7,1},{8,14},{9,15},{10,... | collective-permute-start | bytes 319496 | tf_op jit(solution)/shard_map/ppermute | solution.py:35
  34.7 38.3 %collective-permute-start.18 = (bf16[1,704,256]{2,1,0:T(8,128)(2,1)S(1)}, bf16[1,704,256]{2,1,0:T(8,128)(2,1)}, u32[]{:S(2)}, u32[]{:S(2)}) collective-permute-start(bf16[1,704,256]{2,1,0:T(8,128)(2,1)S(1)} %maximum_bitcast_fusion.2), channel_id=1, source_target_pairs={{0,6},{1,7},{2,4},{3,5},{4,2},{5,3},{6,0},{7,1},{8,14},{9,15},{10,... | collective-permute-start | bytes 1081352 | tf_op jit(solution)/shard_map/ppermute | solution.py:35
  37.1 31.8 %collective-permute-start.2 = (bf16[2,256,1024]{2,1,0:T(8,128)(2,1)}, bf16[2,256,1024]{2,1,0:T(8,128)(2,1)}, u32[]{:S(2)}, u32[]{:S(2)}) collective-permute-start(bf16[2,256,1024]{2,1,0:T(8,128)(2,1)} %fusion.16), channel_id=1, source_target_pairs={{0,16},{8,24},{16,0},{24,8},{1,17},{9,25},{17,1},{25,9},{2,18},{10... | collective-permute-start | bytes 3145736 | tf_op jit(solution)/shard_map/ppermute | solution.py:35
  42.1 13.1 %copy-start.9 = (bf16[2,256,1024]{2,1,0:T(8,128)(2,1)S(1)}, bf16[2,256,1024]{2,1,0:T(8,128)(2,1)}, u32[]{:S(2)}) copy-start(bf16[2,256,1024]{2,1,0:T(8,128)(2,1)} %param.27) | copy-start | bytes 3145732
  42.1 13.1 %copy-start.11 = (bf16[2,256,1024]{2,1,0:T(8,128)(2,1)S(1)}, bf16[2,256,1024]{2,1,0:T(8,128)(2,1)}, u32[]{:S(2)}) copy-start(bf16[2,256,1024]{2,1,0:T(8,128)(2,1)} %param.16) | copy-start | bytes 3145732
  53.5 69.1 %copy-start.2 = (bf16[8,480,256]{2,1,0:T(8,128)(2,1)}, bf16[8,480,256]{2,1,0:T(8,128)(2,1)S(1)}, u32[]{:S(2)}) copy-start(bf16[8,480,256]{2,1,0:T(8,128)(2,1)S(1)} %pad_maximum_fusion.2.od0) | copy-start | bytes 5898244
  53.5 69.2 %collective-permute-start.15 = (bf16[8,480,256]{2,1,0:T(8,128)(2,1)S(1)}, bf16[8,480,256]{2,1,0:T(8,128)(2,1)}, u32[]{:S(2)}, u32[]{:S(2)}) collective-permute-start(bf16[8,480,256]{2,1,0:T(8,128)(2,1)S(1)} %pad_maximum_fusion.2.od0), channel_id=1, source_target_pairs={{0,16},{8,24},{16,0},{24,8},{1,17},{9,25},{17,1},{25,9},{2,18},{10... | collective-permute-start | bytes 5898248 | tf_op jit(solution)/shard_map/ppermute | solution.py:35
  55.1 5.3 %copy-start.25 = (f32[1024,32]{0,1:T(8,128)S(1)}, f32[1024,32]{0,1:T(8,128)}, u32[]{:S(2)}) copy-start(f32[1024,32]{0,1:T(8,128)} %get-tuple-element.111) | copy-start | bytes 393220
  55.1 5.3 %copy-start.26 = (f32[1024,32]{0,1:T(8,128)S(1)}, f32[1024,32]{0,1:T(8,128)}, u32[]{:S(2)}) copy-start(f32[1024,32]{0,1:T(8,128)} %get-tuple-element.112) | copy-start | bytes 393220
  59.0 7.2 %collective-permute-start.9 = (bf16[2,192,256]{2,1,0:T(8,128)(2,1)}, bf16[2,192,256]{2,1,0:T(8,128)(2,1)}, u32[]{:S(2)}, u32[]{:S(2)}) collective-permute-start(bf16[2,192,256]{2,1,0:T(8,128)(2,1)} %pad_maximum_fusion.17), channel_id=1, source_target_pairs={{0,2},{1,3},{2,0},{3,1},{4,6},{5,7},{6,4},{7,5},{8,10},{9,11},{10,... | collective-permute-start | bytes 589832 | tf_op jit(solution)/shard_map/ppermute | solution.py:35
  63.9 52.9 %collective-permute-start = (bf16[256,1024]{1,0:T(8,128)(2,1)}, bf16[256,1024]{1,0:T(8,128)(2,1)S(1)}, u32[]{:S(2)}, u32[]{:S(2)}) collective-permute-start(bf16[256,1024]{1,0:T(8,128)(2,1)} %get-tuple-element.97), channel_id=1, source_target_pairs={{0,16},{8,24},{16,0},{24,8},{1,17},{9,25},{17,1},{25,9},{2,18},{10... | collective-permute-start | bytes 1572872 | tf_op jit(solution)/shard_map/ppermute | solution.py:35
  66.1 5.8 %collective-permute-start.5 = (bf16[2,208,256]{2,1,0:T(8,128)(2,1)S(1)}, bf16[2,208,256]{2,1,0:T(8,128)(2,1)S(1)}, u32[]{:S(2)}, u32[]{:S(2)}) collective-permute-start(bf16[2,208,256]{2,1,0:T(8,128)(2,1)S(1)} %pad_maximum_fusion.16), channel_id=1, source_target_pairs={{0,2},{1,3},{2,0},{3,1},{4,6},{5,7},{6,4},{7,5},{8,10},{9,11},{10,... | collective-permute-start | bytes 638984 | tf_op jit(solution)/shard_map/ppermute | solution.py:35
  68.9 52.6 %collective-permute-start.10 = (bf16[4,192,256]{2,1,0:T(8,128)(2,1)S(1)}, bf16[4,192,256]{2,1,0:T(8,128)(2,1)S(1)}, u32[]{:S(2)}, u32[]{:S(2)}) collective-permute-start(bf16[4,192,256]{2,1,0:T(8,128)(2,1)S(1)} %pad_maximum_fusion.14), channel_id=1, source_target_pairs={{0,16},{8,24},{16,0},{24,8},{1,17},{9,25},{17,1},{25,9},{2,18},{10... | collective-permute-start | bytes 1179656 | tf_op jit(solution)/shard_map/ppermute | solution.py:35
  72.0 64.1 %collective-permute-start.3 = (bf16[2,2,256,1024]{3,2,1,0:T(8,128)(2,1)S(1)}, bf16[2,2,256,1024]{3,2,1,0:T(8,128)(2,1)S(1)}, u32[]{:S(2)}, u32[]{:S(2)}) collective-permute-start(bf16[2,2,256,1024]{3,2,1,0:T(8,128)(2,1)S(1)} %maximum_select_fusion.2), channel_id=1, source_target_pairs={{0,8},{8,0},{16,24},{24,16},{1,9},{9,1},{17,25},{25,17},{2,10},{10... | collective-permute-start | bytes 6291464 | tf_op jit(solution)/shard_map/ppermute | solution.py:35
  73.0 53.5 %collective-permute-start.6 = (bf16[4,208,256]{2,1,0:T(8,128)(2,1)S(1)}, bf16[4,208,256]{2,1,0:T(8,128)(2,1)S(1)}, u32[]{:S(2)}, u32[]{:S(2)}) collective-permute-start(bf16[4,208,256]{2,1,0:T(8,128)(2,1)S(1)} %pad_maximum_fusion.13), channel_id=1, source_target_pairs={{0,1},{1,0},{2,3},{3,2},{4,5},{5,4},{6,7},{7,6},{8,9},{9,8},{10,11... | collective-permute-start | bytes 1277960 | tf_op jit(solution)/shard_map/ppermute | solution.py:35
  116.8 13.2 %collective-permute-start.19 = (bf16[2,704,256]{2,1,0:T(8,128)(2,1)S(1)}, bf16[2,704,256]{2,1,0:T(8,128)(2,1)S(1)}, u32[]{:S(2)}, u32[]{:S(2)}) collective-permute-start(bf16[2,704,256]{2,1,0:T(8,128)(2,1)S(1)} %pad_maximum_fusion.11), channel_id=1, source_target_pairs={{0,2},{1,3},{2,0},{3,1},{4,6},{5,7},{6,4},{7,5},{8,10},{9,11},{10,... | collective-permute-start | bytes 2162696 | tf_op jit(solution)/shard_map/ppermute | solution.py:35
  121.5 12.3 %collective-permute-start.1 = (bf16[2,256,1024]{2,1,0:T(8,128)(2,1)S(1)}, bf16[2,256,1024]{2,1,0:T(8,128)(2,1)S(1)}, u32[]{:S(2)}, u32[]{:S(2)}) collective-permute-start(bf16[2,256,1024]{2,1,0:T(8,128)(2,1)S(1)} %maximum_select_fusion.5), channel_id=1, source_target_pairs={{0,8},{8,0},{16,24},{24,16},{1,9},{9,1},{17,25},{25,17},{2,10},{10... | collective-permute-start | bytes 3145736 | tf_op jit(solution)/shard_map/ppermute | solution.py:35
  122.8 20.0 %collective-permute-start.11 = (bf16[8,192,256]{2,1,0:T(8,128)(2,1)S(1)}, bf16[8,192,256]{2,1,0:T(8,128)(2,1)S(1)}, u32[]{:S(2)}, u32[]{:S(2)}) collective-permute-start(bf16[8,192,256]{2,1,0:T(8,128)(2,1)S(1)} %pad_maximum_fusion.10.a20), channel_id=1, source_target_pairs={{0,1},{1,0},{2,3},{3,2},{4,5},{5,4},{6,7},{7,6},{8,9},{9,8},{10,11... | collective-permute-start | bytes 2359304 | tf_op jit(solution)/shard_map/ppermute | solution.py:35
  126.5 53.5 %collective-permute-start.16 = (bf16[2,2,2,480,256]{4,3,2,1,0:T(8,128)(2,1)}, bf16[2,2,2,480,256]{4,3,2,1,0:T(8,128)(2,1)S(1)}, u32[]{:S(2)}, u32[]{:S(2)}) collective-permute-start(bf16[2,2,2,480,256]{4,3,2,1,0:T(8,128)(2,1)} %pad_maximum_fusion.3), channel_id=1, source_target_pairs={{0,8},{8,0},{16,24},{24,16},{1,9},{9,1},{17,25},{25,17},{2,10},{10... | collective-permute-start | bytes 5898248 | tf_op jit(solution)/shard_map/ppermute | solution.py:35
  129.9 4.7 copy-start.15
  130.0 21.8 %collective-permute-start.7 = (bf16[8,208,256]{2,1,0:T(8,128)(2,1)S(1)}, bf16[8,208,256]{2,1,0:T(8,128)(2,1)S(1)}, u32[]{:S(2)}, u32[]{:S(2)}) collective-permute-start(bf16[8,208,256]{2,1,0:T(8,128)(2,1)S(1)} %pad_maximum_fusion.9.a10), channel_id=1, source_target_pairs={{0,16},{8,24},{16,0},{24,8},{1,17},{9,25},{17,1},{25,9},{2,18},{10... | collective-permute-start | bytes 2555912 | tf_op jit(solution)/shard_map/ppermute | solution.py:35
  133.8 53.3 %collective-permute-start.20 = (bf16[4,704,256]{2,1,0:T(8,128)(2,1)}, bf16[4,704,256]{2,1,0:T(8,128)(2,1)}, u32[]{:S(2)}, u32[]{:S(2)}) collective-permute-start(bf16[4,704,256]{2,1,0:T(8,128)(2,1)} %pad_maximum_fusion.4), channel_id=1, source_target_pairs={{0,16},{8,24},{16,0},{24,8},{1,17},{9,25},{17,1},{25,9},{2,18},{10... | collective-permute-start | bytes 4325384 | tf_op jit(solution)/shard_map/ppermute | solution.py:35
  142.8 9.0 %copy-start.33 = (bf16[8,192,256]{2,1,0:T(8,128)(2,1)}, bf16[8,192,256]{2,1,0:T(8,128)(2,1)S(1)}, u32[]{:S(2)}) copy-start(bf16[8,192,256]{2,1,0:T(8,128)(2,1)S(1)} %collective-permute-done.11.a21) | copy-start | bytes 2359300
  181.3 5.9 %copy-start.16 = (bf16[2,704,256]{2,1,0:T(8,128)(2,1)S(1)}, bf16[2,704,256]{2,1,0:T(8,128)(2,1)}, u32[]{:S(2)}) copy-start(bf16[2,704,256]{2,1,0:T(8,128)(2,1)} %copy-done.15) | copy-start | bytes 2162692
  187.0 7.2 %collective-permute-start.17 = (bf16[1024,1024]{1,0:T(8,128)(2,1)}, bf16[1024,1024]{1,0:T(8,128)(2,1)}, u32[]{:S(2)}, u32[]{:S(2)}) collective-permute-start(bf16[1024,1024]{1,0:T(8,128)(2,1)} %shard_map.222), channel_id=1, source_target_pairs={{0,8},{8,0},{16,24},{24,16},{1,9},{9,1},{17,25},{25,17},{2,10},{10... | collective-permute-start | bytes 6291464 | tf_op jit(solution)/shard_map/ppermute | solution.py:35
  190.0 65.2 %collective-permute-start.21 = (bf16[8,704,256]{2,1,0:T(8,128)(2,1)}, bf16[8,704,256]{2,1,0:T(8,128)(2,1)}, u32[]{:S(2)}, u32[]{:S(2)}) collective-permute-start(bf16[8,704,256]{2,1,0:T(8,128)(2,1)} %pad_maximum_fusion.g0), channel_id=1, source_target_pairs={{0,1},{1,0},{2,3},{3,2},{4,5},{5,4},{6,7},{7,6},{8,9},{9,8},{10,11... | collective-permute-start | bytes 8650760 | tf_op jit(solution)/shard_map/ppermute | solution.py:35
  304.2 18.3 %collective-permute-start.24 = (bf16[1024,1024]{1,0:T(8,128)(2,1)}, bf16[1024,1024]{1,0:T(8,128)(2,1)}, u32[]{:S(2)}, u32[]{:S(2)}) collective-permute-start(bf16[1024,1024]{1,0:T(8,128)(2,1)} %get-tuple-element.42), channel_id=1, source_target_pairs={{0,8},{8,0},{16,24},{24,16},{1,9},{9,1},{17,25},{25,17},{2,10},{10... | collective-permute-start | bytes 6291464 | tf_op jit(solution)/shard_map/ppermute | solution.py:35
  304.3 7.5 %collective-permute-start.22 = (bf16[2,256,1024]{2,1,0:T(8,128)(2,1)}, bf16[2,256,1024]{2,1,0:T(8,128)(2,1)}, u32[]{:S(2)}, u32[]{:S(2)}) collective-permute-start(bf16[2,256,1024]{2,1,0:T(8,128)(2,1)} %get-tuple-element.41), channel_id=1, source_target_pairs={{0,8},{8,0},{16,24},{24,16},{1,9},{9,1},{17,25},{25,17},{2,10},{10... | collective-permute-start | bytes 3145736 | tf_op jit(solution)/shard_map/ppermute | solution.py:35
  304.8 13.7 %collective-permute-start.39 = (bf16[2,2,2,352,256]{4,3,2,1,0:T(8,128)(2,1)}, bf16[2,2,2,352,256]{4,3,2,1,0:T(8,128)(2,1)S(1)}, u32[]{:S(2)}, u32[]{:S(2)}) collective-permute-start(bf16[2,2,2,352,256]{4,3,2,1,0:T(8,128)(2,1)} %get-tuple-element.58), channel_id=1, source_target_pairs={{0,8},{8,0},{16,24},{24,16},{1,9},{9,1},{17,25},{25,17},{2,10},{10... | collective-permute-start | bytes 4325384 | tf_op jit(solution)/shard_map/ppermute | solution.py:35
  304.8 97.5 %collective-permute-start.35 = (bf16[8,704,256]{2,1,0:T(8,128)(2,1)}, bf16[8,704,256]{2,1,0:T(8,128)(2,1)}, u32[]{:S(2)}, u32[]{:S(2)}) collective-permute-start(bf16[8,704,256]{2,1,0:T(8,128)(2,1)} %bitcast.277), channel_id=1, source_target_pairs={{0,1},{1,0},{2,3},{3,2},{4,5},{5,4},{6,7},{7,6},{8,9},{9,8},{10,11... | collective-permute-start | bytes 8650760 | tf_op jit(solution)/shard_map/ppermute | solution.py:35
  311.7 7.8 %copy-start.21 = (bf16[2,2,2,352,256]{4,3,2,1,0:T(8,128)(2,1)S(1)}, bf16[2,2,2,352,256]{4,3,2,1,0:T(8,128)(2,1)}, u32[]{:S(2)}) copy-start(bf16[2,2,2,352,256]{4,3,2,1,0:T(8,128)(2,1)} %get-tuple-element.57) | copy-start | bytes 4325380
  315.8 6.7 %copy-start.5 = (bf16[1024,1024]{1,0:T(8,128)(2,1)S(1)}, bf16[1024,1024]{1,0:T(8,128)(2,1)}, u32[]{:S(2)}) copy-start(bf16[1024,1024]{1,0:T(8,128)(2,1)} %get-tuple-element.42) | copy-start | bytes 6291460
  316.9 82.6 %collective-permute-start.23 = (bf16[256,1024]{1,0:T(8,128)(2,1)}, bf16[256,1024]{1,0:T(8,128)(2,1)}, u32[]{:S(2)}, u32[]{:S(2)}) collective-permute-start(bf16[256,1024]{1,0:T(8,128)(2,1)} %get-tuple-element.95), channel_id=1, source_target_pairs={{0,16},{8,24},{16,0},{24,8},{1,17},{9,25},{17,1},{25,9},{2,18},{10... | collective-permute-start | bytes 1572872 | tf_op jit(solution)/shard_map/ppermute | solution.py:35
  359.3 2.5 collective-permute-start.28
  361.3 34.7 %collective-permute-start.40 = (bf16[8,352,256]{2,1,0:T(8,128)(2,1)}, bf16[8,352,256]{2,1,0:T(8,128)(2,1)}, u32[]{:S(2)}, u32[]{:S(2)}) collective-permute-start(bf16[8,352,256]{2,1,0:T(8,128)(2,1)} %bitcast.85), channel_id=1, source_target_pairs={{0,16},{8,24},{16,0},{24,8},{1,17},{9,25},{17,1},{25,9},{2,18},{10... | collective-permute-start | bytes 4325384 | tf_op jit(solution)/shard_map/ppermute | solution.py:35
  361.8 3.0 collective-permute-start.25
  363.2 44.0 %collective-permute-start.29 = (bf16[256,1024]{1,0:T(8,128)(2,1)}, bf16[256,1024]{1,0:T(8,128)(2,1)}, u32[]{:S(2)}, u32[]{:S(2)}) collective-permute-start(bf16[256,1024]{1,0:T(8,128)(2,1)} %get-tuple-element.82), channel_id=1, source_target_pairs={{0,16},{8,24},{16,0},{24,8},{1,17},{9,25},{17,1},{25,9},{2,18},{10... | collective-permute-start | bytes 1572872 | tf_op jit(solution)/shard_map/ppermute | solution.py:35
  382.6 32.6 %collective-permute-start.26 = (bf16[2,256,1024]{2,1,0:T(8,128)(2,1)}, bf16[2,256,1024]{2,1,0:T(8,128)(2,1)S(1)}, u32[]{:S(2)}, u32[]{:S(2)}) collective-permute-start(bf16[2,256,1024]{2,1,0:T(8,128)(2,1)} %get-tuple-element.52), channel_id=1, source_target_pairs={{0,8},{8,0},{16,24},{24,16},{1,9},{9,1},{17,25},{25,17},{2,10},{10... | collective-permute-start | bytes 3145736 | tf_op jit(solution)/shard_map/ppermute | solution.py:35
  396.0 5.9 %copy-start.34 = (bf16[8,528,256]{2,1,0:T(8,128)(2,1)S(1)}, bf16[8,528,256]{2,1,0:T(8,128)(2,1)}, u32[]{:S(2)}) copy-start(bf16[8,528,256]{2,1,0:T(8,128)(2,1)} %get-tuple-element.54) | copy-start | bytes 6488068
  397.9 17.1 %collective-permute-start.41 = (bf16[4,352,256]{2,1,0:T(8,128)(2,1)S(1)}, bf16[4,352,256]{2,1,0:T(8,128)(2,1)S(1)}, u32[]{:S(2)}, u32[]{:S(2)}) collective-permute-start(bf16[4,352,256]{2,1,0:T(8,128)(2,1)S(1)} %slice.658), channel_id=1, source_target_pairs={{0,1},{1,0},{2,3},{3,2},{4,5},{5,4},{6,7},{7,6},{8,9},{9,8},{10,11... | collective-permute-start | bytes 2162696 | tf_op jit(solution)/shard_map/ppermute | solution.py:35
  401.9 51.6 %collective-permute-start.30 = (bf16[8,528,256]{2,1,0:T(8,128)(2,1)S(1)}, bf16[8,528,256]{2,1,0:T(8,128)(2,1)S(1)}, u32[]{:S(2)}, u32[]{:S(2)}) collective-permute-start(bf16[8,528,256]{2,1,0:T(8,128)(2,1)S(1)} %copy-done.34), channel_id=1, source_target_pairs={{0,16},{8,24},{16,0},{24,8},{1,17},{9,25},{17,1},{25,9},{2,18},{10... | collective-permute-start | bytes 6488072 | tf_op jit(solution)/shard_map/ppermute | solution.py:35
  405.0 79.4 %collective-permute-start.36 = (bf16[4,704,256]{2,1,0:T(8,128)(2,1)S(1)}, bf16[4,704,256]{2,1,0:T(8,128)(2,1)S(1)}, u32[]{:S(2)}, u32[]{:S(2)}) collective-permute-start(bf16[4,704,256]{2,1,0:T(8,128)(2,1)S(1)} %slice.656), channel_id=1, source_target_pairs={{0,16},{8,24},{16,0},{24,8},{1,17},{9,25},{17,1},{25,9},{2,18},{10... | collective-permute-start | bytes 4325384 | tf_op jit(solution)/shard_map/ppermute | solution.py:35
  409.9 5.3 %copy-start.3 = (f32[2,256,1024]{2,1,0:T(8,128)S(1)}, f32[2,256,1024]{2,1,0:T(8,128)}, u32[]{:S(2)}) copy-start(f32[2,256,1024]{2,1,0:T(8,128)} %get-tuple-element.51) | copy-start | bytes 6291460
  415.1 40.6 %collective-permute-start.42 = (bf16[2,352,256]{2,1,0:T(8,128)(2,1)S(1)}, bf16[2,352,256]{2,1,0:T(8,128)(2,1)S(1)}, u32[]{:S(2)}, u32[]{:S(2)}) collective-permute-start(bf16[2,352,256]{2,1,0:T(8,128)(2,1)S(1)} %slice.661), channel_id=1, source_target_pairs={{0,2},{1,3},{2,0},{3,1},{4,6},{5,7},{6,4},{7,5},{8,10},{9,11},{10,... | collective-permute-start | bytes 1081352 | tf_op jit(solution)/shard_map/ppermute | solution.py:35
  416.2 37.3 %copy-start.17 = (bf16[8,528,256]{2,1,0:T(8,128)(2,1)S(1)}, bf16[8,528,256]{2,1,0:T(8,128)(2,1)}, u32[]{:S(2)}) copy-start(bf16[8,528,256]{2,1,0:T(8,128)(2,1)} %get-tuple-element.53) | copy-start | bytes 6488068
  417.1 77.9 %collective-permute-start.27 = (bf16[256,1024]{1,0:T(8,128)(2,1)S(1)}, bf16[256,1024]{1,0:T(8,128)(2,1)S(1)}, u32[]{:S(2)}, u32[]{:S(2)}) collective-permute-start(bf16[256,1024]{1,0:T(8,128)(2,1)S(1)} %fusion.18), channel_id=1, source_target_pairs={{0,16},{8,24},{16,0},{24,8},{1,17},{9,25},{17,1},{25,9},{2,18},{10... | collective-permute-start | bytes 1572872 | tf_op jit(solution)/shard_map/ppermute | solution.py:35
  454.0 31.6 %collective-permute-start.31 = (bf16[4,528,256]{2,1,0:T(8,128)(2,1)S(1)}, bf16[4,528,256]{2,1,0:T(8,128)(2,1)S(1)}, u32[]{:S(2)}, u32[]{:S(2)}) collective-permute-start(bf16[4,528,256]{2,1,0:T(8,128)(2,1)S(1)} %slice.657), channel_id=1, source_target_pairs={{0,1},{1,0},{2,3},{3,2},{4,5},{5,4},{6,7},{7,6},{8,9},{9,8},{10,11... | collective-permute-start | bytes 3244040 | tf_op jit(solution)/shard_map/ppermute | solution.py:35
  455.9 28.9 %collective-permute-start.43 = (bf16[1,352,256]{2,1,0:T(8,128)(2,1)S(1)}, bf16[1,352,256]{2,1,0:T(8,128)(2,1)S(1)}, u32[]{:S(2)}, u32[]{:S(2)}) collective-permute-start(bf16[1,352,256]{2,1,0:T(8,128)(2,1)S(1)} %slice.664), channel_id=1, source_target_pairs={{0,6},{1,7},{2,4},{3,5},{4,2},{5,3},{6,0},{7,1},{8,14},{9,15},{10,... | collective-permute-start | bytes 540680 | tf_op jit(solution)/shard_map/ppermute | solution.py:35
  484.7 19.1 %collective-permute-start.37 = (bf16[2,704,256]{2,1,0:T(8,128)(2,1)S(1)}, bf16[2,704,256]{2,1,0:T(8,128)(2,1)S(1)}, u32[]{:S(2)}, u32[]{:S(2)}) collective-permute-start(bf16[2,704,256]{2,1,0:T(8,128)(2,1)S(1)} %slice.659), channel_id=1, source_target_pairs={{0,2},{1,3},{2,0},{3,1},{4,6},{5,7},{6,4},{7,5},{8,10},{9,11},{10,... | collective-permute-start | bytes 2162696 | tf_op jit(solution)/shard_map/ppermute | solution.py:35
  485.9 28.9 %collective-permute-start.32 = (bf16[2,528,256]{2,1,0:T(8,128)(2,1)S(1)}, bf16[2,528,256]{2,1,0:T(8,128)(2,1)S(1)}, u32[]{:S(2)}, u32[]{:S(2)}) collective-permute-start(bf16[2,528,256]{2,1,0:T(8,128)(2,1)S(1)} %slice.660), channel_id=1, source_target_pairs={{0,2},{1,3},{2,0},{3,1},{4,6},{5,7},{6,4},{7,5},{8,10},{9,11},{10,... | collective-permute-start | bytes 1622024 | tf_op jit(solution)/shard_map/ppermute | solution.py:35
  504.1 19.3 %collective-permute-start.38 = (bf16[1,704,256]{2,1,0:T(8,128)(2,1)S(1)}, bf16[1,704,256]{2,1,0:T(8,128)(2,1)S(1)}, u32[]{:S(2)}, u32[]{:S(2)}) collective-permute-start(bf16[1,704,256]{2,1,0:T(8,128)(2,1)S(1)} %slice.662), channel_id=1, source_target_pairs={{0,6},{1,7},{2,4},{3,5},{4,2},{5,3},{6,0},{7,1},{8,14},{9,15},{10,... | collective-permute-start | bytes 1081352 | tf_op jit(solution)/shard_map/ppermute | solution.py:35
  515.0 12.4 %collective-permute-start.33 = (bf16[1,528,256]{2,1,0:T(8,128)(2,1)S(1)}, bf16[1,528,256]{2,1,0:T(8,128)(2,1)S(1)}, u32[]{:S(2)}, u32[]{:S(2)}) collective-permute-start(bf16[1,528,256]{2,1,0:T(8,128)(2,1)S(1)} %slice.663), channel_id=1, source_target_pairs={{0,6},{1,7},{2,4},{3,5},{4,2},{5,3},{6,0},{7,1},{8,14},{9,15},{10,... | collective-permute-start | bytes 811016 | tf_op jit(solution)/shard_map/ppermute | solution.py:35
  528.0 1.2 collective-permute-start.34
  (17 other events, 40.9 us)

commit v2 on v1

v2 whole, which is shorter than its diff:
```python
import functools

import jax
import jax.numpy as jnp
from jax import lax
from jax.experimental import pallas as pl
from jax.experimental.pallas import tpu as pltpu
from jax.sharding import PartitionSpec as P

HEAD = 64
EPSILON = 1e-06
TILE = 256
BLOCKS = 8
F32 = jnp.float32
BF16 = jnp.bfloat16
MESH_Y, MESH_C = 2, 1
ZM, Z1, X1 = 6, 2, 1
SPLIT = 2


def dot_nn(a, b):
    return lax.dot_general(a, b, (((1,), (0,)), ((), ())), preferred_element_type=F32)


def dot_nt(a, b):
    return lax.dot_general(a, b, (((1,), (1,)), ((), ())), preferred_element_type=F32)


def dot_tn(a, b):
    return lax.dot_general(a, b, (((0,), (0,)), ((), ())), preferred_element_type=F32)


def flip(value, axis, mask):
    pairs = [(i, i ^ mask) for i in range(lax.axis_size(axis))]
    return lax.ppermute(value, axis, pairs)


def pick(flag, when_one, when_zero):
    return jnp.where(flag == 1, when_one, when_zero)


def call(
    body, outs, ins, scratch, flops, moved, exps=0, grid=None, in_specs=None, out_specs=None,
    vmem=56,
):
    spaces = {"v": pltpu.VMEM, "s": pltpu.SMEM, "a": pl.ANY}
    if in_specs is None:
        in_specs = [pl.BlockSpec(memory_space=spaces[kind]) for kind, _ in ins]
        out_specs = [pl.BlockSpec(memory_space=pltpu.VMEM) for _ in outs]
    kwargs = {} if grid is None else {"grid": grid}
    return pl.pallas_call(
        body,
        out_shape=[jax.ShapeDtypeStruct(shape, kind) for shape, kind in outs],
        in_specs=in_specs,
        out_specs=out_specs,
        scratch_shapes=scratch,
        cost_estimate=pl.CostEstimate(flops=flops, bytes_accessed=moved, transcendentals=exps),
        compiler_params=pltpu.CompilerParams(vmem_limit_bytes=vmem << 20),
        **kwargs,
    )(*[value for _, value in ins])


def run_copies(copies):
    for copy in copies:
        copy.start()
    for copy in copies:
        copy.wait()


def turned(values, cosine, signed_sine):
    lane = lax.broadcasted_iota(jnp.int32, values.shape, 1)
    ahead = pltpu.roll(values, 128 - HEAD // 2, 1)
    behind = pltpu.roll(values, HEAD // 2, 1)
    partner = jnp.where(lane % HEAD < HEAD // 2, ahead, behind)
    return values * cosine + partner * signed_sine


def bits(count):
    return [tuple((i >> (count - 1 - j)) & 1 for j in range(count)) for i in range(1 << count)]


def place_of(info, bx, q):
    z = info[3] ^ (q >> 1) ^ (3 * (q & 1))
    return z * 2 + (info[4] ^ bx)


def even_of(info):
    return (info[3] & 1) ^ info[1]


def block_of(info, t):
    return t ^ info[0] ^ (info[3] >> 1) ^ even_of(info)


def column_of(info, by, other):
    block = (info[0] ^ by) * 2 + (info[1] ^ other)
    return pl.multiple_of(block * 256, 256)


def source_of(parts, by, bx, q):
    own, over_x, over_y, corner_y, corner_x = parts
    if by == 0:
        return (own, over_x)[bx].at[q]
    if bx == 0:
        return over_y.at[q]
    split = corner_y.shape[0]
    return corner_y.at[q] if q < split else corner_x.at[q - split]


def put(outs, by, bx, q, rows, value):
    send_x, send_y, keep_x, keep_y, own = outs
    split = keep_x.shape[0]
    if by and bx:
        spot = (send_y, q) if q < split else (send_x, q - split)
    elif by:
        spot = (send_y, split + q) if q < split else (keep_y, q - split)
    elif bx:
        spot = (keep_x, q) if q < split else (send_x, 4 - split + q - split)
    else:
        spot = (own, q)
    spot[0][spot[1], rows, :] = value


def put_lanes(outs, by, bx, q, rows, lanes, value):
    class Cut:
        def __init__(self, ref):
            self.ref = ref
            self.shape = ref.shape

        def __setitem__(self, spot, content):
            self.ref[spot[0], spot[1], lanes] = content

    put(tuple(Cut(ref) for ref in outs), by, bx, q, rows, value)


def pack_body(*refs):
    out = refs[-1]
    at = 0
    for ref in refs[:-1]:
        if len(ref.shape) == 2:
            out[at] = ref[...]
            at += 1
        else:
            out[at : at + ref.shape[0]] = ref[...]
            at += ref.shape[0]


def piece_of(info, t, own, over_y, core):
    near = (t & 1) == info[1]
    mine = jnp.where(near, own[info[0]], core[0])
    other = jnp.where(near, over_y[...], core[1])
    return jnp.where((t >> 1) == info[0], mine, other)


def attn_copies(info, parts, w, sem):
    copies = []
    for by, bx in bits(2):
        for q in range(4):
            copies.append(pltpu.make_async_copy(
                source_of(parts, by, bx, q), w.at[by, place_of(info, bx, q)],
                sem.at[len(copies)]))
    return copies


def qkv_body(*refs):
    info, x_parts, fv_parts, cosine, sine = refs[0], refs[1:4], refs[4:7], refs[7], refs[8]
    parts = refs[9:14]
    x, h1, q, k, b, gains, w, sem = refs[14:]
    run_copies(attn_copies(info, parts, w, sem))
    rows = 128
    width = w.shape[3]
    model = x.shape[1]
    for j in range(2):
        pair = w[0, :, 3 * rows : 3 * rows + 16, j * rows : (j + 1) * rows]
        row = jnp.concatenate([pair[d, 0:1, :] for d in range(BLOCKS)], axis=1).astype(F32)
        gains[j : j + 1, :] = row
    gain = gains[0:1, :]

    def step(t, carry):
        at = pl.ds(pl.multiple_of(t * TILE, TILE), TILE)
        xb = piece_of(info, t, *x_parts)
        x[at, :] = xb
        first = piece_of(info, t, *fv_parts)
        xt = xb.astype(F32)
        inverse = lax.rsqrt(jnp.mean(xt * xt, axis=-1, keepdims=True) + EPSILON)
        h = (xt * inverse * gain).astype(BF16)
        h1[at, :] = h
        cos_t, sin_t = cosine[at, :], sine[at, :]
        quarters = [first[:, i * width : (i + 1) * width] for i in range(4)]
        for by in range(2):
            side = [jnp.where(info[1] == 1, quarters[2 * i + 1], quarters[2 * i]) for i in (0, 1)]
            blend = jnp.where((info[0] ^ by) == 1, side[1], side[0]).astype(F32)
            for n in range(3):
                weight = w[by, :, n * rows : (n + 1) * rows, :].reshape(model, width)
                acc = dot_nn(h, weight)
                cols = pl.ds(by * width, width)
                if n == 2:
                    b[at, cols] = (0.5 * acc + 0.5 * blend).astype(BF16)
                else:
                    halves = [
                        turned(acc[:, j : j + 128], cos_t, sin_t) for j in range(0, width, 128)
                    ]
                    both = jnp.concatenate(halves, axis=1).astype(BF16)
                    (q, k)[n][at, cols] = both * BF16(0.125) if n == 0 else both
        return carry

    lax.fori_loop(0, x.shape[0] // TILE, step, 0)


def split_heads(pair):
    lane = lax.broadcasted_iota(jnp.int32, pair.shape, 1)
    zero = jnp.zeros_like(pair)
    return jnp.concatenate(
        [jnp.where(lane < HEAD, pair, zero), jnp.where(lane < HEAD, zero, pair)], axis=0
    )


def join_heads(both):
    half = both.shape[0] // 2
    lane = lax.broadcasted_iota(jnp.int32, (half, both.shape[1]), 1)
    return jnp.where(lane < HEAD, both[:half], both[half:])


def hide_later(scores, fill):
    length, width = scores.shape
    key_at = lax.broadcasted_iota(jnp.int32, (TILE, width), 0)
    query_at = lax.broadcasted_iota(jnp.int32, (TILE, width), 1) % TILE
    last = jnp.where(key_at <= query_at, scores[length - TILE :], fill)
    if length == TILE:
        return last
    return jnp.concatenate([scores[: length - TILE], last], axis=0)


def attend_body(q, k, b, att, lse):
    for i in range(q.shape[0] // TILE):
        length = (i + 1) * TILE
        queries = split_heads(q[i * TILE : length, :])
        scores = hide_later(dot_nt(k[:length, :], queries), -1e30)
        top = jnp.max(scores, axis=0, keepdims=True)
        grown = jnp.exp(scores - top)
        total = jnp.sum(grown, axis=0, keepdims=True)
        logs = top + jnp.log(total)
        probs = (grown * (1.0 / total)).astype(BF16)
        att[i * TILE : length, :] = join_heads(dot_tn(probs, b[:length, :])).astype(BF16)
        lse[0, 0:1, i * TILE : length] = logs[:, :TILE]
        lse[0, 1:2, i * TILE : length] = logs[:, TILE:]


def attend_back_body(q, k, b, datt, lse, cosine, sine, dq, dk, dv, k_acc, v_acc):
    k_acc[...] = jnp.zeros_like(k_acc)
    v_acc[...] = jnp.zeros_like(v_acc)
    for i in range(q.shape[0] // TILE):
        length = (i + 1) * TILE
        at = slice(i * TILE, length)
        queries = split_heads(q[at, :])
        grads = split_heads(datt[at, :])
        keys = k[:length, :]
        logs = jnp.concatenate([lse[0, 0:1, at], lse[0, 1:2, at]], axis=1)
        probs = jnp.exp(hide_later(dot_nt(keys, queries) - logs, -1e30))
        grad_probs = dot_nt(b[:length, :], grads)
        delta = jnp.sum(probs * grad_probs, axis=0, keepdims=True)
        grad_scores = (probs * (grad_probs - delta)).astype(BF16)
        v_acc[:length, :] += dot_nn(probs.astype(BF16), grads)
        k_acc[:length, :] += dot_nn(grad_scores, queries)
        turned_back = turned(
            0.125 * join_heads(dot_tn(grad_scores, keys)), cosine[at, :], -sine[at, :]
        )
        dq[at, :] = turned_back.astype(BF16)
    for i in range(q.shape[0] // TILE):
        at = slice(i * TILE, (i + 1) * TILE)
        dk[at, :] = turned(k_acc[at, :], cosine[at, :], -sine[at, :]).astype(BF16)
        dv[at, :] = (0.5 * v_acc[at, :]).astype(BF16)


def out_copies(info, parts, wo, sem):
    first = parts[0].shape[1] - 128
    copies = []
    for by, bx, other, t in bits(4):
        row = pl.multiple_of(block_of(info, t) * 256 + (info[4] ^ bx) * 128, 128)
        copies.append(pltpu.make_async_copy(
            source_of(parts, by, bx, other * 2 + t).at[pl.ds(first, 128)],
            wo.at[pl.ds(row, 128), pl.ds(column_of(info, by, other), 256)],
            sem.at[len(copies)]))
    return copies


def out_body(*refs):
    info, att, parts, (part, wo, sem) = refs[0], refs[1], refs[2:7], refs[7:]
    run_copies(out_copies(info, parts, wo, sem))

    def step(t, carry):
        at = pl.ds(pl.multiple_of(t * TILE, TILE), TILE)
        part[at, :] = dot_nn(att[at, :], wo[...]).astype(BF16)
        return carry

    lax.fori_loop(0, att.shape[0] // TILE, step, 0)


def middle_of(x, part, recv, at):
    return x[at, :].astype(F32) + (part[at, :].astype(F32) + recv[at, :].astype(F32))


def out_back_body(*refs):
    info, gh2, gh2_recv, x, part, recv, gy, gains, att, down = refs[:10]
    parts = refs[10:15]
    datt, own_mid, gain_grad = refs[15:18]
    outs, (wo, gb, sem) = refs[18:23], refs[23:]
    down_rows = down.shape[3]
    copies = out_copies(info, parts, wo, sem)
    for copy in copies:
        copy.start()
    gain_grad[...] = jnp.zeros_like(gain_grad)

    def norm_step(t, carry):
        at = pl.ds(pl.multiple_of(t * TILE, TILE), TILE)
        middle = middle_of(x, part, recv, at)
        inverse = lax.rsqrt(jnp.mean(middle * middle, axis=-1, keepdims=True) + EPSILON)
        grad = gh2[at, :].astype(F32) + gh2_recv[at, :].astype(F32)
        scaled = grad * gains[1:2, :]
        share = inverse * inverse * inverse * jnp.mean(scaled * middle, axis=-1, keepdims=True)
        total = gy[at, :].astype(F32) + inverse * scaled - middle * share
        gb[at, :] = total.astype(BF16)
        gain_grad[0:1, :] += jnp.sum(grad * middle * inverse, axis=0, keepdims=True)

        @pl.when((t & 1) == info[1])
        def _():
            own_mid[t >> 1] = total

        return carry

    tiles = att.shape[0] // TILE
    lax.fori_loop(0, tiles, norm_step, 0)
    for copy in copies:
        copy.wait()

    def step(t, carry):
        at = pl.ds(pl.multiple_of(t * TILE, TILE), TILE)
        datt[at, :] = dot_nt(gb[at, :], wo[...]).astype(BF16)
        return carry

    lax.fori_loop(0, tiles, step, 0)
    for by, other in bits(2):
        grad = dot_tn(att[...], gb[:, pl.ds(column_of(info, by, other), 256)]).astype(BF16)
        for t in range(2):
            swap = block_of(info, t) == 1
            block = jnp.where(swap, grad[256:], grad[:256])
            for bx in range(2):
                q = other * 2 + t
                put(outs, by, bx, q, slice(0, down_rows), down[by, bx, q])
                put(outs, by, bx, q, slice(down_rows, down_rows + 128), jnp.where(
                    (info[4] ^ bx) == 1, block[128:], block[:128]))


def crossed(parts, by, bx, q):
    low, low_x, low_y, low_xy, high, high_x, high_y, high_xy = parts
    group = (low, low_x, low_y, low_xy) if q < 2 else (high, high_x, high_y, high_xy)
    return group[by * 2 + bx].at[q & 1]


def ffn_copies(info, first, parts, wgu, wd, sem):
    units = wd.shape[0]
    own = units // 2
    part = own // 2
    copies = []
    for by, bx in bits(2):
        for q in range(4):
            lane = pl.multiple_of(place_of(info, bx, q) * 128, 128)
            if first:
                source = parts[q].at[0] if by + bx == 0 else parts[4 + q].at[by * 2 + bx - 1]
            else:
                source = crossed(parts, by, bx, q)
            for up in range(2):
                copies.append(pltpu.make_async_copy(
                    source.at[pl.ds(0, own), pl.ds(up * 128, 128)],
                    wgu.at[pl.ds(up * units + by * own, own), pl.ds(lane, 128)],
                    sem.at[len(copies)]))
    for by, bx, other, t in bits(4):
        row = pl.multiple_of(block_of(info, t) * own + (info[4] ^ bx) * part, 16)
        q = other * 2 + t
        if first:
            source = source_of(parts[8:], by, bx, q).at[pl.ds(0, part)]
        else:
            source = crossed(parts, by, bx, q).at[pl.ds(own, part)]
        copies.append(pltpu.make_async_copy(
            source, wd.at[pl.ds(row, part), pl.ds(column_of(info, by, other), 256)],
            sem.at[len(copies)]))
    return copies


def ffn_body(first, *refs):
    info = refs[0]
    if first:
        x, part, recv, gains = refs[1:5]
        cot_parts, parts = refs[5:8], refs[8:21]
        h2, gy, gh2, res = refs[21:25]
        outs, refs = refs[25:30], refs[30:]
    else:
        h2, gy, gh2_in, res_in = refs[1:5]
        parts = refs[5:13]
        gh2, rkeep, rsend = refs[13:16]
        outs, down_grad, refs = refs[16:20], refs[20], refs[21:]
    hid, ggu, wgu, wd, sem = refs
    copies = ffn_copies(info, first, parts, wgu, wd, sem)
    for copy in copies:
        copy.start()
    units = wd.shape[0]
    tiles = h2.shape[0] // TILE
    if first:
        live = jnp.where(info[0] < info[5], 1.0, 0.0)

        def norm_step(t, carry):
            at = pl.ds(pl.multiple_of(t * TILE, TILE), TILE)
            middle = middle_of(x, part, recv, at)
            inverse = lax.rsqrt(jnp.mean(middle * middle, axis=-1, keepdims=True) + EPSILON)
            h2[at, :] = (middle * inverse * gains[1:2, :]).astype(BF16)
            gy[at, :] = (piece_of(info, t, *cot_parts).astype(F32) * live).astype(BF16)
            return carry

        lax.fori_loop(0, tiles, norm_step, 0)
    for copy in copies:
        copy.wait()

    def step(t, carry):
        at = pl.ds(pl.multiple_of(t * TILE, TILE), TILE)
        both = dot_nt(wgu[...], h2[at, :])
        gate, up = both[:units], both[units:]
        sig = 1.0 / (1.0 + jnp.exp(-gate))
        act = gate * sig
        hidden = (act * up).astype(BF16)
        hid[:, at] = hidden
        grad_hidden = dot_nt(wd[...], gy[at, :])
        ggu[:units, at] = (grad_hidden * up * (sig + act * (1.0 - sig))).astype(BF16)
        ggu[units:, at] = (grad_hidden * act).astype(BF16)
        grad_h = dot_tn(ggu[:, at], wgu[...])
        result = dot_tn(hidden, wd[...])
        if first:
            gh2[at, :] = grad_h.astype(BF16)
            res[at, :] = result.astype(BF16)
        else:
            gh2[at, :] = (gh2_in[at, :].astype(F32) + grad_h).astype(BF16)
            result = res_in[at, :].astype(F32) + result

            @pl.when((t & 1) == info[1])
            def _():
                rkeep[t >> 1] = result

            @pl.when((t & 1) != info[1])
            def _():
                rsend[t >> 1] = result.astype(BF16)

        return carry

    lax.fori_loop(0, tiles, step, 0)
    own = units // 2
    part = own // 2
    swap = info[4] == 1
    for q in (3, 2, 1, 0):
        z = info[3] ^ (q >> 1) ^ (3 * (q & 1))
        grad = dot_nn(ggu[...], h2[:, pl.ds(pl.multiple_of(z * 256, 256), 256)]).astype(BF16)
        lo, hi = grad[:, :128], grad[:, 128:]
        for bx, side in ((0, jnp.where(swap, hi, lo)), (1, jnp.where(swap, lo, hi))):
            for by, up in bits(2):
                lanes = slice(up * 128, up * 128 + 128)
                piece = side[up * units + by * own : up * units + (by + 1) * own]
                if first:
                    put_lanes(outs, by, bx, q, slice(0, own), lanes, piece)
                else:
                    outs[q][bx * 2 + by, :, lanes] = piece
    for by, other in bits(2):
        grad = dot_nn(hid[...], gy[:, pl.ds(column_of(info, by, other), 256)]).astype(BF16)
        for t in range(2):
            block = jnp.where(block_of(info, t) == 1, grad[own:], grad[:own])
            for bx in range(2):
                q = other * 2 + t
                piece = jnp.where((info[4] ^ bx) == 1, block[part:], block[:part])
                if first:
                    put(outs, by, bx, q, slice(own, own + part), piece)
                else:
                    down_grad[by, bx, q] = piece


def qkv_grad_body(by, *refs):
    info, dq, dk, dv, h1, gains, gain_grad = refs[:7]
    parts, refs = (refs[7:10], refs[10:]) if by else (refs[7:9], refs[9:])
    outs, (w, acc, sem) = refs[:3], refs[3:]
    copies = []
    for bx in range(2):
        for q in range(4):
            if by == 0 or bx == 0:
                source = parts[bx].at[q]
            else:
                split = parts[1].shape[0]
                source = parts[1].at[q] if q < split else parts[2].at[q - split]
            copies.append(pltpu.make_async_copy(
                source, w.at[place_of(info, bx, q)], sem.at[len(copies)]))
    for copy in copies:
        copy.start()
    width = w.shape[2]

    def spot(bx, q):
        if by:
            diagonal, send, keep = outs
            split = send.shape[0] // 2
            if q < split:
                return send, q if bx else split + q
            return (diagonal if bx else keep), q - split
        send, keep, own = outs
        split = keep.shape[0]
        if not bx:
            return own, q
        return (keep, q) if q < split else (send, q - split)

    waiting = True
    ones = jnp.ones((8, 3 * width), BF16)
    three = jnp.concatenate([dq[...], dk[...], dv[...]], axis=1)
    for q in (3, 2, 1, 0):
        z = info[3] ^ (q >> 1) ^ (3 * (q & 1))
        at = pl.ds(pl.multiple_of(z * 256, 256), 256)
        grad = dot_tn(h1[:, at], three)
        if waiting:
            for copy in copies:
                copy.wait()
            waiting = False
        weight = jnp.concatenate(
            [w[pl.ds(z * 2, 2), n * 128 : (n + 1) * 128, :].reshape(256, width)
             for n in range(3)], axis=1)
        shares = dot_nt(ones, (grad * weight.astype(F32)).astype(BF16))
        acc[:, at] = shares / gains[0:1, at]
        grad = grad.astype(BF16)
        for bx in range(2):
            part = jnp.where((info[4] ^ bx) == 1, grad[128:], grad[:128])
            ref, i = spot(bx, q)
            for n in range(3):
                ref[i, n * 128 : (n + 1) * 128, :] = part[:, n * width : (n + 1) * width]
    for bx in range(2):
        for q in range(4):
            at = pl.ds(pl.multiple_of(place_of(info, bx, q) * 128, 128), 128)
            row = jnp.concatenate([acc[0:1, at], gain_grad[0:1, at]], axis=1)
            ref, i = spot(bx, q)
            ref[i, 384:400, :] = jnp.broadcast_to(row, (16, 256)).astype(BF16)


def qkv_back_body(*refs):
    info, grads = refs[0], (refs[1:4], refs[4:7])
    parts = refs[7:12]
    gkeep, gsend, w, sem = refs[12:]
    run_copies(attn_copies(info, parts, w, sem))
    width = w.shape[3]
    model = gkeep.shape[2]

    def step(t, carry):
        at = pl.ds(pl.multiple_of(t * TILE, TILE), TILE)
        grad_h = jnp.zeros((TILE, model), F32)
        for by in range(2):
            for n in range(3):
                weight = w[by, :, n * 128 : (n + 1) * 128, :].reshape(model, width)
                grad_h = grad_h + dot_nt(grads[by][n][at, :], weight)

        @pl.when((t & 1) == info[1])
        def _():
            gkeep[t >> 1] = grad_h

        @pl.when((t & 1) != info[1])
        def _():
            gsend[t >> 1] = grad_h.astype(BF16)

        return carry

    lax.fori_loop(0, gkeep.shape[0] * 2, step, 0)


def input_body(info, gkeep, grecv, x, own_mid, gains, keep, send):
    for half in range(2):
        at = pl.ds(pl.multiple_of((half * 2 + info[1]) * TILE, TILE), TILE)
        xt = x[at, :].astype(F32)
        grad = gkeep[half] + grecv[half].astype(F32)
        inverse = lax.rsqrt(jnp.mean(xt * xt, axis=-1, keepdims=True) + EPSILON)
        scaled = grad * gains[0:1, :]
        share = inverse * inverse * inverse * jnp.mean(scaled * xt, axis=-1, keepdims=True)
        total = own_mid[half] + inverse * scaled - xt * share

        @pl.when(info[0] == half)
        def _():
            keep[...] = total

        @pl.when(info[0] != half)
        def _():
            send[...] = total.astype(BF16)


def gate(live, *names):
    for name, value in zip(names, lax.optimization_barrier([live[name] for name in names])):
        live[name] = value


def plus(*values):
    total = values[0].astype(F32)
    for value in values[1:]:
        total = total + value.astype(F32)
    return total


def on_device(
    tokens, first_values, seq_counts, norm1_gain, query_weight, key_weight, value_weight,
    out_weight, norm2_gain, gate_weight, up_weight, down_weight, output_cotangent,
):
    slots, piece, model = tokens.shape
    length = piece * lax.axis_size("seq")
    wide = lax.axis_size("dp") // BLOCKS
    s = lax.axis_index("seq")
    place = lax.axis_index("dp")
    y, c = s // 2, s % 2
    d = place // wide
    z, x_at = d // 2, d % 2
    info = jnp.stack([y, c, d, z, x_at, seq_counts[0]]).astype(jnp.int32)
    even = (z & 1) ^ c

    def pregather(shard):
        step = 1
        while step < wide:
            other = flip(shard, "dp", step)
            bit = (place // step) % 2
            shard = pick(
                bit, jnp.concatenate([other, shard]), jnp.concatenate([shard, other]))
            step *= 2
        return shard

    def postscatter(total):
        step = wide // 2
        while step >= 1:
            half = total.shape[0] // 2
            bit = (place // step) % 2
            lo, hi = total[:half], total[half:]
            total = pick(bit, hi, lo) + flip(pick(bit, lo, hi), "dp", step)
            step //= 2
        return total

    def far(v):
        return flip(v, "dp", ZM * wide)

    def near(v):
        return flip(v, "dp", Z1 * wide)

    def over_x(v):
        return flip(v, "dp", X1 * wide)

    def over_y(v):
        return flip(v, "seq", MESH_Y)

    def over_core(v):
        return flip(v, "seq", MESH_C)

    def other_slot(block):
        return pick(y, block[0], block[1])

    def mine_of(low, high):
        return jnp.stack([pick(even, low[1], low[0]), pick(even, high[0], high[1])])

    def theirs_of(low, high):
        return jnp.stack([pick(even, low[0], low[1]), pick(even, high[1], high[0])])

    def own_slot(block, recv):
        return jnp.stack([pick(y, block[1], block[0]), recv])

    def pack(*parts):
        rows = parts[0].shape[-2]
        (out,) = call(
            pack_body, [((4, rows, 256), BF16)], [("v", part) for part in parts], [],
            1000, 1 << 20, vmem=8)
        return out

    local = model // 2
    width = local // 2
    v = {}
    v["a0"] = jnp.concatenate(
        [pregather(query_weight), pregather(key_weight), pregather(value_weight),
         jnp.pad(jnp.concatenate([pregather(norm1_gain), pregather(norm2_gain)])[None],
                 ((0, 15), (0, 0)))])
    attn_rows = v["a0"].shape[0]
    down = pregather(down_weight)
    part = down.shape[0] // 2
    own = 2 * part
    units = 2 * own
    ffn = jnp.concatenate([pregather(gate_weight).T, pregather(up_weight).T], axis=1)
    v["b0"] = jnp.concatenate([ffn[part:own], ffn[own + part :]])[None]
    v["g0"] = jnp.concatenate([ffn[:part], ffn[own : own + part], down[:part]])
    v["r0"] = jnp.concatenate([down[part:], pregather(out_weight)])
    out_rows = v["r0"].shape[0] - part
    v["t_send"] = other_slot(tokens)
    v["f_send"] = other_slot(first_values)
    v["c_send"] = other_slot(output_cotangent)
    v["tokens"], v["firsts"], v["cots"] = tokens, first_values, output_cotangent

    gate(v, "a0", "t_send", "b0")
    v["ty"], v["af"], v["an"] = over_y(v["t_send"]), far(v["a0"]), near(v["a0"])
    v["bx"], v["bf0"] = over_x(v["b0"]), far(v["b0"])
    gate(v, "a0", "af", "an", "ty", "tokens", "b0", "bx", "bf0", "f_send", "c_send", "firsts", "cots", "r0", "g0")
    v["fy"], v["anf"], v["rf"] = over_y(v["f_send"]), near(v["af"]), far(v["r0"])
    v["tc"] = over_core(own_slot(v["tokens"], v["ty"]))
    v["bn0"] = near(v["b0"])
    gate(v, "a0", "af", "an", "anf", "fy", "tc", "firsts", "b0", "bx", "bf0", "bn0", "r0", "rf", "g0", "c_send", "cots")
    v["z"] = pack(v["a0"], v["af"], v["an"], v["anf"])
    v["zx"], v["zy"] = over_x(v["z"]), over_y(v["z"])
    v["rlow"] = jnp.stack([v["r0"], v["rf"]])
    v["rhigh"], v["gf"] = near(v["rlow"]), far(v["g0"])
    v["fc"] = over_core(own_slot(v["firsts"], v["fy"]))
    half = HEAD // 2
    frequency = 10000.0 ** (-(jnp.arange(half).astype(F32) * 2.0) / HEAD)
    angles = jnp.arange(length).astype(F32)[:, None] * frequency[None, :]
    v["cosine"] = jnp.tile(jnp.cos(angles), (1, 4))
    v["sine"] = jnp.tile(jnp.concatenate([-jnp.sin(angles), jnp.sin(angles)], axis=1), (1, 2))
    gate(v, "z", "zx", "zy", "rlow", "rhigh", "g0", "gf", "fc", "b0", "bx", "bf0", "bn0", "cosine", "sine", "c_send", "cots")
    v["zu"], v["zv"] = over_y(v["zx"][:SPLIT]), over_x(v["zy"][SPLIT:])
    v["rmine"] = mine_of(v["rlow"], v["rhigh"])
    v["rother"] = over_core(theirs_of(v["rlow"], v["rhigh"]))
    v["b10"] = over_y(jnp.concatenate([v["b0"], v["bx"]]))
    v["glow"] = jnp.stack([v["g0"], v["gf"]])
    v["ghigh"] = near(v["glow"])
    gate(v, "z", "zx", "zy", "zu", "zv", "rmine", "rother", "b0", "bx", "b10", "bf0", "bn0", "glow", "ghigh", "c_send", "cots")
    v["r"] = pack(v["rmine"], v["rother"])
    v["rx"], v["ry"] = over_x(v["r"]), over_y(v["r"])
    v["b3"] = jnp.concatenate([v["bx"], v["b10"]])
    v["bf3"], v["bn3"] = far(v["b3"]), near(v["b3"])
    glow, ghigh = v["glow"][:, own:], v["ghigh"][:, own:]
    v["gmine"], v["gother"] = mine_of(glow, ghigh), over_core(theirs_of(glow, ghigh))

    def weights(name):
        return [("a", v[name + end]) for end in ("", "x", "y", "u", "v")]

    def values(*names):
        return [("v", v[name]) for name in names]

    square = ((length, model), BF16)
    tall = ((length, local), BF16)
    tile = (2, piece, model)
    w_scratch = pltpu.VMEM((2, BLOCKS, attn_rows, width), BF16)
    sem16 = pltpu.SemaphoreType.DMA((16,))
    narrow = 2 * length * model * local
    v["x"], v["h1"], v["q"], v["k"], v["b"], v["gains"] = call(
        qkv_body, [square, square, tall, tall, tall, ((8, model), F32)],
        [("s", info)] + values("tokens", "ty", "tc", "firsts", "fy", "fc", "cosine", "sine") + weights("z"),
        [w_scratch, sem16], 3 * narrow, 14 << 20, vmem=26,
    )
    gate(v, "x", "h1", "q", "k", "b", "gains", "r", "rx", "ry", "b0", "b3", "bf0", "bn0", "bf3", "bn3", "glow", "ghigh", "gmine", "gother", "c_send", "cots")
    v["ru"], v["rv"] = over_y(v["rx"][:SPLIT]), over_x(v["ry"][SPLIT:])
    v["gl"] = jnp.concatenate([v["glow"][:, :own], v["gmine"]], axis=1)
    v["gh"] = jnp.concatenate([v["ghigh"][:, :own], v["gother"]], axis=1)
    v["glx"], v["ghy"] = over_x(v["gl"]), over_y(v["gh"])
    v["bnf3"] = near(v["bf3"])
    head_specs = [pl.BlockSpec((length, 128), lambda i: (0, i))] * 3
    lse_spec = pl.BlockSpec((1, 2, length), lambda i: (i, 0, 0))
    pairs = local // 128
    v["att"], v["lse"] = call(
        attend_body, [tall, ((pairs, 2, length), F32)], values("q", "k", "b"), [],
        4 * length * length * local, 4 << 20, length * length * pairs * 2, vmem=20,
        grid=(pairs,), in_specs=head_specs, out_specs=[head_specs[0], lse_spec],
    )
    v["cy"], v["bnf0"] = over_y(v["c_send"]), near(v["bf0"])
    (v["part"],) = call(
        out_body, [square], [("s", info)] + values("att") + weights("r"),
        [pltpu.VMEM((local, model), BF16), sem16], narrow, 5 << 20, vmem=12,
    )
    gate(v, "att", "lse", "r", "rx", "ry", "ru", "rv", "part", "cy", "cots", "gl", "glx", "gh", "ghy", "b0", "b3", "bf0", "bn0", "bf3", "bn3", "bnf0", "bnf3")
    v["precv"], v["cc"] = over_core(v["part"]), over_core(own_slot(v["cots"], v["cy"]))
    gate(v, "part", "precv", "cc", "gl", "glx", "gh", "ghy")

    def five(rows):
        return [((count, rows, 256), BF16)
                for count in (2 * (4 - SPLIT), 2 * SPLIT, SPLIT, 4 - SPLIT, 4)]

    v["gly"], v["glxy"] = over_y(v["gl"]), over_y(v["glx"])
    v["ghx"], v["ghxy"] = over_x(v["gh"]), over_x(v["ghy"])
    scratch = [pltpu.VMEM((units, length), BF16), pltpu.VMEM((2 * units, length), BF16),
               pltpu.VMEM((2 * units, model), BF16), pltpu.VMEM((units, model), BF16),
               pltpu.SemaphoreType.DMA((48,))]
    ffn_flops = 18 * length * model * units
    v["h2"], v["gy"], v["gh2b"], v["resb"], v["bsx"], v["bsy"], v["bkx"], v["bky"], v["bown"] = call(
        functools.partial(ffn_body, True), [square] * 4 + five(own + part),
        [("s", info)] + values("x", "part", "precv", "gains", "cots", "cy", "cc")
        + [("a", v[name]) for name in ("b0", "bf0", "bn0", "bnf0")]
        + [("a", v[name]) for name in ("b3", "bf3", "bn3", "bnf3")] + weights("r"),
        scratch, ffn_flops, 24 << 20, vmem=40,
    )
    gate(v, "h2", "gy", "gh2b", "resb", "bsx", "bsy", "bkx", "bky", "bown", "gl", "glx", "gly", "glxy", "gh", "ghx", "ghy", "ghxy")
    v["brx"], v["bry"] = over_x(v["bsx"]), over_y(v["bsy"])
    quads = [((4, own, 256), BF16)] * 4 + [((2, 2, 4, part, 256), BF16)]
    (v["gh2"], v["rkeep"], v["rsend"], v["n0"], v["n1"], v["n2"], v["n3"], v["dgrad"]) = call(
        functools.partial(ffn_body, False), [square, (tile, F32), (tile, BF16)] + quads,
        [("s", info)] + values("h2", "gy", "gh2b", "resb")
        + [("a", v[half + over]) for half in ("gl", "gh") for over in ("", "x", "y", "xy")],
        scratch, ffn_flops, 24 << 20, vmem=40,
    )
    gate(v, "gh2", "rkeep", "rsend", "n0", "n1", "n2", "n3", "dgrad", "brx", "bry", "bkx", "bky", "bown", "part", "precv")

    def fold(name):
        v[name + "fx"] = plus(v[name + "kx"], v[name + "ry"][:SPLIT]).astype(BF16)
        v[name + "fy"] = plus(v[name + "ky"], v[name + "rx"][: 4 - SPLIT]).astype(BF16)

    def total_of(name):
        low = plus(v[name + "own"][:SPLIT], v[name + "ry"][SPLIT:], v[name + "rx2"])
        high = plus(v[name + "own"][SPLIT:], v[name + "rx"][4 - SPLIT :], v[name + "ry2"])
        return jnp.concatenate([low, high])

    def rows_out(name, total, first):
        v[name + "t"] = total
        v[name + "m"] = over_core(total[2:, first:].astype(BF16))

    def quarter(name, first, q):
        total, recv = v[name + "t"], v[name + "m"]
        rows = total[q >> 1, first:]
        other = recv[q >> 1].astype(F32)
        mine = pick(even, other, rows) if q in (0, 3) else pick(even, rows, other)
        return mine if first == 0 else jnp.concatenate([total[q, :first], mine])

    def owner_send(halves_of):
        return pick(y, halves_of[0], halves_of[1])

    def owner_keep(halves_of):
        return pick(y, halves_of[1], halves_of[0])

    def both_slots(keep, recv):
        return pick(y, jnp.stack([recv, keep]), jnp.stack([keep, recv]))

    def own_tokens(full):
        cut_up = full.reshape(2, 2, piece, full.shape[-1])
        return pick(c, cut_up[:, 1], cut_up[:, 0])

    v["gh2r"] = over_core(v["gh2"])
    v["rrecv"] = over_core(v["rsend"])
    fold("b")
    v["brx2"], v["bry2"] = over_x(v["bfx"]), over_y(v["bfy"])
    v["nn3"] = near(v["n3"])
    (v["datt"], v["mid"], v["gain2"],
     v["ssx"], v["ssy"], v["skx"], v["sky"], v["sown"]) = call(
        out_back_body, [tall, (tile, F32), ((8, model), F32)] + five(part + out_rows),
        [("s", info)] + values("gh2", "gh2r", "x", "part", "precv", "gy", "gains", "att", "dgrad") + weights("r"),
        [pltpu.VMEM((local, model), BF16), pltpu.VMEM((length, model), BF16), sem16],
        2 * narrow, 20 << 20, vmem=34,
    )
    gate(v, "datt", "mid", "gain2", "ssx", "ssy", "skx", "sky", "sown", "bown", "brx", "bry", "brx2", "bry2", "n0", "n1", "n2", "nn3", "rkeep", "rrecv", "part", "precv")
    v["srx"], v["sry"] = over_x(v["ssx"]), over_y(v["ssy"])
    v["n1"] = plus(v["n1"], v["nn3"]).astype(BF16)
    v["nf1"], v["nn2"] = far(v["n1"][2:]), near(v["n2"])
    rows_out("b", total_of("b"), own)

    def attend_back(side):
        first = side * (pairs // 2)
        column = pl.BlockSpec((length, 128), lambda i: (0, i + first))
        table = pl.BlockSpec((length, 128), lambda i: (0, 0))
        sums = pl.BlockSpec((1, 2, length), lambda i: (i + first, 0, 0))
        target = pl.BlockSpec((length, 128), lambda i: (0, i))
        v[f"dq{side}"], v[f"dk{side}"], v[f"dv{side}"] = call(
            attend_back_body, [((length, width), BF16)] * 3,
            values("q", "k", "b", "datt", "lse", "cosine", "sine"),
            [pltpu.VMEM((length, 128), F32), pltpu.VMEM((length, 128), F32)],
            5 * length * length * local, 4 << 20, length * length * pairs, vmem=26,
            grid=(pairs // 2,), in_specs=[column] * 4 + [sums, table, table],
            out_specs=[target] * 3,
        )

    def attn_grads(side):
        counts = (4 - SPLIT, 2 * SPLIT, 4 - SPLIT) if side else (4 - SPLIT, SPLIT, 4)
        names = ("zy", "zu", "zv") if side else ("z", "zx")
        return call(
            functools.partial(qkv_grad_body, side),
            [((count, attn_rows, width), BF16) for count in counts],
            [("s", info), ("v", v[f"dq{side}"]), ("v", v[f"dk{side}"]), ("v", v[f"dv{side}"])]
            + values("h1", "gains", "gain2") + [("a", v[name]) for name in names],
            [pltpu.VMEM((BLOCKS, attn_rows, width), BF16), pltpu.VMEM((8, model), F32),
             pltpu.SemaphoreType.DMA((8,))], 3 * narrow // 2, 7 << 20, vmem=24,
        )

    attend_back(1)
    v["qdx"], v["qsy"], v["qky"] = attn_grads(1)
    gate(v, "dq1", "dk1", "dv1", "qdx", "qsy", "qky", "q", "k", "b", "datt", "srx", "sry", "skx", "sky", "sown", "n0", "n1", "nf1", "nn2", "bt", "bm", "rkeep", "rrecv", "part", "precv")
    v["qry"], v["qrd"] = over_y(v["qsy"]), over_x(v["qdx"])
    fold("s")
    v["srx2"] = over_x(v["sfx"])
    v["nf0"] = far(v["n1"][:2])
    v["bzn"] = near(jnp.stack([quarter("b", own, 2), quarter("b", own, 3)]).astype(BF16))
    attend_back(0)
    v["qsx"], v["qkx"], v["qown"] = attn_grads(0)
    live_now = jnp.where(y < seq_counts[0], 1.0, 0.0)
    middle_own = own_tokens(v["x"]).astype(F32) + plus(
        own_tokens(v["part"]), own_tokens(v["precv"]))
    result = (live_now * (middle_own + plus(v["rkeep"], v["rrecv"]))).astype(BF16)
    v["okeep"], v["osend"] = owner_keep(result), owner_send(result)
    gate(v, "dq0", "dk0", "dv0", "dq1", "dk1", "dv1", "qsx", "qkx", "qown", "qry", "qrd", "qky", "srx", "sry", "srx2", "sfy", "sown", "n0", "nf0", "nf1", "nn2", "bzn", "bt", "bm", "okeep", "osend")
    v["qrx"] = over_x(v["qsx"])
    v["sry2"] = over_y(v["sfy"])
    v["nt0"] = plus(v["n0"][:2], v["nf0"], v["nn2"][:2])
    v["nx"] = over_x(plus(v["n0"][2:], v["nf1"], v["nn2"][2:]).astype(BF16))
    v["bt0"] = plus(quarter("b", own, 0), v["bzn"][0])
    v["bzf"] = far(plus(quarter("b", own, 1), v["bzn"][1]).astype(BF16))
    v["orecv"] = over_y(v["osend"])
    v["gkeep"], v["gsend"] = call(
        qkv_back_body, [(tile, F32), (tile, BF16)],
        [("s", info)] + values("dq0", "dk0", "dv0", "dq1", "dk1", "dv1") + weights("z"), [w_scratch, sem16],
        3 * narrow, 14 << 20, vmem=18,
    )
    gate(v, "gkeep", "gsend", "qry", "qrd", "qky", "qrx", "qkx", "qown", "bt0", "bzf", "nt0", "nx", "srx", "sry", "srx2", "sry2", "sown", "dv0", "dv1", "okeep", "orecv")
    output = both_slots(v["okeep"], v["orecv"])
    total_b = plus(v["bt0"], v["bzf"])
    v["grecv"] = over_core(v["gsend"])
    v["qfx"] = plus(v["qkx"], v["qry"][:SPLIT]).astype(BF16)
    v["qfy"] = plus(v["qky"], v["qrd"]).astype(BF16)
    v["qrx2"], v["qry2"] = over_x(v["qfx"]), over_y(v["qfy"])
    rows_out("s", total_of("s"), 0)
    v["nt0"] = plus(v["nt0"], v["nx"])
    v["ny"] = over_y(v["nt0"][1].astype(BF16))
    v["ikeep"], v["isend"] = call(
        input_body, [((piece, model), F32), ((piece, model), BF16)],
        [("s", info)] + values("gkeep", "grecv", "x", "mid", "gains"), [], 1000, 8 << 20, vmem=16,
    )
    gate(v, "ikeep", "isend", "qrx", "qry", "qrx2", "qry2", "qown", "st", "sm", "nt0", "ny", "dv0", "dv1")
    total_a = plus(v["nt0"][0], v["ny"])
    low = plus(v["qown"][:SPLIT], v["qry"][SPLIT:], v["qrx2"])
    high = plus(v["qown"][SPLIT:], v["qrx"], v["qry2"])
    v["qt"] = jnp.concatenate([low, high])
    v["qz"], v["sz"] = near(v["qt"][3].astype(BF16)), near(quarter("s", 0, 3).astype(BF16))
    v["irecv"] = over_y(v["isend"])
    cuts = [v[f"dv{side}"].reshape(2, 2, piece, width) for side in range(2)]
    dv_keep = [pick(c, cut[:, 1], cut[:, 0]) for cut in cuts]
    dv_recv = over_core(
        jnp.concatenate([pick(c, cut[:, 0], cut[:, 1]) for cut in cuts], axis=-1))
    dv_recv = [dv_recv[..., :width], dv_recv[..., width:]]
    blocks = []
    for column_y, column_c in bits(2):
        side = y ^ column_y
        mine = pick(side, dv_keep[1], dv_keep[0])
        theirs = pick(side, dv_recv[1], dv_recv[0])
        blocks.append(pick(c ^ column_c, theirs, mine))
    grad_rows = jnp.concatenate(blocks, axis=-1)
    v["fkeep"], v["fsend"] = owner_keep(grad_rows), owner_send(grad_rows)
    gate(v, "qt", "qz", "st", "sm", "sz", "irecv", "ikeep", "fkeep", "fsend")
    v["qzf"] = far(plus(v["qt"][1], v["qz"]).astype(BF16))
    v["szf"] = far(plus(quarter("s", 0, 1), v["sz"]).astype(BF16))
    v["qzn"] = near(v["qt"][2].astype(BF16))
    v["szn"] = near(quarter("s", 0, 2).astype(BF16))
    v["frecv"] = over_y(v["fsend"])
    v["qt0"], v["st0"] = v["qt"][0], quarter("s", 0, 0)
    grad_input = both_slots(v["ikeep"], v["irecv"].astype(F32))
    gate(v, "qt0", "st0", "qzf", "szf", "qzn", "szn", "fkeep", "frecv")
    total = plus(v["qt0"], v["qzf"], v["qzn"])
    gain_total = total[384]
    gain_share = jnp.broadcast_to(gain_total[None, :128], (8, 128))
    gain_sum = gain_total[:128] + over_core(gain_share)[0] + (
        over_y(gain_share)[0] + flip(gain_share, "seq", MESH_Y | MESH_C)[0])
    total_s = plus(v["st0"], v["szf"], v["szn"])
    grad_first = both_slots(v["fkeep"], v["frecv"]).astype(F32)

    def weave(lanes):
        pieces = [total_a[:part, lanes], total_b[:part, lanes],
                  total_a[part:own, lanes], total_b[part:own, lanes]]
        return jnp.concatenate(pieces).T

    return (
        output,
        grad_input,
        grad_first,
        postscatter(gain_sum),
        postscatter(total[:128]),
        postscatter(total[128:256]),
        postscatter(total[256:384]),
        postscatter(total_s[part:]),
        postscatter(gain_total[128:]),
        postscatter(weave(slice(0, 128))),
        postscatter(weave(slice(128, 256))),
        postscatter(jnp.concatenate([total_s[:part], total_b[own:]])),
    )


def solution(mesh):
    cut = P("dp", "seq")
    flat = P("dp")
    whole = P("dp", "seq", None)
    return jax.shard_map(
        on_device,
        mesh=mesh,
        in_specs=(whole, whole, flat, flat, cut, cut, cut, cut, flat, cut, cut, cut, whole),
        out_specs=(whole, whole, whole, flat, cut, cut, cut, cut, flat, cut, cut, cut),
        check_vma=False,
    )
```

time: 539 us -> 383 us (0.71)
  waiting for transfers between devices: 254 us -> 98.3 us
  other arithmetic: 78.5 us -> 32.6 us
  starting transfers between devices: 51.9 us -> 75.8 us
  local copies, waits for them, and re-layouts: 16.9 us -> 36.4 us
  Pallas kernels: 126 us -> 132 us
    ppermute x44 -> x77, waiting for transfers between devices: 254 us -> 98.3 us  [flip(): return lax.ppermute(value, axis, pairs)]
    ppermute x44 -> x77, starting transfers between devices: 51.9 us -> 75.8 us  [flip(): return lax.ppermute(value, axis, pairs)]
    unnamed x76 -> x177, local copies, waits for them, and re-layouts: 4.27 us -> 20.1 us
    select_n x21 -> x20, other arithmetic: 23.5 us -> 8.37 us  [pick(): return jnp.where(flag == 1, when_one, when_zero)]
    concatenate x15 -> x13, other arithmetic: 15.8 us -> 2.96 us  [the longest x1 0.77 us: on_device(): v['b10'] = over_y(jnp.concatenate([v['b0'], v['bx']]))]
    reduce_sum x3 -> x0, other arithmetic: 8.64 us -> none  [the longest x1 3.88 us: on_device(): grad_gain2 = jnp.sum(grad_h2 * middle * inverse2, axis=0, keepdims=True)]
    pallas_call x7 -> x14, Pallas kernels: 126 us -> 132 us  [call(): pl.pallas_call(body, out_shape=[jax.ShapeDtypeStruct(shape, kind) for sha...]
    convert_element_type x6 -> x16, other arithmetic: 12.9 us -> 10.1 us  [the longest x1 3.1 us: on_device(): (live_now * (middle_own + plus(v['rkeep'], v['rrecv']))).astype(BF16)]
  transfers between devices with their start and end apart: 44 -> 77, of which waited for: 22 -> 22; matrix products, arithmetic and copies ran while one was open for 17% -> 9% of each run, Pallas kernels for 15% -> 35%
where the time goes in v2:
time: 383 us; the launch traced here: 378 us
  Pallas kernels  132 us (34%)
  waiting for transfers between devices  98.3 us (26%)
  starting transfers between devices  75.8 us (20%)
  local copies, waits for them, and re-layouts  36.4 us (10%)
  other arithmetic  32.6 us (9%)
    pallas_call x14, Pallas kernels, call(): pl.pallas_call(body, out_shape=[jax.ShapeDtypeStruct(shape, kind) for sha...  132 us
    ppermute x77, waiting for transfers between devices, flip(): return lax.ppermute(value, axis, pairs)  98.3 us
    ppermute x77, starting transfers between devices, flip(): return lax.ppermute(value, axis, pairs)  75.8 us
    unnamed x177, local copies, waits for them, and re-layouts  20.1 us
    select_n x20, other arithmetic, pick(): return jnp.where(flag == 1, when_one, when_zero)  8.37 us
  transfers between devices with their start and end apart: 77, of which 22 were waited for; matrix products, arithmetic and copies ran while one was open for 9% of the time, Pallas kernels for 35%

profile of v2, /device:TPU:0, one launch (start us, length us, event | category | flops | bytes accessed | tf_op | source)
XLA Modules:
  0.0 378.1 jit_solution(13258988327838892053)
XLA Ops:
  3.2 3.0 collective-permute-start.2
  6.2 3.6 collective-permute-start
  9.8 1.5 collective-permute-start.3
  14.0 1.5 collective-permute-done.3
  15.5 7.5 %collective-permute-done.4.refs_9_ = bf16[1,352,256]{2,1,0:T(8,128)(2,1)S(1)} collective-permute-done((bf16[1,352,256]{2,1,0:T(8,128)(2,1)S(1)}, bf16[1,352,256]{2,1,0:T(8,128)(2,1)S(1)}, u32[]{:S(2)}, u32[]{:S(2)}) %collective-permute-start.4) | collective-permute-done | bytes 180256 | tf_op jit(solution)/shard_map/ppermute | solution.py:35
  24.4 3.4 collective-permute-start.5
  27.8 2.5 collective-permute-start.9
  30.3 12.3 %collective-permute-done.9 = bf16[304,256]{1,0:T(8,128)(2,1)S(1)} collective-permute-done((bf16[304,256]{1,0:T(8,128)(2,1)S(1)}, bf16[304,256]{1,0:T(8,128)(2,1)S(1)}, u32[]{:S(2)}, u32[]{:S(2)}) %collective-permute-start.9) | collective-permute-done | bytes 155680 | tf_op jit(solution)/shard_map/ppermute | solution.py:35
  44.3 1.6 collective-permute-start.10
  45.9 1.5 collective-permute-start.11
  48.5 1.4 collective-permute-start.13
  50.5 12.8 %collective-permute-done.13 = bf16[528,256]{1,0:T(8,128)(2,1)S(1)} collective-permute-done((bf16[528,256]{1,0:T(8,128)(2,1)}, bf16[528,256]{1,0:T(8,128)(2,1)S(1)}, u32[]{:S(2)}, u32[]{:S(2)}) %collective-permute-start.13) | collective-permute-done | bytes 270368 | tf_op jit(solution)/shard_map/ppermute | solution.py:35
  63.5 1.6 collective-permute-done.10.refs_10_.refs_8_
  68.1 1.8 pad_maximum_fusion.7
  70.7 1.5 collective-permute-start.18
  72.9 1.8 slice.396
  75.2 1.8 slice.397
  79.6 2.1 copy.25.refs_7_.cosine
  81.7 2.0 copy.26.refs_8_.sine
  83.9 5.6 %collective-permute-done.15.refs_12_.refs_8_.refs_10_ = bf16[2,400,256]{2,1,0:T(8,128)(2,1)S(1)} collective-permute-done((bf16[2,400,256]{2,1,0:T(8,128)(2,1)}, bf16[2,400,256]{2,1,0:T(8,128)(2,1)S(1)}, u32[]{:S(2)}, u32[]{:S(2)}) %collective-permute-start.15) | collective-permute-done | bytes 409632 | tf_op jit(solution)/shard_map/ppermute | solution.py:35
  93.6 1.5 collective-permute-start.21
  98.2 9.9 %shard_map.221 = (bf16[1024,1024]{1,0:T(8,128)(2,1)S(1)}, bf16[1024,1024]{1,0:T(8,128)(2,1)S(1)}, bf16[1024,512]{1,0:T(8,128)(2,1)S(1)}, bf16[1024,512]{1,0:T(8,...) custom-call(s32[6]{0:T(128)S(1)} %copy-done.37, bf16[2,256,1024]{2,1,0:T(8,128)(2,1)S(1)} %copy-done.4, ...), custom_call_target="tpu_custom_call" | custom-call | flops 3221225472 | bytes 14680064 | tf_op jit(solution)/shard_map/pallas_call | solution.py:51
  109.5 6.4 %collective-permute-done.23.refs_14_ = bf16[3,352,256]{2,1,0:T(8,128)(2,1)S(1)} collective-permute-done((bf16[3,352,256]{2,1,0:T(8,128)(2,1)S(1)}, bf16[3,352,256]{2,1,0:T(8,128)(2,1)S(1)}, u32[]{:S(2)}, u32[]{:S(2)}) %collective-permute-start.23) | collective-permute-done | bytes 540704 | tf_op jit(solution)/shard_map/ppermute | solution.py:35
  116.0 1.6 collective-permute-start.25
  121.1 1.4 collective-permute-start.28
  123.0 3.4 collective-permute-done.25.refs_5_.refs_19_.refs_13_
  126.4 1.5 collective-permute-start.27
  127.9 2.8 collective-permute-done.26.refs_6_.refs_20_.refs_14_
  131.1 13.8 %shard_map.223 = (bf16[1024,512]{1,0:T(8,128)(2,1)S(1)}, f32[4,2,1024]{2,1,0:T(2,128)S(1)}) custom-call(bf16[1024,512]{1,0:T(8,128)(2,1)S(1)} %get-tuple-element.537.q, bf16[1024,512]{1,0:T(8,128)(2,1)S(1)} %get-tuple-element.538.k, bf16[1024,512]{1,0:T(8,128)(2,1)S(1)} %get-tuple-element.539.b), custom_call_target="tpu_custom_call" | custom-call | flops 2147483648 | bytes 4194304 | tf_op jit(solution)/shard_map/pallas_call | solution.py:51
  145.9 2.6 shard_map.224.refs_2_.refs_4_
  149.9 4.5 %collective-permute-done.33.refs_7_ = bf16[2,256,1024]{2,1,0:T(8,128)(2,1)S(1)} collective-permute-done((bf16[2,256,1024]{2,1,0:T(8,128)(2,1)S(1)}, bf16[2,256,1024]{2,1,0:T(8,128)(2,1)S(1)}, u32[]{:S(2)}, u32[]{:S(2)}) %collective-permute-start.33) | collective-permute-done | bytes 1048608 | tf_op jit(solution)/shard_map/ppermute | solution.py:35
  154.4 1.5 collective-permute-start.34
  158.5 29.0 %shard_map.225 = (bf16[1024,1024]{1,0:T(8,128)(2,1)S(1)}, bf16[1024,1024]{1,0:T(8,128)(2,1)}, bf16[1024,1024]{1,0:T(8,128)(2,1)}, bf16[1024,1024]{1,0:T(8,128)(2...) custom-call(s32[6]{0:T(128)S(1)} %copy-done.37, ...), custom_call_target="tpu_custom_call" | custom-call | flops 13287555072 | bytes 25165824 | tf_op jit(solution)/shard_map/pallas_call | solution.py:51
  190.5 1.5 collective-permute-start.39
  192.0 26.1 %shard_map.226 = (bf16[1024,1024]{1,0:T(8,128)(2,1)}, f32[2,256,1024]{2,1,0:T(8,128)S(1)}, bf16[2,256,1024]{2,1,0:T(8,128)(2,1)}, bf16[4,352,256]{2,1,0:T(8,128)...) custom-call(s32[6]{0:T(128)S(1)} %copy-done.37, ...), custom_call_target="tpu_custom_call" | custom-call | flops 13287555072 | bytes 25165824 | tf_op jit(solution)/shard_map/pallas_call | solution.py:51
  224.4 1.6 collective-permute-start.43
  227.0 1.4 collective-permute-start.41
  228.4 1.6 copy-done.3
  235.6 10.5 %shard_map.227 = (bf16[1024,512]{1,0:T(8,128)(2,1)S(1)}, f32[2,256,1024]{2,1,0:T(8,128)S(1)}, f32[8,1024]{1,0:T(8,128)S(1)}, bf16[4,304,256]{2,1,0:T(8,128)(2,1)...) custom-call(s32[6]{0:T(128)S(1)} %copy-done.38, ...), custom_call_target="tpu_custom_call" | custom-call | flops 2147483648 | bytes 20971520 | tf_op jit(solution)/shard_map/pallas_call | solution.py:51
  246.2 1.8 convert_add_fusion.1
  252.2 2.5 collective-permute-start.47
  254.7 9.5 %shard_map.228 = (bf16[1024,256]{1,0:T(8,128)(2,1)S(1)}, bf16[1024,256]{1,0:T(8,128)(2,1)S(1)}, bf16[1024,256]{1,0:T(8,128)(2,1)S(1)}) custom-call(bf16[1024,512]{1,0:T(8,128)(2,1)S(1)} %copy-done.55, bf16[1024,512]{1,0:T(8,128)(2,1)S(1)} %copy-done.57, bf16[1024,512]{1,0:T(8,128)(2,1)S(1)} %copy-done.59, bf16[1024,512]{1,0:T(8,128)(2,1)S(1)} %get-tuple-element.540.datt, ...), custom_call_target="tpu_custom_call" | custom-call | flops 2684354560 | bytes 4194304 | tf_op jit(solution)/shard_map/pallas_call | solution.py:51
  264.2 5.3 %shard_map.229 = (bf16[2,400,256]{2,1,0:T(8,128)(2,1)S(1)}, bf16[4,400,256]{2,1,0:T(8,128)(2,1)S(1)}, bf16[2,400,256]{2,1,0:T(8,128)(2,1)S(1)}) custom-call(s32[6]{0:T(128)S(1)} %copy-done.38, bf16[1024,256]{1,0:T(8,128)(2,1)S(1)} %get-tuple-element.571.refs_1_.refs_4_, bf16[1024,256]{1,0:T(8,128)(2,1)S(1)} %get-tuple-element.572.refs_2_.refs_5_, ...), custom_call_target="tpu_custom_call" | custom-call | flops 1610612736 | bytes 7340032 | tf_op jit(solution)/shard_map/pallas_call | solution.py:51
  269.7 5.5 %collective-permute-done.47 = bf16[2,352,256]{2,1,0:T(8,128)(2,1)S(1)} collective-permute-done((bf16[2,352,256]{2,1,0:T(8,128)(2,1)S(1)}, bf16[2,352,256]{2,1,0:T(8,128)(2,1)S(1)}, u32[]{:S(2)}, u32[]{:S(2)}) %collective-permute-start.47) | collective-permute-done | bytes 360480 | tf_op jit(solution)/shard_map/ppermute | solution.py:35
  278.8 1.4 collective-permute-start.53
  281.6 3.1 fusion.1
  284.7 9.5 %shard_map.230 = (bf16[1024,256]{1,0:T(8,128)(2,1)S(1)}, bf16[1024,256]{1,0:T(8,128)(2,1)S(1)}, bf16[1024,256]{1,0:T(8,128)(2,1)S(1)}) custom-call(bf16[1024,512]{1,0:T(8,128)(2,1)S(1)} %copy-done.55, bf16[1024,512]{1,0:T(8,128)(2,1)S(1)} %copy-done.57, bf16[1024,512]{1,0:T(8,128)(2,1)S(1)} %copy-done.59, bf16[1024,512]{1,0:T(8,128)(2,1)S(1)} %get-tuple-element.540.datt, ...), custom_call_target="tpu_custom_call" | custom-call | flops 2684354560 | bytes 4194304 | tf_op jit(solution)/shard_map/pallas_call | solution.py:51
  294.3 6.0 %shard_map.231 = (bf16[2,400,256]{2,1,0:T(8,128)(2,1)S(1)}, bf16[2,400,256]{2,1,0:T(8,128)(2,1)S(1)}, bf16[4,400,256]{2,1,0:T(8,128)(2,1)S(1)}) custom-call(s32[6]{0:T(128)S(1)} %copy-done.38, bf16[1024,256]{1,0:T(8,128)(2,1)S(1)} %get-tuple-element.568.refs_1_, bf16[1024,256]{1,0:T(8,128)(2,1)S(1)} %get-tuple-element.569.refs_2_, ...), custom_call_target="tpu_custom_call" | custom-call | flops 1610612736 | bytes 7340032 | tf_op jit(solution)/shard_map/pallas_call | solution.py:51
  304.4 1.5 collective-permute-start.58
  306.1 2.4 collective-permute-start.56
  308.5 7.7 %shard_map.232 = (f32[2,256,1024]{2,1,0:T(8,128)S(1)}, bf16[2,256,1024]{2,1,0:T(8,128)(2,1)S(1)}) custom-call(s32[6]{0:T(128)S(1)} %copy-done.38, bf16[1024,256]{1,0:T(8,128)(2,1)S(1)} %get-tuple-element.568.refs_1_, bf16[1024,256]{1,0:T(8,128)(2,1)S(1)} %get-tuple-element.569.refs_2_, bf16[1024,256]{1,0:T(8,128)(2,1)S(1)} %get-tuple-element.627.refs_3_, ...), custom_call_target="tpu_custom_call" | custom-call | flops 3221225472 | bytes 14680064 | tf_op jit(solution)/shard_map/pallas_call | solution.py:51
  316.2 5.3 %collective-permute-done.58 = bf16[2,304,256]{2,1,0:T(8,128)(2,1)S(1)} collective-permute-done((bf16[2,304,256]{2,1,0:T(8,128)(2,1)S(1)}, bf16[2,304,256]{2,1,0:T(8,128)(2,1)S(1)}, u32[]{:S(2)}, u32[]{:S(2)}) %collective-permute-start.58) | collective-permute-done | bytes 311328 | tf_op jit(solution)/shard_map/ppermute | solution.py:35
  328.5 1.9 shard_map.233
  330.3 5.6 %collective-permute-done.62 = bf16[2,400,256]{2,1,0:T(8,128)(2,1)S(1)} collective-permute-done((bf16[2,400,256]{2,1,0:T(8,128)(2,1)S(1)}, bf16[2,400,256]{2,1,0:T(8,128)(2,1)S(1)}, u32[]{:S(2)}, u32[]{:S(2)}) %collective-permute-start.62) | collective-permute-done | bytes 409632 | tf_op jit(solution)/shard_map/ppermute | solution.py:35
  342.7 1.5 collective-permute-done.66
  344.2 4.0 %collective-permute-done.65 = bf16[400,256]{1,0:T(8,128)(2,1)S(1)} collective-permute-done((bf16[400,256]{1,0:T(8,128)(2,1)S(1)}, bf16[400,256]{1,0:T(8,128)(2,1)S(1)}, u32[]{:S(2)}, u32[]{:S(2)}) %collective-permute-start.65) | collective-permute-done | bytes 204832 | tf_op jit(solution)/shard_map/ppermute | solution.py:35
  348.1 5.3 %collective-permute-done.67 = bf16[256,1024]{1,0:T(8,128)(2,1)S(1)} collective-permute-done((bf16[256,1024]{1,0:T(8,128)(2,1)S(1)}, bf16[256,1024]{1,0:T(8,128)(2,1)S(1)}, u32[]{:S(2)}, u32[]{:S(2)}) %collective-permute-start.67) | collective-permute-done | bytes 524320 | tf_op jit(solution)/shard_map/ppermute | solution.py:35
  354.6 2.4 collective-permute-start.70
  357.7 1.8 collective-permute-start.69
  359.6 1.5 maximum_select_fusion
  361.1 4.2 %collective-permute-done.70 = bf16[304,256]{1,0:T(8,128)(2,1)S(1)} collective-permute-done((bf16[304,256]{1,0:T(8,128)(2,1)S(1)}, bf16[304,256]{1,0:T(8,128)(2,1)S(1)}, u32[]{:S(2)}, u32[]{:S(2)}) %collective-permute-start.70) | collective-permute-done | bytes 155680 | tf_op jit(solution)/shard_map/ppermute | solution.py:35
  365.2 4.3 %collective-permute-done.69 = bf16[400,256]{1,0:T(8,128)(2,1)S(1)} collective-permute-done((bf16[400,256]{1,0:T(8,128)(2,1)S(1)}, bf16[400,256]{1,0:T(8,128)(2,1)S(1)}, u32[]{:S(2)}, u32[]{:S(2)}) %collective-permute-start.69) | collective-permute-done | bytes 204832 | tf_op jit(solution)/shard_map/ppermute | solution.py:35
  369.5 1.5 collective-permute-done.71
  374.3 1.5 fusion.5
  (391 shorter events, 84.3 us)
Async XLA Ops:
  3.2 19.8 %collective-permute-start.2 = (bf16[256,1024]{1,0:T(8,128)(2,1)S(1)}, bf16[256,1024]{1,0:T(8,128)(2,1)S(1)}, u32[]{:S(2)}, u32[]{:S(2)}) collective-permute-start(bf16[256,1024]{1,0:T(8,128)(2,1)S(1)} %select_bitcast_fusion.6), channel_id=1, source_target_pairs={{0,16},{8,24},{16,0},{24,8},{1,17},{9,25},{17,1},{25,9},{2,18},{10... | collective-permute-start | bytes 1572872 | tf_op jit(solution)/shard_map/ppermute | solution.py:35
  6.2 16.8 %collective-permute-start = (bf16[400,256]{1,0:T(8,128)(2,1)S(1)}, bf16[400,256]{1,0:T(8,128)(2,1)S(1)}, u32[]{:S(2)}, u32[]{:S(2)}) collective-permute-start(bf16[400,256]{1,0:T(8,128)(2,1)S(1)} %fusion.19.refs_0_), channel_id=1, source_target_pairs={{0,6},{1,7},{2,4},{3,5},{4,2},{5,3},{6,0},{7,1},{8,14},{9,15},{10,... | collective-permute-start | bytes 614408 | tf_op jit(solution)/shard_map/ppermute | solution.py:35
  9.8 13.2 %collective-permute-start.1 = (bf16[400,256]{1,0:T(8,128)(2,1)S(1)}, bf16[400,256]{1,0:T(8,128)(2,1)S(1)}, u32[]{:S(2)}, u32[]{:S(2)}) collective-permute-start(bf16[400,256]{1,0:T(8,128)(2,1)S(1)} %fusion.19.refs_0_), channel_id=1, source_target_pairs={{0,2},{1,3},{2,0},{3,1},{4,6},{5,7},{6,4},{7,5},{8,10},{9,11},{10,... | collective-permute-start | bytes 614408 | tf_op jit(solution)/shard_map/ppermute | solution.py:35
  11.3 11.7 %collective-permute-start.4 = (bf16[1,352,256]{2,1,0:T(8,128)(2,1)S(1)}, bf16[1,352,256]{2,1,0:T(8,128)(2,1)S(1)}, u32[]{:S(2)}, u32[]{:S(2)}) collective-permute-start(bf16[1,352,256]{2,1,0:T(8,128)(2,1)S(1)} %maximum_bitcast_fusion.4.refs_8_), channel_id=1, source_target_pairs={{0,6},{1,7},{2,4},{3,5},{4,2},{5,3},{6,0},{7,1},{8,14},{9,15},{10,... | collective-permute-start | bytes 540680 | tf_op jit(solution)/shard_map/ppermute | solution.py:35
  23.9 18.8 %collective-permute-start.7 = (bf16[2,256,1024]{2,1,0:T(8,128)(2,1)S(1)}, bf16[2,256,1024]{2,1,0:T(8,128)(2,1)S(1)}, u32[]{:S(2)}, u32[]{:S(2)}) collective-permute-start(bf16[2,256,1024]{2,1,0:T(8,128)(2,1)S(1)} %pad_maximum_fusion.3), channel_id=1, source_target_pairs={{0,8},{8,0},{16,24},{24,16},{1,9},{9,1},{17,25},{25,17},{2,10},{10... | collective-permute-start | bytes 3145736 | tf_op jit(solution)/shard_map/ppermute | solution.py:35
  23.9 18.8 %collective-permute-start.6 = (bf16[256,1024]{1,0:T(8,128)(2,1)S(1)}, bf16[256,1024]{1,0:T(8,128)(2,1)S(1)}, u32[]{:S(2)}, u32[]{:S(2)}) collective-permute-start(bf16[256,1024]{1,0:T(8,128)(2,1)S(1)} %get-tuple-element.339), channel_id=1, source_target_pairs={{0,16},{8,24},{16,0},{24,8},{1,17},{9,25},{17,1},{25,9},{2,18},{10... | collective-permute-start | bytes 1572872 | tf_op jit(solution)/shard_map/ppermute | solution.py:35
  24.4 18.3 %collective-permute-start.5 = (bf16[400,256]{1,0:T(8,128)(2,1)S(1)}, bf16[400,256]{1,0:T(8,128)(2,1)S(1)}, u32[]{:S(2)}, u32[]{:S(2)}) collective-permute-start(bf16[400,256]{1,0:T(8,128)(2,1)S(1)} %collective-permute-done.refs_1_), channel_id=1, source_target_pairs={{0,2},{1,3},{2,0},{3,1},{4,6},{5,7},{6,4},{7,5},{8,10},{9,11},{10,... | collective-permute-start | bytes 614408 | tf_op jit(solution)/shard_map/ppermute | solution.py:35
  27.8 14.9 %collective-permute-start.8 = (bf16[1,352,256]{2,1,0:T(8,128)(2,1)S(1)}, bf16[1,352,256]{2,1,0:T(8,128)(2,1)S(1)}, u32[]{:S(2)}, u32[]{:S(2)}) collective-permute-start(bf16[1,352,256]{2,1,0:T(8,128)(2,1)S(1)} %maximum_bitcast_fusion.4.refs_8_), channel_id=1, source_target_pairs={{0,2},{1,3},{2,0},{3,1},{4,6},{5,7},{6,4},{7,5},{8,10},{9,11},{10,... | collective-permute-start | bytes 540680 | tf_op jit(solution)/shard_map/ppermute | solution.py:35
  27.8 14.8 %collective-permute-start.9 = (bf16[304,256]{1,0:T(8,128)(2,1)S(1)}, bf16[304,256]{1,0:T(8,128)(2,1)S(1)}, u32[]{:S(2)}, u32[]{:S(2)}) collective-permute-start(bf16[304,256]{1,0:T(8,128)(2,1)S(1)} %pad_maximum_fusion.20), channel_id=1, source_target_pairs={{0,6},{1,7},{2,4},{3,5},{4,2},{5,3},{6,0},{7,1},{8,14},{9,15},{10,... | collective-permute-start | bytes 466952 | tf_op jit(solution)/shard_map/ppermute | solution.py:35
  44.3 22.1 %collective-permute-start.14 = (bf16[2,256,1024]{2,1,0:T(8,128)(2,1)}, bf16[2,256,1024]{2,1,0:T(8,128)(2,1)}, u32[]{:S(2)}, u32[]{:S(2)}) collective-permute-start(bf16[2,256,1024]{2,1,0:T(8,128)(2,1)} %pad_maximum_fusion.4), channel_id=1, source_target_pairs={{0,8},{8,0},{16,24},{24,16},{1,9},{9,1},{17,25},{25,17},{2,10},{10... | collective-permute-start | bytes 3145736 | tf_op jit(solution)/shard_map/ppermute | solution.py:35
  44.3 20.8 %collective-permute-start.10 = (bf16[4,400,256]{2,1,0:T(8,128)(2,1)S(1)}, bf16[4,400,256]{2,1,0:T(8,128)(2,1)}, u32[]{:S(2)}, u32[]{:S(2)}) collective-permute-start(bf16[4,400,256]{2,1,0:T(8,128)(2,1)S(1)} %shard_map.220.refs_9_.refs_7_), channel_id=1, source_target_pairs={{0,1},{1,0},{2,3},{3,2},{4,5},{5,4},{6,7},{7,6},{8,9},{9,8},{10,11... | collective-permute-start | bytes 2457608 | tf_op jit(solution)/shard_map/ppermute | solution.py:35
  45.9 20.5 %collective-permute-start.11 = (bf16[4,400,256]{2,1,0:T(8,128)(2,1)S(1)}, bf16[4,400,256]{2,1,0:T(8,128)(2,1)}, u32[]{:S(2)}, u32[]{:S(2)}) collective-permute-start(bf16[4,400,256]{2,1,0:T(8,128)(2,1)S(1)} %shard_map.220.refs_9_.refs_7_), channel_id=1, source_target_pairs={{0,16},{8,24},{16,0},{24,8},{1,17},{9,25},{17,1},{25,9},{2,18},{10... | collective-permute-start | bytes 2457608 | tf_op jit(solution)/shard_map/ppermute | solution.py:35
  48.5 15.1 %collective-permute-start.12 = (bf16[2,304,256]{2,1,0:T(8,128)(2,1)S(1)}, bf16[2,304,256]{2,1,0:T(8,128)(2,1)S(1)}, u32[]{:S(2)}, u32[]{:S(2)}) collective-permute-start(bf16[2,304,256]{2,1,0:T(8,128)(2,1)S(1)} %pad_maximum_fusion.14), channel_id=1, source_target_pairs={{0,2},{1,3},{2,0},{3,1},{4,6},{5,7},{6,4},{7,5},{8,10},{9,11},{10,... | collective-permute-start | bytes 933896 | tf_op jit(solution)/shard_map/ppermute | solution.py:35
  48.5 14.8 %collective-permute-start.13 = (bf16[528,256]{1,0:T(8,128)(2,1)}, bf16[528,256]{1,0:T(8,128)(2,1)S(1)}, u32[]{:S(2)}, u32[]{:S(2)}) collective-permute-start(bf16[528,256]{1,0:T(8,128)(2,1)} %fusion.18), channel_id=1, source_target_pairs={{0,6},{1,7},{2,4},{3,5},{4,2},{5,3},{6,0},{7,1},{8,14},{9,15},{10,... | collective-permute-start | bytes 811016 | tf_op jit(solution)/shard_map/ppermute | solution.py:35
  69.9 19.5 %collective-permute-start.19 = (bf16[2,528,256]{2,1,0:T(8,128)(2,1)}, bf16[2,528,256]{2,1,0:T(8,128)(2,1)}, u32[]{:S(2)}, u32[]{:S(2)}) collective-permute-start(bf16[2,528,256]{2,1,0:T(8,128)(2,1)} %pad_maximum_fusion.7), channel_id=1, source_target_pairs={{0,2},{1,3},{2,0},{3,1},{4,6},{5,7},{6,4},{7,5},{8,10},{9,11},{10,... | collective-permute-start | bytes 1622024 | tf_op jit(solution)/shard_map/ppermute | solution.py:35
  70.7 13.1 %collective-permute-start.18 = (bf16[2,352,256]{2,1,0:T(8,128)(2,1)}, bf16[2,352,256]{2,1,0:T(8,128)(2,1)}, u32[]{:S(2)}, u32[]{:S(2)}) collective-permute-start(bf16[2,352,256]{2,1,0:T(8,128)(2,1)} %pad_maximum_fusion.12), channel_id=1, source_target_pairs={{0,16},{8,24},{16,0},{24,8},{1,17},{9,25},{17,1},{25,9},{2,18},{10... | collective-permute-start | bytes 1081352 | tf_op jit(solution)/shard_map/ppermute | solution.py:35
  74.7 14.7 %collective-permute-start.15 = (bf16[2,400,256]{2,1,0:T(8,128)(2,1)}, bf16[2,400,256]{2,1,0:T(8,128)(2,1)S(1)}, u32[]{:S(2)}, u32[]{:S(2)}) collective-permute-start(bf16[2,400,256]{2,1,0:T(8,128)(2,1)} %slice.396), channel_id=1, source_target_pairs={{0,16},{8,24},{16,0},{24,8},{1,17},{9,25},{17,1},{25,9},{2,18},{10... | collective-permute-start | bytes 1228808 | tf_op jit(solution)/shard_map/ppermute | solution.py:35
  77.0 12.4 %collective-permute-start.16 = (bf16[2,400,256]{2,1,0:T(8,128)(2,1)}, bf16[2,400,256]{2,1,0:T(8,128)(2,1)}, u32[]{:S(2)}, u32[]{:S(2)}) collective-permute-start(bf16[2,400,256]{2,1,0:T(8,128)(2,1)} %slice.397), channel_id=1, source_target_pairs={{0,1},{1,0},{2,3},{3,2},{4,5},{5,4},{6,7},{7,6},{8,9},{9,8},{10,11... | collective-permute-start | bytes 1228808 | tf_op jit(solution)/shard_map/ppermute | solution.py:35
  90.6 18.9 %collective-permute-start.22 = (bf16[3,352,256]{2,1,0:T(8,128)(2,1)S(1)}, bf16[3,352,256]{2,1,0:T(8,128)(2,1)S(1)}, u32[]{:S(2)}, u32[]{:S(2)}) collective-permute-start(bf16[3,352,256]{2,1,0:T(8,128)(2,1)S(1)} %constant_dynamic-update-slice_fusion.refs_12_), channel_id=1, source_target_pairs={{0,6},{1,7},{2,4},{3,5},{4,2},{5,3},{6,0},{7,1},{8,14},{9,15},{10,... | collective-permute-start | bytes 1622024 | tf_op jit(solution)/shard_map/ppermute | solution.py:35
  92.0 24.0 %collective-permute-start.23 = (bf16[3,352,256]{2,1,0:T(8,128)(2,1)S(1)}, bf16[3,352,256]{2,1,0:T(8,128)(2,1)S(1)}, u32[]{:S(2)}, u32[]{:S(2)}) collective-permute-start(bf16[3,352,256]{2,1,0:T(8,128)(2,1)S(1)} %constant_dynamic-update-slice_fusion.refs_12_), channel_id=1, source_target_pairs={{0,2},{1,3},{2,0},{3,1},{4,6},{5,7},{6,4},{7,5},{8,10},{9,11},{10,... | collective-permute-start | bytes 1622024 | tf_op jit(solution)/shard_map/ppermute | solution.py:35
  92.9 23.1 %collective-permute-start.20 = (bf16[4,304,256]{2,1,0:T(8,128)(2,1)S(1)}, bf16[4,304,256]{2,1,0:T(8,128)(2,1)S(1)}, u32[]{:S(2)}, u32[]{:S(2)}) collective-permute-start(bf16[4,304,256]{2,1,0:T(8,128)(2,1)S(1)} %shard_map.222.refs_2_.refs_16_.refs_10_), channel_id=1, source_target_pairs={{0,1},{1,0},{2,3},{3,2},{4,5},{5,4},{6,7},{7,6},{8,9},{9,8},{10,11... | collective-permute-start | bytes 1867784 | tf_op jit(solution)/shard_map/ppermute | solution.py:35
  93.6 22.4 %collective-permute-start.21 = (bf16[4,304,256]{2,1,0:T(8,128)(2,1)S(1)}, bf16[4,304,256]{2,1,0:T(8,128)(2,1)S(1)}, u32[]{:S(2)}, u32[]{:S(2)}) collective-permute-start(bf16[4,304,256]{2,1,0:T(8,128)(2,1)S(1)} %shard_map.222.refs_2_.refs_16_.refs_10_), channel_id=1, source_target_pairs={{0,16},{8,24},{16,0},{24,8},{1,17},{9,25},{17,1},{25,9},{2,18},{10... | collective-permute-start | bytes 1867784 | tf_op jit(solution)/shard_map/ppermute | solution.py:35
  97.0 12.5 %collective-permute-start.24 = (bf16[2,176,256]{2,1,0:T(8,128)(2,1)S(1)}, bf16[2,176,256]{2,1,0:T(8,128)(2,1)S(1)}, u32[]{:S(2)}, u32[]{:S(2)}) collective-permute-start(bf16[2,176,256]{2,1,0:T(8,128)(2,1)S(1)} %pad_maximum_fusion.19), channel_id=1, source_target_pairs={{0,8},{8,0},{16,24},{24,16},{1,9},{9,1},{17,25},{25,17},{2,10},{10... | collective-permute-start | bytes 540680 | tf_op jit(solution)/shard_map/ppermute | solution.py:35
  116.0 10.4 %collective-permute-start.25 = (bf16[2,304,256]{2,1,0:T(8,128)(2,1)S(1)}, bf16[2,304,256]{2,1,0:T(8,128)(2,1)S(1)}, u32[]{:S(2)}, u32[]{:S(2)}) collective-permute-start(bf16[2,304,256]{2,1,0:T(8,128)(2,1)S(1)} %slice.406), channel_id=1, source_target_pairs={{0,16},{8,24},{16,0},{24,8},{1,17},{9,25},{17,1},{25,9},{2,18},{10... | collective-permute-start | bytes 933896 | tf_op jit(solution)/shard_map/ppermute | solution.py:35
  118.7 29.9 %collective-permute-start.29 = (bf16[2,528,256]{2,1,0:T(8,128)(2,1)S(1)}, bf16[2,528,256]{2,1,0:T(8,128)(2,1)S(1)}, u32[]{:S(2)}, u32[]{:S(2)}) collective-permute-start(bf16[2,528,256]{2,1,0:T(8,128)(2,1)S(1)} %pad_maximum_fusion.9.refs_9_), channel_id=1, source_target_pairs={{0,16},{8,24},{16,0},{24,8},{1,17},{9,25},{17,1},{25,9},{2,18},{10... | collective-permute-start | bytes 1622024 | tf_op jit(solution)/shard_map/ppermute | solution.py:35
  120.3 10.4 %collective-permute-start.26 = (bf16[2,304,256]{2,1,0:T(8,128)(2,1)S(1)}, bf16[2,304,256]{2,1,0:T(8,128)(2,1)S(1)}, u32[]{:S(2)}, u32[]{:S(2)}) collective-permute-start(bf16[2,304,256]{2,1,0:T(8,128)(2,1)S(1)} %slice.407), channel_id=1, source_target_pairs={{0,1},{1,0},{2,3},{3,2},{4,5},{5,4},{6,7},{7,6},{8,9},{9,8},{10,11... | collective-permute-start | bytes 933896 | tf_op jit(solution)/shard_map/ppermute | solution.py:35
  121.1 27.5 %collective-permute-start.28 = (bf16[2,528,256]{2,1,0:T(8,128)(2,1)S(1)}, bf16[2,528,256]{2,1,0:T(8,128)(2,1)S(1)}, u32[]{:S(2)}, u32[]{:S(2)}) collective-permute-start(bf16[2,528,256]{2,1,0:T(8,128)(2,1)S(1)} %pad_maximum_fusion.8.refs_5_), channel_id=1, source_target_pairs={{0,1},{1,0},{2,3},{3,2},{4,5},{5,4},{6,7},{7,6},{8,9},{9,8},{10,11... | collective-permute-start | bytes 1622024 | tf_op jit(solution)/shard_map/ppermute | solution.py:35
  122.5 26.1 %collective-permute-start.31 = (bf16[3,352,256]{2,1,0:T(8,128)(2,1)S(1)}, bf16[3,352,256]{2,1,0:T(8,128)(2,1)S(1)}, u32[]{:S(2)}, u32[]{:S(2)}) collective-permute-start(bf16[3,352,256]{2,1,0:T(8,128)(2,1)S(1)} %collective-permute-done.22.refs_13_), channel_id=1, source_target_pairs={{0,2},{1,3},{2,0},{3,1},{4,6},{5,7},{6,4},{7,5},{8,10},{9,11},{10,... | collective-permute-start | bytes 1622024 | tf_op jit(solution)/shard_map/ppermute | solution.py:35
  126.4 22.2 %collective-permute-start.27 = (bf16[256,1024]{1,0:T(8,128)(2,1)S(1)}, bf16[256,1024]{1,0:T(8,128)(2,1)S(1)}, u32[]{:S(2)}, u32[]{:S(2)}) collective-permute-start(bf16[256,1024]{1,0:T(8,128)(2,1)S(1)} %copy-done.79), channel_id=1, source_target_pairs={{0,16},{8,24},{16,0},{24,8},{1,17},{9,25},{17,1},{25,9},{2,18},{10... | collective-permute-start | bytes 1572872 | tf_op jit(solution)/shard_map/ppermute | solution.py:35
  130.7 17.9 %collective-permute-start.30 = (bf16[1,352,256]{2,1,0:T(8,128)(2,1)S(1)}, bf16[1,352,256]{2,1,0:T(8,128)(2,1)S(1)}, u32[]{:S(2)}, u32[]{:S(2)}) collective-permute-start(bf16[1,352,256]{2,1,0:T(8,128)(2,1)S(1)} %copy-done.49), channel_id=1, source_target_pairs={{0,2},{1,3},{2,0},{3,1},{4,6},{5,7},{6,4},{7,5},{8,10},{9,11},{10,... | collective-permute-start | bytes 540680 | tf_op jit(solution)/shard_map/ppermute | solution.py:35
  154.4 35.4 %collective-permute-start.34 = (bf16[2,528,256]{2,1,0:T(8,128)(2,1)S(1)}, bf16[2,528,256]{2,1,0:T(8,128)(2,1)S(1)}, u32[]{:S(2)}, u32[]{:S(2)}) collective-permute-start(bf16[2,528,256]{2,1,0:T(8,128)(2,1)S(1)} %pad_maximum_fusion.8.refs_5_), channel_id=1, source_target_pairs={{0,16},{8,24},{16,0},{24,8},{1,17},{9,25},{17,1},{25,9},{2,18},{10... | collective-permute-start | bytes 1622024 | tf_op jit(solution)/shard_map/ppermute | solution.py:35
  155.9 33.9 %collective-permute-start.35 = (bf16[2,528,256]{2,1,0:T(8,128)(2,1)S(1)}, bf16[2,528,256]{2,1,0:T(8,128)(2,1)S(1)}, u32[]{:S(2)}, u32[]{:S(2)}) collective-permute-start(bf16[2,528,256]{2,1,0:T(8,128)(2,1)S(1)} %collective-permute-done.28.refs_6_), channel_id=1, source_target_pairs={{0,16},{8,24},{16,0},{24,8},{1,17},{9,25},{17,1},{25,9},{2,18},{10... | collective-permute-start | bytes 1622024 | tf_op jit(solution)/shard_map/ppermute | solution.py:35
  156.4 33.4 %collective-permute-start.36 = (bf16[2,528,256]{2,1,0:T(8,128)(2,1)S(1)}, bf16[2,528,256]{2,1,0:T(8,128)(2,1)S(1)}, u32[]{:S(2)}, u32[]{:S(2)}) collective-permute-start(bf16[2,528,256]{2,1,0:T(8,128)(2,1)S(1)} %pad_maximum_fusion.9.refs_9_), channel_id=1, source_target_pairs={{0,1},{1,0},{2,3},{3,2},{4,5},{5,4},{6,7},{7,6},{8,9},{9,8},{10,11... | collective-permute-start | bytes 1622024 | tf_op jit(solution)/shard_map/ppermute | solution.py:35
  157.0 32.7 %collective-permute-start.37 = (bf16[2,528,256]{2,1,0:T(8,128)(2,1)S(1)}, bf16[2,528,256]{2,1,0:T(8,128)(2,1)S(1)}, u32[]{:S(2)}, u32[]{:S(2)}) collective-permute-start(bf16[2,528,256]{2,1,0:T(8,128)(2,1)S(1)} %collective-permute-done.29.refs_11_), channel_id=1, source_target_pairs={{0,1},{1,0},{2,3},{3,2},{4,5},{5,4},{6,7},{7,6},{8,9},{9,8},{10,11... | collective-permute-start | bytes 1622024 | tf_op jit(solution)/shard_map/ppermute | solution.py:35
  189.8 32.5 %collective-permute-start.38 = (bf16[4,528,256]{2,1,0:T(8,128)(2,1)S(1)}, bf16[4,528,256]{2,1,0:T(8,128)(2,1)S(1)}, u32[]{:S(2)}, u32[]{:S(2)}) collective-permute-start(bf16[4,528,256]{2,1,0:T(8,128)(2,1)S(1)} %get-tuple-element.480), channel_id=1, source_target_pairs={{0,1},{1,0},{2,3},{3,2},{4,5},{5,4},{6,7},{7,6},{8,9},{9,8},{10,11... | collective-permute-start | bytes 3244040 | tf_op jit(solution)/shard_map/ppermute | solution.py:35
  190.5 31.9 %collective-permute-start.39 = (bf16[4,528,256]{2,1,0:T(8,128)(2,1)S(1)}, bf16[4,528,256]{2,1,0:T(8,128)(2,1)S(1)}, u32[]{:S(2)}, u32[]{:S(2)}) collective-permute-start(bf16[4,528,256]{2,1,0:T(8,128)(2,1)S(1)} %get-tuple-element.481), channel_id=1, source_target_pairs={{0,16},{8,24},{16,0},{24,8},{1,17},{9,25},{17,1},{25,9},{2,18},{10... | collective-permute-start | bytes 3244040 | tf_op jit(solution)/shard_map/ppermute | solution.py:35
  222.4 23.7 %collective-permute-start.44 = (bf16[2,256,1024]{2,1,0:T(8,128)(2,1)}, bf16[2,256,1024]{2,1,0:T(8,128)(2,1)}, u32[]{:S(2)}, u32[]{:S(2)}) collective-permute-start(bf16[2,256,1024]{2,1,0:T(8,128)(2,1)} %get-tuple-element.508), channel_id=1, source_target_pairs={{0,8},{8,0},{16,24},{24,16},{1,9},{9,1},{17,25},{25,17},{2,10},{10... | collective-permute-start | bytes 3145736 | tf_op jit(solution)/shard_map/ppermute | solution.py:35
  223.9 22.3 %collective-permute-start.42 = (bf16[2,528,256]{2,1,0:T(8,128)(2,1)}, bf16[2,528,256]{2,1,0:T(8,128)(2,1)}, u32[]{:S(2)}, u32[]{:S(2)}) collective-permute-start(bf16[2,528,256]{2,1,0:T(8,128)(2,1)} %add_convert_fusion.1), channel_id=1, source_target_pairs={{0,16},{8,24},{16,0},{24,8},{1,17},{9,25},{17,1},{25,9},{2,18},{10... | collective-permute-start | bytes 1622024 | tf_op jit(solution)/shard_map/ppermute | solution.py:35
  224.4 21.8 %collective-permute-start.43 = (bf16[4,352,256]{2,1,0:T(8,128)(2,1)}, bf16[4,352,256]{2,1,0:T(8,128)(2,1)}, u32[]{:S(2)}, u32[]{:S(2)}) collective-permute-start(bf16[4,352,256]{2,1,0:T(8,128)(2,1)} %get-tuple-element.506), channel_id=1, source_target_pairs={{0,2},{1,3},{2,0},{3,1},{4,6},{5,7},{6,4},{7,5},{8,10},{9,11},{10,... | collective-permute-start | bytes 2162696 | tf_op jit(solution)/shard_map/ppermute | solution.py:35
  227.0 19.2 %collective-permute-start.41 = (bf16[2,528,256]{2,1,0:T(8,128)(2,1)}, bf16[2,528,256]{2,1,0:T(8,128)(2,1)}, u32[]{:S(2)}, u32[]{:S(2)}) collective-permute-start(bf16[2,528,256]{2,1,0:T(8,128)(2,1)} %add_convert_fusion.2), channel_id=1, source_target_pairs={{0,1},{1,0},{2,3},{3,2},{4,5},{5,4},{6,7},{7,6},{8,9},{9,8},{10,11... | collective-permute-start | bytes 1622024 | tf_op jit(solution)/shard_map/ppermute | solution.py:35
  248.1 21.6 %collective-permute-start.49 = (bf16[2,176,256]{2,1,0:T(8,128)(2,1)S(1)}, bf16[2,176,256]{2,1,0:T(8,128)(2,1)S(1)}, u32[]{:S(2)}, u32[]{:S(2)}) collective-permute-start(bf16[2,176,256]{2,1,0:T(8,128)(2,1)S(1)} %slice.727), channel_id=1, source_target_pairs={{0,8},{8,0},{16,24},{24,16},{1,9},{9,1},{17,25},{25,17},{2,10},{10... | collective-permute-start | bytes 540680 | tf_op jit(solution)/shard_map/ppermute | solution.py:35
  248.2 27.0 %collective-permute-start.48 = (bf16[4,352,256]{2,1,0:T(8,128)(2,1)S(1)}, bf16[4,352,256]{2,1,0:T(8,128)(2,1)S(1)}, u32[]{:S(2)}, u32[]{:S(2)}) collective-permute-start(bf16[4,352,256]{2,1,0:T(8,128)(2,1)S(1)} %copy-done.42), channel_id=1, source_target_pairs={{0,2},{1,3},{2,0},{3,1},{4,6},{5,7},{6,4},{7,5},{8,10},{9,11},{10,... | collective-permute-start | bytes 2162696 | tf_op jit(solution)/shard_map/ppermute | solution.py:35
  248.7 26.5 %collective-permute-start.45 = (bf16[4,304,256]{2,1,0:T(8,128)(2,1)S(1)}, bf16[4,304,256]{2,1,0:T(8,128)(2,1)S(1)}, u32[]{:S(2)}, u32[]{:S(2)}) collective-permute-start(bf16[4,304,256]{2,1,0:T(8,128)(2,1)S(1)} %get-tuple-element.519), channel_id=1, source_target_pairs={{0,1},{1,0},{2,3},{3,2},{4,5},{5,4},{6,7},{7,6},{8,9},{9,8},{10,11... | collective-permute-start | bytes 1867784 | tf_op jit(solution)/shard_map/ppermute | solution.py:35
  249.8 25.4 %collective-permute-start.46 = (bf16[4,304,256]{2,1,0:T(8,128)(2,1)S(1)}, bf16[4,304,256]{2,1,0:T(8,128)(2,1)S(1)}, u32[]{:S(2)}, u32[]{:S(2)}) collective-permute-start(bf16[4,304,256]{2,1,0:T(8,128)(2,1)S(1)} %get-tuple-element.520), channel_id=1, source_target_pairs={{0,16},{8,24},{16,0},{24,8},{1,17},{9,25},{17,1},{25,9},{2,18},{10... | collective-permute-start | bytes 1867784 | tf_op jit(solution)/shard_map/ppermute | solution.py:35
  252.2 23.0 %collective-permute-start.47 = (bf16[2,352,256]{2,1,0:T(8,128)(2,1)S(1)}, bf16[2,352,256]{2,1,0:T(8,128)(2,1)S(1)}, u32[]{:S(2)}, u32[]{:S(2)}) collective-permute-start(bf16[2,352,256]{2,1,0:T(8,128)(2,1)S(1)} %slice.500), channel_id=1, source_target_pairs={{0,6},{1,7},{2,4},{3,5},{4,2},{5,3},{6,0},{7,1},{8,14},{9,15},{10,... | collective-permute-start | bytes 1081352 | tf_op jit(solution)/shard_map/ppermute | solution.py:35
  275.5 24.9 %collective-permute-start.54 = (bf16[2,528,256]{2,1,0:T(8,128)(2,1)S(1)}, bf16[2,528,256]{2,1,0:T(8,128)(2,1)S(1)}, u32[]{:S(2)}, u32[]{:S(2)}) collective-permute-start(bf16[2,528,256]{2,1,0:T(8,128)(2,1)S(1)} %pad_maximum_fusion.10), channel_id=1, source_target_pairs={{0,2},{1,3},{2,0},{3,1},{4,6},{5,7},{6,4},{7,5},{8,10},{9,11},{10,... | collective-permute-start | bytes 1622024 | tf_op jit(solution)/shard_map/ppermute | solution.py:35
  275.7 24.7 %collective-permute-start.52 = (bf16[2,304,256]{2,1,0:T(8,128)(2,1)S(1)}, bf16[2,304,256]{2,1,0:T(8,128)(2,1)}, u32[]{:S(2)}, u32[]{:S(2)}) collective-permute-start(bf16[2,304,256]{2,1,0:T(8,128)(2,1)S(1)} %add_convert_fusion.7), channel_id=1, source_target_pairs={{0,1},{1,0},{2,3},{3,2},{4,5},{5,4},{6,7},{7,6},{8,9},{9,8},{10,11... | collective-permute-start | bytes 933896 | tf_op jit(solution)/shard_map/ppermute | solution.py:35
  276.6 23.8 %collective-permute-start.50 = (bf16[4,400,256]{2,1,0:T(8,128)(2,1)S(1)}, bf16[4,400,256]{2,1,0:T(8,128)(2,1)S(1)}, u32[]{:S(2)}, u32[]{:S(2)}) collective-permute-start(bf16[4,400,256]{2,1,0:T(8,128)(2,1)S(1)} %get-tuple-element.550), channel_id=1, source_target_pairs={{0,16},{8,24},{16,0},{24,8},{1,17},{9,25},{17,1},{25,9},{2,18},{10... | collective-permute-start | bytes 2457608 | tf_op jit(solution)/shard_map/ppermute | solution.py:35
  278.8 21.7 %collective-permute-start.53 = (bf16[2,352,256]{2,1,0:T(8,128)(2,1)}, bf16[2,352,256]{2,1,0:T(8,128)(2,1)S(1)}, u32[]{:S(2)}, u32[]{:S(2)}) collective-permute-start(bf16[2,352,256]{2,1,0:T(8,128)(2,1)} %slice.422), channel_id=1, source_target_pairs={{0,6},{1,7},{2,4},{3,5},{4,2},{5,3},{6,0},{7,1},{8,14},{9,15},{10,... | collective-permute-start | bytes 1081352 | tf_op jit(solution)/shard_map/ppermute | solution.py:35
  280.2 20.2 %collective-permute-start.51 = (bf16[2,400,256]{2,1,0:T(8,128)(2,1)S(1)}, bf16[2,400,256]{2,1,0:T(8,128)(2,1)S(1)}, u32[]{:S(2)}, u32[]{:S(2)}) collective-permute-start(bf16[2,400,256]{2,1,0:T(8,128)(2,1)S(1)} %get-tuple-element.551), channel_id=1, source_target_pairs={{0,1},{1,0},{2,3},{3,2},{4,5},{5,4},{6,7},{7,6},{8,9},{9,8},{10,11... | collective-permute-start | bytes 1228808 | tf_op jit(solution)/shard_map/ppermute | solution.py:35
  301.7 19.8 %collective-permute-start.57 = (bf16[2,352,256]{2,1,0:T(8,128)(2,1)S(1)}, bf16[2,352,256]{2,1,0:T(8,128)(2,1)S(1)}, u32[]{:S(2)}, u32[]{:S(2)}) collective-permute-start(bf16[2,352,256]{2,1,0:T(8,128)(2,1)S(1)} %get-tuple-element.661), channel_id=1, source_target_pairs={{0,1},{1,0},{2,3},{3,2},{4,5},{5,4},{6,7},{7,6},{8,9},{9,8},{10,11... | collective-permute-start | bytes 1081352 | tf_op jit(solution)/shard_map/ppermute | solution.py:35
  302.5 19.0 %collective-permute-start.59 = (bf16[256,1024]{1,0:T(8,128)(2,1)S(1)}, bf16[256,1024]{1,0:T(8,128)(2,1)S(1)}, u32[]{:S(2)}, u32[]{:S(2)}) collective-permute-start(bf16[256,1024]{1,0:T(8,128)(2,1)S(1)} %get-tuple-element.595), channel_id=1, source_target_pairs={{0,16},{8,24},{16,0},{24,8},{1,17},{9,25},{17,1},{25,9},{2,18},{10... | collective-permute-start | bytes 1572872 | tf_op jit(solution)/shard_map/ppermute | solution.py:35
  303.5 18.0 %collective-permute-start.55 = (bf16[2,400,256]{2,1,0:T(8,128)(2,1)S(1)}, bf16[2,400,256]{2,1,0:T(8,128)(2,1)S(1)}, u32[]{:S(2)}, u32[]{:S(2)}) collective-permute-start(bf16[2,400,256]{2,1,0:T(8,128)(2,1)S(1)} %get-tuple-element.579), channel_id=1, source_target_pairs={{0,1},{1,0},{2,3},{3,2},{4,5},{5,4},{6,7},{7,6},{8,9},{9,8},{10,11... | collective-permute-start | bytes 1228808 | tf_op jit(solution)/shard_map/ppermute | solution.py:35
  304.4 17.0 %collective-permute-start.58 = (bf16[2,304,256]{2,1,0:T(8,128)(2,1)S(1)}, bf16[2,304,256]{2,1,0:T(8,128)(2,1)S(1)}, u32[]{:S(2)}, u32[]{:S(2)}) collective-permute-start(bf16[2,304,256]{2,1,0:T(8,128)(2,1)S(1)} %add_convert_fusion.6), channel_id=1, source_target_pairs={{0,16},{8,24},{16,0},{24,8},{1,17},{9,25},{17,1},{25,9},{2,18},{10... | collective-permute-start | bytes 933896 | tf_op jit(solution)/shard_map/ppermute | solution.py:35
  306.1 10.1 %collective-permute-start.56 = (bf16[528,256]{1,0:T(8,128)(2,1)S(1)}, bf16[528,256]{1,0:T(8,128)(2,1)S(1)}, u32[]{:S(2)}, u32[]{:S(2)}) collective-permute-start(bf16[528,256]{1,0:T(8,128)(2,1)S(1)} %get-tuple-element.681), channel_id=1, source_target_pairs={{0,6},{1,7},{2,4},{3,5},{4,2},{5,3},{6,0},{7,1},{8,14},{9,15},{10,... | collective-permute-start | bytes 811016 | tf_op jit(solution)/shard_map/ppermute | solution.py:35
  321.6 8.7 %collective-permute-start.64 = (bf16[352,256]{1,0:T(8,128)(2,1)S(1)}, bf16[352,256]{1,0:T(8,128)(2,1)S(1)}, u32[]{:S(2)}, u32[]{:S(2)}) collective-permute-start(bf16[352,256]{1,0:T(8,128)(2,1)S(1)} %fusion.26), channel_id=1, source_target_pairs={{0,16},{8,24},{16,0},{24,8},{1,17},{9,25},{17,1},{25,9},{2,18},{10... | collective-permute-start | bytes 540680 | tf_op jit(solution)/shard_map/ppermute | solution.py:35
  324.3 11.6 %collective-permute-start.62 = (bf16[2,400,256]{2,1,0:T(8,128)(2,1)S(1)}, bf16[2,400,256]{2,1,0:T(8,128)(2,1)S(1)}, u32[]{:S(2)}, u32[]{:S(2)}) collective-permute-start(bf16[2,400,256]{2,1,0:T(8,128)(2,1)S(1)} %add_convert_fusion.3), channel_id=1, source_target_pairs={{0,16},{8,24},{16,0},{24,8},{1,17},{9,25},{17,1},{25,9},{2,18},{10... | collective-permute-start | bytes 1228808 | tf_op jit(solution)/shard_map/ppermute | solution.py:35
  325.8 11.2 %collective-permute-start.61 = (bf16[2,400,256]{2,1,0:T(8,128)(2,1)S(1)}, bf16[2,400,256]{2,1,0:T(8,128)(2,1)S(1)}, u32[]{:S(2)}, u32[]{:S(2)}) collective-permute-start(bf16[2,400,256]{2,1,0:T(8,128)(2,1)S(1)} %add_convert_fusion.4), channel_id=1, source_target_pairs={{0,1},{1,0},{2,3},{3,2},{4,5},{5,4},{6,7},{7,6},{8,9},{9,8},{10,11... | collective-permute-start | bytes 1228808 | tf_op jit(solution)/shard_map/ppermute | solution.py:35
  338.5 9.7 %collective-permute-start.65 = (bf16[400,256]{1,0:T(8,128)(2,1)S(1)}, bf16[400,256]{1,0:T(8,128)(2,1)S(1)}, u32[]{:S(2)}, u32[]{:S(2)}) collective-permute-start(bf16[400,256]{1,0:T(8,128)(2,1)S(1)} %fusion.20), channel_id=1, source_target_pairs={{0,2},{1,3},{2,0},{3,1},{4,6},{5,7},{6,4},{7,5},{8,10},{9,11},{10,... | collective-permute-start | bytes 614408 | tf_op jit(solution)/shard_map/ppermute | solution.py:35
  339.7 13.8 %collective-permute-start.67 = (bf16[256,1024]{1,0:T(8,128)(2,1)S(1)}, bf16[256,1024]{1,0:T(8,128)(2,1)S(1)}, u32[]{:S(2)}, u32[]{:S(2)}) collective-permute-start(bf16[256,1024]{1,0:T(8,128)(2,1)S(1)} %get-tuple-element.625), channel_id=1, source_target_pairs={{0,16},{8,24},{16,0},{24,8},{1,17},{9,25},{17,1},{25,9},{2,18},{10... | collective-permute-start | bytes 1572872 | tf_op jit(solution)/shard_map/ppermute | solution.py:35
  354.6 10.6 %collective-permute-start.70 = (bf16[304,256]{1,0:T(8,128)(2,1)S(1)}, bf16[304,256]{1,0:T(8,128)(2,1)S(1)}, u32[]{:S(2)}, u32[]{:S(2)}) collective-permute-start(bf16[304,256]{1,0:T(8,128)(2,1)S(1)} %fusion.15), channel_id=1, source_target_pairs={{0,6},{1,7},{2,4},{3,5},{4,2},{5,3},{6,0},{7,1},{8,14},{9,15},{10,... | collective-permute-start | bytes 466952 | tf_op jit(solution)/shard_map/ppermute | solution.py:35
  357.0 14.1 %collective-permute-start.73 = (bf16[256,1024]{1,0:T(8,128)(2,1)S(1)}, bf16[256,1024]{1,0:T(8,128)(2,1)S(1)}, u32[]{:S(2)}, u32[]{:S(2)}) collective-permute-start(bf16[256,1024]{1,0:T(8,128)(2,1)S(1)} %get-tuple-element.637), channel_id=1, source_target_pairs={{0,16},{8,24},{16,0},{24,8},{1,17},{9,25},{17,1},{25,9},{2,18},{10... | collective-permute-start | bytes 1572872 | tf_op jit(solution)/shard_map/ppermute | solution.py:35
  357.7 11.9 %collective-permute-start.69 = (bf16[400,256]{1,0:T(8,128)(2,1)S(1)}, bf16[400,256]{1,0:T(8,128)(2,1)S(1)}, u32[]{:S(2)}, u32[]{:S(2)}) collective-permute-start(bf16[400,256]{1,0:T(8,128)(2,1)S(1)} %fusion.10), channel_id=1, source_target_pairs={{0,6},{1,7},{2,4},{3,5},{4,2},{5,3},{6,0},{7,1},{8,14},{9,15},{10,... | collective-permute-start | bytes 614408 | tf_op jit(solution)/shard_map/ppermute | solution.py:35
  359.4 11.6 %collective-permute-start.71 = (bf16[400,256]{1,0:T(8,128)(2,1)S(1)}, bf16[400,256]{1,0:T(8,128)(2,1)S(1)}, u32[]{:S(2)}, u32[]{:S(2)}) collective-permute-start(bf16[400,256]{1,0:T(8,128)(2,1)S(1)} %fusion.21), channel_id=1, source_target_pairs={{0,2},{1,3},{2,0},{3,1},{4,6},{5,7},{6,4},{7,5},{8,10},{9,11},{10,... | collective-permute-start | bytes 614408 | tf_op jit(solution)/shard_map/ppermute | solution.py:35
  (102 other events, 773.4 us)

commit v3 on v2

--- a/solution.py
+++ b/solution.py
@@ -2,6 +2,7 @@
 
 import jax
 import jax.numpy as jnp
+import numpy as np
 from jax import lax
 from jax.experimental import pallas as pl
 from jax.experimental.pallas import tpu as pltpu
@@ -131,6 +132,16 @@
             self.ref[spot[0], spot[1], lanes] = content
 
     put(tuple(Cut(ref) for ref in outs), by, bx, q, rows, value)
+
+
+def turn_tables(length):
+    half = HEAD // 2
+    steps = np.arange(half, dtype=np.float32) * np.float32(2.0)
+    frequency = np.power(np.float32(10000.0), -steps / np.float32(HEAD), dtype=np.float32)
+    angles = (np.arange(length, dtype=np.float32)[:, None] * frequency[None, :]).astype(np.float64)
+    cosine = np.tile(np.cos(angles), (1, 4))
+    sine = np.tile(np.concatenate([-np.sin(angles), np.sin(angles)], axis=1), (1, 2))
+    return jnp.asarray(cosine.astype(np.float32)), jnp.asarray(sine.astype(np.float32))
 
 
 def pack_body(*refs):
@@ -204,7 +215,7 @@
                     (q, k)[n][at, cols] = both * BF16(0.125) if n == 0 else both
         return carry
 
-    lax.fori_loop(0, x.shape[0] // TILE, step, 0)
+    lax.fori_loop(0, x.shape[0] // TILE, step, 0, unroll=True)
 
 
 def split_heads(pair):
@@ -293,7 +304,7 @@
         part[at, :] = dot_nn(att[at, :], wo[...]).astype(BF16)
         return carry
 
-    lax.fori_loop(0, att.shape[0] // TILE, step, 0)
+    lax.fori_loop(0, att.shape[0] // TILE, step, 0, unroll=True)
 
 
 def middle_of(x, part, recv, at):
@@ -329,7 +340,7 @@
         return carry
 
     tiles = att.shape[0] // TILE
-    lax.fori_loop(0, tiles, norm_step, 0)
+    lax.fori_loop(0, tiles, norm_step, 0, unroll=True)
     for copy in copies:
         copy.wait()
 
@@ -338,7 +349,7 @@
         datt[at, :] = dot_nt(gb[at, :], wo[...]).astype(BF16)
         return carry
 
-    lax.fori_loop(0, tiles, step, 0)
+    lax.fori_loop(0, tiles, step, 0, unroll=True)
     for by, other in bits(2):
         grad = dot_tn(att[...], gb[:, pl.ds(column_of(info, by, other), 256)]).astype(BF16)
         for t in range(2):
@@ -416,7 +427,7 @@
             gy[at, :] = (piece_of(info, t, *cot_parts).astype(F32) * live).astype(BF16)
             return carry
 
-        lax.fori_loop(0, tiles, norm_step, 0)
+        lax.fori_loop(0, tiles, norm_step, 0, unroll=True)
     for copy in copies:
         copy.wait()
 
@@ -450,7 +461,7 @@
 
         return carry
 
-    lax.fori_loop(0, tiles, step, 0)
+    lax.fori_loop(0, tiles, step, 0, unroll=True)
     own = units // 2
     part = own // 2
     swap = info[4] == 1
@@ -566,7 +577,7 @@
 
         return carry
 
-    lax.fori_loop(0, gkeep.shape[0] * 2, step, 0)
+    lax.fori_loop(0, gkeep.shape[0] * 2, step, 0, unroll=True)
 
 
 def input_body(info, gkeep, grecv, x, own_mid, gains, keep, send):
@@ -588,16 +599,16 @@
             send[...] = total.astype(BF16)
 
 
-def gate(live, *names):
-    for name, value in zip(names, lax.optimization_barrier([live[name] for name in names])):
-        live[name] = value
-
-
 def plus(*values):
     total = values[0].astype(F32)
     for value in values[1:]:
         total = total + value.astype(F32)
     return total
+
+
+class Steps(dict):
+    __getattr__ = dict.__getitem__
+    __setattr__ = dict.__setitem__
 
 
 def on_device(
@@ -671,64 +682,65 @@
 
     local = model // 2
     width = local // 2
-    v = {}
-    v["a0"] = jnp.concatenate(
+    v = Steps()
+    v.cosine, v.sine = turn_tables(length)
+    v.a0 = jnp.concatenate(
         [pregather(query_weight), pregather(key_weight), pregather(value_weight),
          jnp.pad(jnp.concatenate([pregather(norm1_gain), pregather(norm2_gain)])[None],
                  ((0, 15), (0, 0)))])
-    attn_rows = v["a0"].shape[0]
+    attn_rows = v.a0.shape[0]
     down = pregather(down_weight)
-    part = down.shape[0] // 2
-    own = 2 * part
-    units = 2 * own
+    part_a = down.shape[0] * 192 // 352 // 16 * 16
+    part_b = down.shape[0] - part_a
+    whole = down.shape[0]
     ffn = jnp.concatenate([pregather(gate_weight).T, pregather(up_weight).T], axis=1)
-    v["b0"] = jnp.concatenate([ffn[part:own], ffn[own + part :]])[None]
-    v["g0"] = jnp.concatenate([ffn[:part], ffn[own : own + part], down[:part]])
-    v["r0"] = jnp.concatenate([down[part:], pregather(out_weight)])
-    out_rows = v["r0"].shape[0] - part
-    v["t_send"] = other_slot(tokens)
-    v["f_send"] = other_slot(first_values)
-    v["c_send"] = other_slot(output_cotangent)
-    v["tokens"], v["firsts"], v["cots"] = tokens, first_values, output_cotangent
-
-    gate(v, "a0", "t_send", "b0")
-    v["ty"], v["af"], v["an"] = over_y(v["t_send"]), far(v["a0"]), near(v["a0"])
-    v["bx"], v["bf0"] = over_x(v["b0"]), far(v["b0"])
-    gate(v, "a0", "af", "an", "ty", "tokens", "b0", "bx", "bf0", "f_send", "c_send", "firsts", "cots", "r0", "g0")
-    v["fy"], v["anf"], v["rf"] = over_y(v["f_send"]), near(v["af"]), far(v["r0"])
-    v["tc"] = over_core(own_slot(v["tokens"], v["ty"]))
-    v["bn0"] = near(v["b0"])
-    gate(v, "a0", "af", "an", "anf", "fy", "tc", "firsts", "b0", "bx", "bf0", "bn0", "r0", "rf", "g0", "c_send", "cots")
-    v["z"] = pack(v["a0"], v["af"], v["an"], v["anf"])
-    v["zx"], v["zy"] = over_x(v["z"]), over_y(v["z"])
-    v["rlow"] = jnp.stack([v["r0"], v["rf"]])
-    v["rhigh"], v["gf"] = near(v["rlow"]), far(v["g0"])
-    v["fc"] = over_core(own_slot(v["firsts"], v["fy"]))
-    half = HEAD // 2
-    frequency = 10000.0 ** (-(jnp.arange(half).astype(F32) * 2.0) / HEAD)
-    angles = jnp.arange(length).astype(F32)[:, None] * frequency[None, :]
-    v["cosine"] = jnp.tile(jnp.cos(angles), (1, 4))
-    v["sine"] = jnp.tile(jnp.concatenate([-jnp.sin(angles), jnp.sin(angles)], axis=1), (1, 2))
-    gate(v, "z", "zx", "zy", "rlow", "rhigh", "g0", "gf", "fc", "b0", "bx", "bf0", "bn0", "cosine", "sine", "c_send", "cots")
-    v["zu"], v["zv"] = over_y(v["zx"][:SPLIT]), over_x(v["zy"][SPLIT:])
-    v["rmine"] = mine_of(v["rlow"], v["rhigh"])
-    v["rother"] = over_core(theirs_of(v["rlow"], v["rhigh"]))
-    v["b10"] = over_y(jnp.concatenate([v["b0"], v["bx"]]))
-    v["glow"] = jnp.stack([v["g0"], v["gf"]])
-    v["ghigh"] = near(v["glow"])
-    gate(v, "z", "zx", "zy", "zu", "zv", "rmine", "rother", "b0", "bx", "b10", "bf0", "bn0", "glow", "ghigh", "c_send", "cots")
-    v["r"] = pack(v["rmine"], v["rother"])
-    v["rx"], v["ry"] = over_x(v["r"]), over_y(v["r"])
-    v["b3"] = jnp.concatenate([v["bx"], v["b10"]])
-    v["bf3"], v["bn3"] = far(v["b3"]), near(v["b3"])
-    glow, ghigh = v["glow"][:, own:], v["ghigh"][:, own:]
-    v["gmine"], v["gother"] = mine_of(glow, ghigh), over_core(theirs_of(glow, ghigh))
-
-    def weights(name):
-        return [("a", v[name + end]) for end in ("", "x", "y", "u", "v")]
-
-    def values(*names):
-        return [("v", v[name]) for name in names]
+    v.b0 = jnp.concatenate([ffn[part_a:whole], ffn[whole + part_a :]])[None]
+    v.g0 = jnp.concatenate([ffn[:part_a], ffn[whole : whole + part_a], down[:part_a]])
+    v.r0 = jnp.concatenate([down[part_a:], pregather(out_weight)])
+    out_rows = v.r0.shape[0] - part_b
+    v.t_send = other_slot(tokens)
+    v.f_send = other_slot(first_values)
+    v.c_send = other_slot(output_cotangent)
+    v.tokens, v.firsts, v.cots = tokens, first_values, output_cotangent
+
+    v.a0, v.t_send, v.b0 = lax.optimization_barrier(
+        (v.a0, v.t_send, v.b0))
+    v.ty, v.af, v.an = over_y(v.t_send), far(v.a0), near(v.a0)
+    v.bx = over_x(v.b0)
+    v.a0, v.af, v.an, v.ty, v.tokens, v.b0, v.bx, v.f_send, v.c_send, v.firsts, v.cots, v.r0, v.g0 = lax.optimization_barrier(
+        (v.a0, v.af, v.an, v.ty, v.tokens, v.b0, v.bx, v.f_send, v.c_send, v.firsts, v.cots, v.r0, v.g0))
+    v.fy, v.anf, v.rf = over_y(v.f_send), near(v.af), far(v.r0)
+    v.bf0 = far(v.b0)
+    v.tc = over_core(own_slot(v.tokens, v.ty))
+    v.a0, v.af, v.an, v.anf, v.fy, v.tc, v.firsts, v.b0, v.bx, v.bf0, v.r0, v.rf, v.g0, v.c_send, v.cots = lax.optimization_barrier(
+        (v.a0, v.af, v.an, v.anf, v.fy, v.tc, v.firsts, v.b0, v.bx, v.bf0, v.r0, v.rf, v.g0, v.c_send, v.cots))
+    v.z = pack(v.a0, v.af, v.an, v.anf)
+    v.zx, v.zy = over_x(v.z), over_y(v.z)
+    v.rlow = jnp.stack([v.r0, v.rf])
+    v.rhigh, v.gf = near(v.rlow), far(v.g0)
+    v.fc = over_core(own_slot(v.firsts, v.fy))
+    v.z, v.zx, v.zy, v.rlow, v.rhigh, v.g0, v.gf, v.fc, v.b0, v.bx, v.bf0, v.c_send, v.cots = lax.optimization_barrier(
+        (v.z, v.zx, v.zy, v.rlow, v.rhigh, v.g0, v.gf, v.fc, v.b0, v.bx, v.bf0, v.c_send, v.cots))
+    v.zu, v.zv = over_y(v.zx[:SPLIT]), over_x(v.zy[SPLIT:])
+    v.rmine = mine_of(v.rlow, v.rhigh)
+    v.rother = over_core(theirs_of(v.rlow, v.rhigh))
+    v.b10 = over_y(jnp.concatenate([v.b0, v.bx]))
+    v.glow = jnp.stack([v.g0, v.gf])
+    v.ghigh = near(v.glow)
+    v.z, v.zx, v.zy, v.zu, v.zv, v.rmine, v.rother, v.b0, v.bx, v.b10, v.bf0, v.glow, v.ghigh, v.c_send, v.cots = lax.optimization_barrier(
+        (v.z, v.zx, v.zy, v.zu, v.zv, v.rmine, v.rother, v.b0, v.bx, v.b10, v.bf0, v.glow, v.ghigh, v.c_send, v.cots))
+    v.r = pack(v.rmine, v.rother)
+    v.rx, v.ry = over_x(v.r), over_y(v.r)
+    v.b3 = jnp.concatenate([v.bx, v.b10])
+    v.bf3, v.bn3 = far(v.b3), near(v.b3)
+    glow, ghigh = v.glow[:, 2 * part_a :], v.ghigh[:, 2 * part_a :]
+    v.gmine, v.gother = mine_of(glow, ghigh), over_core(theirs_of(glow, ghigh))
+
+    def anywhere(*arrays):
+        return [("a", array) for array in arrays]
+
+    def values(*arrays):
+        return [("v", array) for array in arrays]
 
     square = ((length, model), BF16)
     tall = ((length, local), BF16)
@@ -736,61 +748,70 @@
     w_scratch = pltpu.VMEM((2, BLOCKS, attn_rows, width), BF16)
     sem16 = pltpu.SemaphoreType.DMA((16,))
     narrow = 2 * length * model * local
-    v["x"], v["h1"], v["q"], v["k"], v["b"], v["gains"] = call(
+    v.x, v.h1, v.q, v.k, v.b, v.gains = call(
         qkv_body, [square, square, tall, tall, tall, ((8, model), F32)],
-        [("s", info)] + values("tokens", "ty", "tc", "firsts", "fy", "fc", "cosine", "sine") + weights("z"),
+        [("s", info)] + values(v.tokens, v.ty, v.tc, v.firsts, v.fy, v.fc, v.cosine, v.sine) + anywhere(v.z, v.zx, v.zy, v.zu, v.zv),
         [w_scratch, sem16], 3 * narrow, 14 << 20, vmem=26,
     )
-    gate(v, "x", "h1", "q", "k", "b", "gains", "r", "rx", "ry", "b0", "b3", "bf0", "bn0", "bf3", "bn3", "glow", "ghigh", "gmine", "gother", "c_send", "cots")
-    v["ru"], v["rv"] = over_y(v["rx"][:SPLIT]), over_x(v["ry"][SPLIT:])
-    v["gl"] = jnp.concatenate([v["glow"][:, :own], v["gmine"]], axis=1)
-    v["gh"] = jnp.concatenate([v["ghigh"][:, :own], v["gother"]], axis=1)
-    v["glx"], v["ghy"] = over_x(v["gl"]), over_y(v["gh"])
-    v["bnf3"] = near(v["bf3"])
+    v.x, v.h1, v.q, v.k, v.b, v.gains, v.r, v.rx, v.ry, v.b0, v.b3, v.bf0, v.bf3, v.bn3, v.glow, v.ghigh, v.gmine, v.gother, v.c_send, v.cots = lax.optimization_barrier(
+        (v.x, v.h1, v.q, v.k, v.b, v.gains, v.r, v.rx, v.ry, v.b0, v.b3, v.bf0, v.bf3, v.bn3, v.glow, v.ghigh, v.gmine, v.gother, v.c_send, v.cots))
+    v.ru, v.rv = over_y(v.rx[:SPLIT]), over_x(v.ry[SPLIT:])
+    v.gl = jnp.concatenate([v.glow[:, : 2 * part_a], v.gmine], axis=1)
+    v.gh = jnp.concatenate([v.ghigh[:, : 2 * part_a], v.gother], axis=1)
+    v.glx, v.ghy = over_x(v.gl), over_y(v.gh)
+    v.bnf3 = near(v.bf3)
     head_specs = [pl.BlockSpec((length, 128), lambda i: (0, i))] * 3
     lse_spec = pl.BlockSpec((1, 2, length), lambda i: (i, 0, 0))
     pairs = local // 128
-    v["att"], v["lse"] = call(
-        attend_body, [tall, ((pairs, 2, length), F32)], values("q", "k", "b"), [],
+    v.att, v.lse = call(
+        attend_body, [tall, ((pairs, 2, length), F32)], values(v.q, v.k, v.b), [],
         4 * length * length * local, 4 << 20, length * length * pairs * 2, vmem=20,
         grid=(pairs,), in_specs=head_specs, out_specs=[head_specs[0], lse_spec],
     )
-    v["cy"], v["bnf0"] = over_y(v["c_send"]), near(v["bf0"])
-    (v["part"],) = call(
-        out_body, [square], [("s", info)] + values("att") + weights("r"),
+    v.att, v.lse, v.r, v.rx, v.ry, v.ru, v.rv, v.gl, v.glx, v.gh, v.ghy, v.bnf3, v.c_send, v.bf0, v.b0 = lax.optimization_barrier(
+        (v.att, v.lse, v.r, v.rx, v.ry, v.ru, v.rv, v.gl, v.glx, v.gh, v.ghy, v.bnf3, v.c_send, v.bf0, v.b0))
+    v.cy = over_y(v.c_send)
+    v.bnf0, v.bn0 = near(v.bf0), near(v.b0)
+    (v.part,) = call(
+        out_body, [square], [("s", info)] + values(v.att) + anywhere(v.r, v.rx, v.ry, v.ru, v.rv),
         [pltpu.VMEM((local, model), BF16), sem16], narrow, 5 << 20, vmem=12,
     )
-    gate(v, "att", "lse", "r", "rx", "ry", "ru", "rv", "part", "cy", "cots", "gl", "glx", "gh", "ghy", "b0", "b3", "bf0", "bn0", "bf3", "bn3", "bnf0", "bnf3")
-    v["precv"], v["cc"] = over_core(v["part"]), over_core(own_slot(v["cots"], v["cy"]))
-    gate(v, "part", "precv", "cc", "gl", "glx", "gh", "ghy")
+    v.att, v.lse, v.r, v.rx, v.ry, v.ru, v.rv, v.part, v.cy, v.cots, v.gl, v.glx, v.gh, v.ghy, v.b0, v.b3, v.bf0, v.bn0, v.bf3, v.bn3, v.bnf0, v.bnf3 = lax.optimization_barrier(
+        (v.att, v.lse, v.r, v.rx, v.ry, v.ru, v.rv, v.part, v.cy, v.cots, v.gl, v.glx, v.gh, v.ghy, v.b0, v.b3, v.bf0, v.bn0, v.bf3, v.bn3, v.bnf0, v.bnf3))
+    v.precv, v.cc = over_core(v.part), over_core(own_slot(v.cots, v.cy))
+    v.part, v.precv, v.cc, v.gl, v.glx, v.gh, v.ghy = lax.optimization_barrier(
+        (v.part, v.precv, v.cc, v.gl, v.glx, v.gh, v.ghy))
 
     def five(rows):
         return [((count, rows, 256), BF16)
                 for count in (2 * (4 - SPLIT), 2 * SPLIT, SPLIT, 4 - SPLIT, 4)]
 
-    v["gly"], v["glxy"] = over_y(v["gl"]), over_y(v["glx"])
-    v["ghx"], v["ghxy"] = over_x(v["gh"]), over_x(v["ghy"])
-    scratch = [pltpu.VMEM((units, length), BF16), pltpu.VMEM((2 * units, length), BF16),
-               pltpu.VMEM((2 * units, model), BF16), pltpu.VMEM((units, model), BF16),
-               pltpu.SemaphoreType.DMA((48,))]
-    ffn_flops = 18 * length * model * units
-    v["h2"], v["gy"], v["gh2b"], v["resb"], v["bsx"], v["bsy"], v["bkx"], v["bky"], v["bown"] = call(
-        functools.partial(ffn_body, True), [square] * 4 + five(own + part),
-        [("s", info)] + values("x", "part", "precv", "gains", "cots", "cy", "cc")
-        + [("a", v[name]) for name in ("b0", "bf0", "bn0", "bnf0")]
-        + [("a", v[name]) for name in ("b3", "bf3", "bn3", "bnf3")] + weights("r"),
-        scratch, ffn_flops, 24 << 20, vmem=40,
+    v.gly, v.glxy = over_y(v.gl), over_y(v.glx)
+    v.ghx, v.ghxy = over_x(v.gh), over_x(v.ghy)
+    def ffn_scratch(units):
+        return [pltpu.VMEM((units, length), BF16), pltpu.VMEM((2 * units, length), BF16),
+                pltpu.VMEM((2 * units, model), BF16), pltpu.VMEM((units, model), BF16),
+                pltpu.SemaphoreType.DMA((48,))]
+
+    ffn_flops = 36 * length * model
+    v.h2, v.gy, v.gh2b, v.resb, v.bsx, v.bsy, v.bkx, v.bky, v.bown = call(
+        functools.partial(ffn_body, True), [square] * 4 + five(3 * part_b),
+        [("s", info)] + values(v.x, v.part, v.precv, v.gains, v.cots, v.cy, v.cc)
+        + anywhere(v.b0, v.bf0, v.bn0, v.bnf0, v.b3, v.bf3, v.bn3, v.bnf3) + anywhere(v.r, v.rx, v.ry, v.ru, v.rv),
+        ffn_scratch(4 * part_b), ffn_flops * 2 * part_b, 24 << 20, vmem=40,
     )
-    gate(v, "h2", "gy", "gh2b", "resb", "bsx", "bsy", "bkx", "bky", "bown", "gl", "glx", "gly", "glxy", "gh", "ghx", "ghy", "ghxy")
-    v["brx"], v["bry"] = over_x(v["bsx"]), over_y(v["bsy"])
-    quads = [((4, own, 256), BF16)] * 4 + [((2, 2, 4, part, 256), BF16)]
-    (v["gh2"], v["rkeep"], v["rsend"], v["n0"], v["n1"], v["n2"], v["n3"], v["dgrad"]) = call(
+    v.h2, v.gy, v.gh2b, v.resb, v.bsx, v.bsy, v.bkx, v.bky, v.bown, v.gl, v.glx, v.gly, v.glxy, v.gh, v.ghx, v.ghy, v.ghxy = lax.optimization_barrier(
+        (v.h2, v.gy, v.gh2b, v.resb, v.bsx, v.bsy, v.bkx, v.bky, v.bown, v.gl, v.glx, v.gly, v.glxy, v.gh, v.ghx, v.ghy, v.ghxy))
+    v.brx, v.bry = over_x(v.bsx), over_y(v.bsy)
+    quads = [((4, 2 * part_a, 256), BF16)] * 4 + [((2, 2, 4, part_a, 256), BF16)]
+    (v.gh2, v.rkeep, v.rsend, v.n0, v.n1, v.n2, v.n3, v.dgrad) = call(
         functools.partial(ffn_body, False), [square, (tile, F32), (tile, BF16)] + quads,
-        [("s", info)] + values("h2", "gy", "gh2b", "resb")
-        + [("a", v[half + over]) for half in ("gl", "gh") for over in ("", "x", "y", "xy")],
-        scratch, ffn_flops, 24 << 20, vmem=40,
+        [("s", info)] + values(v.h2, v.gy, v.gh2b, v.resb)
+        + anywhere(v.gl, v.glx, v.gly, v.glxy, v.gh, v.ghx, v.ghy, v.ghxy),
+        ffn_scratch(4 * part_a), ffn_flops * 2 * part_a, 24 << 20, vmem=40,
     )
-    gate(v, "gh2", "rkeep", "rsend", "n0", "n1", "n2", "n3", "dgrad", "brx", "bry", "bkx", "bky", "bown", "part", "precv")
+    v.gh2, v.rkeep, v.rsend, v.n0, v.n1, v.n2, v.n3, v.dgrad, v.brx, v.bry, v.bkx, v.bky, v.bown, v.part, v.precv = lax.optimization_barrier(
+        (v.gh2, v.rkeep, v.rsend, v.n0, v.n1, v.n2, v.n3, v.dgrad, v.brx, v.bry, v.bkx, v.bky, v.bown, v.part, v.precv))
 
     def fold(name):
         v[name + "fx"] = plus(v[name + "kx"], v[name + "ry"][:SPLIT]).astype(BF16)
@@ -825,33 +846,39 @@
         cut_up = full.reshape(2, 2, piece, full.shape[-1])
         return pick(c, cut_up[:, 1], cut_up[:, 0])
 
-    v["gh2r"] = over_core(v["gh2"])
-    v["rrecv"] = over_core(v["rsend"])
+    v.gh2r = over_core(v.gh2)
+    v.rrecv = over_core(v.rsend)
     fold("b")
-    v["brx2"], v["bry2"] = over_x(v["bfx"]), over_y(v["bfy"])
-    v["nn3"] = near(v["n3"])
-    (v["datt"], v["mid"], v["gain2"],
-     v["ssx"], v["ssy"], v["skx"], v["sky"], v["sown"]) = call(
-        out_back_body, [tall, (tile, F32), ((8, model), F32)] + five(part + out_rows),
-        [("s", info)] + values("gh2", "gh2r", "x", "part", "precv", "gy", "gains", "att", "dgrad") + weights("r"),
+    v.brx2, v.bry2 = over_x(v.bfx), over_y(v.bfy)
+    v.nn3 = near(v.n3)
+    (v.datt, v.mid, v.gain2,
+     v.ssx, v.ssy, v.skx, v.sky, v.sown) = call(
+        out_back_body, [tall, (tile, F32), ((8, model), F32)] + five(part_a + out_rows),
+        [("s", info)] + values(v.gh2, v.gh2r, v.x, v.part, v.precv, v.gy, v.gains, v.att, v.dgrad) + anywhere(v.r, v.rx, v.ry, v.ru, v.rv),
         [pltpu.VMEM((local, model), BF16), pltpu.VMEM((length, model), BF16), sem16],
-        2 * narrow, 20 << 20, vmem=34,
+        2 * narrow, 20 << 20, vmem=56,
     )
-    gate(v, "datt", "mid", "gain2", "ssx", "ssy", "skx", "sky", "sown", "bown", "brx", "bry", "brx2", "bry2", "n0", "n1", "n2", "nn3", "rkeep", "rrecv", "part", "precv")
-    v["srx"], v["sry"] = over_x(v["ssx"]), over_y(v["ssy"])
-    v["n1"] = plus(v["n1"], v["nn3"]).astype(BF16)
-    v["nf1"], v["nn2"] = far(v["n1"][2:]), near(v["n2"])
-    rows_out("b", total_of("b"), own)
-
+    v.datt, v.mid, v.gain2, v.ssx, v.ssy, v.skx, v.sky, v.sown, v.bown, v.brx, v.bry, v.brx2, v.bry2, v.n0, v.n1, v.n2, v.nn3, v.rkeep, v.rrecv, v.part, v.precv = lax.optimization_barrier(
+        (v.datt, v.mid, v.gain2, v.ssx, v.ssy, v.skx, v.sky, v.sown, v.bown, v.brx, v.bry, v.brx2, v.bry2, v.n0, v.n1, v.n2, v.nn3, v.rkeep, v.rrecv, v.part, v.precv))
+    v.srx, v.sry = over_x(v.ssx), over_y(v.ssy)
+    v.n1 = plus(v.n1, v.nn3).astype(BF16)
+    v.nf1, v.nn2 = far(v.n1[2:]), near(v.n2)
+    rows_out("b", total_of("b"), 2 * part_b)
+
+    live_now = jnp.where(y < seq_counts[0], 1.0, 0.0)
+    middle_own = own_tokens(v.x).astype(F32) + plus(
+        own_tokens(v.part), own_tokens(v.precv))
+    result = (live_now * (middle_own + plus(v.rkeep, v.rrecv))).astype(BF16)
+    v.okeep, v.osend = owner_keep(result), owner_send(result)
     def attend_back(side):
         first = side * (pairs // 2)
         column = pl.BlockSpec((length, 128), lambda i: (0, i + first))
         table = pl.BlockSpec((length, 128), lambda i: (0, 0))
         sums = pl.BlockSpec((1, 2, length), lambda i: (i + first, 0, 0))
         target = pl.BlockSpec((length, 128), lambda i: (0, i))
-        v[f"dq{side}"], v[f"dk{side}"], v[f"dv{side}"] = call(
+        return call(
             attend_back_body, [((length, width), BF16)] * 3,
-            values("q", "k", "b", "datt", "lse", "cosine", "sine"),
+            values(v.q, v.k, v.b, v.datt, v.lse, v.cosine, v.sine),
             [pltpu.VMEM((length, 128), F32), pltpu.VMEM((length, 128), F32)],
             5 * length * length * local, 4 << 20, length * length * pairs, vmem=26,
             grid=(pairs // 2,), in_specs=[column] * 4 + [sums, table, table],
@@ -860,66 +887,65 @@
 
     def attn_grads(side):
         counts = (4 - SPLIT, 2 * SPLIT, 4 - SPLIT) if side else (4 - SPLIT, SPLIT, 4)
-        names = ("zy", "zu", "zv") if side else ("z", "zx")
+        arrays = (v.zy, v.zu, v.zv) if side else (v.z, v.zx)
         return call(
             functools.partial(qkv_grad_body, side),
             [((count, attn_rows, width), BF16) for count in counts],
-            [("s", info), ("v", v[f"dq{side}"]), ("v", v[f"dk{side}"]), ("v", v[f"dv{side}"])]
-            + values("h1", "gains", "gain2") + [("a", v[name]) for name in names],
+            [("s", info)] + values(*(v.grads1 if side else v.grads0), v.h1, v.gains, v.gain2)
+            + anywhere(*arrays),
             [pltpu.VMEM((BLOCKS, attn_rows, width), BF16), pltpu.VMEM((8, model), F32),
              pltpu.SemaphoreType.DMA((8,))], 3 * narrow // 2, 7 << 20, vmem=24,
         )
 
-    attend_back(1)
-    v["qdx"], v["qsy"], v["qky"] = attn_grads(1)
-    gate(v, "dq1", "dk1", "dv1", "qdx", "qsy", "qky", "q", "k", "b", "datt", "srx", "sry", "skx", "sky", "sown", "n0", "n1", "nf1", "nn2", "bt", "bm", "rkeep", "rrecv", "part", "precv")
-    v["qry"], v["qrd"] = over_y(v["qsy"]), over_x(v["qdx"])
+    v.grads1 = attend_back(1)
+    v.qdx, v.qsy, v.qky = attn_grads(1)
+    v.grads1, v.qdx, v.qsy, v.qky, v.q, v.k, v.b, v.datt, v.srx, v.sry, v.skx, v.sky, v.sown, v.n0, v.n1, v.nf1, v.nn2, v.bt, v.bm, v.okeep, v.osend = lax.optimization_barrier(
+        (v.grads1, v.qdx, v.qsy, v.qky, v.q, v.k, v.b, v.datt, v.srx, v.sry, v.skx, v.sky, v.sown, v.n0, v.n1, v.nf1, v.nn2, v.bt, v.bm, v.okeep, v.osend))
+    v.qry, v.qrd = over_y(v.qsy), over_x(v.qdx)
     fold("s")
-    v["srx2"] = over_x(v["sfx"])
-    v["nf0"] = far(v["n1"][:2])
-    v["bzn"] = near(jnp.stack([quarter("b", own, 2), quarter("b", own, 3)]).astype(BF16))
-    attend_back(0)
-    v["qsx"], v["qkx"], v["qown"] = attn_grads(0)
-    live_now = jnp.where(y < seq_counts[0], 1.0, 0.0)
-    middle_own = own_tokens(v["x"]).astype(F32) + plus(
-        own_tokens(v["part"]), own_tokens(v["precv"]))
-    result = (live_now * (middle_own + plus(v["rkeep"], v["rrecv"]))).astype(BF16)
-    v["okeep"], v["osend"] = owner_keep(result), owner_send(result)
-    gate(v, "dq0", "dk0", "dv0", "dq1", "dk1", "dv1", "qsx", "qkx", "qown", "qry", "qrd", "qky", "srx", "sry", "srx2", "sfy", "sown", "n0", "nf0", "nf1", "nn2", "bzn", "bt", "bm", "okeep", "osend")
-    v["qrx"] = over_x(v["qsx"])
-    v["sry2"] = over_y(v["sfy"])
-    v["nt0"] = plus(v["n0"][:2], v["nf0"], v["nn2"][:2])
-    v["nx"] = over_x(plus(v["n0"][2:], v["nf1"], v["nn2"][2:]).astype(BF16))
-    v["bt0"] = plus(quarter("b", own, 0), v["bzn"][0])
-    v["bzf"] = far(plus(quarter("b", own, 1), v["bzn"][1]).astype(BF16))
-    v["orecv"] = over_y(v["osend"])
-    v["gkeep"], v["gsend"] = call(
+    v.srx2 = over_x(v.sfx)
+    v.nf0 = far(v.n1[:2])
+    v.bzn = near(jnp.stack([quarter("b", 2 * part_b, 2), quarter("b", 2 * part_b, 3)]).astype(BF16))
+    v.grads0 = attend_back(0)
+    v.qsx, v.qkx, v.qown = attn_grads(0)
+    v.grads0, v.grads1, v.qsx, v.qkx, v.qown, v.qry, v.qrd, v.qky, v.srx, v.sry, v.srx2, v.sfy, v.sown, v.n0, v.nf0, v.nf1, v.nn2, v.bzn, v.bt, v.bm, v.okeep, v.osend = lax.optimization_barrier(
+        (v.grads0, v.grads1, v.qsx, v.qkx, v.qown, v.qry, v.qrd, v.qky, v.srx, v.sry, v.srx2, v.sfy, v.sown, v.n0, v.nf0, v.nf1, v.nn2, v.bzn, v.bt, v.bm, v.okeep, v.osend))
+    v.qrx = over_x(v.qsx)
+    v.sry2 = over_y(v.sfy)
+    v.nt0 = plus(v.n0[:2], v.nf0, v.nn2[:2])
+    v.nx = over_x(plus(v.n0[2:], v.nf1, v.nn2[2:]).astype(BF16))
+    v.bt0 = plus(quarter("b", 2 * part_b, 0), v.bzn[0])
+    v.bzf = far(plus(quarter("b", 2 * part_b, 1), v.bzn[1]).astype(BF16))
+    v.orecv = over_y(v.osend)
+    v.gkeep, v.gsend = call(
         qkv_back_body, [(tile, F32), (tile, BF16)],
-        [("s", info)] + values("dq0", "dk0", "dv0", "dq1", "dk1", "dv1") + weights("z"), [w_scratch, sem16],
+        [("s", info)] + values(*v.grads0, *v.grads1) + anywhere(v.z, v.zx, v.zy, v.zu, v.zv), [w_scratch, sem16],
         3 * narrow, 14 << 20, vmem=18,
     )
-    gate(v, "gkeep", "gsend", "qry", "qrd", "qky", "qrx", "qkx", "qown", "bt0", "bzf", "nt0", "nx", "srx", "sry", "srx2", "sry2", "sown", "dv0", "dv1", "okeep", "orecv")
-    output = both_slots(v["okeep"], v["orecv"])
-    total_b = plus(v["bt0"], v["bzf"])
-    v["grecv"] = over_core(v["gsend"])
-    v["qfx"] = plus(v["qkx"], v["qry"][:SPLIT]).astype(BF16)
-    v["qfy"] = plus(v["qky"], v["qrd"]).astype(BF16)
-    v["qrx2"], v["qry2"] = over_x(v["qfx"]), over_y(v["qfy"])
+    v.gkeep, v.gsend, v.qry, v.qrd, v.qky, v.qrx, v.qkx, v.qown, v.bt0, v.bzf, v.nt0, v.nx, v.srx, v.sry, v.srx2, v.sry2, v.sown, v.grads0, v.grads1, v.okeep, v.orecv = lax.optimization_barrier(
+        (v.gkeep, v.gsend, v.qry, v.qrd, v.qky, v.qrx, v.qkx, v.qown, v.bt0, v.bzf, v.nt0, v.nx, v.srx, v.sry, v.srx2, v.sry2, v.sown, v.grads0, v.grads1, v.okeep, v.orecv))
+    output = both_slots(v.okeep, v.orecv)
+    total_b = plus(v.bt0, v.bzf)
+    v.grecv = over_core(v.gsend)
+    v.qfx = plus(v.qkx, v.qry[:SPLIT]).astype(BF16)
+    v.qfy = plus(v.qky, v.qrd).astype(BF16)
+    v.qrx2, v.qry2 = over_x(v.qfx), over_y(v.qfy)
     rows_out("s", total_of("s"), 0)
-    v["nt0"] = plus(v["nt0"], v["nx"])
-    v["ny"] = over_y(v["nt0"][1].astype(BF16))
-    v["ikeep"], v["isend"] = call(
+    v.nt0 = plus(v.nt0, v.nx)
+    v.ny = over_y(v.nt0[1].astype(BF16))
+    v.ikeep, v.isend = call(
         input_body, [((piece, model), F32), ((piece, model), BF16)],
-        [("s", info)] + values("gkeep", "grecv", "x", "mid", "gains"), [], 1000, 8 << 20, vmem=16,
+        [("s", info)] + values(v.gkeep, v.grecv, v.x, v.mid, v.gains), [], 1000, 8 << 20, vmem=16,
     )
-    gate(v, "ikeep", "isend", "qrx", "qry", "qrx2", "qry2", "qown", "st", "sm", "nt0", "ny", "dv0", "dv1")
-    total_a = plus(v["nt0"][0], v["ny"])
-    low = plus(v["qown"][:SPLIT], v["qry"][SPLIT:], v["qrx2"])
-    high = plus(v["qown"][SPLIT:], v["qrx"], v["qry2"])
-    v["qt"] = jnp.concatenate([low, high])
-    v["qz"], v["sz"] = near(v["qt"][3].astype(BF16)), near(quarter("s", 0, 3).astype(BF16))
-    v["irecv"] = over_y(v["isend"])
-    cuts = [v[f"dv{side}"].reshape(2, 2, piece, width) for side in range(2)]
+    v.ikeep, v.isend, v.qrx, v.qry, v.qrx2, v.qry2, v.qown, v.st, v.sm, v.nt0, v.ny, v.grads0, v.grads1 = lax.optimization_barrier(
+        (v.ikeep, v.isend, v.qrx, v.qry, v.qrx2, v.qry2, v.qown, v.st, v.sm, v.nt0, v.ny, v.grads0, v.grads1))
+    total_a = plus(v.nt0[0], v.ny)
+    low = plus(v.qown[:SPLIT], v.qry[SPLIT:], v.qrx2)
+    high = plus(v.qown[SPLIT:], v.qrx, v.qry2)
+    v.qt = jnp.concatenate([low, high])
+    v.qz, v.sz = near(v.qt[3].astype(BF16)), near(quarter("s", 0, 3).astype(BF16))
+    v.irecv = over_y(v.isend)
+    cuts = [grads[2].reshape(2, 2, piece, width) for grads in (v.grads0, v.grads1)]
     dv_keep = [pick(c, cut[:, 1], cut[:, 0]) for cut in cuts]
     dv_recv = over_core(
         jnp.concatenate([pick(c, cut[:, 0], cut[:, 1]) for cut in cuts], axis=-1))
@@ -931,27 +957,29 @@
         theirs = pick(side, dv_recv[1], dv_recv[0])
         blocks.append(pick(c ^ column_c, theirs, mine))
     grad_rows = jnp.concatenate(blocks, axis=-1)
-    v["fkeep"], v["fsend"] = owner_keep(grad_rows), owner_send(grad_rows)
-    gate(v, "qt", "qz", "st", "sm", "sz", "irecv", "ikeep", "fkeep", "fsend")
-    v["qzf"] = far(plus(v["qt"][1], v["qz"]).astype(BF16))
-    v["szf"] = far(plus(quarter("s", 0, 1), v["sz"]).astype(BF16))
-    v["qzn"] = near(v["qt"][2].astype(BF16))
-    v["szn"] = near(quarter("s", 0, 2).astype(BF16))
-    v["frecv"] = over_y(v["fsend"])
-    v["qt0"], v["st0"] = v["qt"][0], quarter("s", 0, 0)
-    grad_input = both_slots(v["ikeep"], v["irecv"].astype(F32))
-    gate(v, "qt0", "st0", "qzf", "szf", "qzn", "szn", "fkeep", "frecv")
-    total = plus(v["qt0"], v["qzf"], v["qzn"])
+    v.fkeep, v.fsend = owner_keep(grad_rows), owner_send(grad_rows)
+    v.qt, v.qz, v.st, v.sm, v.sz, v.irecv, v.ikeep, v.fkeep, v.fsend = lax.optimization_barrier(
+        (v.qt, v.qz, v.st, v.sm, v.sz, v.irecv, v.ikeep, v.fkeep, v.fsend))
+    v.qzf = far(plus(v.qt[1], v.qz).astype(BF16))
+    v.szf = far(plus(quarter("s", 0, 1), v.sz).astype(BF16))
+    v.qzn = near(v.qt[2].astype(BF16))
+    v.szn = near(quarter("s", 0, 2).astype(BF16))
+    v.frecv = over_y(v.fsend)
+    v.qt0, v.st0 = v.qt[0], quarter("s", 0, 0)
+    grad_input = both_slots(v.ikeep, v.irecv.astype(F32))
+    v.qt0, v.st0, v.qzf, v.szf, v.qzn, v.szn, v.fkeep, v.frecv = lax.optimization_barrier(
+        (v.qt0, v.st0, v.qzf, v.szf, v.qzn, v.szn, v.fkeep, v.frecv))
+    total = plus(v.qt0, v.qzf, v.qzn)
     gain_total = total[384]
     gain_share = jnp.broadcast_to(gain_total[None, :128], (8, 128))
     gain_sum = gain_total[:128] + over_core(gain_share)[0] + (
         over_y(gain_share)[0] + flip(gain_share, "seq", MESH_Y | MESH_C)[0])
-    total_s = plus(v["st0"], v["szf"], v["szn"])
-    grad_first = both_slots(v["fkeep"], v["frecv"]).astype(F32)
+    total_s = plus(v.st0, v.szf, v.szn)
+    grad_first = both_slots(v.fkeep, v.frecv).astype(F32)
 
     def weave(lanes):
-        pieces = [total_a[:part, lanes], total_b[:part, lanes],
-                  total_a[part:own, lanes], total_b[part:own, lanes]]
+        pieces = [total_a[:part_a, lanes], total_b[:part_b, lanes],
+                  total_a[part_a:, lanes], total_b[part_b : 2 * part_b, lanes]]
         return jnp.concatenate(pieces).T
 
     return (
@@ -962,11 +990,11 @@
         postscatter(total[:128]),
         postscatter(total[128:256]),
         postscatter(total[256:384]),
-        postscatter(total_s[part:]),
+        postscatter(total_s[part_a:]),
         postscatter(gain_total[128:]),
         postscatter(weave(slice(0, 128))),
         postscatter(weave(slice(128, 256))),
-        postscatter(jnp.concatenate([total_s[:part], total_b[own:]])),
+        postscatter(jnp.concatenate([total_s[:part_a], total_b[2 * part_b :]])),
     )
 
 

time: 383 us -> 375 us (0.979)
  local copies, waits for them, and re-layouts: 36.4 us -> 24.2 us
  starting transfers between devices: 75.8 us -> 79.7 us
    unnamed x177 -> x145, local copies, waits for them, and re-layouts: 20.1 us -> 14.9 us
    optimization_barrier x2 -> x0, local copies, waits for them, and re-layouts: 4.11 us -> none  [gate(): lax.optimization_barrier([live[name] for name in names])]
    ppermute x77, starting transfers between devices: 75.8 us -> 79.7 us  [flip(): return lax.ppermute(value, axis, pairs)]
    convert_element_type x11 -> x10, other arithmetic: 6.71 us -> 8.01 us  [the longest x1 4.39 us: on_device(): result = (live_now * (middle_own + plus(v.rkeep, v.rrecv))).astype(BF16)]
  transfers between devices with their start and end apart: 77 -> 77, of which waited for: 22 -> 30; matrix products, arithmetic and copies ran while one was open for 9% -> 7% of each run, Pallas kernels for 35% -> 35%
where the time goes in v3:
time: 375 us; the launch traced here: 371 us
  Pallas kernels  129 us (34%)
  waiting for transfers between devices  101 us (27%)
  starting transfers between devices  79.7 us (21%)
  other arithmetic  34.6 us (9%)
  local copies, waits for them, and re-layouts  24.2 us (6%)
    pallas_call x14, Pallas kernels, call(): pl.pallas_call(body, out_shape=[jax.ShapeDtypeStruct(shape, kind) for sha...  129 us
    ppermute x77, waiting for transfers between devices, flip(): return lax.ppermute(value, axis, pairs)  101 us
    ppermute x77, starting transfers between devices, flip(): return lax.ppermute(value, axis, pairs)  79.7 us
    unnamed x145, local copies, waits for them, and re-layouts  14.9 us
    select_n x20, other arithmetic, pick(): return jnp.where(flag == 1, when_one, when_zero)  9.05 us
  transfers between devices with their start and end apart: 77, of which 30 were waited for; matrix products, arithmetic and copies ran while one was open for 7% of the time, Pallas kernels for 35%

profile of v3, /device:TPU:0, one launch (start us, length us, event | category | flops | bytes accessed | tf_op | source)
XLA Modules:
  0.0 371.5 jit_solution(10370922341752940408)
XLA Ops:
  4.0 3.0 collective-permute-start.2
  7.0 3.6 collective-permute-start
  10.6 1.5 collective-permute-start.3
  13.8 2.2 collective-permute-done.3
  16.8 3.1 collective-permute-done.1.refs_2_
  21.0 1.6 collective-permute-start.4
  22.6 2.5 collective-permute-start.7
  26.4 10.5 %collective-permute-done.8 = bf16[288,256]{1,0:T(8,128)(2,1)S(1)} collective-permute-done((bf16[288,256]{1,0:T(8,128)(2,1)S(1)}, bf16[288,256]{1,0:T(8,128)(2,1)S(1)}, u32[]{:S(2)}, u32[]{:S(2)}) %collective-permute-start.8) | collective-permute-done | bytes 147488 | tf_op jit(solution)/shard_map/ppermute | solution.py:36
  39.8 1.5 collective-permute-start.9
  41.4 2.9 collective-permute-start.11
  44.3 2.6 collective-permute-start.12
  46.9 4.8 %collective-permute-done.11 = bf16[2,288,256]{2,1,0:T(8,128)(2,1)} collective-permute-done((bf16[2,288,256]{2,1,0:T(8,128)(2,1)S(1)}, bf16[2,288,256]{2,1,0:T(8,128)(2,1)}, u32[]{:S(2)}, u32[]{:S(2)}) %collective-permute-start.11) | collective-permute-done | bytes 294944 | tf_op jit(solution)/shard_map/ppermute | solution.py:36
  51.7 8.5 %collective-permute-done.12 = bf16[576,256]{1,0:T(8,128)(2,1)} collective-permute-done((bf16[576,256]{1,0:T(8,128)(2,1)}, bf16[576,256]{1,0:T(8,128)(2,1)}, u32[]{:S(2)}, u32[]{:S(2)}) %collective-permute-start.12) | collective-permute-done | bytes 294944 | tf_op jit(solution)/shard_map/ppermute | solution.py:36
  60.3 1.9 pad_maximum_fusion.7
  62.2 2.9 collective-permute-start.18
  65.1 1.7 pad_maximum_fusion.13
  66.8 1.5 collective-permute-start.17
  68.3 1.8 slice.396
  70.6 1.8 slice.397
  72.4 1.5 collective-permute-start.15
  77.7 7.0 %collective-permute-done.14.refs_12_.refs_8_.refs_10_ = bf16[2,400,256]{2,1,0:T(8,128)(2,1)} collective-permute-done((bf16[2,400,256]{2,1,0:T(8,128)(2,1)}, bf16[2,400,256]{2,1,0:T(8,128)(2,1)}, u32[]{:S(2)}, u32[]{:S(2)}) %collective-permute-start.14) | collective-permute-done | bytes 409632 | tf_op jit(solution)/shard_map/ppermute | solution.py:36
  86.6 2.7 collective-permute-start.21
  89.4 1.6 collective-permute-start.19
  99.7 9.3 %shard_map.239 = (bf16[1024,1024]{1,0:T(8,128)(2,1)S(1)}, bf16[1024,1024]{1,0:T(8,128)(2,1)S(1)}, bf16[1024,512]{1,0:T(8,128)(2,1)S(1)}, bf16[1024,512]{1,0:T(8,...) custom-call(s32[6]{0:T(128)S(1)} %stack.139.refs_0_.info, bf16[2,256,1024]{2,1,0:T(8,128)(2,1)S(1)} %copy-done.5, ...), custom_call_target="tpu_custom_call" | custom-call | flops 3221225472 | bytes 14680064 | tf_op jit(solution)/shard_map/pallas_call | solution.py:52
  114.4 1.6 collective-permute-start.26
  118.2 13.8 %shard_map.241 = (bf16[1024,512]{1,0:T(8,128)(2,1)S(1)}, f32[4,2,1024]{2,1,0:T(2,128)S(1)}) custom-call(bf16[1024,512]{1,0:T(8,128)(2,1)S(1)} %get-tuple-element.551.q, bf16[1024,512]{1,0:T(8,128)(2,1)S(1)} %get-tuple-element.552.k, bf16[1024,512]{1,0:T(8,128)(2,1)S(1)} %get-tuple-element.553.b), custom_call_target="tpu_custom_call" | custom-call | flops 2147483648 | bytes 4194304 | tf_op jit(solution)/shard_map/pallas_call | solution.py:52
  134.0 1.8 collective-permute-done.25.refs_6_.refs_20_.refs_14_
  138.6 2.1 shard_map.242.refs_2_.refs_4_
  140.8 2.3 collective-permute-done.30.refs_10_
  143.0 1.8 collective-permute-done.31.refs_11_
  144.8 3.8 %collective-permute-done.29.refs_6_ = bf16[256,1024]{1,0:T(8,128)(2,1)S(1)} collective-permute-done((bf16[256,1024]{1,0:T(8,128)(2,1)S(1)}, bf16[256,1024]{1,0:T(8,128)(2,1)S(1)}, u32[]{:S(2)}, u32[]{:S(2)}) %collective-permute-start.29) | collective-permute-done | bytes 524320 | tf_op jit(solution)/shard_map/ppermute | solution.py:36
  149.3 4.9 %collective-permute-done.33.refs_7_ = bf16[2,256,1024]{2,1,0:T(8,128)(2,1)S(1)} collective-permute-done((bf16[2,256,1024]{2,1,0:T(8,128)(2,1)S(1)}, bf16[2,256,1024]{2,1,0:T(8,128)(2,1)S(1)}, u32[]{:S(2)}, u32[]{:S(2)}) %collective-permute-start.33) | collective-permute-done | bytes 1048608 | tf_op jit(solution)/shard_map/ppermute | solution.py:36
  156.3 1.5 collective-permute-start.36
  158.3 23.8 %shard_map.243 = (bf16[1024,1024]{1,0:T(8,128)(2,1)S(1)}, bf16[1024,1024]{1,0:T(8,128)(2,1)}, bf16[1024,1024]{1,0:T(8,128)(2,1)}, bf16[1024,1024]{1,0:T(8,128)(2...) custom-call(s32[6]{0:T(128)S(1)} %stack.139.refs_0_.info, ...), custom_call_target="tpu_custom_call" | custom-call | flops 12079595520 | bytes 25165824 | tf_op jit(solution)/shard_map/pallas_call | solution.py:52
  183.7 1.5 collective-permute-start.38
  185.9 26.8 %shard_map.244 = (bf16[1024,1024]{1,0:T(8,128)(2,1)S(1)}, f32[2,256,1024]{2,1,0:T(8,128)}, bf16[2,256,1024]{2,1,0:T(8,128)(2,1)}, bf16[4,384,256]{2,1,0:T(8,128)...) custom-call(s32[6]{0:T(128)S(1)} %stack.139.refs_0_.info, ...), custom_call_target="tpu_custom_call" | custom-call | flops 14495514624 | bytes 25165824 | tf_op jit(solution)/shard_map/pallas_call | solution.py:52
  220.6 13.6 %shard_map.245 = (bf16[1024,512]{1,0:T(8,128)(2,1)}, f32[2,256,1024]{2,1,0:T(8,128)}, f32[8,1024]{1,0:T(8,128)}, bf16[4,320,256]{2,1,0:T(8,128)(2,1)}, bf16[4,32...) custom-call(s32[6]{0:T(128)} %copy-done.30, ...), custom_call_target="tpu_custom_call" | custom-call | flops 2147483648 | bytes 20971520 | tf_op jit(solution)/shard_map/pallas_call | solution.py:52
  235.2 4.4 %fusion.1 = bf16[2,256,1024]{2,1,0:T(8,128)(2,1)S(1)} fusion(f32[2,256,1024]{2,1,0:T(8,128)} %get-tuple-element.549, bf16[2,256,1024]{2,1,0:T(8,128)(2,1)} %collective-permute-done.44, bf16[2,2,256,1024]{3,2,1,0:T(8,128)(2,1)} %bitcast.21, bf16[2,2,256,1024]{3,2,1,0:T(8,128)(2,1)S(1)} %bitcast.187, bf16[2,2,256,1024]{3,2,1,0:T(8,128)(2,1)S(1)} %bitcast.188, ...), kind=kLoop, calls=%fused_computation.3 | loop fusion | flops 6815744 | bytes 10485765 | tf_op jit(solution)/shard_map/convert_element_type | solution.py:871
  241.2 1.7 convert_add_fusion.1
  243.4 1.6 collective-permute-start.45
  248.0 9.4 %shard_map.246 = (bf16[1024,256]{1,0:T(8,128)(2,1)S(1)}, bf16[1024,256]{1,0:T(8,128)(2,1)S(1)}, bf16[1024,256]{1,0:T(8,128)(2,1)S(1)}) custom-call(bf16[1024,512]{1,0:T(8,128)(2,1)S(1)} %copy-done.47, bf16[1024,512]{1,0:T(8,128)(2,1)S(1)} %copy-done.49, bf16[1024,512]{1,0:T(8,128)(2,1)S(1)} %copy-done.51, bf16[1024,512]{1,0:T(8,128)(2,1)S(1)} %copy-done.34, ...), custom_call_target="tpu_custom_call" | custom-call | flops 2684354560 | bytes 4194304 | tf_op jit(solution)/shard_map/pallas_call | solution.py:52
  257.5 5.2 %shard_map.247 = (bf16[2,400,256]{2,1,0:T(8,128)(2,1)S(1)}, bf16[4,400,256]{2,1,0:T(8,128)(2,1)S(1)}, bf16[2,400,256]{2,1,0:T(8,128)(2,1)S(1)}) custom-call(s32[6]{0:T(128)S(1)} %copy-done.31, bf16[1024,256]{1,0:T(8,128)(2,1)S(1)} %get-tuple-element.583.refs_1_.refs_4_, bf16[1024,256]{1,0:T(8,128)(2,1)S(1)} %get-tuple-element.584.refs_2_.refs_5_, ...), custom_call_target="tpu_custom_call" | custom-call | flops 1610612736 | bytes 7340032 | tf_op jit(solution)/shard_map/pallas_call | solution.py:52
  262.9 7.9 %collective-permute-done.47 = bf16[2,384,256]{2,1,0:T(8,128)(2,1)S(1)} collective-permute-done((bf16[2,384,256]{2,1,0:T(8,128)(2,1)S(1)}, bf16[2,384,256]{2,1,0:T(8,128)(2,1)S(1)}, u32[]{:S(2)}, u32[]{:S(2)}) %collective-permute-start.47) | collective-permute-done | bytes 393248 | tf_op jit(solution)/shard_map/ppermute | solution.py:36
  273.9 2.6 collective-permute-start.53
  277.6 9.4 %shard_map.248 = (bf16[1024,256]{1,0:T(8,128)(2,1)S(1)}, bf16[1024,256]{1,0:T(8,128)(2,1)S(1)}, bf16[1024,256]{1,0:T(8,128)(2,1)S(1)}) custom-call(bf16[1024,512]{1,0:T(8,128)(2,1)S(1)} %copy-done.47, bf16[1024,512]{1,0:T(8,128)(2,1)S(1)} %copy-done.49, bf16[1024,512]{1,0:T(8,128)(2,1)S(1)} %copy-done.51, bf16[1024,512]{1,0:T(8,128)(2,1)S(1)} %copy-done.34, ...), custom_call_target="tpu_custom_call" | custom-call | flops 2684354560 | bytes 4194304 | tf_op jit(solution)/shard_map/pallas_call | solution.py:52
  287.0 6.0 %shard_map.249 = (bf16[2,400,256]{2,1,0:T(8,128)(2,1)S(1)}, bf16[2,400,256]{2,1,0:T(8,128)(2,1)S(1)}, bf16[4,400,256]{2,1,0:T(8,128)(2,1)S(1)}) custom-call(s32[6]{0:T(128)S(1)} %copy-done.31, bf16[1024,256]{1,0:T(8,128)(2,1)S(1)} %get-tuple-element.580.refs_1_, bf16[1024,256]{1,0:T(8,128)(2,1)S(1)} %get-tuple-element.581.refs_2_, ...), custom_call_target="tpu_custom_call" | custom-call | flops 1610612736 | bytes 7340032 | tf_op jit(solution)/shard_map/pallas_call | solution.py:52
  293.7 1.7 collective-permute-start.57
  298.1 1.8 collective-permute-start.56
  299.9 8.0 %shard_map.250 = (f32[2,256,1024]{2,1,0:T(8,128)S(1)}, bf16[2,256,1024]{2,1,0:T(8,128)(2,1)S(1)}) custom-call(s32[6]{0:T(128)S(1)} %copy-done.31, bf16[1024,256]{1,0:T(8,128)(2,1)S(1)} %get-tuple-element.580.refs_1_, bf16[1024,256]{1,0:T(8,128)(2,1)S(1)} %get-tuple-element.581.refs_2_, bf16[1024,256]{1,0:T(8,128)(2,1)S(1)} %get-tuple-element.639.refs_3_, ...), custom_call_target="tpu_custom_call" | custom-call | flops 3221225472 | bytes 14680064 | tf_op jit(solution)/shard_map/pallas_call | solution.py:52
  307.9 7.3 %collective-permute-done.58 = bf16[2,320,256]{2,1,0:T(8,128)(2,1)S(1)} collective-permute-done((bf16[2,320,256]{2,1,0:T(8,128)(2,1)S(1)}, bf16[2,320,256]{2,1,0:T(8,128)(2,1)S(1)}, u32[]{:S(2)}, u32[]{:S(2)}) %collective-permute-start.58) | collective-permute-done | bytes 327712 | tf_op jit(solution)/shard_map/ppermute | solution.py:36
  316.8 1.6 collective-permute-start.62
  321.0 1.6 shard_map.251
  322.7 7.1 %collective-permute-done.62 = bf16[2,400,256]{2,1,0:T(8,128)(2,1)S(1)} collective-permute-done((bf16[2,400,256]{2,1,0:T(8,128)(2,1)S(1)}, bf16[2,400,256]{2,1,0:T(8,128)(2,1)S(1)}, u32[]{:S(2)}, u32[]{:S(2)}) %collective-permute-start.62) | collective-permute-done | bytes 409632 | tf_op jit(solution)/shard_map/ppermute | solution.py:36
  330.5 2.1 collective-permute-start.65
  335.2 1.9 collective-permute-done.66
  337.2 4.0 %collective-permute-done.65 = bf16[400,256]{1,0:T(8,128)(2,1)S(1)} collective-permute-done((bf16[400,256]{1,0:T(8,128)(2,1)S(1)}, bf16[400,256]{1,0:T(8,128)(2,1)S(1)}, u32[]{:S(2)}, u32[]{:S(2)}) %collective-permute-start.65) | collective-permute-done | bytes 204832 | tf_op jit(solution)/shard_map/ppermute | solution.py:36
  341.2 5.2 %collective-permute-done.67 = bf16[256,1024]{1,0:T(8,128)(2,1)S(1)} collective-permute-done((bf16[256,1024]{1,0:T(8,128)(2,1)S(1)}, bf16[256,1024]{1,0:T(8,128)(2,1)S(1)}, u32[]{:S(2)}, u32[]{:S(2)}) %collective-permute-start.67) | collective-permute-done | bytes 524320 | tf_op jit(solution)/shard_map/ppermute | solution.py:36
  347.0 1.7 collective-permute-start.70
  349.4 2.1 collective-permute-start.69
  351.6 1.5 maximum_select_fusion
  353.1 6.4 %collective-permute-done.72 = bf16[320,256]{1,0:T(8,128)(2,1)S(1)} collective-permute-done((bf16[320,256]{1,0:T(8,128)(2,1)S(1)}, bf16[320,256]{1,0:T(8,128)(2,1)S(1)}, u32[]{:S(2)}, u32[]{:S(2)}) %collective-permute-start.72) | collective-permute-done | bytes 163872 | tf_op jit(solution)/shard_map/ppermute | solution.py:36
  359.5 1.6 collective-permute-done.69
  361.1 3.1 collective-permute-done.71
  367.5 1.5 fusion.5
  (354 shorter events, 78.9 us)
Async XLA Ops:
  4.0 15.9 %collective-permute-start.2 = (bf16[256,1024]{1,0:T(8,128)(2,1)S(1)}, bf16[256,1024]{1,0:T(8,128)(2,1)S(1)}, u32[]{:S(2)}, u32[]{:S(2)}) collective-permute-start(bf16[256,1024]{1,0:T(8,128)(2,1)S(1)} %select_bitcast_fusion.6), channel_id=1, source_target_pairs={{0,16},{8,24},{16,0},{24,8},{1,17},{9,25},{17,1},{25,9},{2,18},{10... | collective-permute-start | bytes 1572872 | tf_op jit(solution)/shard_map/ppermute | solution.py:36
  7.0 9.8 %collective-permute-start = (bf16[400,256]{1,0:T(8,128)(2,1)S(1)}, bf16[400,256]{1,0:T(8,128)(2,1)S(1)}, u32[]{:S(2)}, u32[]{:S(2)}) collective-permute-start(bf16[400,256]{1,0:T(8,128)(2,1)S(1)} %fusion.26.refs_0_), channel_id=1, source_target_pairs={{0,6},{1,7},{2,4},{3,5},{4,2},{5,3},{6,0},{7,1},{8,14},{9,15},{10,... | collective-permute-start | bytes 614408 | tf_op jit(solution)/shard_map/ppermute | solution.py:36
  10.6 9.3 %collective-permute-start.1 = (bf16[400,256]{1,0:T(8,128)(2,1)S(1)}, bf16[400,256]{1,0:T(8,128)(2,1)S(1)}, u32[]{:S(2)}, u32[]{:S(2)}) collective-permute-start(bf16[400,256]{1,0:T(8,128)(2,1)S(1)} %fusion.26.refs_0_), channel_id=1, source_target_pairs={{0,2},{1,3},{2,0},{3,1},{4,6},{5,7},{6,4},{7,5},{8,10},{9,11},{10,... | collective-permute-start | bytes 614408 | tf_op jit(solution)/shard_map/ppermute | solution.py:36
  20.1 16.9 %collective-permute-start.6 = (bf16[2,256,1024]{2,1,0:T(8,128)(2,1)S(1)}, bf16[2,256,1024]{2,1,0:T(8,128)(2,1)S(1)}, u32[]{:S(2)}, u32[]{:S(2)}) collective-permute-start(bf16[2,256,1024]{2,1,0:T(8,128)(2,1)S(1)} %pad_maximum_fusion.3), channel_id=1, source_target_pairs={{0,8},{8,0},{16,24},{24,16},{1,9},{9,1},{17,25},{25,17},{2,10},{10... | collective-permute-start | bytes 3145736 | tf_op jit(solution)/shard_map/ppermute | solution.py:36
  20.2 16.8 %collective-permute-start.5 = (bf16[256,1024]{1,0:T(8,128)(2,1)S(1)}, bf16[256,1024]{1,0:T(8,128)(2,1)S(1)}, u32[]{:S(2)}, u32[]{:S(2)}) collective-permute-start(bf16[256,1024]{1,0:T(8,128)(2,1)S(1)} %get-tuple-element.345), channel_id=1, source_target_pairs={{0,16},{8,24},{16,0},{24,8},{1,17},{9,25},{17,1},{25,9},{2,18},{10... | collective-permute-start | bytes 1572872 | tf_op jit(solution)/shard_map/ppermute | solution.py:36
  21.0 16.0 %collective-permute-start.4 = (bf16[400,256]{1,0:T(8,128)(2,1)S(1)}, bf16[400,256]{1,0:T(8,128)(2,1)S(1)}, u32[]{:S(2)}, u32[]{:S(2)}) collective-permute-start(bf16[400,256]{1,0:T(8,128)(2,1)S(1)} %collective-permute-done.refs_1_), channel_id=1, source_target_pairs={{0,2},{1,3},{2,0},{3,1},{4,6},{5,7},{6,4},{7,5},{8,10},{9,11},{10,... | collective-permute-start | bytes 614408 | tf_op jit(solution)/shard_map/ppermute | solution.py:36
  22.6 14.4 %collective-permute-start.7 = (bf16[1,320,256]{2,1,0:T(8,128)(2,1)S(1)}, bf16[1,320,256]{2,1,0:T(8,128)(2,1)S(1)}, u32[]{:S(2)}, u32[]{:S(2)}) collective-permute-start(bf16[1,320,256]{2,1,0:T(8,128)(2,1)S(1)} %fusion.38.refs_8_), channel_id=1, source_target_pairs={{0,6},{1,7},{2,4},{3,5},{4,2},{5,3},{6,0},{7,1},{8,14},{9,15},{10,... | collective-permute-start | bytes 491528 | tf_op jit(solution)/shard_map/ppermute | solution.py:36
  25.1 11.9 %collective-permute-start.8 = (bf16[288,256]{1,0:T(8,128)(2,1)S(1)}, bf16[288,256]{1,0:T(8,128)(2,1)S(1)}, u32[]{:S(2)}, u32[]{:S(2)}) collective-permute-start(bf16[288,256]{1,0:T(8,128)(2,1)S(1)} %pad_maximum_fusion.19), channel_id=1, source_target_pairs={{0,6},{1,7},{2,4},{3,5},{4,2},{5,3},{6,0},{7,1},{8,14},{9,15},{10,... | collective-permute-start | bytes 442376 | tf_op jit(solution)/shard_map/ppermute | solution.py:36
  39.2 21.1 %collective-permute-start.13 = (bf16[2,256,1024]{2,1,0:T(8,128)(2,1)}, bf16[2,256,1024]{2,1,0:T(8,128)(2,1)}, u32[]{:S(2)}, u32[]{:S(2)}) collective-permute-start(bf16[2,256,1024]{2,1,0:T(8,128)(2,1)} %pad_maximum_fusion.4), channel_id=1, source_target_pairs={{0,8},{8,0},{16,24},{24,16},{1,9},{9,1},{17,25},{25,17},{2,10},{10... | collective-permute-start | bytes 3145736 | tf_op jit(solution)/shard_map/ppermute | solution.py:36
  39.3 20.9 %collective-permute-start.10 = (bf16[4,400,256]{2,1,0:T(8,128)(2,1)S(1)}, bf16[4,400,256]{2,1,0:T(8,128)(2,1)}, u32[]{:S(2)}, u32[]{:S(2)}) collective-permute-start(bf16[4,400,256]{2,1,0:T(8,128)(2,1)S(1)} %shard_map.238.refs_9_.refs_7_), channel_id=1, source_target_pairs={{0,16},{8,24},{16,0},{24,8},{1,17},{9,25},{17,1},{25,9},{2,18},{10... | collective-permute-start | bytes 2457608 | tf_op jit(solution)/shard_map/ppermute | solution.py:36
  39.8 20.5 %collective-permute-start.9 = (bf16[4,400,256]{2,1,0:T(8,128)(2,1)S(1)}, bf16[4,400,256]{2,1,0:T(8,128)(2,1)}, u32[]{:S(2)}, u32[]{:S(2)}) collective-permute-start(bf16[4,400,256]{2,1,0:T(8,128)(2,1)S(1)} %shard_map.238.refs_9_.refs_7_), channel_id=1, source_target_pairs={{0,1},{1,0},{2,3},{3,2},{4,5},{5,4},{6,7},{7,6},{8,9},{9,8},{10,11... | collective-permute-start | bytes 2457608 | tf_op jit(solution)/shard_map/ppermute | solution.py:36
  41.4 10.3 %collective-permute-start.11 = (bf16[2,288,256]{2,1,0:T(8,128)(2,1)S(1)}, bf16[2,288,256]{2,1,0:T(8,128)(2,1)}, u32[]{:S(2)}, u32[]{:S(2)}) collective-permute-start(bf16[2,288,256]{2,1,0:T(8,128)(2,1)S(1)} %pad_maximum_fusion.14), channel_id=1, source_target_pairs={{0,2},{1,3},{2,0},{3,1},{4,6},{5,7},{6,4},{7,5},{8,10},{9,11},{10,... | collective-permute-start | bytes 884744 | tf_op jit(solution)/shard_map/ppermute | solution.py:36
  44.3 15.9 %collective-permute-start.12 = (bf16[576,256]{1,0:T(8,128)(2,1)}, bf16[576,256]{1,0:T(8,128)(2,1)}, u32[]{:S(2)}, u32[]{:S(2)}) collective-permute-start(bf16[576,256]{1,0:T(8,128)(2,1)} %fusion.24), channel_id=1, source_target_pairs={{0,6},{1,7},{2,4},{3,5},{4,2},{5,3},{6,0},{7,1},{8,14},{9,15},{10,... | collective-permute-start | bytes 884744 | tf_op jit(solution)/shard_map/ppermute | solution.py:36
  62.2 22.5 %collective-permute-start.18 = (bf16[2,576,256]{2,1,0:T(8,128)(2,1)}, bf16[2,576,256]{2,1,0:T(8,128)(2,1)}, u32[]{:S(2)}, u32[]{:S(2)}) collective-permute-start(bf16[2,576,256]{2,1,0:T(8,128)(2,1)} %pad_maximum_fusion.7), channel_id=1, source_target_pairs={{0,2},{1,3},{2,0},{3,1},{4,6},{5,7},{6,4},{7,5},{8,10},{9,11},{10,... | collective-permute-start | bytes 1769480 | tf_op jit(solution)/shard_map/ppermute | solution.py:36
  66.8 11.0 %collective-permute-start.17 = (bf16[2,320,256]{2,1,0:T(8,128)(2,1)}, bf16[2,320,256]{2,1,0:T(8,128)(2,1)}, u32[]{:S(2)}, u32[]{:S(2)}) collective-permute-start(bf16[2,320,256]{2,1,0:T(8,128)(2,1)} %pad_maximum_fusion.13), channel_id=1, source_target_pairs={{0,16},{8,24},{16,0},{24,8},{1,17},{9,25},{17,1},{25,9},{2,18},{10... | collective-permute-start | bytes 983048 | tf_op jit(solution)/shard_map/ppermute | solution.py:36
  70.1 14.6 %collective-permute-start.14 = (bf16[2,400,256]{2,1,0:T(8,128)(2,1)}, bf16[2,400,256]{2,1,0:T(8,128)(2,1)}, u32[]{:S(2)}, u32[]{:S(2)}) collective-permute-start(bf16[2,400,256]{2,1,0:T(8,128)(2,1)} %slice.396), channel_id=1, source_target_pairs={{0,16},{8,24},{16,0},{24,8},{1,17},{9,25},{17,1},{25,9},{2,18},{10... | collective-permute-start | bytes 1228808 | tf_op jit(solution)/shard_map/ppermute | solution.py:36
  72.4 12.3 %collective-permute-start.15 = (bf16[2,400,256]{2,1,0:T(8,128)(2,1)}, bf16[2,400,256]{2,1,0:T(8,128)(2,1)}, u32[]{:S(2)}, u32[]{:S(2)}) collective-permute-start(bf16[2,400,256]{2,1,0:T(8,128)(2,1)} %slice.397), channel_id=1, source_target_pairs={{0,1},{1,0},{2,3},{3,2},{4,5},{5,4},{6,7},{7,6},{8,9},{9,8},{10,11... | collective-permute-start | bytes 1228808 | tf_op jit(solution)/shard_map/ppermute | solution.py:36
  86.6 22.4 %collective-permute-start.21 = (bf16[3,320,256]{2,1,0:T(8,128)(2,1)S(1)}, bf16[3,320,256]{2,1,0:T(8,128)(2,1)S(1)}, u32[]{:S(2)}, u32[]{:S(2)}) collective-permute-start(bf16[3,320,256]{2,1,0:T(8,128)(2,1)S(1)} %constant_dynamic-update-slice_fusion.refs_12_), channel_id=1, source_target_pairs={{0,6},{1,7},{2,4},{3,5},{4,2},{5,3},{6,0},{7,1},{8,14},{9,15},{10,... | collective-permute-start | bytes 1474568 | tf_op jit(solution)/shard_map/ppermute | solution.py:36
  89.3 21.2 %collective-permute-start.22 = (bf16[3,320,256]{2,1,0:T(8,128)(2,1)S(1)}, bf16[3,320,256]{2,1,0:T(8,128)(2,1)S(1)}, u32[]{:S(2)}, u32[]{:S(2)}) collective-permute-start(bf16[3,320,256]{2,1,0:T(8,128)(2,1)S(1)} %constant_dynamic-update-slice_fusion.refs_12_), channel_id=1, source_target_pairs={{0,2},{1,3},{2,0},{3,1},{4,6},{5,7},{6,4},{7,5},{8,10},{9,11},{10,... | collective-permute-start | bytes 1474568 | tf_op jit(solution)/shard_map/ppermute | solution.py:36
  89.4 21.2 %collective-permute-start.19 = (bf16[4,288,256]{2,1,0:T(8,128)(2,1)S(1)}, bf16[4,288,256]{2,1,0:T(8,128)(2,1)S(1)}, u32[]{:S(2)}, u32[]{:S(2)}) collective-permute-start(bf16[4,288,256]{2,1,0:T(8,128)(2,1)S(1)} %shard_map.240.refs_2_.refs_16_.refs_10_), channel_id=1, source_target_pairs={{0,1},{1,0},{2,3},{3,2},{4,5},{5,4},{6,7},{7,6},{8,9},{9,8},{10,11... | collective-permute-start | bytes 1769480 | tf_op jit(solution)/shard_map/ppermute | solution.py:36
  91.0 19.6 %collective-permute-start.20 = (bf16[4,288,256]{2,1,0:T(8,128)(2,1)S(1)}, bf16[4,288,256]{2,1,0:T(8,128)(2,1)S(1)}, u32[]{:S(2)}, u32[]{:S(2)}) collective-permute-start(bf16[4,288,256]{2,1,0:T(8,128)(2,1)S(1)} %shard_map.240.refs_2_.refs_16_.refs_10_), channel_id=1, source_target_pairs={{0,16},{8,24},{16,0},{24,8},{1,17},{9,25},{17,1},{25,9},{2,18},{10... | collective-permute-start | bytes 1769480 | tf_op jit(solution)/shard_map/ppermute | solution.py:36
  94.3 14.7 %collective-permute-start.23 = (bf16[2,192,256]{2,1,0:T(8,128)(2,1)S(1)}, bf16[2,192,256]{2,1,0:T(8,128)(2,1)S(1)}, u32[]{:S(2)}, u32[]{:S(2)}) collective-permute-start(bf16[2,192,256]{2,1,0:T(8,128)(2,1)S(1)} %pad_maximum_fusion.18), channel_id=1, source_target_pairs={{0,8},{8,0},{16,24},{24,16},{1,9},{9,1},{17,25},{25,17},{2,10},{10... | collective-permute-start | bytes 589832 | tf_op jit(solution)/shard_map/ppermute | solution.py:36
  111.9 23.9 %collective-permute-start.27 = (bf16[2,576,256]{2,1,0:T(8,128)(2,1)S(1)}, bf16[2,576,256]{2,1,0:T(8,128)(2,1)S(1)}, u32[]{:S(2)}, u32[]{:S(2)}) collective-permute-start(bf16[2,576,256]{2,1,0:T(8,128)(2,1)S(1)} %pad_maximum_fusion.9.refs_9_), channel_id=1, source_target_pairs={{0,16},{8,24},{16,0},{24,8},{1,17},{9,25},{17,1},{25,9},{2,18},{10... | collective-permute-start | bytes 1769480 | tf_op jit(solution)/shard_map/ppermute | solution.py:36
  114.4 21.4 %collective-permute-start.26 = (bf16[2,576,256]{2,1,0:T(8,128)(2,1)S(1)}, bf16[2,576,256]{2,1,0:T(8,128)(2,1)S(1)}, u32[]{:S(2)}, u32[]{:S(2)}) collective-permute-start(bf16[2,576,256]{2,1,0:T(8,128)(2,1)S(1)} %pad_maximum_fusion.8.refs_5_), channel_id=1, source_target_pairs={{0,1},{1,0},{2,3},{3,2},{4,5},{5,4},{6,7},{7,6},{8,9},{9,8},{10,11... | collective-permute-start | bytes 1769480 | tf_op jit(solution)/shard_map/ppermute | solution.py:36
  116.0 19.8 %collective-permute-start.28 = (bf16[3,320,256]{2,1,0:T(8,128)(2,1)S(1)}, bf16[3,320,256]{2,1,0:T(8,128)(2,1)S(1)}, u32[]{:S(2)}, u32[]{:S(2)}) collective-permute-start(bf16[3,320,256]{2,1,0:T(8,128)(2,1)S(1)} %collective-permute-done.21.refs_13_), channel_id=1, source_target_pairs={{0,2},{1,3},{2,0},{3,1},{4,6},{5,7},{6,4},{7,5},{8,10},{9,11},{10,... | collective-permute-start | bytes 1474568 | tf_op jit(solution)/shard_map/ppermute | solution.py:36
  116.8 17.2 %collective-permute-start.24 = (bf16[2,288,256]{2,1,0:T(8,128)(2,1)S(1)}, bf16[2,288,256]{2,1,0:T(8,128)(2,1)S(1)}, u32[]{:S(2)}, u32[]{:S(2)}) collective-permute-start(bf16[2,288,256]{2,1,0:T(8,128)(2,1)S(1)} %slice.406), channel_id=1, source_target_pairs={{0,16},{8,24},{16,0},{24,8},{1,17},{9,25},{17,1},{25,9},{2,18},{10... | collective-permute-start | bytes 884744 | tf_op jit(solution)/shard_map/ppermute | solution.py:36
  117.6 18.2 %collective-permute-start.25 = (bf16[2,288,256]{2,1,0:T(8,128)(2,1)S(1)}, bf16[2,288,256]{2,1,0:T(8,128)(2,1)S(1)}, u32[]{:S(2)}, u32[]{:S(2)}) collective-permute-start(bf16[2,288,256]{2,1,0:T(8,128)(2,1)S(1)} %slice.407), channel_id=1, source_target_pairs={{0,1},{1,0},{2,3},{3,2},{4,5},{5,4},{6,7},{7,6},{8,9},{9,8},{10,11... | collective-permute-start | bytes 884744 | tf_op jit(solution)/shard_map/ppermute | solution.py:36
  135.8 12.7 %collective-permute-start.29 = (bf16[256,1024]{1,0:T(8,128)(2,1)S(1)}, bf16[256,1024]{1,0:T(8,128)(2,1)S(1)}, u32[]{:S(2)}, u32[]{:S(2)}) collective-permute-start(bf16[256,1024]{1,0:T(8,128)(2,1)S(1)} %copy-done.62), channel_id=1, source_target_pairs={{0,16},{8,24},{16,0},{24,8},{1,17},{9,25},{17,1},{25,9},{2,18},{10... | collective-permute-start | bytes 1572872 | tf_op jit(solution)/shard_map/ppermute | solution.py:36
  137.7 7.1 %collective-permute-start.31 = (bf16[1,320,256]{2,1,0:T(8,128)(2,1)S(1)}, bf16[1,320,256]{2,1,0:T(8,128)(2,1)S(1)}, u32[]{:S(2)}, u32[]{:S(2)}) collective-permute-start(bf16[1,320,256]{2,1,0:T(8,128)(2,1)S(1)} %copy-done.38), channel_id=1, source_target_pairs={{0,2},{1,3},{2,0},{3,1},{4,6},{5,7},{6,4},{7,5},{8,10},{9,11},{10,... | collective-permute-start | bytes 491528 | tf_op jit(solution)/shard_map/ppermute | solution.py:36
  154.2 29.2 %collective-permute-start.34 = (bf16[2,576,256]{2,1,0:T(8,128)(2,1)S(1)}, bf16[2,576,256]{2,1,0:T(8,128)(2,1)S(1)}, u32[]{:S(2)}, u32[]{:S(2)}) collective-permute-start(bf16[2,576,256]{2,1,0:T(8,128)(2,1)S(1)} %pad_maximum_fusion.8.refs_5_), channel_id=1, source_target_pairs={{0,16},{8,24},{16,0},{24,8},{1,17},{9,25},{17,1},{25,9},{2,18},{10... | collective-permute-start | bytes 1769480 | tf_op jit(solution)/shard_map/ppermute | solution.py:36
  155.0 28.5 %collective-permute-start.35 = (bf16[2,576,256]{2,1,0:T(8,128)(2,1)S(1)}, bf16[2,576,256]{2,1,0:T(8,128)(2,1)S(1)}, u32[]{:S(2)}, u32[]{:S(2)}) collective-permute-start(bf16[2,576,256]{2,1,0:T(8,128)(2,1)S(1)} %collective-permute-done.26.refs_6_), channel_id=1, source_target_pairs={{0,16},{8,24},{16,0},{24,8},{1,17},{9,25},{17,1},{25,9},{2,18},{10... | collective-permute-start | bytes 1769480 | tf_op jit(solution)/shard_map/ppermute | solution.py:36
  156.3 27.2 %collective-permute-start.36 = (bf16[2,576,256]{2,1,0:T(8,128)(2,1)S(1)}, bf16[2,576,256]{2,1,0:T(8,128)(2,1)S(1)}, u32[]{:S(2)}, u32[]{:S(2)}) collective-permute-start(bf16[2,576,256]{2,1,0:T(8,128)(2,1)S(1)} %pad_maximum_fusion.9.refs_9_), channel_id=1, source_target_pairs={{0,1},{1,0},{2,3},{3,2},{4,5},{5,4},{6,7},{7,6},{8,9},{9,8},{10,11... | collective-permute-start | bytes 1769480 | tf_op jit(solution)/shard_map/ppermute | solution.py:36
  157.8 26.0 %collective-permute-start.37 = (bf16[2,576,256]{2,1,0:T(8,128)(2,1)S(1)}, bf16[2,576,256]{2,1,0:T(8,128)(2,1)S(1)}, u32[]{:S(2)}, u32[]{:S(2)}) collective-permute-start(bf16[2,576,256]{2,1,0:T(8,128)(2,1)S(1)} %collective-permute-done.27.refs_11_), channel_id=1, source_target_pairs={{0,1},{1,0},{2,3},{3,2},{4,5},{5,4},{6,7},{7,6},{8,9},{9,8},{10,11... | collective-permute-start | bytes 1769480 | tf_op jit(solution)/shard_map/ppermute | solution.py:36
  183.7 31.0 %collective-permute-start.38 = (bf16[4,480,256]{2,1,0:T(8,128)(2,1)S(1)}, bf16[4,480,256]{2,1,0:T(8,128)(2,1)S(1)}, u32[]{:S(2)}, u32[]{:S(2)}) collective-permute-start(bf16[4,480,256]{2,1,0:T(8,128)(2,1)S(1)} %get-tuple-element.494), channel_id=1, source_target_pairs={{0,1},{1,0},{2,3},{3,2},{4,5},{5,4},{6,7},{7,6},{8,9},{9,8},{10,11... | collective-permute-start | bytes 2949128 | tf_op jit(solution)/shard_map/ppermute | solution.py:36
  185.2 29.6 %collective-permute-start.39 = (bf16[4,480,256]{2,1,0:T(8,128)(2,1)S(1)}, bf16[4,480,256]{2,1,0:T(8,128)(2,1)S(1)}, u32[]{:S(2)}, u32[]{:S(2)}) collective-permute-start(bf16[4,480,256]{2,1,0:T(8,128)(2,1)S(1)} %get-tuple-element.495), channel_id=1, source_target_pairs={{0,16},{8,24},{16,0},{24,8},{1,17},{9,25},{17,1},{25,9},{2,18},{10... | collective-permute-start | bytes 2949128 | tf_op jit(solution)/shard_map/ppermute | solution.py:36
  214.9 20.3 %collective-permute-start.44 = (bf16[2,256,1024]{2,1,0:T(8,128)(2,1)}, bf16[2,256,1024]{2,1,0:T(8,128)(2,1)}, u32[]{:S(2)}, u32[]{:S(2)}) collective-permute-start(bf16[2,256,1024]{2,1,0:T(8,128)(2,1)} %get-tuple-element.522), channel_id=1, source_target_pairs={{0,8},{8,0},{16,24},{24,16},{1,9},{9,1},{17,25},{25,17},{2,10},{10... | collective-permute-start | bytes 3145736 | tf_op jit(solution)/shard_map/ppermute | solution.py:36
  215.4 19.8 %collective-permute-start.43 = (bf16[4,384,256]{2,1,0:T(8,128)(2,1)}, bf16[4,384,256]{2,1,0:T(8,128)(2,1)}, u32[]{:S(2)}, u32[]{:S(2)}) collective-permute-start(bf16[4,384,256]{2,1,0:T(8,128)(2,1)} %get-tuple-element.520), channel_id=1, source_target_pairs={{0,2},{1,3},{2,0},{3,1},{4,6},{5,7},{6,4},{7,5},{8,10},{9,11},{10,... | collective-permute-start | bytes 2359304 | tf_op jit(solution)/shard_map/ppermute | solution.py:36
  216.9 17.4 %collective-permute-start.42 = (bf16[2,480,256]{2,1,0:T(8,128)(2,1)}, bf16[2,480,256]{2,1,0:T(8,128)(2,1)S(1)}, u32[]{:S(2)}, u32[]{:S(2)}) collective-permute-start(bf16[2,480,256]{2,1,0:T(8,128)(2,1)} %add_convert_fusion.1), channel_id=1, source_target_pairs={{0,16},{8,24},{16,0},{24,8},{1,17},{9,25},{17,1},{25,9},{2,18},{10... | collective-permute-start | bytes 1474568 | tf_op jit(solution)/shard_map/ppermute | solution.py:36
  219.0 15.3 %collective-permute-start.41 = (bf16[2,480,256]{2,1,0:T(8,128)(2,1)}, bf16[2,480,256]{2,1,0:T(8,128)(2,1)}, u32[]{:S(2)}, u32[]{:S(2)}) collective-permute-start(bf16[2,480,256]{2,1,0:T(8,128)(2,1)} %add_convert_fusion.2), channel_id=1, source_target_pairs={{0,1},{1,0},{2,3},{3,2},{4,5},{5,4},{6,7},{7,6},{8,9},{9,8},{10,11... | collective-permute-start | bytes 1474568 | tf_op jit(solution)/shard_map/ppermute | solution.py:36
  242.9 19.9 %collective-permute-start.49 = (bf16[2,160,256]{2,1,0:T(8,128)(2,1)S(1)}, bf16[2,160,256]{2,1,0:T(8,128)(2,1)S(1)}, u32[]{:S(2)}, u32[]{:S(2)}) collective-permute-start(bf16[2,160,256]{2,1,0:T(8,128)(2,1)S(1)} %slice.703), channel_id=1, source_target_pairs={{0,8},{8,0},{16,24},{24,16},{1,9},{9,1},{17,25},{25,17},{2,10},{10... | collective-permute-start | bytes 491528 | tf_op jit(solution)/shard_map/ppermute | solution.py:36
  243.0 28.4 %collective-permute-start.48 = (bf16[4,384,256]{2,1,0:T(8,128)(2,1)S(1)}, bf16[4,384,256]{2,1,0:T(8,128)(2,1)S(1)}, u32[]{:S(2)}, u32[]{:S(2)}) collective-permute-start(bf16[4,384,256]{2,1,0:T(8,128)(2,1)S(1)} %copy-done.36), channel_id=1, source_target_pairs={{0,2},{1,3},{2,0},{3,1},{4,6},{5,7},{6,4},{7,5},{8,10},{9,11},{10,... | collective-permute-start | bytes 2359304 | tf_op jit(solution)/shard_map/ppermute | solution.py:36
  243.4 27.4 %collective-permute-start.45 = (bf16[4,320,256]{2,1,0:T(8,128)(2,1)S(1)}, bf16[4,320,256]{2,1,0:T(8,128)(2,1)S(1)}, u32[]{:S(2)}, u32[]{:S(2)}) collective-permute-start(bf16[4,320,256]{2,1,0:T(8,128)(2,1)S(1)} %copy-done.71), channel_id=1, source_target_pairs={{0,1},{1,0},{2,3},{3,2},{4,5},{5,4},{6,7},{7,6},{8,9},{9,8},{10,11... | collective-permute-start | bytes 1966088 | tf_op jit(solution)/shard_map/ppermute | solution.py:36
  245.0 25.8 %collective-permute-start.46 = (bf16[4,320,256]{2,1,0:T(8,128)(2,1)S(1)}, bf16[4,320,256]{2,1,0:T(8,128)(2,1)S(1)}, u32[]{:S(2)}, u32[]{:S(2)}) collective-permute-start(bf16[4,320,256]{2,1,0:T(8,128)(2,1)S(1)} %copy-done.70), channel_id=1, source_target_pairs={{0,16},{8,24},{16,0},{24,8},{1,17},{9,25},{17,1},{25,9},{2,18},{10... | collective-permute-start | bytes 1966088 | tf_op jit(solution)/shard_map/ppermute | solution.py:36
  246.9 23.9 %collective-permute-start.47 = (bf16[2,384,256]{2,1,0:T(8,128)(2,1)S(1)}, bf16[2,384,256]{2,1,0:T(8,128)(2,1)S(1)}, u32[]{:S(2)}, u32[]{:S(2)}) collective-permute-start(bf16[2,384,256]{2,1,0:T(8,128)(2,1)S(1)} %slice.494), channel_id=1, source_target_pairs={{0,6},{1,7},{2,4},{3,5},{4,2},{5,3},{6,0},{7,1},{8,14},{9,15},{10,... | collective-permute-start | bytes 1179656 | tf_op jit(solution)/shard_map/ppermute | solution.py:36
  271.7 21.7 %collective-permute-start.54 = (bf16[2,480,256]{2,1,0:T(8,128)(2,1)S(1)}, bf16[2,480,256]{2,1,0:T(8,128)(2,1)S(1)}, u32[]{:S(2)}, u32[]{:S(2)}) collective-permute-start(bf16[2,480,256]{2,1,0:T(8,128)(2,1)S(1)} %pad_maximum_fusion.11), channel_id=1, source_target_pairs={{0,2},{1,3},{2,0},{3,1},{4,6},{5,7},{6,4},{7,5},{8,10},{9,11},{10,... | collective-permute-start | bytes 1474568 | tf_op jit(solution)/shard_map/ppermute | solution.py:36
  271.8 21.6 %collective-permute-start.50 = (bf16[4,400,256]{2,1,0:T(8,128)(2,1)S(1)}, bf16[4,400,256]{2,1,0:T(8,128)(2,1)S(1)}, u32[]{:S(2)}, u32[]{:S(2)}) collective-permute-start(bf16[4,400,256]{2,1,0:T(8,128)(2,1)S(1)} %get-tuple-element.564), channel_id=1, source_target_pairs={{0,16},{8,24},{16,0},{24,8},{1,17},{9,25},{17,1},{25,9},{2,18},{10... | collective-permute-start | bytes 2457608 | tf_op jit(solution)/shard_map/ppermute | solution.py:36
  273.3 19.9 %collective-permute-start.52 = (bf16[2,320,256]{2,1,0:T(8,128)(2,1)S(1)}, bf16[2,320,256]{2,1,0:T(8,128)(2,1)S(1)}, u32[]{:S(2)}, u32[]{:S(2)}) collective-permute-start(bf16[2,320,256]{2,1,0:T(8,128)(2,1)S(1)} %add_convert_fusion.7), channel_id=1, source_target_pairs={{0,1},{1,0},{2,3},{3,2},{4,5},{5,4},{6,7},{7,6},{8,9},{9,8},{10,11... | collective-permute-start | bytes 983048 | tf_op jit(solution)/shard_map/ppermute | solution.py:36
  273.9 19.5 %collective-permute-start.53 = (bf16[2,384,256]{2,1,0:T(8,128)(2,1)S(1)}, bf16[2,384,256]{2,1,0:T(8,128)(2,1)S(1)}, u32[]{:S(2)}, u32[]{:S(2)}) collective-permute-start(bf16[2,384,256]{2,1,0:T(8,128)(2,1)S(1)} %slice.430), channel_id=1, source_target_pairs={{0,6},{1,7},{2,4},{3,5},{4,2},{5,3},{6,0},{7,1},{8,14},{9,15},{10,... | collective-permute-start | bytes 1179656 | tf_op jit(solution)/shard_map/ppermute | solution.py:36
  276.5 16.9 %collective-permute-start.51 = (bf16[2,400,256]{2,1,0:T(8,128)(2,1)S(1)}, bf16[2,400,256]{2,1,0:T(8,128)(2,1)S(1)}, u32[]{:S(2)}, u32[]{:S(2)}) collective-permute-start(bf16[2,400,256]{2,1,0:T(8,128)(2,1)S(1)} %get-tuple-element.565), channel_id=1, source_target_pairs={{0,1},{1,0},{2,3},{3,2},{4,5},{5,4},{6,7},{7,6},{8,9},{9,8},{10,11... | collective-permute-start | bytes 1228808 | tf_op jit(solution)/shard_map/ppermute | solution.py:36
  293.7 21.5 %collective-permute-start.57 = (bf16[2,384,256]{2,1,0:T(8,128)(2,1)S(1)}, bf16[2,384,256]{2,1,0:T(8,128)(2,1)S(1)}, u32[]{:S(2)}, u32[]{:S(2)}) collective-permute-start(bf16[2,384,256]{2,1,0:T(8,128)(2,1)S(1)} %get-tuple-element.673), channel_id=1, source_target_pairs={{0,1},{1,0},{2,3},{3,2},{4,5},{5,4},{6,7},{7,6},{8,9},{9,8},{10,11... | collective-permute-start | bytes 1179656 | tf_op jit(solution)/shard_map/ppermute | solution.py:36
  295.5 19.7 %collective-permute-start.59 = (bf16[256,1024]{1,0:T(8,128)(2,1)S(1)}, bf16[256,1024]{1,0:T(8,128)(2,1)S(1)}, u32[]{:S(2)}, u32[]{:S(2)}) collective-permute-start(bf16[256,1024]{1,0:T(8,128)(2,1)S(1)} %get-tuple-element.607), channel_id=1, source_target_pairs={{0,16},{8,24},{16,0},{24,8},{1,17},{9,25},{17,1},{25,9},{2,18},{10... | collective-permute-start | bytes 1572872 | tf_op jit(solution)/shard_map/ppermute | solution.py:36
  296.0 19.1 %collective-permute-start.55 = (bf16[2,400,256]{2,1,0:T(8,128)(2,1)S(1)}, bf16[2,400,256]{2,1,0:T(8,128)(2,1)S(1)}, u32[]{:S(2)}, u32[]{:S(2)}) collective-permute-start(bf16[2,400,256]{2,1,0:T(8,128)(2,1)S(1)} %get-tuple-element.591), channel_id=1, source_target_pairs={{0,1},{1,0},{2,3},{3,2},{4,5},{5,4},{6,7},{7,6},{8,9},{9,8},{10,11... | collective-permute-start | bytes 1228808 | tf_op jit(solution)/shard_map/ppermute | solution.py:36
  297.3 17.8 %collective-permute-start.58 = (bf16[2,320,256]{2,1,0:T(8,128)(2,1)S(1)}, bf16[2,320,256]{2,1,0:T(8,128)(2,1)S(1)}, u32[]{:S(2)}, u32[]{:S(2)}) collective-permute-start(bf16[2,320,256]{2,1,0:T(8,128)(2,1)S(1)} %add_convert_fusion.6), channel_id=1, source_target_pairs={{0,16},{8,24},{16,0},{24,8},{1,17},{9,25},{17,1},{25,9},{2,18},{10... | collective-permute-start | bytes 983048 | tf_op jit(solution)/shard_map/ppermute | solution.py:36
  298.1 9.8 %collective-permute-start.56 = (bf16[480,256]{1,0:T(8,128)(2,1)S(1)}, bf16[480,256]{1,0:T(8,128)(2,1)S(1)}, u32[]{:S(2)}, u32[]{:S(2)}) collective-permute-start(bf16[480,256]{1,0:T(8,128)(2,1)S(1)} %get-tuple-element.697), channel_id=1, source_target_pairs={{0,6},{1,7},{2,4},{3,5},{4,2},{5,3},{6,0},{7,1},{8,14},{9,15},{10,... | collective-permute-start | bytes 737288 | tf_op jit(solution)/shard_map/ppermute | solution.py:36
  315.3 7.4 %collective-permute-start.64 = (bf16[384,256]{1,0:T(8,128)(2,1)S(1)}, bf16[384,256]{1,0:T(8,128)(2,1)S(1)}, u32[]{:S(2)}, u32[]{:S(2)}) collective-permute-start(bf16[384,256]{1,0:T(8,128)(2,1)S(1)} %fusion.29), channel_id=1, source_target_pairs={{0,16},{8,24},{16,0},{24,8},{1,17},{9,25},{17,1},{25,9},{2,18},{10... | collective-permute-start | bytes 589832 | tf_op jit(solution)/shard_map/ppermute | solution.py:36
  316.8 13.0 %collective-permute-start.62 = (bf16[2,400,256]{2,1,0:T(8,128)(2,1)S(1)}, bf16[2,400,256]{2,1,0:T(8,128)(2,1)S(1)}, u32[]{:S(2)}, u32[]{:S(2)}) collective-permute-start(bf16[2,400,256]{2,1,0:T(8,128)(2,1)S(1)} %add_convert_fusion.3), channel_id=1, source_target_pairs={{0,16},{8,24},{16,0},{24,8},{1,17},{9,25},{17,1},{25,9},{2,18},{10... | collective-permute-start | bytes 1228808 | tf_op jit(solution)/shard_map/ppermute | solution.py:36
  318.6 11.3 %collective-permute-start.61 = (bf16[2,400,256]{2,1,0:T(8,128)(2,1)S(1)}, bf16[2,400,256]{2,1,0:T(8,128)(2,1)S(1)}, u32[]{:S(2)}, u32[]{:S(2)}) collective-permute-start(bf16[2,400,256]{2,1,0:T(8,128)(2,1)S(1)} %add_convert_fusion.4), channel_id=1, source_target_pairs={{0,1},{1,0},{2,3},{3,2},{4,5},{5,4},{6,7},{7,6},{8,9},{9,8},{10,11... | collective-permute-start | bytes 1228808 | tf_op jit(solution)/shard_map/ppermute | solution.py:36
  330.5 10.6 %collective-permute-start.65 = (bf16[400,256]{1,0:T(8,128)(2,1)S(1)}, bf16[400,256]{1,0:T(8,128)(2,1)S(1)}, u32[]{:S(2)}, u32[]{:S(2)}) collective-permute-start(bf16[400,256]{1,0:T(8,128)(2,1)S(1)} %fusion.27), channel_id=1, source_target_pairs={{0,2},{1,3},{2,0},{3,1},{4,6},{5,7},{6,4},{7,5},{8,10},{9,11},{10,... | collective-permute-start | bytes 614408 | tf_op jit(solution)/shard_map/ppermute | solution.py:36
  332.6 13.8 %collective-permute-start.67 = (bf16[256,1024]{1,0:T(8,128)(2,1)S(1)}, bf16[256,1024]{1,0:T(8,128)(2,1)S(1)}, u32[]{:S(2)}, u32[]{:S(2)}) collective-permute-start(bf16[256,1024]{1,0:T(8,128)(2,1)S(1)} %get-tuple-element.637), channel_id=1, source_target_pairs={{0,16},{8,24},{16,0},{24,8},{1,17},{9,25},{17,1},{25,9},{2,18},{10... | collective-permute-start | bytes 1572872 | tf_op jit(solution)/shard_map/ppermute | solution.py:36
  346.5 13.0 %collective-permute-start.72 = (bf16[320,256]{1,0:T(8,128)(2,1)S(1)}, bf16[320,256]{1,0:T(8,128)(2,1)S(1)}, u32[]{:S(2)}, u32[]{:S(2)}) collective-permute-start(bf16[320,256]{1,0:T(8,128)(2,1)S(1)} %fusion.35), channel_id=1, source_target_pairs={{0,2},{1,3},{2,0},{3,1},{4,6},{5,7},{6,4},{7,5},{8,10},{9,11},{10,... | collective-permute-start | bytes 491528 | tf_op jit(solution)/shard_map/ppermute | solution.py:36
  347.0 12.5 %collective-permute-start.70 = (bf16[320,256]{1,0:T(8,128)(2,1)S(1)}, bf16[320,256]{1,0:T(8,128)(2,1)S(1)}, u32[]{:S(2)}, u32[]{:S(2)}) collective-permute-start(bf16[320,256]{1,0:T(8,128)(2,1)S(1)} %fusion.17), channel_id=1, source_target_pairs={{0,6},{1,7},{2,4},{3,5},{4,2},{5,3},{6,0},{7,1},{8,14},{9,15},{10,... | collective-permute-start | bytes 491528 | tf_op jit(solution)/shard_map/ppermute | solution.py:36
  348.7 15.5 %collective-permute-start.73 = (bf16[256,1024]{1,0:T(8,128)(2,1)S(1)}, bf16[256,1024]{1,0:T(8,128)(2,1)S(1)}, u32[]{:S(2)}, u32[]{:S(2)}) collective-permute-start(bf16[256,1024]{1,0:T(8,128)(2,1)S(1)} %get-tuple-element.649), channel_id=1, source_target_pairs={{0,16},{8,24},{16,0},{24,8},{1,17},{9,25},{17,1},{25,9},{2,18},{10... | collective-permute-start | bytes 1572872 | tf_op jit(solution)/shard_map/ppermute | solution.py:36
  349.4 11.7 %collective-permute-start.69 = (bf16[400,256]{1,0:T(8,128)(2,1)S(1)}, bf16[400,256]{1,0:T(8,128)(2,1)S(1)}, u32[]{:S(2)}, u32[]{:S(2)}) collective-permute-start(bf16[400,256]{1,0:T(8,128)(2,1)S(1)} %fusion.12), channel_id=1, source_target_pairs={{0,6},{1,7},{2,4},{3,5},{4,2},{5,3},{6,0},{7,1},{8,14},{9,15},{10,... | collective-permute-start | bytes 614408 | tf_op jit(solution)/shard_map/ppermute | solution.py:36
  351.5 12.7 %collective-permute-start.71 = (bf16[400,256]{1,0:T(8,128)(2,1)S(1)}, bf16[400,256]{1,0:T(8,128)(2,1)S(1)}, u32[]{:S(2)}, u32[]{:S(2)}) collective-permute-start(bf16[400,256]{1,0:T(8,128)(2,1)S(1)} %fusion.28), channel_id=1, source_target_pairs={{0,2},{1,3},{2,0},{3,1},{4,6},{5,7},{6,4},{7,5},{8,10},{9,11},{10,... | collective-permute-start | bytes 614408 | tf_op jit(solution)/shard_map/ppermute | solution.py:36
  (88 other events, 946.1 us)

commit v4 on v3

--- a/solution.py
+++ b/solution.py
@@ -476,7 +476,7 @@
                 if first:
                     put_lanes(outs, by, bx, q, slice(0, own), lanes, piece)
                 else:
-                    outs[q][bx * 2 + by, :, lanes] = piece
+                    outs[q][by * 2 + bx, :, lanes] = piece
     for by, other in bits(2):
         grad = dot_nn(hid[...], gy[:, pl.ds(column_of(info, by, other), 256)]).astype(BF16)
         for t in range(2):
@@ -869,7 +869,7 @@
     middle_own = own_tokens(v.x).astype(F32) + plus(
         own_tokens(v.part), own_tokens(v.precv))
     result = (live_now * (middle_own + plus(v.rkeep, v.rrecv))).astype(BF16)
-    v.okeep, v.osend = owner_keep(result), owner_send(result)
+    v.okeep, v.orecv = owner_keep(result), over_y(owner_send(result))
     def attend_back(side):
         first = side * (pairs // 2)
         column = pl.BlockSpec((length, 128), lambda i: (0, i + first))
@@ -899,8 +899,8 @@
 
     v.grads1 = attend_back(1)
     v.qdx, v.qsy, v.qky = attn_grads(1)
-    v.grads1, v.qdx, v.qsy, v.qky, v.q, v.k, v.b, v.datt, v.srx, v.sry, v.skx, v.sky, v.sown, v.n0, v.n1, v.nf1, v.nn2, v.bt, v.bm, v.okeep, v.osend = lax.optimization_barrier(
-        (v.grads1, v.qdx, v.qsy, v.qky, v.q, v.k, v.b, v.datt, v.srx, v.sry, v.skx, v.sky, v.sown, v.n0, v.n1, v.nf1, v.nn2, v.bt, v.bm, v.okeep, v.osend))
+    v.grads1, v.qdx, v.qsy, v.qky, v.q, v.k, v.b, v.datt, v.srx, v.sry, v.skx, v.sky, v.sown, v.n0, v.n1, v.nf1, v.nn2, v.bt, v.bm, v.okeep, v.orecv = lax.optimization_barrier(
+        (v.grads1, v.qdx, v.qsy, v.qky, v.q, v.k, v.b, v.datt, v.srx, v.sry, v.skx, v.sky, v.sown, v.n0, v.n1, v.nf1, v.nn2, v.bt, v.bm, v.okeep, v.orecv))
     v.qry, v.qrd = over_y(v.qsy), over_x(v.qdx)
     fold("s")
     v.srx2 = over_x(v.sfx)
@@ -908,15 +908,14 @@
     v.bzn = near(jnp.stack([quarter("b", 2 * part_b, 2), quarter("b", 2 * part_b, 3)]).astype(BF16))
     v.grads0 = attend_back(0)
     v.qsx, v.qkx, v.qown = attn_grads(0)
-    v.grads0, v.grads1, v.qsx, v.qkx, v.qown, v.qry, v.qrd, v.qky, v.srx, v.sry, v.srx2, v.sfy, v.sown, v.n0, v.nf0, v.nf1, v.nn2, v.bzn, v.bt, v.bm, v.okeep, v.osend = lax.optimization_barrier(
-        (v.grads0, v.grads1, v.qsx, v.qkx, v.qown, v.qry, v.qrd, v.qky, v.srx, v.sry, v.srx2, v.sfy, v.sown, v.n0, v.nf0, v.nf1, v.nn2, v.bzn, v.bt, v.bm, v.okeep, v.osend))
+    v.grads0, v.grads1, v.qsx, v.qkx, v.qown, v.qry, v.qrd, v.qky, v.srx, v.sry, v.srx2, v.sfy, v.sown, v.n0, v.nf0, v.nf1, v.nn2, v.bzn, v.bt, v.bm, v.okeep, v.orecv = lax.optimization_barrier(
+        (v.grads0, v.grads1, v.qsx, v.qkx, v.qown, v.qry, v.qrd, v.qky, v.srx, v.sry, v.srx2, v.sfy, v.sown, v.n0, v.nf0, v.nf1, v.nn2, v.bzn, v.bt, v.bm, v.okeep, v.orecv))
     v.qrx = over_x(v.qsx)
     v.sry2 = over_y(v.sfy)
     v.nt0 = plus(v.n0[:2], v.nf0, v.nn2[:2])
-    v.nx = over_x(plus(v.n0[2:], v.nf1, v.nn2[2:]).astype(BF16))
+    v.nx = over_y(plus(v.n0[2:], v.nf1, v.nn2[2:]).astype(BF16))
     v.bt0 = plus(quarter("b", 2 * part_b, 0), v.bzn[0])
     v.bzf = far(plus(quarter("b", 2 * part_b, 1), v.bzn[1]).astype(BF16))
-    v.orecv = over_y(v.osend)
     v.gkeep, v.gsend = call(
         qkv_back_body, [(tile, F32), (tile, BF16)],
         [("s", info)] + values(*v.grads0, *v.grads1) + anywhere(v.z, v.zx, v.zy, v.zu, v.zv), [w_scratch, sem16],
@@ -932,7 +931,7 @@
     v.qrx2, v.qry2 = over_x(v.qfx), over_y(v.qfy)
     rows_out("s", total_of("s"), 0)
     v.nt0 = plus(v.nt0, v.nx)
-    v.ny = over_y(v.nt0[1].astype(BF16))
+    v.ny = over_x(v.nt0[1].astype(BF16))
     v.ikeep, v.isend = call(
         input_body, [((piece, model), F32), ((piece, model), BF16)],
         [("s", info)] + values(v.gkeep, v.grecv, v.x, v.mid, v.gains), [], 1000, 8 << 20, vmem=16,

time: 375 us -> 371 us (0.989)
  waiting for transfers between devices: 101 us -> 94.5 us
    ppermute x77, waiting for transfers between devices: 101 us -> 94.5 us  [flip(): return lax.ppermute(value, axis, pairs)]
  transfers between devices with their start and end apart: 77 -> 77, of which waited for: 30 -> 30; matrix products, arithmetic and copies ran while one was open for 7% -> 8% of each run, Pallas kernels for 35% -> 35%
where the time goes in v4:
time: 371 us; the launch traced here: 367 us
  Pallas kernels  129 us (35%)
  waiting for transfers between devices  94.5 us (25%)
  starting transfers between devices  83.3 us (22%)
  other arithmetic  34.5 us (9%)
  local copies, waits for them, and re-layouts  22.8 us (6%)
    pallas_call x14, Pallas kernels, call(): pl.pallas_call(body, out_shape=[jax.ShapeDtypeStruct(shape, kind) for sha...  129 us
    ppermute x77, waiting for transfers between devices, flip(): return lax.ppermute(value, axis, pairs)  94.5 us
    ppermute x77, starting transfers between devices, flip(): return lax.ppermute(value, axis, pairs)  83.3 us
    unnamed x145, local copies, waits for them, and re-layouts  13.6 us
    select_n x20, other arithmetic, pick(): return jnp.where(flag == 1, when_one, when_zero)  9.05 us
  transfers between devices with their start and end apart: 77, of which 30 were waited for; matrix products, arithmetic and copies ran while one was open for 8% of the time, Pallas kernels for 35%

profile of v4, /device:TPU:0, one launch (start us, length us, event | category | flops | bytes accessed | tf_op | source)
XLA Modules:
  0.0 367.3 jit_solution(7109375425160983784)
XLA Ops:
  4.0 3.0 collective-permute-start.2
  7.0 3.6 collective-permute-start
  10.6 1.5 collective-permute-start.3
  13.8 2.2 collective-permute-done.3
  16.8 3.1 collective-permute-done.1.refs_2_
  21.0 1.6 collective-permute-start.4
  22.6 2.5 collective-permute-start.7
  26.4 10.5 %collective-permute-done.8 = bf16[288,256]{1,0:T(8,128)(2,1)S(1)} collective-permute-done((bf16[288,256]{1,0:T(8,128)(2,1)S(1)}, bf16[288,256]{1,0:T(8,128)(2,1)S(1)}, u32[]{:S(2)}, u32[]{:S(2)}) %collective-permute-start.8) | collective-permute-done | bytes 147488 | tf_op jit(solution)/shard_map/ppermute | solution.py:36
  39.8 1.5 collective-permute-start.9
  41.4 2.9 collective-permute-start.11
  44.3 2.6 collective-permute-start.12
  46.9 4.8 %collective-permute-done.11 = bf16[2,288,256]{2,1,0:T(8,128)(2,1)} collective-permute-done((bf16[2,288,256]{2,1,0:T(8,128)(2,1)S(1)}, bf16[2,288,256]{2,1,0:T(8,128)(2,1)}, u32[]{:S(2)}, u32[]{:S(2)}) %collective-permute-start.11) | collective-permute-done | bytes 294944 | tf_op jit(solution)/shard_map/ppermute | solution.py:36
  51.7 8.5 %collective-permute-done.12 = bf16[576,256]{1,0:T(8,128)(2,1)} collective-permute-done((bf16[576,256]{1,0:T(8,128)(2,1)}, bf16[576,256]{1,0:T(8,128)(2,1)}, u32[]{:S(2)}, u32[]{:S(2)}) %collective-permute-start.12) | collective-permute-done | bytes 294944 | tf_op jit(solution)/shard_map/ppermute | solution.py:36
  60.3 1.9 pad_maximum_fusion.7
  62.2 2.9 collective-permute-start.18
  65.1 1.7 pad_maximum_fusion.13
  66.8 1.5 collective-permute-start.17
  68.3 1.8 slice.396
  70.6 1.8 slice.397
  72.4 1.5 collective-permute-start.15
  77.7 7.0 %collective-permute-done.14.refs_12_.refs_8_.refs_10_ = bf16[2,400,256]{2,1,0:T(8,128)(2,1)} collective-permute-done((bf16[2,400,256]{2,1,0:T(8,128)(2,1)}, bf16[2,400,256]{2,1,0:T(8,128)(2,1)}, u32[]{:S(2)}, u32[]{:S(2)}) %collective-permute-start.14) | collective-permute-done | bytes 409632 | tf_op jit(solution)/shard_map/ppermute | solution.py:36
  86.6 2.7 collective-permute-start.21
  89.4 1.6 collective-permute-start.19
  91.0 1.4 collective-permute-start.20
  99.7 9.3 %shard_map.239 = (bf16[1024,1024]{1,0:T(8,128)(2,1)S(1)}, bf16[1024,1024]{1,0:T(8,128)(2,1)S(1)}, bf16[1024,512]{1,0:T(8,128)(2,1)S(1)}, bf16[1024,512]{1,0:T(8,...) custom-call(s32[6]{0:T(128)S(1)} %stack.139.refs_0_.info, bf16[2,256,1024]{2,1,0:T(8,128)(2,1)S(1)} %copy-done.5, ...), custom_call_target="tpu_custom_call" | custom-call | flops 3221225472 | bytes 14680064 | tf_op jit(solution)/shard_map/pallas_call | solution.py:52
  109.1 1.5 collective-permute-done.22.refs_14_
  114.4 1.6 collective-permute-start.26
  118.2 13.8 %shard_map.241 = (bf16[1024,512]{1,0:T(8,128)(2,1)S(1)}, f32[4,2,1024]{2,1,0:T(2,128)S(1)}) custom-call(bf16[1024,512]{1,0:T(8,128)(2,1)S(1)} %get-tuple-element.551.q, bf16[1024,512]{1,0:T(8,128)(2,1)S(1)} %get-tuple-element.552.k, bf16[1024,512]{1,0:T(8,128)(2,1)S(1)} %get-tuple-element.553.b), custom_call_target="tpu_custom_call" | custom-call | flops 2147483648 | bytes 4194304 | tf_op jit(solution)/shard_map/pallas_call | solution.py:52
  134.0 1.8 collective-permute-done.25.refs_6_.refs_20_.refs_14_
  138.6 2.1 shard_map.242.refs_2_.refs_4_
  140.8 2.3 collective-permute-done.30.refs_10_
  143.0 1.8 collective-permute-done.31.refs_11_
  144.8 3.8 %collective-permute-done.29.refs_6_ = bf16[256,1024]{1,0:T(8,128)(2,1)S(1)} collective-permute-done((bf16[256,1024]{1,0:T(8,128)(2,1)S(1)}, bf16[256,1024]{1,0:T(8,128)(2,1)S(1)}, u32[]{:S(2)}, u32[]{:S(2)}) %collective-permute-start.29) | collective-permute-done | bytes 524320 | tf_op jit(solution)/shard_map/ppermute | solution.py:36
  149.3 4.9 %collective-permute-done.33.refs_7_ = bf16[2,256,1024]{2,1,0:T(8,128)(2,1)S(1)} collective-permute-done((bf16[2,256,1024]{2,1,0:T(8,128)(2,1)S(1)}, bf16[2,256,1024]{2,1,0:T(8,128)(2,1)S(1)}, u32[]{:S(2)}, u32[]{:S(2)}) %collective-permute-start.33) | collective-permute-done | bytes 1048608 | tf_op jit(solution)/shard_map/ppermute | solution.py:36
  156.3 1.5 collective-permute-start.36
  158.3 23.8 %shard_map.243 = (bf16[1024,1024]{1,0:T(8,128)(2,1)S(1)}, bf16[1024,1024]{1,0:T(8,128)(2,1)}, bf16[1024,1024]{1,0:T(8,128)(2,1)}, bf16[1024,1024]{1,0:T(8,128)(2...) custom-call(s32[6]{0:T(128)S(1)} %stack.139.refs_0_.info, ...), custom_call_target="tpu_custom_call" | custom-call | flops 12079595520 | bytes 25165824 | tf_op jit(solution)/shard_map/pallas_call | solution.py:52
  183.7 1.5 collective-permute-start.38
  185.9 26.8 %shard_map.244 = (bf16[1024,1024]{1,0:T(8,128)(2,1)S(1)}, f32[2,256,1024]{2,1,0:T(8,128)}, bf16[2,256,1024]{2,1,0:T(8,128)(2,1)}, bf16[4,384,256]{2,1,0:T(8,128)...) custom-call(s32[6]{0:T(128)S(1)} %stack.139.refs_0_.info, ...), custom_call_target="tpu_custom_call" | custom-call | flops 14495514624 | bytes 25165824 | tf_op jit(solution)/shard_map/pallas_call | solution.py:52
  220.6 13.6 %shard_map.245 = (bf16[1024,512]{1,0:T(8,128)(2,1)}, f32[2,256,1024]{2,1,0:T(8,128)}, f32[8,1024]{1,0:T(8,128)}, bf16[4,320,256]{2,1,0:T(8,128)(2,1)}, bf16[4,32...) custom-call(s32[6]{0:T(128)} %copy-done.30, ...), custom_call_target="tpu_custom_call" | custom-call | flops 2147483648 | bytes 20971520 | tf_op jit(solution)/shard_map/pallas_call | solution.py:52
  235.2 4.4 %fusion.1 = bf16[2,256,1024]{2,1,0:T(8,128)(2,1)S(1)} fusion(f32[2,256,1024]{2,1,0:T(8,128)} %get-tuple-element.549, bf16[2,256,1024]{2,1,0:T(8,128)(2,1)} %collective-permute-done.44, bf16[2,2,256,1024]{3,2,1,0:T(8,128)(2,1)} %bitcast.21, bf16[2,2,256,1024]{3,2,1,0:T(8,128)(2,1)S(1)} %bitcast.187, bf16[2,2,256,1024]{3,2,1,0:T(8,128)(2,1)S(1)} %bitcast.188, ...), kind=kLoop, calls=%fused_computation.3 | loop fusion | flops 6815744 | bytes 10485765 | tf_op jit(solution)/shard_map/convert_element_type | solution.py:871
  241.2 1.7 convert_add_fusion.1
  243.4 1.6 collective-permute-start.45
  248.4 9.4 %shard_map.246 = (bf16[1024,256]{1,0:T(8,128)(2,1)S(1)}, bf16[1024,256]{1,0:T(8,128)(2,1)S(1)}, bf16[1024,256]{1,0:T(8,128)(2,1)S(1)}) custom-call(bf16[1024,512]{1,0:T(8,128)(2,1)S(1)} %copy-done.47, bf16[1024,512]{1,0:T(8,128)(2,1)S(1)} %copy-done.49, bf16[1024,512]{1,0:T(8,128)(2,1)S(1)} %copy-done.51, bf16[1024,512]{1,0:T(8,128)(2,1)S(1)} %copy-done.34, ...), custom_call_target="tpu_custom_call" | custom-call | flops 2684354560 | bytes 4194304 | tf_op jit(solution)/shard_map/pallas_call | solution.py:52
  257.8 5.2 %shard_map.247 = (bf16[2,400,256]{2,1,0:T(8,128)(2,1)S(1)}, bf16[4,400,256]{2,1,0:T(8,128)(2,1)S(1)}, bf16[2,400,256]{2,1,0:T(8,128)(2,1)S(1)}) custom-call(s32[6]{0:T(128)S(1)} %copy-done.31, bf16[1024,256]{1,0:T(8,128)(2,1)S(1)} %get-tuple-element.583.refs_1_.refs_4_, bf16[1024,256]{1,0:T(8,128)(2,1)S(1)} %get-tuple-element.584.refs_2_.refs_5_, ...), custom_call_target="tpu_custom_call" | custom-call | flops 1610612736 | bytes 7340032 | tf_op jit(solution)/shard_map/pallas_call | solution.py:52
  263.2 7.5 %collective-permute-done.47 = bf16[2,384,256]{2,1,0:T(8,128)(2,1)S(1)} collective-permute-done((bf16[2,384,256]{2,1,0:T(8,128)(2,1)S(1)}, bf16[2,384,256]{2,1,0:T(8,128)(2,1)S(1)}, u32[]{:S(2)}, u32[]{:S(2)}) %collective-permute-start.47) | collective-permute-done | bytes 393248 | tf_op jit(solution)/shard_map/ppermute | solution.py:36
  273.9 2.7 collective-permute-start.54
  277.5 9.4 %shard_map.248 = (bf16[1024,256]{1,0:T(8,128)(2,1)S(1)}, bf16[1024,256]{1,0:T(8,128)(2,1)S(1)}, bf16[1024,256]{1,0:T(8,128)(2,1)S(1)}) custom-call(bf16[1024,512]{1,0:T(8,128)(2,1)S(1)} %copy-done.47, bf16[1024,512]{1,0:T(8,128)(2,1)S(1)} %copy-done.49, bf16[1024,512]{1,0:T(8,128)(2,1)S(1)} %copy-done.51, bf16[1024,512]{1,0:T(8,128)(2,1)S(1)} %copy-done.34, ...), custom_call_target="tpu_custom_call" | custom-call | flops 2684354560 | bytes 4194304 | tf_op jit(solution)/shard_map/pallas_call | solution.py:52
  287.0 6.0 %shard_map.249 = (bf16[2,400,256]{2,1,0:T(8,128)(2,1)S(1)}, bf16[2,400,256]{2,1,0:T(8,128)(2,1)S(1)}, bf16[4,400,256]{2,1,0:T(8,128)(2,1)S(1)}) custom-call(s32[6]{0:T(128)S(1)} %copy-done.31, bf16[1024,256]{1,0:T(8,128)(2,1)S(1)} %get-tuple-element.580.refs_1_, bf16[1024,256]{1,0:T(8,128)(2,1)S(1)} %get-tuple-element.581.refs_2_, ...), custom_call_target="tpu_custom_call" | custom-call | flops 1610612736 | bytes 7340032 | tf_op jit(solution)/shard_map/pallas_call | solution.py:52
  297.7 1.7 collective-permute-start.57
  299.4 8.0 %shard_map.250 = (f32[2,256,1024]{2,1,0:T(8,128)S(1)}, bf16[2,256,1024]{2,1,0:T(8,128)(2,1)S(1)}) custom-call(s32[6]{0:T(128)S(1)} %copy-done.31, bf16[1024,256]{1,0:T(8,128)(2,1)S(1)} %get-tuple-element.580.refs_1_, bf16[1024,256]{1,0:T(8,128)(2,1)S(1)} %get-tuple-element.581.refs_2_, bf16[1024,256]{1,0:T(8,128)(2,1)S(1)} %get-tuple-element.639.refs_3_, ...), custom_call_target="tpu_custom_call" | custom-call | flops 3221225472 | bytes 14680064 | tf_op jit(solution)/shard_map/pallas_call | solution.py:52
  307.4 3.5 collective-permute-done.59
  311.1 1.6 collective-permute-start.64
  317.6 1.6 shard_map.251
  319.2 5.9 %collective-permute-done.62 = bf16[2,400,256]{2,1,0:T(8,128)(2,1)S(1)} collective-permute-done((bf16[2,400,256]{2,1,0:T(8,128)(2,1)S(1)}, bf16[2,400,256]{2,1,0:T(8,128)(2,1)S(1)}, u32[]{:S(2)}, u32[]{:S(2)}) %collective-permute-start.62) | collective-permute-done | bytes 409632 | tf_op jit(solution)/shard_map/ppermute | solution.py:36
  326.4 2.1 collective-permute-start.65
  333.1 4.0 %collective-permute-done.65 = bf16[400,256]{1,0:T(8,128)(2,1)S(1)} collective-permute-done((bf16[400,256]{1,0:T(8,128)(2,1)S(1)}, bf16[400,256]{1,0:T(8,128)(2,1)S(1)}, u32[]{:S(2)}, u32[]{:S(2)}) %collective-permute-start.65) | collective-permute-done | bytes 204832 | tf_op jit(solution)/shard_map/ppermute | solution.py:36
  337.1 5.2 %collective-permute-done.67 = bf16[256,1024]{1,0:T(8,128)(2,1)S(1)} collective-permute-done((bf16[256,1024]{1,0:T(8,128)(2,1)S(1)}, bf16[256,1024]{1,0:T(8,128)(2,1)S(1)}, u32[]{:S(2)}, u32[]{:S(2)}) %collective-permute-start.67) | collective-permute-done | bytes 524320 | tf_op jit(solution)/shard_map/ppermute | solution.py:36
  342.9 1.6 collective-permute-start.70
  345.8 2.3 collective-permute-start.69
  348.3 1.5 maximum_select_fusion
  349.8 3.1 collective-permute-done.70
  352.9 4.3 %collective-permute-done.69 = bf16[400,256]{1,0:T(8,128)(2,1)S(1)} collective-permute-done((bf16[400,256]{1,0:T(8,128)(2,1)S(1)}, bf16[400,256]{1,0:T(8,128)(2,1)S(1)}, u32[]{:S(2)}, u32[]{:S(2)}) %collective-permute-start.69) | collective-permute-done | bytes 204832 | tf_op jit(solution)/shard_map/ppermute | solution.py:36
  357.2 2.9 collective-permute-done.71
  363.3 1.5 fusion.5
  (354 shorter events, 81.6 us)
Async XLA Ops:
  4.0 15.9 %collective-permute-start.2 = (bf16[256,1024]{1,0:T(8,128)(2,1)S(1)}, bf16[256,1024]{1,0:T(8,128)(2,1)S(1)}, u32[]{:S(2)}, u32[]{:S(2)}) collective-permute-start(bf16[256,1024]{1,0:T(8,128)(2,1)S(1)} %select_bitcast_fusion.6), channel_id=1, source_target_pairs={{0,16},{8,24},{16,0},{24,8},{1,17},{9,25},{17,1},{25,9},{2,18},{10... | collective-permute-start | bytes 1572872 | tf_op jit(solution)/shard_map/ppermute | solution.py:36
  7.0 9.8 %collective-permute-start = (bf16[400,256]{1,0:T(8,128)(2,1)S(1)}, bf16[400,256]{1,0:T(8,128)(2,1)S(1)}, u32[]{:S(2)}, u32[]{:S(2)}) collective-permute-start(bf16[400,256]{1,0:T(8,128)(2,1)S(1)} %fusion.26.refs_0_), channel_id=1, source_target_pairs={{0,6},{1,7},{2,4},{3,5},{4,2},{5,3},{6,0},{7,1},{8,14},{9,15},{10,... | collective-permute-start | bytes 614408 | tf_op jit(solution)/shard_map/ppermute | solution.py:36
  10.6 9.3 %collective-permute-start.1 = (bf16[400,256]{1,0:T(8,128)(2,1)S(1)}, bf16[400,256]{1,0:T(8,128)(2,1)S(1)}, u32[]{:S(2)}, u32[]{:S(2)}) collective-permute-start(bf16[400,256]{1,0:T(8,128)(2,1)S(1)} %fusion.26.refs_0_), channel_id=1, source_target_pairs={{0,2},{1,3},{2,0},{3,1},{4,6},{5,7},{6,4},{7,5},{8,10},{9,11},{10,... | collective-permute-start | bytes 614408 | tf_op jit(solution)/shard_map/ppermute | solution.py:36
  20.1 16.9 %collective-permute-start.6 = (bf16[2,256,1024]{2,1,0:T(8,128)(2,1)S(1)}, bf16[2,256,1024]{2,1,0:T(8,128)(2,1)S(1)}, u32[]{:S(2)}, u32[]{:S(2)}) collective-permute-start(bf16[2,256,1024]{2,1,0:T(8,128)(2,1)S(1)} %pad_maximum_fusion.3), channel_id=1, source_target_pairs={{0,8},{8,0},{16,24},{24,16},{1,9},{9,1},{17,25},{25,17},{2,10},{10... | collective-permute-start | bytes 3145736 | tf_op jit(solution)/shard_map/ppermute | solution.py:36
  20.2 16.8 %collective-permute-start.5 = (bf16[256,1024]{1,0:T(8,128)(2,1)S(1)}, bf16[256,1024]{1,0:T(8,128)(2,1)S(1)}, u32[]{:S(2)}, u32[]{:S(2)}) collective-permute-start(bf16[256,1024]{1,0:T(8,128)(2,1)S(1)} %get-tuple-element.345), channel_id=1, source_target_pairs={{0,16},{8,24},{16,0},{24,8},{1,17},{9,25},{17,1},{25,9},{2,18},{10... | collective-permute-start | bytes 1572872 | tf_op jit(solution)/shard_map/ppermute | solution.py:36
  21.0 16.0 %collective-permute-start.4 = (bf16[400,256]{1,0:T(8,128)(2,1)S(1)}, bf16[400,256]{1,0:T(8,128)(2,1)S(1)}, u32[]{:S(2)}, u32[]{:S(2)}) collective-permute-start(bf16[400,256]{1,0:T(8,128)(2,1)S(1)} %collective-permute-done.refs_1_), channel_id=1, source_target_pairs={{0,2},{1,3},{2,0},{3,1},{4,6},{5,7},{6,4},{7,5},{8,10},{9,11},{10,... | collective-permute-start | bytes 614408 | tf_op jit(solution)/shard_map/ppermute | solution.py:36
  22.6 14.4 %collective-permute-start.7 = (bf16[1,320,256]{2,1,0:T(8,128)(2,1)S(1)}, bf16[1,320,256]{2,1,0:T(8,128)(2,1)S(1)}, u32[]{:S(2)}, u32[]{:S(2)}) collective-permute-start(bf16[1,320,256]{2,1,0:T(8,128)(2,1)S(1)} %fusion.38.refs_8_), channel_id=1, source_target_pairs={{0,6},{1,7},{2,4},{3,5},{4,2},{5,3},{6,0},{7,1},{8,14},{9,15},{10,... | collective-permute-start | bytes 491528 | tf_op jit(solution)/shard_map/ppermute | solution.py:36
  25.1 11.9 %collective-permute-start.8 = (bf16[288,256]{1,0:T(8,128)(2,1)S(1)}, bf16[288,256]{1,0:T(8,128)(2,1)S(1)}, u32[]{:S(2)}, u32[]{:S(2)}) collective-permute-start(bf16[288,256]{1,0:T(8,128)(2,1)S(1)} %pad_maximum_fusion.19), channel_id=1, source_target_pairs={{0,6},{1,7},{2,4},{3,5},{4,2},{5,3},{6,0},{7,1},{8,14},{9,15},{10,... | collective-permute-start | bytes 442376 | tf_op jit(solution)/shard_map/ppermute | solution.py:36
  39.2 21.1 %collective-permute-start.13 = (bf16[2,256,1024]{2,1,0:T(8,128)(2,1)}, bf16[2,256,1024]{2,1,0:T(8,128)(2,1)}, u32[]{:S(2)}, u32[]{:S(2)}) collective-permute-start(bf16[2,256,1024]{2,1,0:T(8,128)(2,1)} %pad_maximum_fusion.4), channel_id=1, source_target_pairs={{0,8},{8,0},{16,24},{24,16},{1,9},{9,1},{17,25},{25,17},{2,10},{10... | collective-permute-start | bytes 3145736 | tf_op jit(solution)/shard_map/ppermute | solution.py:36
  39.3 20.9 %collective-permute-start.10 = (bf16[4,400,256]{2,1,0:T(8,128)(2,1)S(1)}, bf16[4,400,256]{2,1,0:T(8,128)(2,1)}, u32[]{:S(2)}, u32[]{:S(2)}) collective-permute-start(bf16[4,400,256]{2,1,0:T(8,128)(2,1)S(1)} %shard_map.238.refs_9_.refs_7_), channel_id=1, source_target_pairs={{0,16},{8,24},{16,0},{24,8},{1,17},{9,25},{17,1},{25,9},{2,18},{10... | collective-permute-start | bytes 2457608 | tf_op jit(solution)/shard_map/ppermute | solution.py:36
  39.8 20.5 %collective-permute-start.9 = (bf16[4,400,256]{2,1,0:T(8,128)(2,1)S(1)}, bf16[4,400,256]{2,1,0:T(8,128)(2,1)}, u32[]{:S(2)}, u32[]{:S(2)}) collective-permute-start(bf16[4,400,256]{2,1,0:T(8,128)(2,1)S(1)} %shard_map.238.refs_9_.refs_7_), channel_id=1, source_target_pairs={{0,1},{1,0},{2,3},{3,2},{4,5},{5,4},{6,7},{7,6},{8,9},{9,8},{10,11... | collective-permute-start | bytes 2457608 | tf_op jit(solution)/shard_map/ppermute | solution.py:36
  41.4 10.3 %collective-permute-start.11 = (bf16[2,288,256]{2,1,0:T(8,128)(2,1)S(1)}, bf16[2,288,256]{2,1,0:T(8,128)(2,1)}, u32[]{:S(2)}, u32[]{:S(2)}) collective-permute-start(bf16[2,288,256]{2,1,0:T(8,128)(2,1)S(1)} %pad_maximum_fusion.14), channel_id=1, source_target_pairs={{0,2},{1,3},{2,0},{3,1},{4,6},{5,7},{6,4},{7,5},{8,10},{9,11},{10,... | collective-permute-start | bytes 884744 | tf_op jit(solution)/shard_map/ppermute | solution.py:36
  44.3 15.9 %collective-permute-start.12 = (bf16[576,256]{1,0:T(8,128)(2,1)}, bf16[576,256]{1,0:T(8,128)(2,1)}, u32[]{:S(2)}, u32[]{:S(2)}) collective-permute-start(bf16[576,256]{1,0:T(8,128)(2,1)} %fusion.24), channel_id=1, source_target_pairs={{0,6},{1,7},{2,4},{3,5},{4,2},{5,3},{6,0},{7,1},{8,14},{9,15},{10,... | collective-permute-start | bytes 884744 | tf_op jit(solution)/shard_map/ppermute | solution.py:36
  62.2 22.5 %collective-permute-start.18 = (bf16[2,576,256]{2,1,0:T(8,128)(2,1)}, bf16[2,576,256]{2,1,0:T(8,128)(2,1)}, u32[]{:S(2)}, u32[]{:S(2)}) collective-permute-start(bf16[2,576,256]{2,1,0:T(8,128)(2,1)} %pad_maximum_fusion.7), channel_id=1, source_target_pairs={{0,2},{1,3},{2,0},{3,1},{4,6},{5,7},{6,4},{7,5},{8,10},{9,11},{10,... | collective-permute-start | bytes 1769480 | tf_op jit(solution)/shard_map/ppermute | solution.py:36
  66.8 11.0 %collective-permute-start.17 = (bf16[2,320,256]{2,1,0:T(8,128)(2,1)}, bf16[2,320,256]{2,1,0:T(8,128)(2,1)}, u32[]{:S(2)}, u32[]{:S(2)}) collective-permute-start(bf16[2,320,256]{2,1,0:T(8,128)(2,1)} %pad_maximum_fusion.13), channel_id=1, source_target_pairs={{0,16},{8,24},{16,0},{24,8},{1,17},{9,25},{17,1},{25,9},{2,18},{10... | collective-permute-start | bytes 983048 | tf_op jit(solution)/shard_map/ppermute | solution.py:36
  70.1 14.6 %collective-permute-start.14 = (bf16[2,400,256]{2,1,0:T(8,128)(2,1)}, bf16[2,400,256]{2,1,0:T(8,128)(2,1)}, u32[]{:S(2)}, u32[]{:S(2)}) collective-permute-start(bf16[2,400,256]{2,1,0:T(8,128)(2,1)} %slice.396), channel_id=1, source_target_pairs={{0,16},{8,24},{16,0},{24,8},{1,17},{9,25},{17,1},{25,9},{2,18},{10... | collective-permute-start | bytes 1228808 | tf_op jit(solution)/shard_map/ppermute | solution.py:36
  72.4 12.3 %collective-permute-start.15 = (bf16[2,400,256]{2,1,0:T(8,128)(2,1)}, bf16[2,400,256]{2,1,0:T(8,128)(2,1)}, u32[]{:S(2)}, u32[]{:S(2)}) collective-permute-start(bf16[2,400,256]{2,1,0:T(8,128)(2,1)} %slice.397), channel_id=1, source_target_pairs={{0,1},{1,0},{2,3},{3,2},{4,5},{5,4},{6,7},{7,6},{8,9},{9,8},{10,11... | collective-permute-start | bytes 1228808 | tf_op jit(solution)/shard_map/ppermute | solution.py:36
  86.6 22.4 %collective-permute-start.21 = (bf16[3,320,256]{2,1,0:T(8,128)(2,1)S(1)}, bf16[3,320,256]{2,1,0:T(8,128)(2,1)S(1)}, u32[]{:S(2)}, u32[]{:S(2)}) collective-permute-start(bf16[3,320,256]{2,1,0:T(8,128)(2,1)S(1)} %constant_dynamic-update-slice_fusion.refs_12_), channel_id=1, source_target_pairs={{0,6},{1,7},{2,4},{3,5},{4,2},{5,3},{6,0},{7,1},{8,14},{9,15},{10,... | collective-permute-start | bytes 1474568 | tf_op jit(solution)/shard_map/ppermute | solution.py:36
  89.3 21.2 %collective-permute-start.22 = (bf16[3,320,256]{2,1,0:T(8,128)(2,1)S(1)}, bf16[3,320,256]{2,1,0:T(8,128)(2,1)S(1)}, u32[]{:S(2)}, u32[]{:S(2)}) collective-permute-start(bf16[3,320,256]{2,1,0:T(8,128)(2,1)S(1)} %constant_dynamic-update-slice_fusion.refs_12_), channel_id=1, source_target_pairs={{0,2},{1,3},{2,0},{3,1},{4,6},{5,7},{6,4},{7,5},{8,10},{9,11},{10,... | collective-permute-start | bytes 1474568 | tf_op jit(solution)/shard_map/ppermute | solution.py:36
  89.4 21.2 %collective-permute-start.19 = (bf16[4,288,256]{2,1,0:T(8,128)(2,1)S(1)}, bf16[4,288,256]{2,1,0:T(8,128)(2,1)S(1)}, u32[]{:S(2)}, u32[]{:S(2)}) collective-permute-start(bf16[4,288,256]{2,1,0:T(8,128)(2,1)S(1)} %shard_map.240.refs_2_.refs_16_.refs_10_), channel_id=1, source_target_pairs={{0,1},{1,0},{2,3},{3,2},{4,5},{5,4},{6,7},{7,6},{8,9},{9,8},{10,11... | collective-permute-start | bytes 1769480 | tf_op jit(solution)/shard_map/ppermute | solution.py:36
  91.0 19.6 %collective-permute-start.20 = (bf16[4,288,256]{2,1,0:T(8,128)(2,1)S(1)}, bf16[4,288,256]{2,1,0:T(8,128)(2,1)S(1)}, u32[]{:S(2)}, u32[]{:S(2)}) collective-permute-start(bf16[4,288,256]{2,1,0:T(8,128)(2,1)S(1)} %shard_map.240.refs_2_.refs_16_.refs_10_), channel_id=1, source_target_pairs={{0,16},{8,24},{16,0},{24,8},{1,17},{9,25},{17,1},{25,9},{2,18},{10... | collective-permute-start | bytes 1769480 | tf_op jit(solution)/shard_map/ppermute | solution.py:36
  94.3 14.7 %collective-permute-start.23 = (bf16[2,192,256]{2,1,0:T(8,128)(2,1)S(1)}, bf16[2,192,256]{2,1,0:T(8,128)(2,1)S(1)}, u32[]{:S(2)}, u32[]{:S(2)}) collective-permute-start(bf16[2,192,256]{2,1,0:T(8,128)(2,1)S(1)} %pad_maximum_fusion.18), channel_id=1, source_target_pairs={{0,8},{8,0},{16,24},{24,16},{1,9},{9,1},{17,25},{25,17},{2,10},{10... | collective-permute-start | bytes 589832 | tf_op jit(solution)/shard_map/ppermute | solution.py:36
  111.9 23.9 %collective-permute-start.27 = (bf16[2,576,256]{2,1,0:T(8,128)(2,1)S(1)}, bf16[2,576,256]{2,1,0:T(8,128)(2,1)S(1)}, u32[]{:S(2)}, u32[]{:S(2)}) collective-permute-start(bf16[2,576,256]{2,1,0:T(8,128)(2,1)S(1)} %pad_maximum_fusion.9.refs_9_), channel_id=1, source_target_pairs={{0,16},{8,24},{16,0},{24,8},{1,17},{9,25},{17,1},{25,9},{2,18},{10... | collective-permute-start | bytes 1769480 | tf_op jit(solution)/shard_map/ppermute | solution.py:36
  114.4 21.4 %collective-permute-start.26 = (bf16[2,576,256]{2,1,0:T(8,128)(2,1)S(1)}, bf16[2,576,256]{2,1,0:T(8,128)(2,1)S(1)}, u32[]{:S(2)}, u32[]{:S(2)}) collective-permute-start(bf16[2,576,256]{2,1,0:T(8,128)(2,1)S(1)} %pad_maximum_fusion.8.refs_5_), channel_id=1, source_target_pairs={{0,1},{1,0},{2,3},{3,2},{4,5},{5,4},{6,7},{7,6},{8,9},{9,8},{10,11... | collective-permute-start | bytes 1769480 | tf_op jit(solution)/shard_map/ppermute | solution.py:36
  116.0 19.8 %collective-permute-start.28 = (bf16[3,320,256]{2,1,0:T(8,128)(2,1)S(1)}, bf16[3,320,256]{2,1,0:T(8,128)(2,1)S(1)}, u32[]{:S(2)}, u32[]{:S(2)}) collective-permute-start(bf16[3,320,256]{2,1,0:T(8,128)(2,1)S(1)} %collective-permute-done.21.refs_13_), channel_id=1, source_target_pairs={{0,2},{1,3},{2,0},{3,1},{4,6},{5,7},{6,4},{7,5},{8,10},{9,11},{10,... | collective-permute-start | bytes 1474568 | tf_op jit(solution)/shard_map/ppermute | solution.py:36
  116.8 17.2 %collective-permute-start.24 = (bf16[2,288,256]{2,1,0:T(8,128)(2,1)S(1)}, bf16[2,288,256]{2,1,0:T(8,128)(2,1)S(1)}, u32[]{:S(2)}, u32[]{:S(2)}) collective-permute-start(bf16[2,288,256]{2,1,0:T(8,128)(2,1)S(1)} %slice.406), channel_id=1, source_target_pairs={{0,16},{8,24},{16,0},{24,8},{1,17},{9,25},{17,1},{25,9},{2,18},{10... | collective-permute-start | bytes 884744 | tf_op jit(solution)/shard_map/ppermute | solution.py:36
  117.6 18.2 %collective-permute-start.25 = (bf16[2,288,256]{2,1,0:T(8,128)(2,1)S(1)}, bf16[2,288,256]{2,1,0:T(8,128)(2,1)S(1)}, u32[]{:S(2)}, u32[]{:S(2)}) collective-permute-start(bf16[2,288,256]{2,1,0:T(8,128)(2,1)S(1)} %slice.407), channel_id=1, source_target_pairs={{0,1},{1,0},{2,3},{3,2},{4,5},{5,4},{6,7},{7,6},{8,9},{9,8},{10,11... | collective-permute-start | bytes 884744 | tf_op jit(solution)/shard_map/ppermute | solution.py:36
  135.8 12.7 %collective-permute-start.29 = (bf16[256,1024]{1,0:T(8,128)(2,1)S(1)}, bf16[256,1024]{1,0:T(8,128)(2,1)S(1)}, u32[]{:S(2)}, u32[]{:S(2)}) collective-permute-start(bf16[256,1024]{1,0:T(8,128)(2,1)S(1)} %copy-done.62), channel_id=1, source_target_pairs={{0,16},{8,24},{16,0},{24,8},{1,17},{9,25},{17,1},{25,9},{2,18},{10... | collective-permute-start | bytes 1572872 | tf_op jit(solution)/shard_map/ppermute | solution.py:36
  137.7 7.1 %collective-permute-start.31 = (bf16[1,320,256]{2,1,0:T(8,128)(2,1)S(1)}, bf16[1,320,256]{2,1,0:T(8,128)(2,1)S(1)}, u32[]{:S(2)}, u32[]{:S(2)}) collective-permute-start(bf16[1,320,256]{2,1,0:T(8,128)(2,1)S(1)} %copy-done.38), channel_id=1, source_target_pairs={{0,2},{1,3},{2,0},{3,1},{4,6},{5,7},{6,4},{7,5},{8,10},{9,11},{10,... | collective-permute-start | bytes 491528 | tf_op jit(solution)/shard_map/ppermute | solution.py:36
  154.2 29.2 %collective-permute-start.34 = (bf16[2,576,256]{2,1,0:T(8,128)(2,1)S(1)}, bf16[2,576,256]{2,1,0:T(8,128)(2,1)S(1)}, u32[]{:S(2)}, u32[]{:S(2)}) collective-permute-start(bf16[2,576,256]{2,1,0:T(8,128)(2,1)S(1)} %pad_maximum_fusion.8.refs_5_), channel_id=1, source_target_pairs={{0,16},{8,24},{16,0},{24,8},{1,17},{9,25},{17,1},{25,9},{2,18},{10... | collective-permute-start | bytes 1769480 | tf_op jit(solution)/shard_map/ppermute | solution.py:36
  155.0 28.5 %collective-permute-start.35 = (bf16[2,576,256]{2,1,0:T(8,128)(2,1)S(1)}, bf16[2,576,256]{2,1,0:T(8,128)(2,1)S(1)}, u32[]{:S(2)}, u32[]{:S(2)}) collective-permute-start(bf16[2,576,256]{2,1,0:T(8,128)(2,1)S(1)} %collective-permute-done.26.refs_6_), channel_id=1, source_target_pairs={{0,16},{8,24},{16,0},{24,8},{1,17},{9,25},{17,1},{25,9},{2,18},{10... | collective-permute-start | bytes 1769480 | tf_op jit(solution)/shard_map/ppermute | solution.py:36
  156.3 27.2 %collective-permute-start.36 = (bf16[2,576,256]{2,1,0:T(8,128)(2,1)S(1)}, bf16[2,576,256]{2,1,0:T(8,128)(2,1)S(1)}, u32[]{:S(2)}, u32[]{:S(2)}) collective-permute-start(bf16[2,576,256]{2,1,0:T(8,128)(2,1)S(1)} %pad_maximum_fusion.9.refs_9_), channel_id=1, source_target_pairs={{0,1},{1,0},{2,3},{3,2},{4,5},{5,4},{6,7},{7,6},{8,9},{9,8},{10,11... | collective-permute-start | bytes 1769480 | tf_op jit(solution)/shard_map/ppermute | solution.py:36
  157.8 26.0 %collective-permute-start.37 = (bf16[2,576,256]{2,1,0:T(8,128)(2,1)S(1)}, bf16[2,576,256]{2,1,0:T(8,128)(2,1)S(1)}, u32[]{:S(2)}, u32[]{:S(2)}) collective-permute-start(bf16[2,576,256]{2,1,0:T(8,128)(2,1)S(1)} %collective-permute-done.27.refs_11_), channel_id=1, source_target_pairs={{0,1},{1,0},{2,3},{3,2},{4,5},{5,4},{6,7},{7,6},{8,9},{9,8},{10,11... | collective-permute-start | bytes 1769480 | tf_op jit(solution)/shard_map/ppermute | solution.py:36
  183.7 31.0 %collective-permute-start.38 = (bf16[4,480,256]{2,1,0:T(8,128)(2,1)S(1)}, bf16[4,480,256]{2,1,0:T(8,128)(2,1)S(1)}, u32[]{:S(2)}, u32[]{:S(2)}) collective-permute-start(bf16[4,480,256]{2,1,0:T(8,128)(2,1)S(1)} %get-tuple-element.494), channel_id=1, source_target_pairs={{0,1},{1,0},{2,3},{3,2},{4,5},{5,4},{6,7},{7,6},{8,9},{9,8},{10,11... | collective-permute-start | bytes 2949128 | tf_op jit(solution)/shard_map/ppermute | solution.py:36
  185.2 29.6 %collective-permute-start.39 = (bf16[4,480,256]{2,1,0:T(8,128)(2,1)S(1)}, bf16[4,480,256]{2,1,0:T(8,128)(2,1)S(1)}, u32[]{:S(2)}, u32[]{:S(2)}) collective-permute-start(bf16[4,480,256]{2,1,0:T(8,128)(2,1)S(1)} %get-tuple-element.495), channel_id=1, source_target_pairs={{0,16},{8,24},{16,0},{24,8},{1,17},{9,25},{17,1},{25,9},{2,18},{10... | collective-permute-start | bytes 2949128 | tf_op jit(solution)/shard_map/ppermute | solution.py:36
  214.9 20.3 %collective-permute-start.44 = (bf16[2,256,1024]{2,1,0:T(8,128)(2,1)}, bf16[2,256,1024]{2,1,0:T(8,128)(2,1)}, u32[]{:S(2)}, u32[]{:S(2)}) collective-permute-start(bf16[2,256,1024]{2,1,0:T(8,128)(2,1)} %get-tuple-element.522), channel_id=1, source_target_pairs={{0,8},{8,0},{16,24},{24,16},{1,9},{9,1},{17,25},{25,17},{2,10},{10... | collective-permute-start | bytes 3145736 | tf_op jit(solution)/shard_map/ppermute | solution.py:36
  215.4 19.8 %collective-permute-start.43 = (bf16[4,384,256]{2,1,0:T(8,128)(2,1)}, bf16[4,384,256]{2,1,0:T(8,128)(2,1)}, u32[]{:S(2)}, u32[]{:S(2)}) collective-permute-start(bf16[4,384,256]{2,1,0:T(8,128)(2,1)} %get-tuple-element.520), channel_id=1, source_target_pairs={{0,2},{1,3},{2,0},{3,1},{4,6},{5,7},{6,4},{7,5},{8,10},{9,11},{10,... | collective-permute-start | bytes 2359304 | tf_op jit(solution)/shard_map/ppermute | solution.py:36
  216.9 17.4 %collective-permute-start.42 = (bf16[2,480,256]{2,1,0:T(8,128)(2,1)}, bf16[2,480,256]{2,1,0:T(8,128)(2,1)S(1)}, u32[]{:S(2)}, u32[]{:S(2)}) collective-permute-start(bf16[2,480,256]{2,1,0:T(8,128)(2,1)} %add_convert_fusion.1), channel_id=1, source_target_pairs={{0,16},{8,24},{16,0},{24,8},{1,17},{9,25},{17,1},{25,9},{2,18},{10... | collective-permute-start | bytes 1474568 | tf_op jit(solution)/shard_map/ppermute | solution.py:36
  219.0 15.3 %collective-permute-start.41 = (bf16[2,480,256]{2,1,0:T(8,128)(2,1)}, bf16[2,480,256]{2,1,0:T(8,128)(2,1)}, u32[]{:S(2)}, u32[]{:S(2)}) collective-permute-start(bf16[2,480,256]{2,1,0:T(8,128)(2,1)} %add_convert_fusion.2), channel_id=1, source_target_pairs={{0,1},{1,0},{2,3},{3,2},{4,5},{5,4},{6,7},{7,6},{8,9},{9,8},{10,11... | collective-permute-start | bytes 1474568 | tf_op jit(solution)/shard_map/ppermute | solution.py:36
  239.8 31.0 %collective-permute-start.50 = (bf16[256,1024]{1,0:T(8,128)(2,1)S(1)}, bf16[256,1024]{1,0:T(8,128)(2,1)S(1)}, u32[]{:S(2)}, u32[]{:S(2)}) collective-permute-start(bf16[256,1024]{1,0:T(8,128)(2,1)S(1)} %get-tuple-element.680), channel_id=1, source_target_pairs={{0,16},{8,24},{16,0},{24,8},{1,17},{9,25},{17,1},{25,9},{2,18},{10... | collective-permute-start | bytes 1572872 | tf_op jit(solution)/shard_map/ppermute | solution.py:36
  243.1 28.4 %collective-permute-start.48 = (bf16[4,384,256]{2,1,0:T(8,128)(2,1)S(1)}, bf16[4,384,256]{2,1,0:T(8,128)(2,1)S(1)}, u32[]{:S(2)}, u32[]{:S(2)}) collective-permute-start(bf16[4,384,256]{2,1,0:T(8,128)(2,1)S(1)} %copy-done.36), channel_id=1, source_target_pairs={{0,2},{1,3},{2,0},{3,1},{4,6},{5,7},{6,4},{7,5},{8,10},{9,11},{10,... | collective-permute-start | bytes 2359304 | tf_op jit(solution)/shard_map/ppermute | solution.py:36
  243.4 27.3 %collective-permute-start.45 = (bf16[4,320,256]{2,1,0:T(8,128)(2,1)S(1)}, bf16[4,320,256]{2,1,0:T(8,128)(2,1)S(1)}, u32[]{:S(2)}, u32[]{:S(2)}) collective-permute-start(bf16[4,320,256]{2,1,0:T(8,128)(2,1)S(1)} %copy-done.71), channel_id=1, source_target_pairs={{0,1},{1,0},{2,3},{3,2},{4,5},{5,4},{6,7},{7,6},{8,9},{9,8},{10,11... | collective-permute-start | bytes 1966088 | tf_op jit(solution)/shard_map/ppermute | solution.py:36
  245.0 25.8 %collective-permute-start.46 = (bf16[4,320,256]{2,1,0:T(8,128)(2,1)S(1)}, bf16[4,320,256]{2,1,0:T(8,128)(2,1)S(1)}, u32[]{:S(2)}, u32[]{:S(2)}) collective-permute-start(bf16[4,320,256]{2,1,0:T(8,128)(2,1)S(1)} %copy-done.70), channel_id=1, source_target_pairs={{0,16},{8,24},{16,0},{24,8},{1,17},{9,25},{17,1},{25,9},{2,18},{10... | collective-permute-start | bytes 1966088 | tf_op jit(solution)/shard_map/ppermute | solution.py:36
  247.2 23.6 %collective-permute-start.47 = (bf16[2,384,256]{2,1,0:T(8,128)(2,1)S(1)}, bf16[2,384,256]{2,1,0:T(8,128)(2,1)S(1)}, u32[]{:S(2)}, u32[]{:S(2)}) collective-permute-start(bf16[2,384,256]{2,1,0:T(8,128)(2,1)S(1)} %slice.494), channel_id=1, source_target_pairs={{0,6},{1,7},{2,4},{3,5},{4,2},{5,3},{6,0},{7,1},{8,14},{9,15},{10,... | collective-permute-start | bytes 1179656 | tf_op jit(solution)/shard_map/ppermute | solution.py:36
  271.7 21.8 %collective-permute-start.55 = (bf16[2,480,256]{2,1,0:T(8,128)(2,1)S(1)}, bf16[2,480,256]{2,1,0:T(8,128)(2,1)S(1)}, u32[]{:S(2)}, u32[]{:S(2)}) collective-permute-start(bf16[2,480,256]{2,1,0:T(8,128)(2,1)S(1)} %pad_maximum_fusion.11), channel_id=1, source_target_pairs={{0,2},{1,3},{2,0},{3,1},{4,6},{5,7},{6,4},{7,5},{8,10},{9,11},{10,... | collective-permute-start | bytes 1474568 | tf_op jit(solution)/shard_map/ppermute | solution.py:36
  271.8 21.7 %collective-permute-start.51 = (bf16[4,400,256]{2,1,0:T(8,128)(2,1)S(1)}, bf16[4,400,256]{2,1,0:T(8,128)(2,1)S(1)}, u32[]{:S(2)}, u32[]{:S(2)}) collective-permute-start(bf16[4,400,256]{2,1,0:T(8,128)(2,1)S(1)} %get-tuple-element.564), channel_id=1, source_target_pairs={{0,16},{8,24},{16,0},{24,8},{1,17},{9,25},{17,1},{25,9},{2,18},{10... | collective-permute-start | bytes 2457608 | tf_op jit(solution)/shard_map/ppermute | solution.py:36
  273.2 19.9 %collective-permute-start.53 = (bf16[2,320,256]{2,1,0:T(8,128)(2,1)S(1)}, bf16[2,320,256]{2,1,0:T(8,128)(2,1)S(1)}, u32[]{:S(2)}, u32[]{:S(2)}) collective-permute-start(bf16[2,320,256]{2,1,0:T(8,128)(2,1)S(1)} %add_convert_fusion.7), channel_id=1, source_target_pairs={{0,1},{1,0},{2,3},{3,2},{4,5},{5,4},{6,7},{7,6},{8,9},{9,8},{10,11... | collective-permute-start | bytes 983048 | tf_op jit(solution)/shard_map/ppermute | solution.py:36
  273.9 19.6 %collective-permute-start.54 = (bf16[2,384,256]{2,1,0:T(8,128)(2,1)S(1)}, bf16[2,384,256]{2,1,0:T(8,128)(2,1)S(1)}, u32[]{:S(2)}, u32[]{:S(2)}) collective-permute-start(bf16[2,384,256]{2,1,0:T(8,128)(2,1)S(1)} %slice.430), channel_id=1, source_target_pairs={{0,6},{1,7},{2,4},{3,5},{4,2},{5,3},{6,0},{7,1},{8,14},{9,15},{10,... | collective-permute-start | bytes 1179656 | tf_op jit(solution)/shard_map/ppermute | solution.py:36
  276.6 16.9 %collective-permute-start.52 = (bf16[2,400,256]{2,1,0:T(8,128)(2,1)S(1)}, bf16[2,400,256]{2,1,0:T(8,128)(2,1)S(1)}, u32[]{:S(2)}, u32[]{:S(2)}) collective-permute-start(bf16[2,400,256]{2,1,0:T(8,128)(2,1)S(1)} %get-tuple-element.565), channel_id=1, source_target_pairs={{0,1},{1,0},{2,3},{3,2},{4,5},{5,4},{6,7},{7,6},{8,9},{9,8},{10,11... | collective-permute-start | bytes 1228808 | tf_op jit(solution)/shard_map/ppermute | solution.py:36
  293.8 17.1 %collective-permute-start.58 = (bf16[2,384,256]{2,1,0:T(8,128)(2,1)S(1)}, bf16[2,384,256]{2,1,0:T(8,128)(2,1)S(1)}, u32[]{:S(2)}, u32[]{:S(2)}) collective-permute-start(bf16[2,384,256]{2,1,0:T(8,128)(2,1)S(1)} %get-tuple-element.673), channel_id=1, source_target_pairs={{0,16},{8,24},{16,0},{24,8},{1,17},{9,25},{17,1},{25,9},{2,18},{10... | collective-permute-start | bytes 1179656 | tf_op jit(solution)/shard_map/ppermute | solution.py:36
  295.2 15.7 %collective-permute-start.56 = (bf16[2,400,256]{2,1,0:T(8,128)(2,1)S(1)}, bf16[2,400,256]{2,1,0:T(8,128)(2,1)S(1)}, u32[]{:S(2)}, u32[]{:S(2)}) collective-permute-start(bf16[2,400,256]{2,1,0:T(8,128)(2,1)S(1)} %get-tuple-element.591), channel_id=1, source_target_pairs={{0,1},{1,0},{2,3},{3,2},{4,5},{5,4},{6,7},{7,6},{8,9},{9,8},{10,11... | collective-permute-start | bytes 1228808 | tf_op jit(solution)/shard_map/ppermute | solution.py:36
  296.3 14.6 %collective-permute-start.59 = (bf16[2,320,256]{2,1,0:T(8,128)(2,1)S(1)}, bf16[2,320,256]{2,1,0:T(8,128)(2,1)S(1)}, u32[]{:S(2)}, u32[]{:S(2)}) collective-permute-start(bf16[2,320,256]{2,1,0:T(8,128)(2,1)S(1)} %add_convert_fusion.6), channel_id=1, source_target_pairs={{0,16},{8,24},{16,0},{24,8},{1,17},{9,25},{17,1},{25,9},{2,18},{10... | collective-permute-start | bytes 983048 | tf_op jit(solution)/shard_map/ppermute | solution.py:36
  297.7 9.7 %collective-permute-start.57 = (bf16[480,256]{1,0:T(8,128)(2,1)S(1)}, bf16[480,256]{1,0:T(8,128)(2,1)S(1)}, u32[]{:S(2)}, u32[]{:S(2)}) collective-permute-start(bf16[480,256]{1,0:T(8,128)(2,1)S(1)} %get-tuple-element.697), channel_id=1, source_target_pairs={{0,6},{1,7},{2,4},{3,5},{4,2},{5,3},{6,0},{7,1},{8,14},{9,15},{10,... | collective-permute-start | bytes 737288 | tf_op jit(solution)/shard_map/ppermute | solution.py:36
  311.1 8.1 %collective-permute-start.64 = (bf16[384,256]{1,0:T(8,128)(2,1)S(1)}, bf16[384,256]{1,0:T(8,128)(2,1)S(1)}, u32[]{:S(2)}, u32[]{:S(2)}) collective-permute-start(bf16[384,256]{1,0:T(8,128)(2,1)S(1)} %fusion.29), channel_id=1, source_target_pairs={{0,1},{1,0},{2,3},{3,2},{4,5},{5,4},{6,7},{7,6},{8,9},{9,8},{10,11... | collective-permute-start | bytes 589832 | tf_op jit(solution)/shard_map/ppermute | solution.py:36
  313.7 11.5 %collective-permute-start.62 = (bf16[2,400,256]{2,1,0:T(8,128)(2,1)S(1)}, bf16[2,400,256]{2,1,0:T(8,128)(2,1)S(1)}, u32[]{:S(2)}, u32[]{:S(2)}) collective-permute-start(bf16[2,400,256]{2,1,0:T(8,128)(2,1)S(1)} %add_convert_fusion.3), channel_id=1, source_target_pairs={{0,16},{8,24},{16,0},{24,8},{1,17},{9,25},{17,1},{25,9},{2,18},{10... | collective-permute-start | bytes 1228808 | tf_op jit(solution)/shard_map/ppermute | solution.py:36
  314.6 11.2 %collective-permute-start.61 = (bf16[2,400,256]{2,1,0:T(8,128)(2,1)S(1)}, bf16[2,400,256]{2,1,0:T(8,128)(2,1)S(1)}, u32[]{:S(2)}, u32[]{:S(2)}) collective-permute-start(bf16[2,400,256]{2,1,0:T(8,128)(2,1)S(1)} %add_convert_fusion.4), channel_id=1, source_target_pairs={{0,1},{1,0},{2,3},{3,2},{4,5},{5,4},{6,7},{7,6},{8,9},{9,8},{10,11... | collective-permute-start | bytes 1228808 | tf_op jit(solution)/shard_map/ppermute | solution.py:36
  326.0 7.1 %collective-permute-start.66 = (bf16[320,256]{1,0:T(8,128)(2,1)S(1)}, bf16[320,256]{1,0:T(8,128)(2,1)S(1)}, u32[]{:S(2)}, u32[]{:S(2)}) collective-permute-start(bf16[320,256]{1,0:T(8,128)(2,1)S(1)} %fusion.34), channel_id=1, source_target_pairs={{0,2},{1,3},{2,0},{3,1},{4,6},{5,7},{6,4},{7,5},{8,10},{9,11},{10,... | collective-permute-start | bytes 491528 | tf_op jit(solution)/shard_map/ppermute | solution.py:36
  326.4 10.7 %collective-permute-start.65 = (bf16[400,256]{1,0:T(8,128)(2,1)S(1)}, bf16[400,256]{1,0:T(8,128)(2,1)S(1)}, u32[]{:S(2)}, u32[]{:S(2)}) collective-permute-start(bf16[400,256]{1,0:T(8,128)(2,1)S(1)} %fusion.27), channel_id=1, source_target_pairs={{0,2},{1,3},{2,0},{3,1},{4,6},{5,7},{6,4},{7,5},{8,10},{9,11},{10,... | collective-permute-start | bytes 614408 | tf_op jit(solution)/shard_map/ppermute | solution.py:36
  328.5 13.8 %collective-permute-start.67 = (bf16[256,1024]{1,0:T(8,128)(2,1)S(1)}, bf16[256,1024]{1,0:T(8,128)(2,1)S(1)}, u32[]{:S(2)}, u32[]{:S(2)}) collective-permute-start(bf16[256,1024]{1,0:T(8,128)(2,1)S(1)} %get-tuple-element.637), channel_id=1, source_target_pairs={{0,16},{8,24},{16,0},{24,8},{1,17},{9,25},{17,1},{25,9},{2,18},{10... | collective-permute-start | bytes 1572872 | tf_op jit(solution)/shard_map/ppermute | solution.py:36
  342.4 7.4 %collective-permute-start.72 = (bf16[320,256]{1,0:T(8,128)(2,1)S(1)}, bf16[320,256]{1,0:T(8,128)(2,1)S(1)}, u32[]{:S(2)}, u32[]{:S(2)}) collective-permute-start(bf16[320,256]{1,0:T(8,128)(2,1)S(1)} %fusion.35), channel_id=1, source_target_pairs={{0,2},{1,3},{2,0},{3,1},{4,6},{5,7},{6,4},{7,5},{8,10},{9,11},{10,... | collective-permute-start | bytes 491528 | tf_op jit(solution)/shard_map/ppermute | solution.py:36
  342.9 10.0 %collective-permute-start.70 = (bf16[320,256]{1,0:T(8,128)(2,1)S(1)}, bf16[320,256]{1,0:T(8,128)(2,1)S(1)}, u32[]{:S(2)}, u32[]{:S(2)}) collective-permute-start(bf16[320,256]{1,0:T(8,128)(2,1)S(1)} %fusion.17), channel_id=1, source_target_pairs={{0,6},{1,7},{2,4},{3,5},{4,2},{5,3},{6,0},{7,1},{8,14},{9,15},{10,... | collective-permute-start | bytes 491528 | tf_op jit(solution)/shard_map/ppermute | solution.py:36
  344.5 15.6 %collective-permute-start.73 = (bf16[256,1024]{1,0:T(8,128)(2,1)S(1)}, bf16[256,1024]{1,0:T(8,128)(2,1)S(1)}, u32[]{:S(2)}, u32[]{:S(2)}) collective-permute-start(bf16[256,1024]{1,0:T(8,128)(2,1)S(1)} %get-tuple-element.649), channel_id=1, source_target_pairs={{0,16},{8,24},{16,0},{24,8},{1,17},{9,25},{17,1},{25,9},{2,18},{10... | collective-permute-start | bytes 1572872 | tf_op jit(solution)/shard_map/ppermute | solution.py:36
  345.8 11.3 %collective-permute-start.69 = (bf16[400,256]{1,0:T(8,128)(2,1)S(1)}, bf16[400,256]{1,0:T(8,128)(2,1)S(1)}, u32[]{:S(2)}, u32[]{:S(2)}) collective-permute-start(bf16[400,256]{1,0:T(8,128)(2,1)S(1)} %fusion.12), channel_id=1, source_target_pairs={{0,6},{1,7},{2,4},{3,5},{4,2},{5,3},{6,0},{7,1},{8,14},{9,15},{10,... | collective-permute-start | bytes 614408 | tf_op jit(solution)/shard_map/ppermute | solution.py:36
  348.2 11.9 %collective-permute-start.71 = (bf16[400,256]{1,0:T(8,128)(2,1)S(1)}, bf16[400,256]{1,0:T(8,128)(2,1)S(1)}, u32[]{:S(2)}, u32[]{:S(2)}) collective-permute-start(bf16[400,256]{1,0:T(8,128)(2,1)S(1)} %fusion.28), channel_id=1, source_target_pairs={{0,2},{1,3},{2,0},{3,1},{4,6},{5,7},{6,4},{7,5},{8,10},{9,11},{10,... | collective-permute-start | bytes 614408 | tf_op jit(solution)/shard_map/ppermute | solution.py:36
  (88 other events, 950.6 us)

commit v5 on v4

--- a/solution.py
+++ b/solution.py
@@ -880,7 +880,7 @@
             attend_back_body, [((length, width), BF16)] * 3,
             values(v.q, v.k, v.b, v.datt, v.lse, v.cosine, v.sine),
             [pltpu.VMEM((length, 128), F32), pltpu.VMEM((length, 128), F32)],
-            5 * length * length * local, 4 << 20, length * length * pairs, vmem=26,
+            5 * length * length * local, 4 << 20, length * length * pairs, vmem=16,
             grid=(pairs // 2,), in_specs=[column] * 4 + [sums, table, table],
             out_specs=[target] * 3,
         )
@@ -894,7 +894,7 @@
             [("s", info)] + values(*(v.grads1 if side else v.grads0), v.h1, v.gains, v.gain2)
             + anywhere(*arrays),
             [pltpu.VMEM((BLOCKS, attn_rows, width), BF16), pltpu.VMEM((8, model), F32),
-             pltpu.SemaphoreType.DMA((8,))], 3 * narrow // 2, 7 << 20, vmem=24,
+             pltpu.SemaphoreType.DMA((8,))], 3 * narrow // 2, 7 << 20, vmem=14,
         )
 
     v.grads1 = attend_back(1)
@@ -919,7 +919,7 @@
     v.gkeep, v.gsend = call(
         qkv_back_body, [(tile, F32), (tile, BF16)],
         [("s", info)] + values(*v.grads0, *v.grads1) + anywhere(v.z, v.zx, v.zy, v.zu, v.zv), [w_scratch, sem16],
-        3 * narrow, 14 << 20, vmem=18,
+        3 * narrow, 14 << 20, vmem=14,
     )
     v.gkeep, v.gsend, v.qry, v.qrd, v.qky, v.qrx, v.qkx, v.qown, v.bt0, v.bzf, v.nt0, v.nx, v.srx, v.sry, v.srx2, v.sry2, v.sown, v.grads0, v.grads1, v.okeep, v.orecv = lax.optimization_barrier(
         (v.gkeep, v.gsend, v.qry, v.qrd, v.qky, v.qrx, v.qkx, v.qown, v.bt0, v.bzf, v.nt0, v.nx, v.srx, v.sry, v.srx2, v.sry2, v.sown, v.grads0, v.grads1, v.okeep, v.orecv))
@@ -934,7 +934,7 @@
     v.ny = over_x(v.nt0[1].astype(BF16))
     v.ikeep, v.isend = call(
         input_body, [((piece, model), F32), ((piece, model), BF16)],
-        [("s", info)] + values(v.gkeep, v.grecv, v.x, v.mid, v.gains), [], 1000, 8 << 20, vmem=16,
+        [("s", info)] + values(v.gkeep, v.grecv, v.x, v.mid, v.gains), [], 1000, 8 << 20, vmem=12,
     )
     v.ikeep, v.isend, v.qrx, v.qry, v.qrx2, v.qry2, v.qown, v.st, v.sm, v.nt0, v.ny, v.grads0, v.grads1 = lax.optimization_barrier(
         (v.ikeep, v.isend, v.qrx, v.qry, v.qrx2, v.qry2, v.qown, v.st, v.sm, v.nt0, v.ny, v.grads0, v.grads1))

time: 371 us -> 371 us (level)
  no operation moved by 1% of the time
where the time goes in v5:
time: 371 us; the launch traced here: 367 us
  Pallas kernels  129 us (35%)
  waiting for transfers between devices  94.6 us (25%)
  starting transfers between devices  83.3 us (22%)
  other arithmetic  34.5 us (9%)
  local copies, waits for them, and re-layouts  22.8 us (6%)
    pallas_call x14, Pallas kernels, call(): pl.pallas_call(body, out_shape=[jax.ShapeDtypeStruct(shape, kind) for sha...  129 us
    ppermute x77, waiting for transfers between devices, flip(): return lax.ppermute(value, axis, pairs)  94.6 us
    ppermute x77, starting transfers between devices, flip(): return lax.ppermute(value, axis, pairs)  83.3 us
    unnamed x145, local copies, waits for them, and re-layouts  13.5 us
    select_n x20, other arithmetic, pick(): return jnp.where(flag == 1, when_one, when_zero)  9.04 us
  transfers between devices with their start and end apart: 77, of which 30 were waited for; matrix products, arithmetic and copies ran while one was open for 8% of the time, Pallas kernels for 35%

profile of v5, /device:TPU:0, one launch (start us, length us, event | category | flops | bytes accessed | tf_op | source)
XLA Modules:
  0.0 367.4 jit_solution(10002193668306825895)
XLA Ops:
  4.0 3.0 collective-permute-start.2
  7.0 3.6 collective-permute-start
  10.6 1.5 collective-permute-start.3
  13.8 2.2 collective-permute-done.3
  16.8 3.1 collective-permute-done.1.refs_2_
  21.0 1.6 collective-permute-start.4
  22.6 2.5 collective-permute-start.7
  26.4 10.5 %collective-permute-done.8 = bf16[288,256]{1,0:T(8,128)(2,1)S(1)} collective-permute-done((bf16[288,256]{1,0:T(8,128)(2,1)S(1)}, bf16[288,256]{1,0:T(8,128)(2,1)S(1)}, u32[]{:S(2)}, u32[]{:S(2)}) %collective-permute-start.8) | collective-permute-done | bytes 147488 | tf_op jit(solution)/shard_map/ppermute | solution.py:36
  39.8 1.5 collective-permute-start.9
  41.4 2.9 collective-permute-start.11
  44.3 2.6 collective-permute-start.12
  46.9 4.8 %collective-permute-done.11 = bf16[2,288,256]{2,1,0:T(8,128)(2,1)} collective-permute-done((bf16[2,288,256]{2,1,0:T(8,128)(2,1)S(1)}, bf16[2,288,256]{2,1,0:T(8,128)(2,1)}, u32[]{:S(2)}, u32[]{:S(2)}) %collective-permute-start.11) | collective-permute-done | bytes 294944 | tf_op jit(solution)/shard_map/ppermute | solution.py:36
  51.7 8.5 %collective-permute-done.12 = bf16[576,256]{1,0:T(8,128)(2,1)} collective-permute-done((bf16[576,256]{1,0:T(8,128)(2,1)}, bf16[576,256]{1,0:T(8,128)(2,1)}, u32[]{:S(2)}, u32[]{:S(2)}) %collective-permute-start.12) | collective-permute-done | bytes 294944 | tf_op jit(solution)/shard_map/ppermute | solution.py:36
  60.3 1.9 pad_maximum_fusion.7
  62.2 2.9 collective-permute-start.18
  65.1 1.7 pad_maximum_fusion.13
  66.8 1.5 collective-permute-start.17
  68.3 1.8 slice.396
  70.6 1.8 slice.397
  72.4 1.5 collective-permute-start.15
  77.7 7.0 %collective-permute-done.14.refs_12_.refs_8_.refs_10_ = bf16[2,400,256]{2,1,0:T(8,128)(2,1)} collective-permute-done((bf16[2,400,256]{2,1,0:T(8,128)(2,1)}, bf16[2,400,256]{2,1,0:T(8,128)(2,1)}, u32[]{:S(2)}, u32[]{:S(2)}) %collective-permute-start.14) | collective-permute-done | bytes 409632 | tf_op jit(solution)/shard_map/ppermute | solution.py:36
  86.6 2.7 collective-permute-start.21
  89.4 1.6 collective-permute-start.19
  91.0 1.4 collective-permute-start.20
  99.7 9.3 %shard_map.239 = (bf16[1024,1024]{1,0:T(8,128)(2,1)S(1)}, bf16[1024,1024]{1,0:T(8,128)(2,1)S(1)}, bf16[1024,512]{1,0:T(8,128)(2,1)S(1)}, bf16[1024,512]{1,0:T(8,...) custom-call(s32[6]{0:T(128)S(1)} %stack.139.refs_0_.info, bf16[2,256,1024]{2,1,0:T(8,128)(2,1)S(1)} %copy-done.5, ...), custom_call_target="tpu_custom_call" | custom-call | flops 3221225472 | bytes 14680064 | tf_op jit(solution)/shard_map/pallas_call | solution.py:52
  109.1 1.5 collective-permute-done.22.refs_14_
  114.4 1.6 collective-permute-start.26
  118.2 13.8 %shard_map.241 = (bf16[1024,512]{1,0:T(8,128)(2,1)S(1)}, f32[4,2,1024]{2,1,0:T(2,128)S(1)}) custom-call(bf16[1024,512]{1,0:T(8,128)(2,1)S(1)} %get-tuple-element.551.q, bf16[1024,512]{1,0:T(8,128)(2,1)S(1)} %get-tuple-element.552.k, bf16[1024,512]{1,0:T(8,128)(2,1)S(1)} %get-tuple-element.553.b), custom_call_target="tpu_custom_call" | custom-call | flops 2147483648 | bytes 4194304 | tf_op jit(solution)/shard_map/pallas_call | solution.py:52
  134.0 1.8 collective-permute-done.25.refs_6_.refs_20_.refs_14_
  138.6 2.1 shard_map.242.refs_2_.refs_4_
  140.8 2.3 collective-permute-done.30.refs_10_
  143.0 1.8 collective-permute-done.31.refs_11_
  144.8 3.8 %collective-permute-done.29.refs_6_ = bf16[256,1024]{1,0:T(8,128)(2,1)S(1)} collective-permute-done((bf16[256,1024]{1,0:T(8,128)(2,1)S(1)}, bf16[256,1024]{1,0:T(8,128)(2,1)S(1)}, u32[]{:S(2)}, u32[]{:S(2)}) %collective-permute-start.29) | collective-permute-done | bytes 524320 | tf_op jit(solution)/shard_map/ppermute | solution.py:36
  149.3 4.9 %collective-permute-done.33.refs_7_ = bf16[2,256,1024]{2,1,0:T(8,128)(2,1)S(1)} collective-permute-done((bf16[2,256,1024]{2,1,0:T(8,128)(2,1)S(1)}, bf16[2,256,1024]{2,1,0:T(8,128)(2,1)S(1)}, u32[]{:S(2)}, u32[]{:S(2)}) %collective-permute-start.33) | collective-permute-done | bytes 1048608 | tf_op jit(solution)/shard_map/ppermute | solution.py:36
  156.3 1.5 collective-permute-start.36
  158.3 23.8 %shard_map.243 = (bf16[1024,1024]{1,0:T(8,128)(2,1)S(1)}, bf16[1024,1024]{1,0:T(8,128)(2,1)}, bf16[1024,1024]{1,0:T(8,128)(2,1)}, bf16[1024,1024]{1,0:T(8,128)(2...) custom-call(s32[6]{0:T(128)S(1)} %stack.139.refs_0_.info, ...), custom_call_target="tpu_custom_call" | custom-call | flops 12079595520 | bytes 25165824 | tf_op jit(solution)/shard_map/pallas_call | solution.py:52
  183.7 1.5 collective-permute-start.38
  185.9 26.8 %shard_map.244 = (bf16[1024,1024]{1,0:T(8,128)(2,1)S(1)}, f32[2,256,1024]{2,1,0:T(8,128)}, bf16[2,256,1024]{2,1,0:T(8,128)(2,1)}, bf16[4,384,256]{2,1,0:T(8,128)...) custom-call(s32[6]{0:T(128)S(1)} %stack.139.refs_0_.info, ...), custom_call_target="tpu_custom_call" | custom-call | flops 14495514624 | bytes 25165824 | tf_op jit(solution)/shard_map/pallas_call | solution.py:52
  220.6 13.6 %shard_map.245 = (bf16[1024,512]{1,0:T(8,128)(2,1)}, f32[2,256,1024]{2,1,0:T(8,128)}, f32[8,1024]{1,0:T(8,128)}, bf16[4,320,256]{2,1,0:T(8,128)(2,1)}, bf16[4,32...) custom-call(s32[6]{0:T(128)} %copy-done.30, ...), custom_call_target="tpu_custom_call" | custom-call | flops 2147483648 | bytes 20971520 | tf_op jit(solution)/shard_map/pallas_call | solution.py:52
  235.2 4.4 %fusion.1 = bf16[2,256,1024]{2,1,0:T(8,128)(2,1)S(1)} fusion(f32[2,256,1024]{2,1,0:T(8,128)} %get-tuple-element.549, bf16[2,256,1024]{2,1,0:T(8,128)(2,1)} %collective-permute-done.44, bf16[2,2,256,1024]{3,2,1,0:T(8,128)(2,1)} %bitcast.21, bf16[2,2,256,1024]{3,2,1,0:T(8,128)(2,1)S(1)} %bitcast.187, bf16[2,2,256,1024]{3,2,1,0:T(8,128)(2,1)S(1)} %bitcast.188, ...), kind=kLoop, calls=%fused_computation.3 | loop fusion | flops 6815744 | bytes 10485765 | tf_op jit(solution)/shard_map/convert_element_type | solution.py:871
  241.2 1.7 convert_add_fusion.1
  243.4 1.6 collective-permute-start.45
  248.4 9.4 %shard_map.246 = (bf16[1024,256]{1,0:T(8,128)(2,1)S(1)}, bf16[1024,256]{1,0:T(8,128)(2,1)S(1)}, bf16[1024,256]{1,0:T(8,128)(2,1)S(1)}) custom-call(bf16[1024,512]{1,0:T(8,128)(2,1)S(1)} %copy-done.47, bf16[1024,512]{1,0:T(8,128)(2,1)S(1)} %copy-done.49, bf16[1024,512]{1,0:T(8,128)(2,1)S(1)} %copy-done.51, bf16[1024,512]{1,0:T(8,128)(2,1)S(1)} %copy-done.34, ...), custom_call_target="tpu_custom_call" | custom-call | flops 2684354560 | bytes 4194304 | tf_op jit(solution)/shard_map/pallas_call | solution.py:52
  257.8 5.2 %shard_map.247 = (bf16[2,400,256]{2,1,0:T(8,128)(2,1)S(1)}, bf16[4,400,256]{2,1,0:T(8,128)(2,1)S(1)}, bf16[2,400,256]{2,1,0:T(8,128)(2,1)S(1)}) custom-call(s32[6]{0:T(128)S(1)} %copy-done.31, bf16[1024,256]{1,0:T(8,128)(2,1)S(1)} %get-tuple-element.583.refs_1_.refs_4_, bf16[1024,256]{1,0:T(8,128)(2,1)S(1)} %get-tuple-element.584.refs_2_.refs_5_, ...), custom_call_target="tpu_custom_call" | custom-call | flops 1610612736 | bytes 7340032 | tf_op jit(solution)/shard_map/pallas_call | solution.py:52
  263.1 7.6 %collective-permute-done.47 = bf16[2,384,256]{2,1,0:T(8,128)(2,1)S(1)} collective-permute-done((bf16[2,384,256]{2,1,0:T(8,128)(2,1)S(1)}, bf16[2,384,256]{2,1,0:T(8,128)(2,1)S(1)}, u32[]{:S(2)}, u32[]{:S(2)}) %collective-permute-start.47) | collective-permute-done | bytes 393248 | tf_op jit(solution)/shard_map/ppermute | solution.py:36
  273.9 2.7 collective-permute-start.54
  277.5 9.4 %shard_map.248 = (bf16[1024,256]{1,0:T(8,128)(2,1)S(1)}, bf16[1024,256]{1,0:T(8,128)(2,1)S(1)}, bf16[1024,256]{1,0:T(8,128)(2,1)S(1)}) custom-call(bf16[1024,512]{1,0:T(8,128)(2,1)S(1)} %copy-done.47, bf16[1024,512]{1,0:T(8,128)(2,1)S(1)} %copy-done.49, bf16[1024,512]{1,0:T(8,128)(2,1)S(1)} %copy-done.51, bf16[1024,512]{1,0:T(8,128)(2,1)S(1)} %copy-done.34, ...), custom_call_target="tpu_custom_call" | custom-call | flops 2684354560 | bytes 4194304 | tf_op jit(solution)/shard_map/pallas_call | solution.py:52
  287.0 6.0 %shard_map.249 = (bf16[2,400,256]{2,1,0:T(8,128)(2,1)S(1)}, bf16[2,400,256]{2,1,0:T(8,128)(2,1)S(1)}, bf16[4,400,256]{2,1,0:T(8,128)(2,1)S(1)}) custom-call(s32[6]{0:T(128)S(1)} %copy-done.31, bf16[1024,256]{1,0:T(8,128)(2,1)S(1)} %get-tuple-element.580.refs_1_, bf16[1024,256]{1,0:T(8,128)(2,1)S(1)} %get-tuple-element.581.refs_2_, ...), custom_call_target="tpu_custom_call" | custom-call | flops 1610612736 | bytes 7340032 | tf_op jit(solution)/shard_map/pallas_call | solution.py:52
  297.7 1.7 collective-permute-start.57
  299.4 8.0 %shard_map.250 = (f32[2,256,1024]{2,1,0:T(8,128)S(1)}, bf16[2,256,1024]{2,1,0:T(8,128)(2,1)S(1)}) custom-call(s32[6]{0:T(128)S(1)} %copy-done.31, bf16[1024,256]{1,0:T(8,128)(2,1)S(1)} %get-tuple-element.580.refs_1_, bf16[1024,256]{1,0:T(8,128)(2,1)S(1)} %get-tuple-element.581.refs_2_, bf16[1024,256]{1,0:T(8,128)(2,1)S(1)} %get-tuple-element.639.refs_3_, ...), custom_call_target="tpu_custom_call" | custom-call | flops 3221225472 | bytes 14680064 | tf_op jit(solution)/shard_map/pallas_call | solution.py:52
  307.4 3.5 collective-permute-done.59
  311.1 1.6 collective-permute-start.64
  317.7 1.6 shard_map.251
  319.3 5.9 %collective-permute-done.62 = bf16[2,400,256]{2,1,0:T(8,128)(2,1)S(1)} collective-permute-done((bf16[2,400,256]{2,1,0:T(8,128)(2,1)S(1)}, bf16[2,400,256]{2,1,0:T(8,128)(2,1)S(1)}, u32[]{:S(2)}, u32[]{:S(2)}) %collective-permute-start.62) | collective-permute-done | bytes 409632 | tf_op jit(solution)/shard_map/ppermute | solution.py:36
  326.4 2.1 collective-permute-start.65
  333.1 4.0 %collective-permute-done.65 = bf16[400,256]{1,0:T(8,128)(2,1)S(1)} collective-permute-done((bf16[400,256]{1,0:T(8,128)(2,1)S(1)}, bf16[400,256]{1,0:T(8,128)(2,1)S(1)}, u32[]{:S(2)}, u32[]{:S(2)}) %collective-permute-start.65) | collective-permute-done | bytes 204832 | tf_op jit(solution)/shard_map/ppermute | solution.py:36
  337.1 5.2 %collective-permute-done.67 = bf16[256,1024]{1,0:T(8,128)(2,1)S(1)} collective-permute-done((bf16[256,1024]{1,0:T(8,128)(2,1)S(1)}, bf16[256,1024]{1,0:T(8,128)(2,1)S(1)}, u32[]{:S(2)}, u32[]{:S(2)}) %collective-permute-start.67) | collective-permute-done | bytes 524320 | tf_op jit(solution)/shard_map/ppermute | solution.py:36
  342.9 1.6 collective-permute-start.70
  345.8 2.4 collective-permute-start.69
  348.3 1.5 maximum_select_fusion
  349.8 3.1 collective-permute-done.70
  352.9 4.3 %collective-permute-done.69 = bf16[400,256]{1,0:T(8,128)(2,1)S(1)} collective-permute-done((bf16[400,256]{1,0:T(8,128)(2,1)S(1)}, bf16[400,256]{1,0:T(8,128)(2,1)S(1)}, u32[]{:S(2)}, u32[]{:S(2)}) %collective-permute-start.69) | collective-permute-done | bytes 204832 | tf_op jit(solution)/shard_map/ppermute | solution.py:36
  357.2 2.9 collective-permute-done.71
  363.4 1.6 fusion.5
  (354 shorter events, 81.6 us)
Async XLA Ops:
  4.0 15.9 %collective-permute-start.2 = (bf16[256,1024]{1,0:T(8,128)(2,1)S(1)}, bf16[256,1024]{1,0:T(8,128)(2,1)S(1)}, u32[]{:S(2)}, u32[]{:S(2)}) collective-permute-start(bf16[256,1024]{1,0:T(8,128)(2,1)S(1)} %select_bitcast_fusion.6), channel_id=1, source_target_pairs={{0,16},{8,24},{16,0},{24,8},{1,17},{9,25},{17,1},{25,9},{2,18},{10... | collective-permute-start | bytes 1572872 | tf_op jit(solution)/shard_map/ppermute | solution.py:36
  7.0 9.8 %collective-permute-start = (bf16[400,256]{1,0:T(8,128)(2,1)S(1)}, bf16[400,256]{1,0:T(8,128)(2,1)S(1)}, u32[]{:S(2)}, u32[]{:S(2)}) collective-permute-start(bf16[400,256]{1,0:T(8,128)(2,1)S(1)} %fusion.26.refs_0_), channel_id=1, source_target_pairs={{0,6},{1,7},{2,4},{3,5},{4,2},{5,3},{6,0},{7,1},{8,14},{9,15},{10,... | collective-permute-start | bytes 614408 | tf_op jit(solution)/shard_map/ppermute | solution.py:36
  10.6 9.3 %collective-permute-start.1 = (bf16[400,256]{1,0:T(8,128)(2,1)S(1)}, bf16[400,256]{1,0:T(8,128)(2,1)S(1)}, u32[]{:S(2)}, u32[]{:S(2)}) collective-permute-start(bf16[400,256]{1,0:T(8,128)(2,1)S(1)} %fusion.26.refs_0_), channel_id=1, source_target_pairs={{0,2},{1,3},{2,0},{3,1},{4,6},{5,7},{6,4},{7,5},{8,10},{9,11},{10,... | collective-permute-start | bytes 614408 | tf_op jit(solution)/shard_map/ppermute | solution.py:36
  20.1 16.9 %collective-permute-start.6 = (bf16[2,256,1024]{2,1,0:T(8,128)(2,1)S(1)}, bf16[2,256,1024]{2,1,0:T(8,128)(2,1)S(1)}, u32[]{:S(2)}, u32[]{:S(2)}) collective-permute-start(bf16[2,256,1024]{2,1,0:T(8,128)(2,1)S(1)} %pad_maximum_fusion.3), channel_id=1, source_target_pairs={{0,8},{8,0},{16,24},{24,16},{1,9},{9,1},{17,25},{25,17},{2,10},{10... | collective-permute-start | bytes 3145736 | tf_op jit(solution)/shard_map/ppermute | solution.py:36
  20.2 16.8 %collective-permute-start.5 = (bf16[256,1024]{1,0:T(8,128)(2,1)S(1)}, bf16[256,1024]{1,0:T(8,128)(2,1)S(1)}, u32[]{:S(2)}, u32[]{:S(2)}) collective-permute-start(bf16[256,1024]{1,0:T(8,128)(2,1)S(1)} %get-tuple-element.345), channel_id=1, source_target_pairs={{0,16},{8,24},{16,0},{24,8},{1,17},{9,25},{17,1},{25,9},{2,18},{10... | collective-permute-start | bytes 1572872 | tf_op jit(solution)/shard_map/ppermute | solution.py:36
  21.0 16.0 %collective-permute-start.4 = (bf16[400,256]{1,0:T(8,128)(2,1)S(1)}, bf16[400,256]{1,0:T(8,128)(2,1)S(1)}, u32[]{:S(2)}, u32[]{:S(2)}) collective-permute-start(bf16[400,256]{1,0:T(8,128)(2,1)S(1)} %collective-permute-done.refs_1_), channel_id=1, source_target_pairs={{0,2},{1,3},{2,0},{3,1},{4,6},{5,7},{6,4},{7,5},{8,10},{9,11},{10,... | collective-permute-start | bytes 614408 | tf_op jit(solution)/shard_map/ppermute | solution.py:36
  22.6 14.4 %collective-permute-start.7 = (bf16[1,320,256]{2,1,0:T(8,128)(2,1)S(1)}, bf16[1,320,256]{2,1,0:T(8,128)(2,1)S(1)}, u32[]{:S(2)}, u32[]{:S(2)}) collective-permute-start(bf16[1,320,256]{2,1,0:T(8,128)(2,1)S(1)} %fusion.38.refs_8_), channel_id=1, source_target_pairs={{0,6},{1,7},{2,4},{3,5},{4,2},{5,3},{6,0},{7,1},{8,14},{9,15},{10,... | collective-permute-start | bytes 491528 | tf_op jit(solution)/shard_map/ppermute | solution.py:36
  25.1 11.9 %collective-permute-start.8 = (bf16[288,256]{1,0:T(8,128)(2,1)S(1)}, bf16[288,256]{1,0:T(8,128)(2,1)S(1)}, u32[]{:S(2)}, u32[]{:S(2)}) collective-permute-start(bf16[288,256]{1,0:T(8,128)(2,1)S(1)} %pad_maximum_fusion.19), channel_id=1, source_target_pairs={{0,6},{1,7},{2,4},{3,5},{4,2},{5,3},{6,0},{7,1},{8,14},{9,15},{10,... | collective-permute-start | bytes 442376 | tf_op jit(solution)/shard_map/ppermute | solution.py:36
  39.2 21.1 %collective-permute-start.13 = (bf16[2,256,1024]{2,1,0:T(8,128)(2,1)}, bf16[2,256,1024]{2,1,0:T(8,128)(2,1)}, u32[]{:S(2)}, u32[]{:S(2)}) collective-permute-start(bf16[2,256,1024]{2,1,0:T(8,128)(2,1)} %pad_maximum_fusion.4), channel_id=1, source_target_pairs={{0,8},{8,0},{16,24},{24,16},{1,9},{9,1},{17,25},{25,17},{2,10},{10... | collective-permute-start | bytes 3145736 | tf_op jit(solution)/shard_map/ppermute | solution.py:36
  39.3 20.9 %collective-permute-start.10 = (bf16[4,400,256]{2,1,0:T(8,128)(2,1)S(1)}, bf16[4,400,256]{2,1,0:T(8,128)(2,1)}, u32[]{:S(2)}, u32[]{:S(2)}) collective-permute-start(bf16[4,400,256]{2,1,0:T(8,128)(2,1)S(1)} %shard_map.238.refs_9_.refs_7_), channel_id=1, source_target_pairs={{0,16},{8,24},{16,0},{24,8},{1,17},{9,25},{17,1},{25,9},{2,18},{10... | collective-permute-start | bytes 2457608 | tf_op jit(solution)/shard_map/ppermute | solution.py:36
  39.8 20.5 %collective-permute-start.9 = (bf16[4,400,256]{2,1,0:T(8,128)(2,1)S(1)}, bf16[4,400,256]{2,1,0:T(8,128)(2,1)}, u32[]{:S(2)}, u32[]{:S(2)}) collective-permute-start(bf16[4,400,256]{2,1,0:T(8,128)(2,1)S(1)} %shard_map.238.refs_9_.refs_7_), channel_id=1, source_target_pairs={{0,1},{1,0},{2,3},{3,2},{4,5},{5,4},{6,7},{7,6},{8,9},{9,8},{10,11... | collective-permute-start | bytes 2457608 | tf_op jit(solution)/shard_map/ppermute | solution.py:36
  41.4 10.3 %collective-permute-start.11 = (bf16[2,288,256]{2,1,0:T(8,128)(2,1)S(1)}, bf16[2,288,256]{2,1,0:T(8,128)(2,1)}, u32[]{:S(2)}, u32[]{:S(2)}) collective-permute-start(bf16[2,288,256]{2,1,0:T(8,128)(2,1)S(1)} %pad_maximum_fusion.14), channel_id=1, source_target_pairs={{0,2},{1,3},{2,0},{3,1},{4,6},{5,7},{6,4},{7,5},{8,10},{9,11},{10,... | collective-permute-start | bytes 884744 | tf_op jit(solution)/shard_map/ppermute | solution.py:36
  44.3 15.9 %collective-permute-start.12 = (bf16[576,256]{1,0:T(8,128)(2,1)}, bf16[576,256]{1,0:T(8,128)(2,1)}, u32[]{:S(2)}, u32[]{:S(2)}) collective-permute-start(bf16[576,256]{1,0:T(8,128)(2,1)} %fusion.24), channel_id=1, source_target_pairs={{0,6},{1,7},{2,4},{3,5},{4,2},{5,3},{6,0},{7,1},{8,14},{9,15},{10,... | collective-permute-start | bytes 884744 | tf_op jit(solution)/shard_map/ppermute | solution.py:36
  62.2 22.5 %collective-permute-start.18 = (bf16[2,576,256]{2,1,0:T(8,128)(2,1)}, bf16[2,576,256]{2,1,0:T(8,128)(2,1)}, u32[]{:S(2)}, u32[]{:S(2)}) collective-permute-start(bf16[2,576,256]{2,1,0:T(8,128)(2,1)} %pad_maximum_fusion.7), channel_id=1, source_target_pairs={{0,2},{1,3},{2,0},{3,1},{4,6},{5,7},{6,4},{7,5},{8,10},{9,11},{10,... | collective-permute-start | bytes 1769480 | tf_op jit(solution)/shard_map/ppermute | solution.py:36
  66.8 11.0 %collective-permute-start.17 = (bf16[2,320,256]{2,1,0:T(8,128)(2,1)}, bf16[2,320,256]{2,1,0:T(8,128)(2,1)}, u32[]{:S(2)}, u32[]{:S(2)}) collective-permute-start(bf16[2,320,256]{2,1,0:T(8,128)(2,1)} %pad_maximum_fusion.13), channel_id=1, source_target_pairs={{0,16},{8,24},{16,0},{24,8},{1,17},{9,25},{17,1},{25,9},{2,18},{10... | collective-permute-start | bytes 983048 | tf_op jit(solution)/shard_map/ppermute | solution.py:36
  70.1 14.6 %collective-permute-start.14 = (bf16[2,400,256]{2,1,0:T(8,128)(2,1)}, bf16[2,400,256]{2,1,0:T(8,128)(2,1)}, u32[]{:S(2)}, u32[]{:S(2)}) collective-permute-start(bf16[2,400,256]{2,1,0:T(8,128)(2,1)} %slice.396), channel_id=1, source_target_pairs={{0,16},{8,24},{16,0},{24,8},{1,17},{9,25},{17,1},{25,9},{2,18},{10... | collective-permute-start | bytes 1228808 | tf_op jit(solution)/shard_map/ppermute | solution.py:36
  72.4 12.3 %collective-permute-start.15 = (bf16[2,400,256]{2,1,0:T(8,128)(2,1)}, bf16[2,400,256]{2,1,0:T(8,128)(2,1)}, u32[]{:S(2)}, u32[]{:S(2)}) collective-permute-start(bf16[2,400,256]{2,1,0:T(8,128)(2,1)} %slice.397), channel_id=1, source_target_pairs={{0,1},{1,0},{2,3},{3,2},{4,5},{5,4},{6,7},{7,6},{8,9},{9,8},{10,11... | collective-permute-start | bytes 1228808 | tf_op jit(solution)/shard_map/ppermute | solution.py:36
  86.6 22.4 %collective-permute-start.21 = (bf16[3,320,256]{2,1,0:T(8,128)(2,1)S(1)}, bf16[3,320,256]{2,1,0:T(8,128)(2,1)S(1)}, u32[]{:S(2)}, u32[]{:S(2)}) collective-permute-start(bf16[3,320,256]{2,1,0:T(8,128)(2,1)S(1)} %constant_dynamic-update-slice_fusion.refs_12_), channel_id=1, source_target_pairs={{0,6},{1,7},{2,4},{3,5},{4,2},{5,3},{6,0},{7,1},{8,14},{9,15},{10,... | collective-permute-start | bytes 1474568 | tf_op jit(solution)/shard_map/ppermute | solution.py:36
  89.3 21.2 %collective-permute-start.22 = (bf16[3,320,256]{2,1,0:T(8,128)(2,1)S(1)}, bf16[3,320,256]{2,1,0:T(8,128)(2,1)S(1)}, u32[]{:S(2)}, u32[]{:S(2)}) collective-permute-start(bf16[3,320,256]{2,1,0:T(8,128)(2,1)S(1)} %constant_dynamic-update-slice_fusion.refs_12_), channel_id=1, source_target_pairs={{0,2},{1,3},{2,0},{3,1},{4,6},{5,7},{6,4},{7,5},{8,10},{9,11},{10,... | collective-permute-start | bytes 1474568 | tf_op jit(solution)/shard_map/ppermute | solution.py:36
  89.4 21.2 %collective-permute-start.19 = (bf16[4,288,256]{2,1,0:T(8,128)(2,1)S(1)}, bf16[4,288,256]{2,1,0:T(8,128)(2,1)S(1)}, u32[]{:S(2)}, u32[]{:S(2)}) collective-permute-start(bf16[4,288,256]{2,1,0:T(8,128)(2,1)S(1)} %shard_map.240.refs_2_.refs_16_.refs_10_), channel_id=1, source_target_pairs={{0,1},{1,0},{2,3},{3,2},{4,5},{5,4},{6,7},{7,6},{8,9},{9,8},{10,11... | collective-permute-start | bytes 1769480 | tf_op jit(solution)/shard_map/ppermute | solution.py:36
  91.0 19.6 %collective-permute-start.20 = (bf16[4,288,256]{2,1,0:T(8,128)(2,1)S(1)}, bf16[4,288,256]{2,1,0:T(8,128)(2,1)S(1)}, u32[]{:S(2)}, u32[]{:S(2)}) collective-permute-start(bf16[4,288,256]{2,1,0:T(8,128)(2,1)S(1)} %shard_map.240.refs_2_.refs_16_.refs_10_), channel_id=1, source_target_pairs={{0,16},{8,24},{16,0},{24,8},{1,17},{9,25},{17,1},{25,9},{2,18},{10... | collective-permute-start | bytes 1769480 | tf_op jit(solution)/shard_map/ppermute | solution.py:36
  94.3 14.7 %collective-permute-start.23 = (bf16[2,192,256]{2,1,0:T(8,128)(2,1)S(1)}, bf16[2,192,256]{2,1,0:T(8,128)(2,1)S(1)}, u32[]{:S(2)}, u32[]{:S(2)}) collective-permute-start(bf16[2,192,256]{2,1,0:T(8,128)(2,1)S(1)} %pad_maximum_fusion.18), channel_id=1, source_target_pairs={{0,8},{8,0},{16,24},{24,16},{1,9},{9,1},{17,25},{25,17},{2,10},{10... | collective-permute-start | bytes 589832 | tf_op jit(solution)/shard_map/ppermute | solution.py:36
  111.9 23.9 %collective-permute-start.27 = (bf16[2,576,256]{2,1,0:T(8,128)(2,1)S(1)}, bf16[2,576,256]{2,1,0:T(8,128)(2,1)S(1)}, u32[]{:S(2)}, u32[]{:S(2)}) collective-permute-start(bf16[2,576,256]{2,1,0:T(8,128)(2,1)S(1)} %pad_maximum_fusion.9.refs_9_), channel_id=1, source_target_pairs={{0,16},{8,24},{16,0},{24,8},{1,17},{9,25},{17,1},{25,9},{2,18},{10... | collective-permute-start | bytes 1769480 | tf_op jit(solution)/shard_map/ppermute | solution.py:36
  114.4 21.4 %collective-permute-start.26 = (bf16[2,576,256]{2,1,0:T(8,128)(2,1)S(1)}, bf16[2,576,256]{2,1,0:T(8,128)(2,1)S(1)}, u32[]{:S(2)}, u32[]{:S(2)}) collective-permute-start(bf16[2,576,256]{2,1,0:T(8,128)(2,1)S(1)} %pad_maximum_fusion.8.refs_5_), channel_id=1, source_target_pairs={{0,1},{1,0},{2,3},{3,2},{4,5},{5,4},{6,7},{7,6},{8,9},{9,8},{10,11... | collective-permute-start | bytes 1769480 | tf_op jit(solution)/shard_map/ppermute | solution.py:36
  116.0 19.8 %collective-permute-start.28 = (bf16[3,320,256]{2,1,0:T(8,128)(2,1)S(1)}, bf16[3,320,256]{2,1,0:T(8,128)(2,1)S(1)}, u32[]{:S(2)}, u32[]{:S(2)}) collective-permute-start(bf16[3,320,256]{2,1,0:T(8,128)(2,1)S(1)} %collective-permute-done.21.refs_13_), channel_id=1, source_target_pairs={{0,2},{1,3},{2,0},{3,1},{4,6},{5,7},{6,4},{7,5},{8,10},{9,11},{10,... | collective-permute-start | bytes 1474568 | tf_op jit(solution)/shard_map/ppermute | solution.py:36
  116.8 17.2 %collective-permute-start.24 = (bf16[2,288,256]{2,1,0:T(8,128)(2,1)S(1)}, bf16[2,288,256]{2,1,0:T(8,128)(2,1)S(1)}, u32[]{:S(2)}, u32[]{:S(2)}) collective-permute-start(bf16[2,288,256]{2,1,0:T(8,128)(2,1)S(1)} %slice.406), channel_id=1, source_target_pairs={{0,16},{8,24},{16,0},{24,8},{1,17},{9,25},{17,1},{25,9},{2,18},{10... | collective-permute-start | bytes 884744 | tf_op jit(solution)/shard_map/ppermute | solution.py:36
  117.6 18.2 %collective-permute-start.25 = (bf16[2,288,256]{2,1,0:T(8,128)(2,1)S(1)}, bf16[2,288,256]{2,1,0:T(8,128)(2,1)S(1)}, u32[]{:S(2)}, u32[]{:S(2)}) collective-permute-start(bf16[2,288,256]{2,1,0:T(8,128)(2,1)S(1)} %slice.407), channel_id=1, source_target_pairs={{0,1},{1,0},{2,3},{3,2},{4,5},{5,4},{6,7},{7,6},{8,9},{9,8},{10,11... | collective-permute-start | bytes 884744 | tf_op jit(solution)/shard_map/ppermute | solution.py:36
  135.8 12.7 %collective-permute-start.29 = (bf16[256,1024]{1,0:T(8,128)(2,1)S(1)}, bf16[256,1024]{1,0:T(8,128)(2,1)S(1)}, u32[]{:S(2)}, u32[]{:S(2)}) collective-permute-start(bf16[256,1024]{1,0:T(8,128)(2,1)S(1)} %copy-done.62), channel_id=1, source_target_pairs={{0,16},{8,24},{16,0},{24,8},{1,17},{9,25},{17,1},{25,9},{2,18},{10... | collective-permute-start | bytes 1572872 | tf_op jit(solution)/shard_map/ppermute | solution.py:36
  137.7 7.1 %collective-permute-start.31 = (bf16[1,320,256]{2,1,0:T(8,128)(2,1)S(1)}, bf16[1,320,256]{2,1,0:T(8,128)(2,1)S(1)}, u32[]{:S(2)}, u32[]{:S(2)}) collective-permute-start(bf16[1,320,256]{2,1,0:T(8,128)(2,1)S(1)} %copy-done.38), channel_id=1, source_target_pairs={{0,2},{1,3},{2,0},{3,1},{4,6},{5,7},{6,4},{7,5},{8,10},{9,11},{10,... | collective-permute-start | bytes 491528 | tf_op jit(solution)/shard_map/ppermute | solution.py:36
  154.2 29.2 %collective-permute-start.34 = (bf16[2,576,256]{2,1,0:T(8,128)(2,1)S(1)}, bf16[2,576,256]{2,1,0:T(8,128)(2,1)S(1)}, u32[]{:S(2)}, u32[]{:S(2)}) collective-permute-start(bf16[2,576,256]{2,1,0:T(8,128)(2,1)S(1)} %pad_maximum_fusion.8.refs_5_), channel_id=1, source_target_pairs={{0,16},{8,24},{16,0},{24,8},{1,17},{9,25},{17,1},{25,9},{2,18},{10... | collective-permute-start | bytes 1769480 | tf_op jit(solution)/shard_map/ppermute | solution.py:36
  155.0 28.5 %collective-permute-start.35 = (bf16[2,576,256]{2,1,0:T(8,128)(2,1)S(1)}, bf16[2,576,256]{2,1,0:T(8,128)(2,1)S(1)}, u32[]{:S(2)}, u32[]{:S(2)}) collective-permute-start(bf16[2,576,256]{2,1,0:T(8,128)(2,1)S(1)} %collective-permute-done.26.refs_6_), channel_id=1, source_target_pairs={{0,16},{8,24},{16,0},{24,8},{1,17},{9,25},{17,1},{25,9},{2,18},{10... | collective-permute-start | bytes 1769480 | tf_op jit(solution)/shard_map/ppermute | solution.py:36
  156.3 27.2 %collective-permute-start.36 = (bf16[2,576,256]{2,1,0:T(8,128)(2,1)S(1)}, bf16[2,576,256]{2,1,0:T(8,128)(2,1)S(1)}, u32[]{:S(2)}, u32[]{:S(2)}) collective-permute-start(bf16[2,576,256]{2,1,0:T(8,128)(2,1)S(1)} %pad_maximum_fusion.9.refs_9_), channel_id=1, source_target_pairs={{0,1},{1,0},{2,3},{3,2},{4,5},{5,4},{6,7},{7,6},{8,9},{9,8},{10,11... | collective-permute-start | bytes 1769480 | tf_op jit(solution)/shard_map/ppermute | solution.py:36
  157.8 26.0 %collective-permute-start.37 = (bf16[2,576,256]{2,1,0:T(8,128)(2,1)S(1)}, bf16[2,576,256]{2,1,0:T(8,128)(2,1)S(1)}, u32[]{:S(2)}, u32[]{:S(2)}) collective-permute-start(bf16[2,576,256]{2,1,0:T(8,128)(2,1)S(1)} %collective-permute-done.27.refs_11_), channel_id=1, source_target_pairs={{0,1},{1,0},{2,3},{3,2},{4,5},{5,4},{6,7},{7,6},{8,9},{9,8},{10,11... | collective-permute-start | bytes 1769480 | tf_op jit(solution)/shard_map/ppermute | solution.py:36
  183.7 31.0 %collective-permute-start.38 = (bf16[4,480,256]{2,1,0:T(8,128)(2,1)S(1)}, bf16[4,480,256]{2,1,0:T(8,128)(2,1)S(1)}, u32[]{:S(2)}, u32[]{:S(2)}) collective-permute-start(bf16[4,480,256]{2,1,0:T(8,128)(2,1)S(1)} %get-tuple-element.494), channel_id=1, source_target_pairs={{0,1},{1,0},{2,3},{3,2},{4,5},{5,4},{6,7},{7,6},{8,9},{9,8},{10,11... | collective-permute-start | bytes 2949128 | tf_op jit(solution)/shard_map/ppermute | solution.py:36
  185.2 29.6 %collective-permute-start.39 = (bf16[4,480,256]{2,1,0:T(8,128)(2,1)S(1)}, bf16[4,480,256]{2,1,0:T(8,128)(2,1)S(1)}, u32[]{:S(2)}, u32[]{:S(2)}) collective-permute-start(bf16[4,480,256]{2,1,0:T(8,128)(2,1)S(1)} %get-tuple-element.495), channel_id=1, source_target_pairs={{0,16},{8,24},{16,0},{24,8},{1,17},{9,25},{17,1},{25,9},{2,18},{10... | collective-permute-start | bytes 2949128 | tf_op jit(solution)/shard_map/ppermute | solution.py:36
  214.9 20.3 %collective-permute-start.44 = (bf16[2,256,1024]{2,1,0:T(8,128)(2,1)}, bf16[2,256,1024]{2,1,0:T(8,128)(2,1)}, u32[]{:S(2)}, u32[]{:S(2)}) collective-permute-start(bf16[2,256,1024]{2,1,0:T(8,128)(2,1)} %get-tuple-element.522), channel_id=1, source_target_pairs={{0,8},{8,0},{16,24},{24,16},{1,9},{9,1},{17,25},{25,17},{2,10},{10... | collective-permute-start | bytes 3145736 | tf_op jit(solution)/shard_map/ppermute | solution.py:36
  215.4 19.8 %collective-permute-start.43 = (bf16[4,384,256]{2,1,0:T(8,128)(2,1)}, bf16[4,384,256]{2,1,0:T(8,128)(2,1)}, u32[]{:S(2)}, u32[]{:S(2)}) collective-permute-start(bf16[4,384,256]{2,1,0:T(8,128)(2,1)} %get-tuple-element.520), channel_id=1, source_target_pairs={{0,2},{1,3},{2,0},{3,1},{4,6},{5,7},{6,4},{7,5},{8,10},{9,11},{10,... | collective-permute-start | bytes 2359304 | tf_op jit(solution)/shard_map/ppermute | solution.py:36
  216.9 17.4 %collective-permute-start.42 = (bf16[2,480,256]{2,1,0:T(8,128)(2,1)}, bf16[2,480,256]{2,1,0:T(8,128)(2,1)S(1)}, u32[]{:S(2)}, u32[]{:S(2)}) collective-permute-start(bf16[2,480,256]{2,1,0:T(8,128)(2,1)} %add_convert_fusion.1), channel_id=1, source_target_pairs={{0,16},{8,24},{16,0},{24,8},{1,17},{9,25},{17,1},{25,9},{2,18},{10... | collective-permute-start | bytes 1474568 | tf_op jit(solution)/shard_map/ppermute | solution.py:36
  219.0 15.3 %collective-permute-start.41 = (bf16[2,480,256]{2,1,0:T(8,128)(2,1)}, bf16[2,480,256]{2,1,0:T(8,128)(2,1)}, u32[]{:S(2)}, u32[]{:S(2)}) collective-permute-start(bf16[2,480,256]{2,1,0:T(8,128)(2,1)} %add_convert_fusion.2), channel_id=1, source_target_pairs={{0,1},{1,0},{2,3},{3,2},{4,5},{5,4},{6,7},{7,6},{8,9},{9,8},{10,11... | collective-permute-start | bytes 1474568 | tf_op jit(solution)/shard_map/ppermute | solution.py:36
  239.8 31.0 %collective-permute-start.50 = (bf16[256,1024]{1,0:T(8,128)(2,1)S(1)}, bf16[256,1024]{1,0:T(8,128)(2,1)S(1)}, u32[]{:S(2)}, u32[]{:S(2)}) collective-permute-start(bf16[256,1024]{1,0:T(8,128)(2,1)S(1)} %get-tuple-element.680), channel_id=1, source_target_pairs={{0,16},{8,24},{16,0},{24,8},{1,17},{9,25},{17,1},{25,9},{2,18},{10... | collective-permute-start | bytes 1572872 | tf_op jit(solution)/shard_map/ppermute | solution.py:36
  243.1 28.4 %collective-permute-start.48 = (bf16[4,384,256]{2,1,0:T(8,128)(2,1)S(1)}, bf16[4,384,256]{2,1,0:T(8,128)(2,1)S(1)}, u32[]{:S(2)}, u32[]{:S(2)}) collective-permute-start(bf16[4,384,256]{2,1,0:T(8,128)(2,1)S(1)} %copy-done.36), channel_id=1, source_target_pairs={{0,2},{1,3},{2,0},{3,1},{4,6},{5,7},{6,4},{7,5},{8,10},{9,11},{10,... | collective-permute-start | bytes 2359304 | tf_op jit(solution)/shard_map/ppermute | solution.py:36
  243.4 27.3 %collective-permute-start.45 = (bf16[4,320,256]{2,1,0:T(8,128)(2,1)S(1)}, bf16[4,320,256]{2,1,0:T(8,128)(2,1)S(1)}, u32[]{:S(2)}, u32[]{:S(2)}) collective-permute-start(bf16[4,320,256]{2,1,0:T(8,128)(2,1)S(1)} %copy-done.71), channel_id=1, source_target_pairs={{0,1},{1,0},{2,3},{3,2},{4,5},{5,4},{6,7},{7,6},{8,9},{9,8},{10,11... | collective-permute-start | bytes 1966088 | tf_op jit(solution)/shard_map/ppermute | solution.py:36
  245.0 25.8 %collective-permute-start.46 = (bf16[4,320,256]{2,1,0:T(8,128)(2,1)S(1)}, bf16[4,320,256]{2,1,0:T(8,128)(2,1)S(1)}, u32[]{:S(2)}, u32[]{:S(2)}) collective-permute-start(bf16[4,320,256]{2,1,0:T(8,128)(2,1)S(1)} %copy-done.70), channel_id=1, source_target_pairs={{0,16},{8,24},{16,0},{24,8},{1,17},{9,25},{17,1},{25,9},{2,18},{10... | collective-permute-start | bytes 1966088 | tf_op jit(solution)/shard_map/ppermute | solution.py:36
  247.2 23.6 %collective-permute-start.47 = (bf16[2,384,256]{2,1,0:T(8,128)(2,1)S(1)}, bf16[2,384,256]{2,1,0:T(8,128)(2,1)S(1)}, u32[]{:S(2)}, u32[]{:S(2)}) collective-permute-start(bf16[2,384,256]{2,1,0:T(8,128)(2,1)S(1)} %slice.494), channel_id=1, source_target_pairs={{0,6},{1,7},{2,4},{3,5},{4,2},{5,3},{6,0},{7,1},{8,14},{9,15},{10,... | collective-permute-start | bytes 1179656 | tf_op jit(solution)/shard_map/ppermute | solution.py:36
  271.7 21.7 %collective-permute-start.55 = (bf16[2,480,256]{2,1,0:T(8,128)(2,1)S(1)}, bf16[2,480,256]{2,1,0:T(8,128)(2,1)S(1)}, u32[]{:S(2)}, u32[]{:S(2)}) collective-permute-start(bf16[2,480,256]{2,1,0:T(8,128)(2,1)S(1)} %pad_maximum_fusion.11), channel_id=1, source_target_pairs={{0,2},{1,3},{2,0},{3,1},{4,6},{5,7},{6,4},{7,5},{8,10},{9,11},{10,... | collective-permute-start | bytes 1474568 | tf_op jit(solution)/shard_map/ppermute | solution.py:36
  271.8 21.7 %collective-permute-start.51 = (bf16[4,400,256]{2,1,0:T(8,128)(2,1)S(1)}, bf16[4,400,256]{2,1,0:T(8,128)(2,1)S(1)}, u32[]{:S(2)}, u32[]{:S(2)}) collective-permute-start(bf16[4,400,256]{2,1,0:T(8,128)(2,1)S(1)} %get-tuple-element.564), channel_id=1, source_target_pairs={{0,16},{8,24},{16,0},{24,8},{1,17},{9,25},{17,1},{25,9},{2,18},{10... | collective-permute-start | bytes 2457608 | tf_op jit(solution)/shard_map/ppermute | solution.py:36
  273.2 19.9 %collective-permute-start.53 = (bf16[2,320,256]{2,1,0:T(8,128)(2,1)S(1)}, bf16[2,320,256]{2,1,0:T(8,128)(2,1)S(1)}, u32[]{:S(2)}, u32[]{:S(2)}) collective-permute-start(bf16[2,320,256]{2,1,0:T(8,128)(2,1)S(1)} %add_convert_fusion.7), channel_id=1, source_target_pairs={{0,1},{1,0},{2,3},{3,2},{4,5},{5,4},{6,7},{7,6},{8,9},{9,8},{10,11... | collective-permute-start | bytes 983048 | tf_op jit(solution)/shard_map/ppermute | solution.py:36
  273.9 19.6 %collective-permute-start.54 = (bf16[2,384,256]{2,1,0:T(8,128)(2,1)S(1)}, bf16[2,384,256]{2,1,0:T(8,128)(2,1)S(1)}, u32[]{:S(2)}, u32[]{:S(2)}) collective-permute-start(bf16[2,384,256]{2,1,0:T(8,128)(2,1)S(1)} %slice.430), channel_id=1, source_target_pairs={{0,6},{1,7},{2,4},{3,5},{4,2},{5,3},{6,0},{7,1},{8,14},{9,15},{10,... | collective-permute-start | bytes 1179656 | tf_op jit(solution)/shard_map/ppermute | solution.py:36
  276.6 16.9 %collective-permute-start.52 = (bf16[2,400,256]{2,1,0:T(8,128)(2,1)S(1)}, bf16[2,400,256]{2,1,0:T(8,128)(2,1)S(1)}, u32[]{:S(2)}, u32[]{:S(2)}) collective-permute-start(bf16[2,400,256]{2,1,0:T(8,128)(2,1)S(1)} %get-tuple-element.565), channel_id=1, source_target_pairs={{0,1},{1,0},{2,3},{3,2},{4,5},{5,4},{6,7},{7,6},{8,9},{9,8},{10,11... | collective-permute-start | bytes 1228808 | tf_op jit(solution)/shard_map/ppermute | solution.py:36
  293.8 17.1 %collective-permute-start.58 = (bf16[2,384,256]{2,1,0:T(8,128)(2,1)S(1)}, bf16[2,384,256]{2,1,0:T(8,128)(2,1)S(1)}, u32[]{:S(2)}, u32[]{:S(2)}) collective-permute-start(bf16[2,384,256]{2,1,0:T(8,128)(2,1)S(1)} %get-tuple-element.673), channel_id=1, source_target_pairs={{0,16},{8,24},{16,0},{24,8},{1,17},{9,25},{17,1},{25,9},{2,18},{10... | collective-permute-start | bytes 1179656 | tf_op jit(solution)/shard_map/ppermute | solution.py:36
  295.2 15.7 %collective-permute-start.56 = (bf16[2,400,256]{2,1,0:T(8,128)(2,1)S(1)}, bf16[2,400,256]{2,1,0:T(8,128)(2,1)S(1)}, u32[]{:S(2)}, u32[]{:S(2)}) collective-permute-start(bf16[2,400,256]{2,1,0:T(8,128)(2,1)S(1)} %get-tuple-element.591), channel_id=1, source_target_pairs={{0,1},{1,0},{2,3},{3,2},{4,5},{5,4},{6,7},{7,6},{8,9},{9,8},{10,11... | collective-permute-start | bytes 1228808 | tf_op jit(solution)/shard_map/ppermute | solution.py:36
  296.3 14.6 %collective-permute-start.59 = (bf16[2,320,256]{2,1,0:T(8,128)(2,1)S(1)}, bf16[2,320,256]{2,1,0:T(8,128)(2,1)S(1)}, u32[]{:S(2)}, u32[]{:S(2)}) collective-permute-start(bf16[2,320,256]{2,1,0:T(8,128)(2,1)S(1)} %add_convert_fusion.6), channel_id=1, source_target_pairs={{0,16},{8,24},{16,0},{24,8},{1,17},{9,25},{17,1},{25,9},{2,18},{10... | collective-permute-start | bytes 983048 | tf_op jit(solution)/shard_map/ppermute | solution.py:36
  297.7 9.7 %collective-permute-start.57 = (bf16[480,256]{1,0:T(8,128)(2,1)S(1)}, bf16[480,256]{1,0:T(8,128)(2,1)S(1)}, u32[]{:S(2)}, u32[]{:S(2)}) collective-permute-start(bf16[480,256]{1,0:T(8,128)(2,1)S(1)} %get-tuple-element.697), channel_id=1, source_target_pairs={{0,6},{1,7},{2,4},{3,5},{4,2},{5,3},{6,0},{7,1},{8,14},{9,15},{10,... | collective-permute-start | bytes 737288 | tf_op jit(solution)/shard_map/ppermute | solution.py:36
  311.1 8.2 %collective-permute-start.64 = (bf16[384,256]{1,0:T(8,128)(2,1)S(1)}, bf16[384,256]{1,0:T(8,128)(2,1)S(1)}, u32[]{:S(2)}, u32[]{:S(2)}) collective-permute-start(bf16[384,256]{1,0:T(8,128)(2,1)S(1)} %fusion.29), channel_id=1, source_target_pairs={{0,1},{1,0},{2,3},{3,2},{4,5},{5,4},{6,7},{7,6},{8,9},{9,8},{10,11... | collective-permute-start | bytes 589832 | tf_op jit(solution)/shard_map/ppermute | solution.py:36
  313.7 11.5 %collective-permute-start.62 = (bf16[2,400,256]{2,1,0:T(8,128)(2,1)S(1)}, bf16[2,400,256]{2,1,0:T(8,128)(2,1)S(1)}, u32[]{:S(2)}, u32[]{:S(2)}) collective-permute-start(bf16[2,400,256]{2,1,0:T(8,128)(2,1)S(1)} %add_convert_fusion.3), channel_id=1, source_target_pairs={{0,16},{8,24},{16,0},{24,8},{1,17},{9,25},{17,1},{25,9},{2,18},{10... | collective-permute-start | bytes 1228808 | tf_op jit(solution)/shard_map/ppermute | solution.py:36
  314.6 11.2 %collective-permute-start.61 = (bf16[2,400,256]{2,1,0:T(8,128)(2,1)S(1)}, bf16[2,400,256]{2,1,0:T(8,128)(2,1)S(1)}, u32[]{:S(2)}, u32[]{:S(2)}) collective-permute-start(bf16[2,400,256]{2,1,0:T(8,128)(2,1)S(1)} %add_convert_fusion.4), channel_id=1, source_target_pairs={{0,1},{1,0},{2,3},{3,2},{4,5},{5,4},{6,7},{7,6},{8,9},{9,8},{10,11... | collective-permute-start | bytes 1228808 | tf_op jit(solution)/shard_map/ppermute | solution.py:36
  326.1 7.1 %collective-permute-start.66 = (bf16[320,256]{1,0:T(8,128)(2,1)S(1)}, bf16[320,256]{1,0:T(8,128)(2,1)S(1)}, u32[]{:S(2)}, u32[]{:S(2)}) collective-permute-start(bf16[320,256]{1,0:T(8,128)(2,1)S(1)} %fusion.34), channel_id=1, source_target_pairs={{0,2},{1,3},{2,0},{3,1},{4,6},{5,7},{6,4},{7,5},{8,10},{9,11},{10,... | collective-permute-start | bytes 491528 | tf_op jit(solution)/shard_map/ppermute | solution.py:36
  326.4 10.7 %collective-permute-start.65 = (bf16[400,256]{1,0:T(8,128)(2,1)S(1)}, bf16[400,256]{1,0:T(8,128)(2,1)S(1)}, u32[]{:S(2)}, u32[]{:S(2)}) collective-permute-start(bf16[400,256]{1,0:T(8,128)(2,1)S(1)} %fusion.27), channel_id=1, source_target_pairs={{0,2},{1,3},{2,0},{3,1},{4,6},{5,7},{6,4},{7,5},{8,10},{9,11},{10,... | collective-permute-start | bytes 614408 | tf_op jit(solution)/shard_map/ppermute | solution.py:36
  328.5 13.8 %collective-permute-start.67 = (bf16[256,1024]{1,0:T(8,128)(2,1)S(1)}, bf16[256,1024]{1,0:T(8,128)(2,1)S(1)}, u32[]{:S(2)}, u32[]{:S(2)}) collective-permute-start(bf16[256,1024]{1,0:T(8,128)(2,1)S(1)} %get-tuple-element.637), channel_id=1, source_target_pairs={{0,16},{8,24},{16,0},{24,8},{1,17},{9,25},{17,1},{25,9},{2,18},{10... | collective-permute-start | bytes 1572872 | tf_op jit(solution)/shard_map/ppermute | solution.py:36
  342.4 7.4 %collective-permute-start.72 = (bf16[320,256]{1,0:T(8,128)(2,1)S(1)}, bf16[320,256]{1,0:T(8,128)(2,1)S(1)}, u32[]{:S(2)}, u32[]{:S(2)}) collective-permute-start(bf16[320,256]{1,0:T(8,128)(2,1)S(1)} %fusion.35), channel_id=1, source_target_pairs={{0,2},{1,3},{2,0},{3,1},{4,6},{5,7},{6,4},{7,5},{8,10},{9,11},{10,... | collective-permute-start | bytes 491528 | tf_op jit(solution)/shard_map/ppermute | solution.py:36
  342.9 10.0 %collective-permute-start.70 = (bf16[320,256]{1,0:T(8,128)(2,1)S(1)}, bf16[320,256]{1,0:T(8,128)(2,1)S(1)}, u32[]{:S(2)}, u32[]{:S(2)}) collective-permute-start(bf16[320,256]{1,0:T(8,128)(2,1)S(1)} %fusion.17), channel_id=1, source_target_pairs={{0,6},{1,7},{2,4},{3,5},{4,2},{5,3},{6,0},{7,1},{8,14},{9,15},{10,... | collective-permute-start | bytes 491528 | tf_op jit(solution)/shard_map/ppermute | solution.py:36
  344.5 15.6 %collective-permute-start.73 = (bf16[256,1024]{1,0:T(8,128)(2,1)S(1)}, bf16[256,1024]{1,0:T(8,128)(2,1)S(1)}, u32[]{:S(2)}, u32[]{:S(2)}) collective-permute-start(bf16[256,1024]{1,0:T(8,128)(2,1)S(1)} %get-tuple-element.649), channel_id=1, source_target_pairs={{0,16},{8,24},{16,0},{24,8},{1,17},{9,25},{17,1},{25,9},{2,18},{10... | collective-permute-start | bytes 1572872 | tf_op jit(solution)/shard_map/ppermute | solution.py:36
  345.8 11.4 %collective-permute-start.69 = (bf16[400,256]{1,0:T(8,128)(2,1)S(1)}, bf16[400,256]{1,0:T(8,128)(2,1)S(1)}, u32[]{:S(2)}, u32[]{:S(2)}) collective-permute-start(bf16[400,256]{1,0:T(8,128)(2,1)S(1)} %fusion.12), channel_id=1, source_target_pairs={{0,6},{1,7},{2,4},{3,5},{4,2},{5,3},{6,0},{7,1},{8,14},{9,15},{10,... | collective-permute-start | bytes 614408 | tf_op jit(solution)/shard_map/ppermute | solution.py:36
  348.2 11.9 %collective-permute-start.71 = (bf16[400,256]{1,0:T(8,128)(2,1)S(1)}, bf16[400,256]{1,0:T(8,128)(2,1)S(1)}, u32[]{:S(2)}, u32[]{:S(2)}) collective-permute-start(bf16[400,256]{1,0:T(8,128)(2,1)S(1)} %fusion.28), channel_id=1, source_target_pairs={{0,2},{1,3},{2,0},{3,1},{4,6},{5,7},{6,4},{7,5},{8,10},{9,11},{10,... | collective-permute-start | bytes 614408 | tf_op jit(solution)/shard_map/ppermute | solution.py:36
  (88 other events, 950.8 us)
